TPU v7x, 32 devices: a whole 2x2x4 slice. The times are simulated.
32 devices in a mesh: dp: 4 (over z), seq: 8 (over y, x, core).
Axes of the slice: x: 2, y: 2, z: 4, core: 2. Of those that a mesh axis runs over, the one named last changes fastest.
Arguments:
- tokens: bfloat16 [8, 1024, 768], P('dp', 'seq'), may hold values from -6 to 6
- cotangent: bfloat16 [8, 1024, 768], P('dp', 'seq'), may hold values from -6 to 6
- token_docs: int32 [8, 1024], P('dp', 'seq'), may hold values from -1 to 3, as said below
- segment_docs: int32 [8, 8], P('dp'), may hold values from 0 to 3, as said below
- segment_positions: int32 [8, 8], P('dp', 'seq'), may hold values from 0 to 7, as said below
- local_mix: bfloat16 [768, 2304], P(('dp', 'seq')), may hold values from -0.21875 to 0.21875
- local_out: bfloat16 [768, 768], P(('dp', 'seq')), may hold values from -0.625 to 0.625
- local_up: bfloat16 [768, 3072], P(('dp', 'seq')), may hold values from -0.21875 to 0.21875
- local_down: bfloat16 [3072, 768], P(('dp', 'seq')), may hold values from -0.109375 to 0.109375
- local_vectors: bfloat16 [8, 768], P(None, ('dp', 'seq'))
- local_up_bias: bfloat16 [3072], P(('dp', 'seq')), may hold values from -3 to 3
- cross_mix: bfloat16 [768, 2304], P(('dp', 'seq')), may hold values from -0.21875 to 0.21875
- cross_out: bfloat16 [768, 768], P(('dp', 'seq')), may hold values from -0.4375 to 0.4375
- cross_up: bfloat16 [768, 3072], P(('dp', 'seq')), may hold values from -0.21875 to 0.21875
- cross_down: bfloat16 [3072, 768], P(('dp', 'seq')), may hold values from -0.109375 to 0.109375
- cross_vectors: bfloat16 [8, 768], P(None, ('dp', 'seq'))
- cross_up_bias: bfloat16 [3072], P(('dp', 'seq')), may hold values from -3 to 3
- position_table: bfloat16 [64, 768], P(None, ('dp', 'seq')), may hold values from -3 to 3
Outputs:
- layer_out: bfloat16 [8, 1024, 768], P('dp', 'seq')
- input_grad: float32 [8, 1024, 768], P('dp', 'seq')
- local_mix_grad: float32 [768, 2304], P(('dp', 'seq'))
- local_out_grad: float32 [768, 768], P(('dp', 'seq'))
- local_up_grad: float32 [768, 3072], P(('dp', 'seq'))
- local_down_grad: float32 [3072, 768], P(('dp', 'seq'))
- local_vectors_grad: float32 [8, 768], P(None, ('dp', 'seq'))
- local_up_bias_grad: float32 [3072], P(('dp', 'seq'))
- cross_mix_grad: float32 [768, 2304], P(('dp', 'seq'))
- cross_out_grad: float32 [768, 768], P(('dp', 'seq'))
- cross_up_grad: float32 [768, 3072], P(('dp', 'seq'))
- cross_down_grad: float32 [3072, 768], P(('dp', 'seq'))
- cross_vectors_grad: float32 [8, 768], P(None, ('dp', 'seq'))
- cross_up_bias_grad: float32 [3072], P(('dp', 'seq'))
- position_table_grad: float32 [64, 768], P(None, ('dp', 'seq'))
Inputs may be any that keep to these rules, and one draw needn't show every extreme that they name: `token_docs`: each segment of 128 tokens belongs to one document: its live tokens carry that document's number and the padding at the end of a document's last segment carries -1; a document's last segment holds 72 to 128 live tokens, every other segment is full, and every segment's first token is live. `segment_docs`: the document number of each segment, equal to token_docs of its first token; in each sequence the numbers start at 0 and rise by one at each new document; every document but a sequence's last covers two segments or more. `segment_positions`: a segment's place within its document, counted from 0; a document covers at most 16 segments.
All inputs are finite; a program needn't handle non-finite values.
Results may differ from a plain program's by a relative error of at most 0.02.
Values may be sent and summed in bfloat16 or wider, within the bound.
No kernel may reach another device: no remote copies, remote signals or barrier semaphores. Data moves between devices by JAX's collectives and lax.ppermute only.
A program may use at most 320 MiB of HBM per device.

v0:
```python
from functools import partial
import math

import jax
import jax.numpy as jnp
from jax import lax
from jax.sharding import PartitionSpec as P

D = 768
HEADS = 12
HEAD_DIM = 64
SEG = 128
MICRO = 2


epsilon = 1e-05
masked_score = -1000000000.0
owner_dims = (0, 0, 0, 0, 1, 0, 0, 0, 0, 0, 1, 0, 1)


def layer_norm(values, gain_row, shift_row):
    centered = values - jnp.mean(values, axis=-1, keepdims=True)
    variance = jnp.mean(centered * centered, axis=-1, keepdims=True)
    return centered * lax.rsqrt(variance + epsilon) * gain_row + shift_row


def gelu_exact(hidden):
    return jax.nn.gelu(hidden, approximate=False)


def contract(left_side, right_side, left_dim, right_dim):
    return lax.dot_general(
        left_side,
        right_side,
        (((left_dim,), (right_dim,)), ((), ())),
        preferred_element_type=jnp.float32,
    )


def contract_exact(left_side, right_side, left_dim, right_dim):
    return lax.dot_general(
        left_side,
        right_side,
        (((left_dim,), (right_dim,)), ((), ())),
        precision=lax.Precision.HIGHEST,
        preferred_element_type=jnp.float32,
    )


def owner_pack(grads, devices):
    pieces = []
    for grad_value, split_dim in zip(grads, owner_dims):
        if split_dim == 0:
            pieces.append(grad_value.reshape(devices, -1))
        else:
            row_count = grad_value.shape[0]
            pieces.append(
                grad_value.reshape(row_count, devices, -1).transpose(1, 0, 2).reshape(devices, -1)
            )
    return jnp.concatenate(pieces, axis=1)


def owner_unpack(packed, shard_shapes):
    results = []
    offset = 0
    for shard_shape in shard_shapes:
        length = math.prod(shard_shape)
        results.append(packed[0, offset : offset + length].reshape(shard_shape))
        offset = offset + length
    return tuple(results)


def fetch_weights(
    local_mix,
    local_out,
    local_up,
    local_down,
    local_vectors,
    local_up_bias,
    cross_mix,
    cross_out,
    cross_up,
    cross_down,
    cross_vectors,
    cross_up_bias,
    position_table,
):
    return (
        lax.all_gather(local_mix, ("dp", "seq"), axis=0, tiled=True),
        lax.all_gather(local_out, ("dp", "seq"), axis=0, tiled=True),
        lax.all_gather(local_up, ("dp", "seq"), axis=0, tiled=True),
        lax.all_gather(local_down, ("dp", "seq"), axis=0, tiled=True),
        lax.all_gather(local_vectors, ("dp", "seq"), axis=1, tiled=True),
        lax.all_gather(local_up_bias, ("dp", "seq"), axis=0, tiled=True),
        lax.all_gather(cross_mix, ("dp", "seq"), axis=0, tiled=True),
        lax.all_gather(cross_out, ("dp", "seq"), axis=0, tiled=True),
        lax.all_gather(cross_up, ("dp", "seq"), axis=0, tiled=True),
        lax.all_gather(cross_down, ("dp", "seq"), axis=0, tiled=True),
        lax.all_gather(cross_vectors, ("dp", "seq"), axis=1, tiled=True),
        lax.all_gather(cross_up_bias, ("dp", "seq"), axis=0, tiled=True),
        lax.all_gather(position_table, ("dp", "seq"), axis=1, tiled=True),
    )


def segment_parts(mixed_rows, token_docs):
    segment_count = token_docs.shape[0]
    split_heads = mixed_rows.reshape(segment_count, SEG, 3, HEADS, HEAD_DIM)
    allowed = token_docs[:, None, :, None] == token_docs[:, None, None, :]
    scores = jnp.einsum(
        "nqhd,nkhd->nhqk",
        split_heads[:, :, 0],
        split_heads[:, :, 1],
        preferred_element_type=jnp.float32,
    ) * HEAD_DIM ** (-0.5)
    scores = jnp.where(allowed, scores, masked_score)
    return (split_heads, scores)


def segment_forward(mixed_rows, token_docs):
    split_heads, scores = segment_parts(mixed_rows, token_docs)
    log_total = jax.nn.logsumexp(scores, axis=-1)
    weights = jax.nn.softmax(scores, axis=-1).astype(jnp.bfloat16)
    context = jnp.einsum(
        "nhqk,nkhd->nqhd", weights, split_heads[:, :, 2], preferred_element_type=jnp.float32
    )
    return (context.reshape(-1, D).astype(jnp.bfloat16), log_total)


def segment_backward(context_grad, log_total, mixed_rows, token_docs):
    split_heads, scores = segment_parts(mixed_rows, token_docs)
    segment_count = token_docs.shape[0]
    probs = jnp.exp(scores - log_total[..., None])
    grad_heads = context_grad.reshape(segment_count, SEG, HEADS, HEAD_DIM)
    prob_grad = jnp.einsum(
        "nqhd,nkhd->nhqk", grad_heads, split_heads[:, :, 2], preferred_element_type=jnp.float32
    )
    value_grad = jnp.einsum(
        "nhqk,nqhd->nkhd",
        probs.astype(jnp.bfloat16),
        grad_heads,
        preferred_element_type=jnp.float32,
    )
    score_grad = probs * (prob_grad - jnp.sum(probs * prob_grad, axis=-1, keepdims=True))
    score_low = score_grad.astype(jnp.bfloat16) * HEAD_DIM ** (-0.5)
    query_grad = jnp.einsum(
        "nhqk,nkhd->nqhd", score_low, split_heads[:, :, 1], preferred_element_type=jnp.float32
    )
    key_grad = jnp.einsum(
        "nhqk,nqhd->nkhd", score_low, split_heads[:, :, 0], preferred_element_type=jnp.float32
    )
    row_total = segment_count * SEG
    return jnp.concatenate(
        [
            query_grad.reshape(row_total, D),
            key_grad.reshape(row_total, D),
            value_grad.reshape(row_total, D),
        ],
        axis=1,
    )


def cross_parts(mixed_rows, gathered, segment_docs):
    group_size = segment_docs.shape[0]
    per_device = mixed_rows.shape[0] // group_size
    query_rows = mixed_rows[:, :D].reshape(group_size, per_device, HEADS, HEAD_DIM)
    key_rows = gathered[:, :, :D].reshape(group_size, -1, HEADS, HEAD_DIM)
    value_rows = gathered[:, :, D:].reshape(group_size, -1, HEADS, HEAD_DIM)
    own_docs = lax.dynamic_slice_in_dim(
        segment_docs, lax.axis_index("seq") * per_device, per_device, 1
    )
    allowed = own_docs[:, None, :, None] == segment_docs[:, None, None, :]
    scores = jnp.einsum(
        "bqhd,bkhd->bhqk", query_rows, key_rows, preferred_element_type=jnp.float32
    ) * HEAD_DIM ** (-0.5)
    scores = jnp.where(allowed, scores, masked_score)
    return (query_rows, key_rows, value_rows, scores)


def cross_forward(mixed_rows, segment_docs):
    group_size = segment_docs.shape[0]
    per_device = mixed_rows.shape[0] // group_size
    pair_rows = mixed_rows[:, D:].reshape(group_size, per_device, 2 * D)
    gathered = lax.all_gather(pair_rows, "seq", axis=1, tiled=True)
    query_rows, key_rows, value_rows, scores = cross_parts(mixed_rows, gathered, segment_docs)
    log_total = jax.nn.logsumexp(scores, axis=-1)
    weights = jax.nn.softmax(scores, axis=-1).astype(jnp.bfloat16)
    context = jnp.einsum("bhqk,bkhd->bqhd", weights, value_rows, preferred_element_type=jnp.float32)
    return (context.reshape(-1, D).astype(jnp.bfloat16), (gathered, log_total))


def cross_backward(context_grad, cross_kept, mixed_rows, segment_docs):
    gathered, log_total = cross_kept
    group_size = segment_docs.shape[0]
    row_total = mixed_rows.shape[0]
    per_device = row_total // group_size
    query_rows, key_rows, value_rows, scores = cross_parts(mixed_rows, gathered, segment_docs)
    probs = jnp.exp(scores - log_total[..., None])
    grad_heads = context_grad.reshape(group_size, per_device, HEADS, HEAD_DIM)
    prob_grad = jnp.einsum(
        "bqhd,bkhd->bhqk", grad_heads, value_rows, preferred_element_type=jnp.float32
    )
    value_grad = jnp.einsum(
        "bhqk,bqhd->bkhd",
        probs.astype(jnp.bfloat16),
        grad_heads,
        preferred_element_type=jnp.float32,
    )
    score_grad = probs * (prob_grad - jnp.sum(probs * prob_grad, axis=-1, keepdims=True))
    score_low = score_grad.astype(jnp.bfloat16) * HEAD_DIM ** (-0.5)
    query_grad = jnp.einsum(
        "bhqk,bkhd->bqhd", score_low, key_rows, preferred_element_type=jnp.float32
    )
    key_grad = jnp.einsum(
        "bhqk,bqhd->bkhd", score_low, query_rows, preferred_element_type=jnp.float32
    )
    pair_grads = jnp.concatenate(
        [key_grad.reshape(group_size, -1, D), value_grad.reshape(group_size, -1, D)], axis=2
    )
    own_pairs = lax.psum_scatter(
        pair_grads.astype(jnp.bfloat16), "seq", scatter_dimension=1, tiled=True
    ).astype(jnp.float32)
    return jnp.concatenate(
        [query_grad.reshape(row_total, D), own_pairs.reshape(row_total, 2 * D)], axis=1
    )


def block_forward(inputs, weights, attend):
    mix_weight, out_weight, up_weight, down_weight, vectors, up_bias = weights
    vector_rows = vectors.astype(jnp.float32)
    in_bias = jnp.concatenate([vector_rows[0], jnp.zeros_like(vector_rows[0]), vector_rows[1]])
    rounded = inputs.astype(jnp.bfloat16)
    mixed_rows = (
        jnp.dot(rounded, mix_weight, preferred_element_type=jnp.float32) + in_bias
    ).astype(jnp.bfloat16)
    context, attend_kept = attend(mixed_rows)
    first_sum = (
        inputs + jnp.dot(context, out_weight, preferred_element_type=jnp.float32) + vector_rows[2]
    )
    first_norm = layer_norm(first_sum, vector_rows[3], vector_rows[4])
    first_low = first_norm.astype(jnp.bfloat16)
    hidden = jnp.dot(first_low, up_weight, preferred_element_type=jnp.float32) + up_bias.astype(
        jnp.float32
    )
    active = gelu_exact(hidden).astype(jnp.bfloat16)
    second_sum = (
        first_norm
        + jnp.dot(active, down_weight, preferred_element_type=jnp.float32)
        + vector_rows[5]
    )
    output = layer_norm(second_sum, vector_rows[6], vector_rows[7])
    return (
        output,
        (
            rounded,
            mixed_rows,
            attend_kept,
            context,
            first_sum,
            first_low,
            hidden,
            active,
            second_sum,
        ),
    )


def block_backward(output_grad, block_kept, weights, attend_back):
    mix_weight, out_weight, up_weight, down_weight, vectors, up_bias = weights
    vector_rows = vectors.astype(jnp.float32)
    rounded, mixed_rows, attend_kept, context, first_sum, first_low, hidden, active, second_sum = (
        block_kept
    )
    unused, second_pull = jax.vjp(layer_norm, second_sum, vector_rows[6], vector_rows[7])
    second_grad, gain_two, shift_two = second_pull(output_grad)
    second_low = second_grad.astype(jnp.bfloat16)
    down_grad = contract(active, second_low, 0, 0)
    down_bias = jnp.sum(second_low.astype(jnp.float32), axis=0)
    active_grad = contract(second_low, down_weight, 1, 1)
    unused, gelu_pull = jax.vjp(gelu_exact, hidden)
    hidden_grad = gelu_pull(active_grad)[0]
    hidden_low = hidden_grad.astype(jnp.bfloat16)
    up_grad = contract(first_low, hidden_low, 0, 0)
    up_bias_grad = jnp.sum(hidden_low.astype(jnp.float32), axis=0)
    first_grad = second_grad + contract(hidden_low, up_weight, 1, 1)
    unused, first_pull = jax.vjp(layer_norm, first_sum, vector_rows[3], vector_rows[4])
    sum_grad, gain_one, shift_one = first_pull(first_grad)
    branch_low = sum_grad.astype(jnp.bfloat16)
    out_grad = contract(context, branch_low, 0, 0)
    out_bias = jnp.sum(branch_low.astype(jnp.float32), axis=0)
    context_low = contract(branch_low, out_weight, 1, 1).astype(jnp.bfloat16)
    mixed_low = attend_back(context_low, attend_kept, mixed_rows).astype(jnp.bfloat16)
    mix_grad = contract(rounded, mixed_low, 0, 0)
    mixed_sums = jnp.sum(mixed_low.astype(jnp.float32), axis=0)
    input_grad = sum_grad + contract(mixed_low, mix_weight, 1, 1)
    vectors_grad = jnp.stack(
        [
            mixed_sums[:D],
            mixed_sums[2 * D :],
            out_bias,
            gain_one,
            shift_one,
            down_bias,
            gain_two,
            shift_two,
        ]
    )
    return (input_grad, (mix_grad, out_grad, up_grad, down_grad, vectors_grad, up_bias_grad))


def shards(
    tokens,
    cotangent,
    token_docs,
    segment_docs,
    segment_positions,
    local_mix,
    local_out,
    local_up,
    local_down,
    local_vectors,
    local_up_bias,
    cross_mix,
    cross_out,
    cross_up,
    cross_down,
    cross_vectors,
    cross_up_bias,
    position_table,
):
    sequence_count, span, width = tokens.shape
    group_size = sequence_count // MICRO
    segment_count = span // SEG
    devices = lax.axis_size(("dp", "seq"))
    shard_shapes = tuple(
        (
            array_in.shape
            for array_in in (
                local_mix,
                local_out,
                local_up,
                local_down,
                local_vectors,
                local_up_bias,
                cross_mix,
                cross_out,
                cross_up,
                cross_down,
                cross_vectors,
                cross_up_bias,
                position_table,
            )
        )
    )
    layer_outputs = []
    input_grads = []
    totals = ()
    for micro_step in range(MICRO):
        lower_row = micro_step * group_size
        upper_row = lower_row + group_size
        gathered = fetch_weights(
            local_mix,
            local_out,
            local_up,
            local_down,
            local_vectors,
            local_up_bias,
            cross_mix,
            cross_out,
            cross_up,
            cross_down,
            cross_vectors,
            cross_up_bias,
            position_table,
        )
        local_weights = gathered[0:6]
        cross_weights = gathered[6:12]
        position_rows = gathered[12]
        inputs = tokens[lower_row:upper_row].reshape(group_size * span, width).astype(jnp.float32)
        docs_here = token_docs[lower_row:upper_row]
        segments_here = segment_docs[lower_row:upper_row]
        first_out, first_kept = block_forward(
            inputs, local_weights, partial(segment_forward, token_docs=docs_here)
        )
        segment_grid = first_out.reshape(group_size * segment_count, SEG, width)
        places = segment_positions[lower_row:upper_row].reshape(group_size * segment_count)
        position_picks = (
            places[:, None] == jnp.arange(position_rows.shape[0], dtype=jnp.int32)[None, :]
        ).astype(jnp.bfloat16)
        heads_in = segment_grid[:, 0, :] + jnp.dot(
            position_picks, position_rows, preferred_element_type=jnp.float32
        )
        heads_out, cross_kept = block_forward(
            heads_in, cross_weights, partial(cross_forward, segment_docs=segments_here)
        )
        joined = jnp.concatenate([heads_out[:, None, :], segment_grid[:, 1:, :]], axis=1)
        layer_outputs.append(joined.astype(jnp.bfloat16))
        gathered = fetch_weights(
            local_mix,
            local_out,
            local_up,
            local_down,
            local_vectors,
            local_up_bias,
            cross_mix,
            cross_out,
            cross_up,
            cross_down,
            cross_vectors,
            cross_up_bias,
            position_table,
        )
        local_weights = gathered[0:6]
        cross_weights = gathered[6:12]
        output_grad = cotangent[lower_row:upper_row].astype(jnp.float32)
        heads_grad, cross_grads = block_backward(
            output_grad[:, 0, :],
            cross_kept,
            cross_weights,
            partial(cross_backward, segment_docs=segments_here),
        )
        table_grad = contract_exact(position_picks.astype(jnp.float32), heads_grad, 0, 0)
        first_grad = jnp.concatenate(
            [heads_grad[:, None, :], output_grad[:, 1:, :]], axis=1
        ).reshape(group_size * span, width)
        input_grad, local_grads = block_backward(
            first_grad, first_kept, local_weights, partial(segment_backward, token_docs=docs_here)
        )
        input_grads.append(input_grad.reshape(group_size, span, width))
        step_grads = local_grads + cross_grads + (table_grad,)
        if micro_step == 0:
            totals = tuple(step_grads)
        else:
            totals = tuple(
                (total_sum + step_sum for total_sum, step_sum in zip(totals, step_grads))
            )
    packed_total = lax.psum_scatter(
        owner_pack(totals, devices), ("dp", "seq"), scatter_dimension=0, tiled=True
    )
    summed = owner_unpack(packed_total, shard_shapes)
    layer_output = jnp.concatenate(layer_outputs, axis=0)
    input_gradient = jnp.concatenate(input_grads, axis=0)
    return (layer_output, input_gradient) + tuple(summed)


def solution(mesh):
    return jax.shard_map(
        shards,
        mesh=mesh,
        in_specs=(
            P("dp", "seq", None),
            P("dp", "seq", None),
            P("dp", "seq"),
            P("dp", None),
            P("dp", "seq"),
            P(("dp", "seq"), None),
            P(("dp", "seq"), None),
            P(("dp", "seq"), None),
            P(("dp", "seq"), None),
            P(None, ("dp", "seq")),
            P(("dp", "seq")),
            P(("dp", "seq"), None),
            P(("dp", "seq"), None),
            P(("dp", "seq"), None),
            P(("dp", "seq"), None),
            P(None, ("dp", "seq")),
            P(("dp", "seq")),
            P(None, ("dp", "seq")),
        ),
        out_specs=(
            P("dp", "seq", None),
            P("dp", "seq", None),
            P(("dp", "seq"), None),
            P(("dp", "seq"), None),
            P(("dp", "seq"), None),
            P(("dp", "seq"), None),
            P(None, ("dp", "seq")),
            P(("dp", "seq")),
            P(("dp", "seq"), None),
            P(("dp", "seq"), None),
            P(("dp", "seq"), None),
            P(("dp", "seq"), None),
            P(None, ("dp", "seq")),
            P(("dp", "seq")),
            P(None, ("dp", "seq")),
        ),
        check_vma=False,
    )
```

profile of v0, /device:TPU:0, one launch (start us, length us, event | category | flops | bytes accessed | tf_op | source)
XLA Modules:
  0.0 1765.6 jit_solution(7214784092006602842)
XLA Ops:
  14.9 44.0 %all_gather.36 = bf16[64,768]{0,1:T(8,128)(2,1)S(1)} all-gather(bf16[64,24]{0,1:T(8,128)(2,1)S(1)} %copy-done.159), channel_id=1, replica_groups=mesh['dp'=4,'seq'=8] {'dp','seq'}, dimensions={1}, use_global_device_ids=true | all-gather | bytes 101376 | tf_op jit(solution)/shard_map/all_gather | solution.py:101
  63.1 36.8 %all-gather.2 = bf16[32,24,8]{1,2,0:T(8,128)(2,1)S(1)} all-gather(bf16[1,24,8]{1,2,0:T(8,128)(2,1)S(1)} %bitcast.497), channel_id=1, replica_groups=mesh['dp'=4,'seq'=8] {'dp','seq'}, dimensions={0}, use_global_device_ids=true | all-gather | bytes 12672 | tf_op jit(solution)/shard_map/all_gather | solution.py:93
  100.9 37.4 %all-reduce.5 = (bf16[3072]{0:T(1024)(128)(2,1)S(1)}, bf16[3072]{0:T(1024)(128)(2,1)}) all-reduce(bf16[3072]{0:T(1024)(128)(2,1)S(1)} %dynamic-update-slice, bf16[3072]{0:T(1024)(128)(2,1)S(1)} %dynamic-update-slice.1), channel_id=1, replica_groups=mesh['dp'=4,'seq'=8] {'dp','seq'}, use_global_device_ids=true, to_apply=%add | all-reduce | flops 6144 | bytes 24576
  138.4 42.1 %all-gather.3 = bf16[32,24,8]{1,2,0:T(8,128)(2,1)S(1)} all-gather(bf16[1,24,8]{1,2,0:T(8,128)(2,1)S(1)} %bitcast.498), channel_id=1, replica_groups=mesh['dp'=4,'seq'=8] {'dp','seq'}, dimensions={0}, use_global_device_ids=true | all-gather | bytes 12672 | tf_op jit(solution)/shard_map/all_gather | solution.py:99
  201.3 8.7 multiply_convert_fusion.1
  210.0 51.0 %all-gather.21.cloned.1.call-done = bf16[3072,768]{1,0:T(8,128)(2,1)} async-done(((bf16[96,768]{1,0:T(8,128)(2,1)}), bf16[3072,768]{1,0:T(8,128)(2,1)}) %all-gather.21.cloned.1.call-update) | async-done | bytes 4718608 | tf_op jit(solution)/shard_map/all_gather | solution.py:92
  264.7 6.1 multiply_convert_fusion
  275.7 46.9 %all-gather.23.cloned.1.call-done = bf16[768,2304]{1,0:T(8,128)(2,1)} async-done(((bf16[24,2304]{1,0:T(8,128)(2,1)}), bf16[768,2304]{1,0:T(8,128)(2,1)}) %all-gather.23.cloned.1.call-update) | async-done | bytes 3538960 | tf_op jit(solution)/shard_map/all_gather | solution.py:95
  329.0 9.1 all-gather.5
  346.4 8.7 all-gather.4
  370.0 8.3 all-gather.25.cloned.1.call-done
  387.8 56.0 %all-gather.27.cloned.1.call-done = bf16[768,3072]{1,0:T(8,128)(2,1)} async-done(((bf16[24,3072]{1,0:T(8,128)(2,1)}), bf16[768,3072]{1,0:T(8,128)(2,1)}) %all-gather.27.cloned.1.call-update) | async-done | bytes 4718608 | tf_op jit(solution)/shard_map/all_gather | solution.py:97
  448.8 60.4 %all-gather.29.cloned.1.call-done = bf16[3072,768]{1,0:T(8,128)(2,1)} async-done(((bf16[96,768]{1,0:T(8,128)(2,1)}), bf16[3072,768]{1,0:T(8,128)(2,1)}) %all-gather.29.cloned.1.call-update) | async-done | bytes 4718608 | tf_op jit(solution)/shard_map/all_gather | solution.py:98
  608.2 25.1 %all-reduce.6 = (bf16[1,8,1536]{2,1,0:T(8,128)(2,1)}, bf16[1,8,1536]{2,1,0:T(8,128)(2,1)}) all-reduce(bf16[1,8,1536]{2,1,0:T(8,128)(2,1)} %pad_maximum_fusion.4, bf16[1,8,1536]{2,1,0:T(8,128)(2,1)} %pad_maximum_fusion.3), channel_id=5, replica_groups=mesh['dp'=4,'seq'=8] {'seq'}, use_global_device_ids=true, to_apply=%region_43.44.clone | all-reduce | flops 24576 | bytes 98304
  707.4 7.0 add_bitcast_fusion
  714.4 8.0 copy.125
  722.5 6.7 reshape.1696
  729.1 6.6 constant_dynamic-update-slice_fusion.35
  740.5 8.7 convolution_add_fusion.1
  749.2 8.2 reshape.1698
  757.4 8.8 convolution_add_fusion
  766.3 8.1 reshape.1699
  780.4 7.0 reshape.1701
  794.4 8.1 reshape.1703
  807.1 8.1 reshape.1704
  822.3 8.4 constant_dynamic-update-slice_fusion.33
  837.8 20.7 %dynamic-update-slice.8 = f32[32,444480]{1,0:T(8,128)} dynamic-update-slice(f32[32,444480]{1,0:T(8,128)} %dynamic-update-slice.7, f32[32,55296]{1,0:T(8,128)} %reshape.1701, s32[]{} %constant.286, s32[]{} %constant.292) | dynamic-update-slice | bytes 14155780
  858.5 8.9 dynamic-update-slice.9
  867.4 28.8 %dynamic-update-slice.10 = f32[32,444480]{1,0:T(8,128)} dynamic-update-slice(f32[32,444480]{1,0:T(8,128)} %dynamic-update-slice.9, f32[32,73728]{1,0:T(8,128)} %reshape.1703, s32[]{} %constant.286, s32[]{} %constant.294) | dynamic-update-slice | bytes 18874372
  896.2 28.6 %dynamic-update-slice.11 = f32[32,444480]{1,0:T(8,128)} dynamic-update-slice(f32[32,444480]{1,0:T(8,128)} %dynamic-update-slice.10, f32[32,73728]{1,0:T(8,128)} %reshape.1704, s32[]{} %constant.286, s32[]{} %constant.295) | dynamic-update-slice | bytes 18874372
  937.0 798.7 %all-reduce.9.cloned.1.call-done = f32[32,444480]{1,0:T(8,128)} async-done(((f32[32,444480]{1,0:T(8,128)}), f32[32,444480]{1,0:T(8,128)}) %all-reduce.9.cloned.1.call-update) | async-done | bytes 56893456
  1742.1 7.2 dynamic-slice_reduce_fusion
  (786 shorter events, 311.0 us)
Async XLA Ops:
  7.2 180.7 %all-gather.15.cloned.1.call-start = ((), (), s32[]{:S(2)}) async-start(), calls=%async_computation | async-start | bytes 3649536 | tf_op jit(solution)/shard_map/all_gather | solution.py:89
  7.9 184.5 %all-gather.17.cloned.1.call-start = ((), (), s32[]{:S(2)}) async-start(), calls=%async_computation.1 | async-start | bytes 1216512 | tf_op jit(solution)/shard_map/all_gather | solution.py:90
  8.7 192.6 %all-gather.19.cloned.1.call-start = ((), (), s32[]{:S(2)}) async-start(), calls=%async_computation.2 | async-start | bytes 4866048 | tf_op jit(solution)/shard_map/all_gather | solution.py:91
  9.4 251.6 %all-gather.21.cloned.1.call-start = ((), (), s32[]{:S(2)}) async-start(), calls=%async_computation.3 | async-start | bytes 4866048 | tf_op jit(solution)/shard_map/all_gather | solution.py:92
  10.0 312.6 %all-gather.23.cloned.1.call-start = ((), (), s32[]{:S(2)}) async-start(), calls=%async_computation.4 | async-start | bytes 3649536 | tf_op jit(solution)/shard_map/all_gather | solution.py:95
  10.6 367.8 %all-gather.25.cloned.1.call-start = ((), (), s32[]{:S(2)}) async-start(), calls=%async_computation.5 | async-start | bytes 1216512 | tf_op jit(solution)/shard_map/all_gather | solution.py:96
  11.1 432.7 %all-gather.27.cloned.1.call-start = ((), (), s32[]{:S(2)}) async-start(), calls=%async_computation.6 | async-start | bytes 4866048 | tf_op jit(solution)/shard_map/all_gather | solution.py:97
  11.9 47.1 %copy-start.171 = (s32[2,1]{0,1:T(1,128)S(1)}, s32[2,1]{0,1:T(1,128)}, u32[]{:S(2)}) copy-start(s32[2,1]{0,1:T(1,128)} %param.22) | copy-start | bytes 28
  11.9 497.3 %all-gather.29.cloned.1.call-start = ((), (), s32[]{:S(2)}) async-start(), calls=%async_computation.7 | async-start | bytes 4866048 | tf_op jit(solution)/shard_map/all_gather | solution.py:98
  12.7 1723.1 %all-reduce.9.cloned.1.call-start = ((), (), s32[]{:S(2)}) async-start(), calls=%async_computation.8 | async-start | bytes 113803264
  12.7 50.4 %copy-start.169 = (bf16[8,24]{1,0:T(8,128)(2,1)S(1)}, bf16[8,24]{1,0:T(8,128)(2,1)}, u32[]{:S(2)}) copy-start(bf16[8,24]{1,0:T(8,128)(2,1)} %param.27) | copy-start | bytes 1156
  13.8 47.4 %copy-start.39 = (f32[1,128,768]{2,1,0:T(8,128)}, f32[1,128,768]{2,1,0:T(8,128)S(1)}, u32[]{:S(2)}) copy-start(f32[1,128,768]{2,1,0:T(8,128)S(1)} %get-tuple-element.198) | copy-start | bytes 1179652
  13.8 49.3 %copy-start.40 = (f32[1,128,768]{2,1,0:T(8,128)}, f32[1,128,768]{2,1,0:T(8,128)S(1)}, u32[]{:S(2)}) copy-start(f32[1,128,768]{2,1,0:T(8,128)S(1)} %get-tuple-element.199) | copy-start | bytes 1179652
  13.8 86.5 %copy-start.185 = (bf16[96]{0:T(256)(128)(2,1)S(1)}, bf16[96]{0:T(256)(128)(2,1)}, u32[]{:S(2)}) copy-start(bf16[96]{0:T(256)(128)(2,1)} %param.28) | copy-start | bytes 580
  13.8 86.8 %copy-start.186 = (bf16[96]{0:T(256)(128)(2,1)S(1)}, bf16[96]{0:T(256)(128)(2,1)}, u32[]{:S(2)}) copy-start(bf16[96]{0:T(256)(128)(2,1)} %param.34) | copy-start | bytes 580
  13.9 124.4 %copy-start.172 = (s32[2,128]{1,0:T(2,128)S(1)}, s32[2,128]{1,0:T(2,128)}, u32[]{:S(2)}) copy-start(s32[2,128]{1,0:T(2,128)} %param.20) | copy-start | bytes 3076
  13.9 124.6 %copy-start.170 = (bf16[8,24]{1,0:T(8,128)(2,1)S(1)}, bf16[8,24]{1,0:T(8,128)(2,1)}, u32[]{:S(2)}) copy-start(bf16[8,24]{1,0:T(8,128)(2,1)} %param.33) | copy-start | bytes 1156
  13.9 167.6 %copy-start.164 = (s32[2,8]{1,0:T(2,128)S(1)}, s32[2,8]{1,0:T(2,128)}, u32[]{:S(2)}) copy-start(s32[2,8]{1,0:T(2,128)} %param.21) | copy-start | bytes 196
  13.9 173.4 %copy-start.187 = (u32[32]{0:T(128)S(1)}, u32[32]{0:T(128)}, u32[]{:S(2)}) copy-start(u32[32]{0:T(128)} %constant.204) | copy-start | bytes 388
  13.9 174.0 %copy-start.19 = (bf16[2,128,768]{2,1,0:T(8,128)(2,1)S(1)}, bf16[2,128,768]{2,1,0:T(8,128)(2,1)}, u32[]{:S(2)}) copy-start(bf16[2,128,768]{2,1,0:T(8,128)(2,1)} %param.18) | copy-start | bytes 1179652
  100.3 171.7 %copy-start.78 = (f32[768]{0:T(1024)}, f32[768]{0:T(1024)S(1)}, u32[]{:S(2)}) copy-start(f32[768]{0:T(1024)S(1)} %get-tuple-element.107) | copy-start | bytes 9220
  194.2 66.8 %copy-start.5 = (f32[128,768]{1,0:T(8,128)}, f32[128,768]{1,0:T(8,128)S(1)}, u32[]{:S(2)}) copy-start(f32[128,768]{1,0:T(8,128)S(1)} %get-tuple-element.253) | copy-start | bytes 1179652
  194.2 66.8 %copy-start.113 = (f32[128]{0:T(128)}, f32[128]{0:T(128)S(1)}, u32[]{:S(2)}) copy-start(f32[128]{0:T(128)S(1)} %broadcast_multiply_fusion.3) | copy-start | bytes 1540
  194.4 66.6 %copy-start.139 = (f32[128]{0:T(128)}, f32[128]{0:T(128)S(1)}, u32[]{:S(2)}) copy-start(f32[128]{0:T(128)S(1)} %fusion.163) | copy-start | bytes 1540
  199.8 71.0 %copy-start.8 = (f32[128,768]{1,0:T(8,128)}, f32[128,768]{1,0:T(8,128)S(1)}, u32[]{:S(2)}) copy-start(f32[128,768]{1,0:T(8,128)S(1)} %get-tuple-element.260) | copy-start | bytes 1179652
  199.9 71.0 %copy-start.136 = (f32[128]{0:T(128)}, f32[128]{0:T(128)S(1)}, u32[]{:S(2)}) copy-start(f32[128]{0:T(128)S(1)} %broadcast_multiply_fusion.1) | copy-start | bytes 1540
  200.1 70.7 %copy-start.148 = (f32[128]{0:T(128)}, f32[128]{0:T(128)S(1)}, u32[]{:S(2)}) copy-start(f32[128]{0:T(128)S(1)} %fusion.165) | copy-start | bytes 1540
  210.0 54.4 %copy-start.17 = (bf16[128,3072]{1,0:T(8,128)(2,1)}, bf16[128,3072]{1,0:T(8,128)(2,1)S(1)}, u32[]{:S(2)}) copy-start(bf16[128,3072]{1,0:T(8,128)(2,1)S(1)} %get-tuple-element.186) | copy-start | bytes 2359300
  327.6 29.5 %copy-start.116 = (bf16[768]{0:T(1024)(128)(2,1)}, bf16[768]{0:T(1024)(128)(2,1)S(1)}, u32[]{:S(2)}) copy-start(bf16[768]{0:T(1024)(128)(2,1)S(1)} %slice_reduce_fusion) | copy-start | bytes 4612
  684.8 21.5 %copy-start.35 = (bf16[12,64,128]{2,1,0:T(8,128)(2,1)}, bf16[12,64,128]{2,1,0:T(8,128)(2,1)S(1)}, u32[]{:S(2)}) copy-start(bf16[12,64,128]{2,1,0:T(8,128)(2,1)S(1)} %convolution_convert_fusion.4) | copy-start | bytes 589828
  837.8 20.7 %copy-start.15 = (f32[32,18432]{1,0:T(8,128)S(1)}, f32[32,18432]{1,0:T(8,128)}, u32[]{:S(2)}) copy-start(f32[32,18432]{1,0:T(8,128)} %reshape.1702) | copy-start | bytes 7077892
  896.2 31.6 %copy-start.59 = (f32[32,1536]{1,0:T(8,128)S(1)}, f32[32,1536]{1,0:T(8,128)}, u32[]{:S(2)}) copy-start(f32[32,1536]{1,0:T(8,128)} %reshape.1709) | copy-start | bytes 589828
  (178 other events, 722.1 us)
Sparse Core Ops, SparseCore 0:
  10.9 63.2 all-gather.14
  77.1 53.0 all-gather.16
  133.1 62.6 all-gather.18
  198.5 62.3 all-gather.20
  263.7 58.8 all-gather.22
  325.4 52.9 all-gather.24
  381.2 62.5 all-gather.26
  446.7 62.4 all-gather.28
  930.0 805.7 all-reduce.8
where the time goes:
time: 1780 us; the launch traced here: 1770 us
  waiting for transfers between devices  1030 us (58%)
  local copies, waits for them, and re-layouts  274 us (15%)
  blocking collectives  203 us (11%)
  matrix products  155 us (9%)
  other arithmetic  79.1 us (4%)
  between operations  27.5 us (2%)
    unnamed x10, waiting for transfers between devices  804 us
    unnamed x452, local copies, waits for them, and re-layouts  127 us
    dot_general x24, matrix products, contract(): lax.dot_general(left_side, right_side, (((left_dim,), (right_dim,)), ((),...  79.8 us
    unnamed x2, blocking collectives  62.5 us
    all_gather x1, waiting for transfers between devices, fetch_weights(): lax.all_gather(cross_down, ('dp', 'seq'), axis=0, tiled=True)  60.4 us
    all_gather x1, waiting for transfers between devices, fetch_weights(): lax.all_gather(cross_up, ('dp', 'seq'), axis=0, tiled=True)  56 us
    all_gather x1, waiting for transfers between devices, fetch_weights(): lax.all_gather(local_down, ('dp', 'seq'), axis=0, tiled=True)  51 us
    reshape x8, local copies, waits for them, and re-layouts, owner_pack(): pieces.append(grad_value.reshape(devices, -1))  50.6 us
  transfers between devices with their start and end apart: 9, of which 6 were waited for; matrix products, arithmetic and copies ran while one was open for 5% of the time, Pallas kernels for 0%

commit v1 on v0

--- a/solution.py
+++ b/solution.py
@@ -4,6 +4,8 @@
 import jax
 import jax.numpy as jnp
 from jax import lax
+from jax.experimental import pallas as pl
+from jax.experimental.pallas import tpu as pltpu
 from jax.sharding import PartitionSpec as P
 
 D = 768
@@ -442,9 +444,566 @@
     return (layer_output, input_gradient) + tuple(summed)
 
 
+PLANE = 4
+
+
+def swap_dp(array_in, shift):
+    return lax.ppermute(array_in, "dp", [(i, (i + shift) % 4) for i in range(4)])
+
+
+def swap_core(array_in):
+    return lax.ppermute(array_in, "seq", [(i, i ^ 1) for i in range(8)])
+
+
+def swap_chip(array_in, mask):
+    return lax.ppermute(array_in, "seq", [(i, i ^ (2 * mask)) for i in range(8)])
+
+
+def swap_one(array_in):
+    return lax.ppermute(array_in, "seq", [(i, i ^ (2 if i % 2 == 0 else 4)) for i in range(8)])
+
+
+def swap_two(array_in):
+    return lax.ppermute(array_in, "seq", [(i, i ^ (4 if i % 2 == 0 else 2)) for i in range(8)])
+
+
+def place_in():
+    layer = lax.axis_index("dp")
+    spot = lax.axis_index("seq")
+    return layer, spot // 2, spot % 2
+
+
+def copies(pieces, shape, spots):
+    count = len(pieces)
+
+    def kernel(*refs):
+        total, held, sems = refs[count], refs[count + 1 : -1], refs[-1]
+        places = spots(*place_in())
+        inward = [
+            pltpu.make_async_copy(refs[i], held[i], sems.at[0, i]) for i in range(count)
+        ]
+        outward = [
+            pltpu.make_async_copy(held[i], total.at[places[i]], sems.at[1, i])
+            for i in range(count)
+        ]
+        for copy in inward:
+            copy.start()
+        for before, after in zip(inward, outward):
+            before.wait()
+            after.start()
+        for copy in outward:
+            copy.wait()
+
+    size = 2 * math.prod(shape) * pieces[0].dtype.itemsize
+    return pl.pallas_call(
+        kernel,
+        out_shape=jax.ShapeDtypeStruct(shape, pieces[0].dtype),
+        in_specs=[pl.BlockSpec(memory_space=pl.ANY)] * count,
+        out_specs=pl.BlockSpec(memory_space=pl.ANY),
+        scratch_shapes=[pltpu.VMEM(piece.shape, piece.dtype) for piece in pieces]
+        + [pltpu.SemaphoreType.DMA((2, count))],
+        compiler_params=pltpu.CompilerParams(vmem_limit_bytes=24 * 2**20),
+        cost_estimate=pl.CostEstimate(flops=0, bytes_accessed=size, transcendentals=0),
+    )(*pieces)
+
+
+def gather_dp(shard):
+    pieces = [shard] + [swap_dp(shard, shift) for shift in (1, 2, 3)]
+    return copies(
+        pieces,
+        (4,) + shard.shape,
+        lambda layer, chip, core: [lax.rem(layer + 4 - shift, 4) for shift in range(4)],
+    )
+
+
+def gather_core(piece, axis):
+    other = swap_core(piece)
+    shape = piece.shape[:axis] + (2,) + piece.shape[axis:]
+    every = (slice(None),) * axis
+    return copies([piece, other], shape, lambda layer, chip, core: [every + (core,), every + (1 - core,)])
+
+
+def gather_all(shard):
+    column = gather_dp(shard)
+    first = swap_one(column)
+    second = swap_two(column)
+    third = swap_two(first)
+    mine = [column, first, second, third]
+    every = slice(None)
+
+    def spots(layer, chip, core):
+        near, far = chip ^ (1 + core), chip ^ (2 - core)
+        found = [(every, spot, core) for spot in (chip, near, far, chip ^ 3)]
+        return found + [(every, spot, 1 - core) for spot in (chip, far, near, chip ^ 3)]
+
+    return copies(mine + [swap_core(piece) for piece in mine], (4, 4, 2) + shard.shape, spots)
+
+
+def pick(array_in, index, axis):
+    return lax.dynamic_index_in_dim(array_in, index, axis, keepdims=False)
+
+
+def wide(array_in):
+    return array_in.astype(jnp.float32)
+
+
+def low(array_in):
+    return array_in.astype(jnp.bfloat16)
+
+
+def scatter_sum(parts):
+    layer, chip, core = place_in()
+    rows, columns = parts.shape[3:]
+    spots = jnp.stack([chip ^ (1 + core), chip ^ 3, chip ^ (2 - core), chip, core, layer])
+
+    def whole(take):
+        return pl.BlockSpec((None, None, None, rows, columns), take)
+
+    def part(take):
+        return pl.BlockSpec((None, None, rows, columns), take)
+
+    def single(take):
+        return pl.BlockSpec((None, rows, columns), take)
+
+    def run(kernel, grid, in_specs, out_specs, out_shape, *operands):
+        size = sum(math.prod(a.shape) * a.dtype.itemsize for a in jax.tree.leaves(out_shape))
+        return pl.pallas_call(
+            kernel,
+            grid_spec=pltpu.PrefetchScalarGridSpec(
+                num_scalar_prefetch=1, grid=grid, in_specs=in_specs, out_specs=out_specs
+            ),
+            out_shape=out_shape,
+            cost_estimate=pl.CostEstimate(
+                flops=size, bytes_accessed=3 * size, transcendentals=0
+            ),
+        )(spots, *operands)
+
+    def shaped(*lead, dtype=jnp.bfloat16):
+        return jax.ShapeDtypeStruct(lead + (rows, columns), dtype)
+
+    def take_out(parts_ref, gone_ref, held, sems):
+        other = 1 - lax.rem(lax.axis_index("seq"), 2)
+        inward = [
+            pltpu.make_async_copy(parts_ref.at[z, :, other], held.at[z], sems.at[0, z])
+            for z in range(4)
+        ]
+        outward = [
+            pltpu.make_async_copy(held.at[z], gone_ref.at[z], sems.at[1, z]) for z in range(4)
+        ]
+        for copy in inward:
+            copy.start()
+        for before, after in zip(inward, outward):
+            before.wait()
+            after.start()
+        for copy in outward:
+            copy.wait()
+
+    gone = pl.pallas_call(
+        take_out,
+        out_shape=shaped(4, 4),
+        in_specs=[pl.BlockSpec(memory_space=pl.ANY)],
+        out_specs=pl.BlockSpec(memory_space=pl.ANY),
+        scratch_shapes=[
+            pltpu.VMEM((4, 4, rows, columns), jnp.bfloat16),
+            pltpu.SemaphoreType.DMA((2, 4)),
+        ],
+        compiler_params=pltpu.CompilerParams(vmem_limit_bytes=24 * 2**20),
+        cost_estimate=pl.CostEstimate(flops=0, bytes_accessed=parts.size * 2, transcendentals=0),
+    )(parts)
+    got = swap_core(gone)
+
+    def add_two(spots_ref, a_ref, b_ref, o_ref):
+        o_ref[...] = low(wide(a_ref[...]) + wide(b_ref[...]))
+
+    sent = run(
+        add_two,
+        (2, 4),
+        [
+            whole(lambda i, z, s: (z, s[i], s[4], 0, 0)),
+            part(lambda i, z, s: (z, s[i], 0, 0)),
+        ],
+        part(lambda i, z, s: (i, z, 0, 0)),
+        shaped(2, 4),
+        parts,
+        got,
+    )
+    back = swap_one(sent)
+
+    def add_three(spots_ref, a_ref, b_ref, c_ref, o_ref):
+        o_ref[...] = low(wide(a_ref[...]) + wide(b_ref[...]) + wide(c_ref[...]))
+
+    onward = run(
+        add_three,
+        (4,),
+        [
+            whole(lambda z, s: (z, s[2], s[4], 0, 0)),
+            part(lambda z, s: (z, s[2], 0, 0)),
+            part(lambda z, s: (1, z, 0, 0)),
+        ],
+        single(lambda z, s: (z, 0, 0)),
+        shaped(4),
+        parts,
+        got,
+        back,
+    )
+    last = swap_two(onward)
+
+    def add_four(spots_ref, a_ref, b_ref, c_ref, d_ref, own_ref, out_a, out_b, out_c):
+        total = wide(a_ref[...]) + wide(b_ref[...]) + wide(c_ref[...]) + wide(d_ref[...])
+        step = pl.program_id(0)
+
+        @pl.when(step == 3)
+        def _():
+            own_ref[...] = total
+
+        for shift, ref in ((1, out_a), (2, out_b), (3, out_c)):
+
+            @pl.when(step == shift - 1)
+            def _(ref=ref):
+                ref[...] = low(total)
+
+    flat = pl.BlockSpec((rows, columns), lambda k, s: (0, 0))
+
+    def level(k, s):
+        return lax.rem(s[5] + 1 + k, 4)
+
+    own, *others = run(
+        add_four,
+        (4,),
+        [
+            whole(lambda k, s: (level(k, s), s[3], s[4], 0, 0)),
+            part(lambda k, s: (level(k, s), s[3], 0, 0)),
+            part(lambda k, s: (0, level(k, s), 0, 0)),
+            single(lambda k, s: (level(k, s), 0, 0)),
+        ],
+        [flat] * 4,
+        [shaped(dtype=jnp.float32)] + [shaped()] * 3,
+        parts,
+        got,
+        back,
+        last,
+    )
+    total = own
+    for shift, other in zip((1, 2, 3), others):
+        total = total + wide(swap_dp(other, shift))
+    return total
+
+
+def plane_pieces(piece):
+    return [piece] + [swap_chip(piece, mask) for mask in (1, 2, 3)]
+
+
+def plane_gather(piece):
+    layer, chip, core = place_in()
+    pieces = jnp.stack(plane_pieces(piece))
+    return jnp.stack([pick(pieces, chip ^ spot, 0) for spot in range(4)])
+
+
+def plane_sum(piece):
+    pieces = plane_pieces(piece)
+    return (pieces[0] + pieces[1]) + (pieces[2] + pieces[3])
+
+
+def own_rows(pair_in):
+    layer, chip, core = place_in()
+    kept = pick(pair_in, core, 0)
+    got = swap_core(pick(pair_in, 1 - core, 0))
+    both = jnp.where(core == 0, jnp.stack([kept, got]), jnp.stack([got, kept]))
+    return plane_gather(both).reshape((8,) + pair_in.shape[1:])
+
+
+def give_rows(both):
+    layer, chip, core = place_in()
+    kept = pick(both, core, 0)
+    got = swap_core(pick(both, 1 - core, 0))
+    return jnp.where(core == 0, jnp.stack([kept, got]), jnp.stack([got, kept]))
+
+
+def norm_parts(values):
+    centered = values - jnp.mean(values, axis=-1, keepdims=True)
+    variance = jnp.mean(centered * centered, axis=-1, keepdims=True)
+    scale = lax.rsqrt(variance + epsilon)
+    return centered * scale, scale
+
+
+def norm_back(grad, normed, scale, gain):
+    scaled = grad * gain
+    return scale * (
+        scaled
+        - jnp.mean(scaled, axis=-1, keepdims=True)
+        - normed * jnp.mean(scaled * normed, axis=-1, keepdims=True)
+    )
+
+
+def gelu_slope(hidden):
+    return 0.5 * (1.0 + lax.erf(hidden * math.sqrt(0.5))) + hidden * jnp.exp(
+        -0.5 * hidden * hidden
+    ) * (1.0 / math.sqrt(2.0 * math.pi))
+
+
+def cross_weights(cross_mix, cross_up, cross_down):
+    mix_parts = cross_mix.reshape(24, 3, 4, 192).transpose(2, 0, 1, 3).reshape(4, 24, 576)
+    up_parts = cross_up.reshape(24, 4, 4, 192).transpose(2, 0, 1, 3).reshape(4, 24, 768)
+    parts = jnp.concatenate([mix_parts, up_parts], axis=2)
+    chip = place_in()[1]
+    pieces = [
+        swap_chip(pick(parts, chip ^ mask, 0), mask) if mask else pick(parts, chip, 0)
+        for mask in range(4)
+    ]
+    rows = copies(
+        pieces, (4, 24, 1344), lambda layer, chip, core: [chip ^ mask for mask in range(4)]
+    )
+    column = gather_dp(jnp.concatenate([rows.reshape(96, 1344), cross_down], axis=1))
+    mix_up = gather_core(column[:, :, :1344].reshape(4, 4, 24, 1344), 2).reshape(768, 1344)
+    down = gather_core(column[:, :, 1344:], 1).reshape(768, 768)
+    return mix_up[:, :576], mix_up[:, 576:], down
+
+
+def plane_shards(
+    tokens,
+    cotangent,
+    token_docs,
+    segment_docs,
+    segment_positions,
+    local_mix,
+    local_out,
+    local_up,
+    local_down,
+    local_vectors,
+    local_up_bias,
+    cross_mix,
+    cross_out,
+    cross_up,
+    cross_down,
+    cross_vectors,
+    cross_up_bias,
+    position_table,
+):
+    layer, chip, core = place_in()
+    rank = lax.axis_index(("dp", "seq"))
+    small = jnp.concatenate(
+        [
+            local_vectors,
+            cross_vectors,
+            position_table,
+            local_up_bias.reshape(4, 24),
+            cross_up_bias.reshape(4, 24),
+        ]
+    )
+    small_pad = jnp.pad(small.T, ((0, 0), (0, 40)))
+    first_group = gather_all(jnp.concatenate([local_mix, local_out, small_pad], axis=1)).reshape(
+        768, 3200
+    )
+    second_group = gather_all(jnp.concatenate([local_up, cross_out], axis=1)).reshape(768, 3840)
+    down_weight = gather_all(local_down).reshape(3072, 768)
+    mix_weight, out_weight = first_group[:, :2304], first_group[:, 2304:3072]
+    rows = first_group[:, 3072:3160].T
+    up_weight, cross_out_weight = second_group[:, :3072], second_group[:, 3072:]
+    position_rows = rows[16:80]
+    up_bias = rows[80:84].reshape(4, 32, 24).transpose(1, 0, 2).reshape(3072)
+    cross_bias = rows[84:88].reshape(4, 4, 4, 2, 24).transpose(1, 2, 3, 0, 4).reshape(4, 4, 192)
+    local_weights = (mix_weight, out_weight, up_weight, down_weight, rows[:8], up_bias)
+    mix_part, up_part, down_part = cross_weights(cross_mix, cross_up, cross_down)
+    cross_rows = wide(rows[8:16])
+
+    inputs = wide(tokens).reshape(256, D)
+    first_out, first_kept = block_forward(
+        inputs, local_weights, partial(segment_forward, token_docs=token_docs)
+    )
+    segment_grid = first_out.reshape(2, SEG, D)
+    places = segment_positions.reshape(2)
+    position_picks = low(places[:, None] == jnp.arange(64, dtype=jnp.int32)[None, :])
+    heads_in = segment_grid[:, 0, :] + jnp.dot(
+        position_picks, position_rows, preferred_element_type=jnp.float32
+    )
+
+    docs = pick(segment_docs, core, 0)
+    allowed = docs[:, None] == docs[None, :]
+    row_in = own_rows(heads_in)
+    row_low = low(row_in)
+    query_bias = pick(cross_rows[0].reshape(4, 192), chip, 0)
+    value_bias = pick(cross_rows[1].reshape(4, 192), chip, 0)
+    part_bias = jnp.concatenate([query_bias, jnp.zeros_like(query_bias), value_bias])
+    mixed = low(jnp.dot(row_low, mix_part, preferred_element_type=jnp.float32) + part_bias)
+    heads = mixed.reshape(8, 3, 3, HEAD_DIM)
+    query, key, value = heads[:, 0], heads[:, 1], heads[:, 2]
+    scores = jnp.einsum("qhd,khd->hqk", query, key, preferred_element_type=jnp.float32) * (
+        HEAD_DIM ** (-0.5)
+    )
+    probs = jax.nn.softmax(jnp.where(allowed[None], scores, masked_score), axis=-1)
+    probs_low = low(probs)
+    context_part = low(
+        jnp.einsum("hqk,khd->qhd", probs_low, value, preferred_element_type=jnp.float32)
+    ).reshape(8, 192)
+    context = plane_gather(context_part).transpose(1, 0, 2).reshape(8, D)
+    first_sum = (
+        row_in
+        + jnp.dot(context, cross_out_weight, preferred_element_type=jnp.float32)
+        + cross_rows[2]
+    )
+    first_n, first_scale = norm_parts(first_sum)
+    first_norm = first_n * cross_rows[3] + cross_rows[4]
+    first_low = low(first_norm)
+    hidden = jnp.dot(first_low, up_part, preferred_element_type=jnp.float32) + wide(
+        pick(cross_bias, chip, 1)
+    ).reshape(768)
+    active = low(gelu_exact(hidden))
+    second_sum = (
+        first_norm
+        + plane_sum(jnp.dot(active, down_part, preferred_element_type=jnp.float32))
+        + cross_rows[5]
+    )
+    second_n, second_scale = norm_parts(second_sum)
+    row_out = second_n * cross_rows[6] + cross_rows[7]
+    heads_out = give_rows(lax.dynamic_slice_in_dim(row_out, 2 * chip, 2, 0))
+    layer_output = low(jnp.concatenate([heads_out[:, None, :], segment_grid[:, 1:, :]], axis=1))
+
+    row_grad = wide(own_rows(cotangent[:, 0, :]))
+    second_grad = norm_back(row_grad, second_n, second_scale, cross_rows[6])
+    second_low = low(second_grad)
+    hidden_low = low(contract(second_low, down_part, 1, 1) * gelu_slope(hidden))
+    first_grad = second_grad + plane_sum(contract(hidden_low, up_part, 1, 1))
+    sum_grad = norm_back(first_grad, first_n, first_scale, cross_rows[3])
+    branch_low = low(sum_grad)
+    out_part = lax.dynamic_slice_in_dim(cross_out_weight, 192 * chip, 192, 0)
+    context_low = low(contract(branch_low, out_part, 1, 1)).reshape(8, 3, HEAD_DIM)
+    prob_grad = jnp.einsum("qhd,khd->hqk", context_low, value, preferred_element_type=jnp.float32)
+    value_grad = jnp.einsum(
+        "hqk,qhd->khd", probs_low, context_low, preferred_element_type=jnp.float32
+    )
+    score_low = low(probs * (prob_grad - jnp.sum(probs * prob_grad, axis=-1, keepdims=True)))
+    query_grad = jnp.einsum("hqk,khd->qhd", score_low, key, preferred_element_type=jnp.float32)
+    key_grad = jnp.einsum("hqk,qhd->khd", score_low, query, preferred_element_type=jnp.float32)
+    scale = HEAD_DIM ** (-0.5)
+    mixed_low = low(
+        jnp.stack([query_grad * scale, key_grad * scale, value_grad], axis=1)
+    ).reshape(8, 576)
+    row_parts = contract(mixed_low, mix_part, 1, 1).reshape(4, 2, D)
+    pair_grad = pick(row_parts, chip, 0) + lax.dynamic_slice_in_dim(sum_grad, 2 * chip, 2, 0)
+    for mask in (1, 2, 3):
+        pair_grad = pair_grad + swap_chip(pick(row_parts, chip ^ mask, 0), mask)
+    heads_grad = give_rows(pair_grad)
+
+    def pair_of(array_in):
+        return lax.dynamic_slice_in_dim(array_in, 2 * chip, 2, 0)
+
+    sums = jnp.stack(
+        [
+            jnp.sum(first_grad * first_n, axis=0),
+            jnp.sum(first_grad, axis=0),
+            jnp.sum(row_grad * second_n, axis=0),
+            jnp.sum(row_grad, axis=0),
+        ]
+    )
+    my_sum = low(pick(sums, chip, 0))[None]
+    my_places = jnp.broadcast_to(low(wide(places))[:, None], (2, D))
+    pairs = [pair_of(a) for a in (row_low, context, first_low, branch_low, second_low)]
+    packed = jnp.concatenate(
+        [hidden_low, active]
+        + [mixed_low.reshape(6, D)]
+        + pairs
+        + [low(pair_of(sum_grad)), my_sum, my_places]
+    )
+    packed = jnp.pad(packed, ((0, 5), (0, 0)))
+    everyone = gather_all(packed)
+
+    def all_rows(piece):
+        return piece.transpose(0, 2, 1, 3, 4).reshape(64, -1)
+
+    hidden_all = everyone[:, :, :, 0:8]
+    active_all = everyone[:, :, :, 8:16]
+    mixed_all = everyone[:, :, :, 16:22].reshape(4, 4, 2, 8, 3, 192)
+    mixed_all = mixed_all.transpose(0, 2, 3, 4, 1, 5).reshape(64, 3 * D)
+    singles = [all_rows(everyone[:, :, :, 22 + 2 * i : 24 + 2 * i]) for i in range(6)]
+    singles = [s.reshape(64, D) for s in singles]
+    row_all, context_all, first_all, branch_all, second_all, sum_all = singles
+    sums_all = jnp.sum(wide(everyone[:, :, :, 34]), axis=(0, 2))
+    places_all = everyone[:, :, :, 35:37, 0]
+
+    def own_columns(array_in):
+        return lax.dynamic_slice_in_dim(array_in, 24 * rank, 24, 1)
+
+    hidden_rows = (
+        hidden_all.reshape(4, 4, 2, 8, 4, 2, 96)
+        .transpose(0, 2, 3, 4, 1, 5, 6)
+        .reshape(64, 3072)
+    )
+    active_own = lax.dynamic_slice(
+        active_all, (0, chip, 0, 0, 192 * layer + 96 * core), (4, 1, 2, 8, 96)
+    ).reshape(64, 96)
+    cross_mix_grad = contract(own_columns(row_all), mixed_all, 0, 0)
+    cross_out_grad = contract(own_columns(context_all), branch_all, 0, 0)
+    cross_up_grad = contract(own_columns(first_all), hidden_rows, 0, 0)
+    cross_down_grad = contract(active_own, second_all, 0, 0)
+    mixed_sum = jnp.sum(wide(mixed_all), axis=0)
+    cross_vectors_grad = own_columns(
+        jnp.stack(
+            [
+                mixed_sum[:D],
+                mixed_sum[2 * D :],
+                jnp.sum(wide(branch_all), axis=0),
+                sums_all[0],
+                sums_all[1],
+                jnp.sum(wide(second_all), axis=0),
+                sums_all[2],
+                sums_all[3],
+            ]
+        )
+    )
+    cross_bias_grad = lax.dynamic_slice_in_dim(
+        jnp.sum(wide(hidden_rows), axis=0), 96 * rank, 96, 0
+    )
+    grads_all = wide(own_columns(sum_all)) + contract(mixed_all, cross_mix, 1, 1)
+    places_rows = places_all.transpose(0, 3, 1, 2).reshape(64)
+    picks_all = wide(
+        wide(places_rows)[:, None] == jnp.arange(64, dtype=jnp.float32)[None, :]
+    )
+    table_grad = contract_exact(picks_all, grads_all, 0, 0)
+
+    output_grad = wide(cotangent)
+    local_grad = jnp.concatenate([heads_grad[:, None, :], output_grad[:, 1:, :]], axis=1).reshape(
+        256, D
+    )
+    input_grad, local_grads = block_backward(
+        local_grad, first_kept, local_weights, partial(segment_backward, token_docs=token_docs)
+    )
+    mix_grad, out_grad, up_grad, down_grad, vectors_grad, bias_grad = local_grads
+    down_sum = scatter_sum(low(down_grad).reshape(4, 4, 2, 96, D))
+    up_sum = scatter_sum(low(up_grad).reshape(4, 4, 2, 24, 3072))
+    small_grads = jnp.concatenate(
+        [
+            vectors_grad.reshape(8, 32, 24).transpose(1, 2, 0),
+            bias_grad.reshape(32, 4, 24).transpose(0, 2, 1),
+        ],
+        axis=2,
+    ).reshape(D, 12)
+    mix_parts = jnp.concatenate(
+        [low(mix_grad), low(out_grad), low(jnp.pad(small_grads, ((0, 0), (0, 116))))], axis=1
+    )
+    mix_sum = scatter_sum(mix_parts.reshape(4, 4, 2, 24, 3200))
+    return (
+        layer_output,
+        input_grad.reshape(2, SEG, D),
+        mix_sum[:, :2304],
+        mix_sum[:, 2304:3072],
+        up_sum,
+        down_sum,
+        mix_sum[:, 3072:3080].T,
+        mix_sum[:, 3080:3084].T.reshape(96),
+        cross_mix_grad,
+        cross_out_grad,
+        cross_up_grad,
+        cross_down_grad,
+        cross_vectors_grad,
+        cross_bias_grad,
+        table_grad,
+    )
+
+
 def solution(mesh):
+    flat = dict(mesh.shape) == {"dp": 4, "seq": 8}
     return jax.shard_map(
-        shards,
+        plane_shards if flat else shards,
         mesh=mesh,
         in_specs=(
             P("dp", "seq", None),

time: 1780 us -> 466 us (0.26)
  waiting for transfers between devices: 1030 us -> 101 us
  blocking collectives: 203 us -> 0 us
  local copies, waits for them, and re-layouts: 274 us -> 89.7 us
  starting transfers between devices: 0.34 us -> 106 us
  matrix products: 155 us -> 73 us
  Pallas kernels: 0 us -> 67.4 us
  other arithmetic: 79.1 us -> 20.8 us
  between operations: 27.5 us -> 3.1 us
    unnamed x10 -> x0, waiting for transfers between devices: 804 us -> none
    all_gather x8 -> x0, waiting for transfers between devices: 223 us -> none  [the longest x1 60.4 us: fetch_weights(): lax.all_gather(cross_down, ('dp', 'seq'), axis=0, tiled=True)]
    all_gather x5 -> x0, blocking collectives: 141 us -> none  [the longest x1 44 us: fetch_weights(): lax.all_gather(position_table, ('dp', 'seq'), axis=1, tiled=True)]
    ppermute x0 -> x88, starting transfers between devices: none -> 106 us  [the longest x24 57.9 us: swap_dp(): lax.ppermute(array_in, 'dp', [(i, (i + shift) % 4) for i in range(4)])]
    ppermute x0 -> x88, waiting for transfers between devices: none -> 101 us  [the longest x24 50.6 us: swap_dp(): lax.ppermute(array_in, 'dp', [(i, (i + shift) % 4) for i in range(4)])]
    unnamed x452 -> x240, local copies, waits for them, and re-layouts: 127 us -> 31.6 us
    pallas_call x0 -> x24, Pallas kernels: none -> 67.4 us  [the longest x9 44.9 us: run(): pl.pallas_call(kernel, grid_spec=pltpu.PrefetchScalarGridSpec(num_scalar_...]
    unnamed x2 -> x0, blocking collectives: 62.5 us -> none
  transfers between devices with their start and end apart: 9 -> 88, of which waited for: 6 -> 30; matrix products, arithmetic and copies ran while one was open for 5% -> 28% of each run, Pallas kernels for 0% -> 14%
where the time goes in v1:
time: 466 us; the launch traced here: 461 us
  starting transfers between devices  106 us (23%)
  waiting for transfers between devices  101 us (22%)
  local copies, waits for them, and re-layouts  89.7 us (19%)
  matrix products  73 us (16%)
  Pallas kernels  67.4 us (14%)
  other arithmetic  20.8 us (4%)
    ppermute x24, starting transfers between devices, swap_dp(): lax.ppermute(array_in, 'dp', [(i, (i + shift) % 4) for i in range(4)])  57.9 us
    ppermute x24, waiting for transfers between devices, swap_dp(): lax.ppermute(array_in, 'dp', [(i, (i + shift) % 4) for i in range(4)])  50.6 us
    pallas_call x9, Pallas kernels, run(): pl.pallas_call(kernel, grid_spec=pltpu.PrefetchScalarGridSpec(num_scalar_...  44.9 us
    dot_general x17, matrix products, contract(): lax.dot_general(left_side, right_side, (((left_dim,), (right_dim,)), ((),...  34.8 us
    unnamed x240, local copies, waits for them, and re-layouts  31.6 us
    ppermute x11, waiting for transfers between devices, swap_two(): lax.ppermute(array_in, 'seq', [(i, i ^ (4 if i % 2 == 0 else 2)) for i in...  27.1 us
    ppermute x21, starting transfers between devices, swap_chip(): return lax.ppermute(array_in, 'seq', [(i, i ^ 2 * mask) for i in range(8)])  24.8 us
    pallas_call x12, Pallas kernels, copies(): pl.pallas_call(kernel, out_shape=jax.ShapeDtypeStruct(shape, pieces[0].dt...  17.2 us
  transfers between devices with their start and end apart: 88, of which 30 were waited for; matrix products, arithmetic and copies ran while one was open for 28% of the time, Pallas kernels for 14%

profile of v1, /device:TPU:0, one launch (start us, length us, event | category | flops | bytes accessed | tf_op | source)
XLA Modules:
  0.0 460.8 jit_solution(11658624994521296412)
XLA Ops:
  30.9 11.1 %collective-permute-done.22.refs_3_ = bf16[96,768]{1,0:T(8,128)(2,1)S(1)} collective-permute-done((bf16[96,768]{1,0:T(8,128)(2,1)S(1)}, bf16[96,768]{1,0:T(8,128)(2,1)S(1)}, u32[]{:S(2)}, u32[]{:S(2)}) %collective-permute-start.22) | collective-permute-done | bytes 147488 | tf_op jit(solution)/shard_map/ppermute | solution.py:451
  42.1 14.9 %collective-permute-start.37 = (bf16[96,2112]{1,0:T(8,128)(2,1)S(1)}, bf16[96,2112]{1,0:T(8,128)(2,1)S(1)}, u32[]{:S(2)}, u32[]{:S(2)}) collective-permute-start(bf16[96,2112]{1,0:T(8,128)(2,1)S(1)} %pad_maximum_fusion.1.refs_0_), channel_id=1, source_target_pairs={{0,8},{8,16},{16,24},{24,0},{1,9},{9,17},{17,25},{25,1},{2,10},{10... | collective-permute-start | bytes 1216520 | tf_op jit(solution)/shard_map/ppermute | solution.py:451
  62.8 22.3 %collective-permute-done.11.refs_2_ = bf16[24,3840]{1,0:T(8,128)(2,1)S(1)} collective-permute-done((bf16[24,3840]{1,0:T(8,128)(2,1)S(1)}, bf16[24,3840]{1,0:T(8,128)(2,1)S(1)}, u32[]{:S(2)}, u32[]{:S(2)}) %collective-permute-start.11) | collective-permute-done | bytes 184352 | tf_op jit(solution)/shard_map/ppermute | solution.py:451
  85.1 13.5 %collective-permute-start.39 = (bf16[96,2112]{1,0:T(8,128)(2,1)S(1)}, bf16[96,2112]{1,0:T(8,128)(2,1)S(1)}, u32[]{:S(2)}, u32[]{:S(2)}) collective-permute-start(bf16[96,2112]{1,0:T(8,128)(2,1)S(1)} %pad_maximum_fusion.1.refs_0_), channel_id=1, source_target_pairs={{0,24},{8,0},{16,8},{24,16},{1,25},{9,1},{17,9},{25,17},{2,26},{10... | collective-permute-start | bytes 1216520 | tf_op jit(solution)/shard_map/ppermute | solution.py:451
  101.9 4.5 collective-permute-done.39.refs_3_
  109.8 5.1 %collective-permute-done.24.refs_2_ = bf16[4,96,768]{2,1,0:T(8,128)(2,1)S(1)} collective-permute-done((bf16[4,96,768]{2,1,0:T(8,128)(2,1)S(1)}, bf16[4,96,768]{2,1,0:T(8,128)(2,1)S(1)}, u32[]{:S(2)}, u32[]{:S(2)}) %collective-permute-start.24) | collective-permute-done | bytes 589856 | tf_op jit(solution)/shard_map/ppermute | solution.py:467
  119.0 9.1 %collective-permute-done.4.refs_2_ = bf16[4,24,3200]{2,1,0:T(8,128)(2,1)} collective-permute-done((bf16[4,24,3200]{2,1,0:T(8,128)(2,1)S(1)}, bf16[4,24,3200]{2,1,0:T(8,128)(2,1)}, u32[]{:S(2)}, u32[]{:S(2)}) %collective-permute-start.4) | collective-permute-done | bytes 614432 | tf_op jit(solution)/shard_map/ppermute | solution.py:467
  156.0 3.9 collective-permute-done.15.refs_3_
  168.6 4.4 fusion.13
  173.0 3.5 reshape.677
  187.8 9.9 %multiply_convert_fusion = (bf16[256,3072]{1,0:T(8,128)(2,1)S(1)}, f32[256,3072]{1,0:T(8,128)}, f32[256,3072]{1,0:T(8,128)}) fusion(f32[3072]{0:T(1024)S(1)} %copy-done.85, bf16[768,3840]{1,0:T(8,128)(2,1)S(1)} %bitcast.281, f32[256,768]{1,0:T(8,128)S(1)} %copy-done.41, f32[768]{0:T(1024)S(1)} %get-tuple-element.240, f32[768]{0:T(1024)S(1)} %get-tuple-element.239, ...), kind=kOutput, calls=%fused_computation.20 | convolution fusion | flops 1260847104 | bytes 13391872 | tf_op jit(solution)/shard_map/dot_general | solution.py:243
  253.7 4.1 collective-permute-start.80
  261.0 4.8 %fusion.175 = (bf16[3072]{0:T(1024)(128)(2,1)S(1)}, bf16[256,3072]{1,0:T(8,128)(2,1)S(1)}) fusion(f32[256,3072]{1,0:T(8,128)S(1)} %copy-done.105, f32[256,3072]{1,0:T(8,128)S(1)} %copy-done.106, bf16[256,768]{1,0:T(8,128)(2,1)S(1)} %get-tuple-element.152, bf16[3072,768]{1,0:T(8,128)(2,1)} %bitcast.294), kind=kOutput, calls=%fused_computation.391 | convolution fusion | flops 1219752960 | bytes 12982272 | tf_op jit(solution)/shard_map/dot_general | solution.py:34
  274.3 3.9 fusion.55
  278.2 4.4 fusion.52
  289.5 3.8 convolution_convert_fusion.1
  293.3 3.5 convolution_convert_fusion
  308.6 7.4 %collective-permute-done.81.refs_1_ = bf16[4,42,768]{2,1,0:T(8,128)(2,1)S(1)} collective-permute-done((bf16[4,42,768]{2,1,0:T(8,128)(2,1)S(1)}, bf16[4,42,768]{2,1,0:T(8,128)(2,1)S(1)}, u32[]{:S(2)}, u32[]{:S(2)}) %collective-permute-start.81) | collective-permute-done | bytes 258080 | tf_op jit(solution)/shard_map/ppermute | solution.py:463
  319.1 7.4 %copy.261 = bf16[768,3200]{1,0:T(8,128)(2,1)} copy(bf16[768,3200]{0,1:T(8,128)(2,1)} %fusion.3) | data formatting | bytes 9830400 | tf_op jit(solution)/shard_map/concatenate | solution.py:980
  331.7 4.0 fusion.37
  357.9 6.4 %shard_map.304 = bf16[2,4,24,3072]{3,2,1,0:T(8,128)(2,1)} custom-call(s32[6]{0:T(128)} %stack.274.spots_ref, bf16[4,4,2,24,3072]{4,3,2,1,0:T(8,128)(2,1)} %bitcast.269, bf16[4,4,24,3072]{3,2,1,0:T(8,128)(2,1)} %collective-permute-done.66.b_ref), custom_call_target="tpu_custom_call" | custom-call | flops 1179648 | bytes 3538944 | tf_op jit(solution)/shard_map/pallas_call | solution.py:570
  365.8 6.4 %shard_map.308 = bf16[2,4,96,768]{3,2,1,0:T(8,128)(2,1)} custom-call(s32[6]{0:T(128)} %stack.274.spots_ref, bf16[4,4,2,96,768]{4,3,2,1,0:T(8,128)(2,1)} %bitcast.265, bf16[4,4,96,768]{3,2,1,0:T(8,128)(2,1)} %collective-permute-done.72.b_ref), custom_call_target="tpu_custom_call" | custom-call | flops 1179648 | bytes 3538944 | tf_op jit(solution)/shard_map/pallas_call | solution.py:570
  377.7 6.4 %shard_map.300 = bf16[2,4,24,3200]{3,2,1,0:T(8,128)(2,1)} custom-call(s32[6]{0:T(128)} %stack.274.spots_ref, bf16[4,4,2,24,3200]{4,3,2,1,0:T(8,128)(2,1)} %bitcast.273, bf16[4,4,24,3200]{3,2,1,0:T(8,128)(2,1)} %collective-permute-done.60.b_ref), custom_call_target="tpu_custom_call" | custom-call | flops 1228800 | bytes 3686400 | tf_op jit(solution)/shard_map/pallas_call | solution.py:570
  387.2 4.4 shard_map.305
  395.2 4.2 shard_map.309
  402.5 5.5 %collective-permute-done.68.d_ref = bf16[4,24,3072]{2,1,0:T(8,128)(2,1)S(1)} collective-permute-done((bf16[4,24,3072]{2,1,0:T(8,128)(2,1)}, bf16[4,24,3072]{2,1,0:T(8,128)(2,1)S(1)}, u32[]{:S(2)}, u32[]{:S(2)}) %collective-permute-start.68) | collective-permute-done | bytes 589856 | tf_op jit(solution)/shard_map/ppermute | solution.py:467
  409.0 4.2 shard_map.306
  418.8 4.2 shard_map.301
  426.1 4.3 shard_map.310
  436.1 4.4 shard_map.302
  443.4 8.4 %collective-permute-done.76 = bf16[96,768]{1,0:T(8,128)(2,1)S(1)} collective-permute-done((bf16[96,768]{1,0:T(8,128)(2,1)}, bf16[96,768]{1,0:T(8,128)(2,1)S(1)}, u32[]{:S(2)}, u32[]{:S(2)}) %collective-permute-start.76) | collective-permute-done | bytes 147488 | tf_op jit(solution)/shard_map/ppermute | solution.py:451
  452.6 4.1 collective-permute-done.64
  (669 shorter events, 249.0 us)
Async XLA Ops:
  0.7 28.1 %collective-permute-start.20 = (bf16[96,768]{1,0:T(8,128)(2,1)}, bf16[96,768]{1,0:T(8,128)(2,1)S(1)}, u32[]{:S(2)}, u32[]{:S(2)}) collective-permute-start(bf16[96,768]{1,0:T(8,128)(2,1)} %refs_0_.1), channel_id=1, source_target_pairs={{0,8},{8,16},{16,24},{24,0},{1,9},{9,17},{17,25},{25,1},{2,10},{10... | collective-permute-start | bytes 442376 | tf_op jit(solution)/shard_map/ppermute | solution.py:451
  3.8 25.7 %collective-permute-start.21 = (bf16[96,768]{1,0:T(8,128)(2,1)}, bf16[96,768]{1,0:T(8,128)(2,1)S(1)}, u32[]{:S(2)}, u32[]{:S(2)}) collective-permute-start(bf16[96,768]{1,0:T(8,128)(2,1)} %refs_0_.1), channel_id=1, source_target_pairs={{0,16},{8,24},{16,0},{24,8},{1,17},{9,25},{17,1},{25,9},{2,18},{10... | collective-permute-start | bytes 442376 | tf_op jit(solution)/shard_map/ppermute | solution.py:451
  24.8 32.1 %collective-permute-start = (bf16[24,3200]{1,0:T(8,128)(2,1)S(1)}, bf16[24,3200]{1,0:T(8,128)(2,1)S(1)}, u32[]{:S(2)}, u32[]{:S(2)}) collective-permute-start(bf16[24,3200]{1,0:T(8,128)(2,1)S(1)} %fusion.96.refs_0_), channel_id=1, source_target_pairs={{0,8},{8,16},{16,24},{24,0},{1,9},{9,17},{17,25},{25,1},{2,10},{10... | collective-permute-start | bytes 460808 | tf_op jit(solution)/shard_map/ppermute | solution.py:451
  25.1 31.8 %collective-permute-start.1 = (bf16[24,3200]{1,0:T(8,128)(2,1)S(1)}, bf16[24,3200]{1,0:T(8,128)(2,1)S(1)}, u32[]{:S(2)}, u32[]{:S(2)}) collective-permute-start(bf16[24,3200]{1,0:T(8,128)(2,1)S(1)} %fusion.96.refs_0_), channel_id=1, source_target_pairs={{0,16},{8,24},{16,0},{24,8},{1,17},{9,25},{17,1},{25,9},{2,18},{10... | collective-permute-start | bytes 460808 | tf_op jit(solution)/shard_map/ppermute | solution.py:451
  27.1 32.8 %collective-permute-start.2 = (bf16[24,3200]{1,0:T(8,128)(2,1)S(1)}, bf16[24,3200]{1,0:T(8,128)(2,1)S(1)}, u32[]{:S(2)}, u32[]{:S(2)}) collective-permute-start(bf16[24,3200]{1,0:T(8,128)(2,1)S(1)} %fusion.96.refs_0_), channel_id=1, source_target_pairs={{0,24},{8,0},{16,8},{24,16},{1,25},{9,1},{17,9},{25,17},{2,26},{10... | collective-permute-start | bytes 460808 | tf_op jit(solution)/shard_map/ppermute | solution.py:451
  29.5 32.0 %collective-permute-start.10 = (bf16[24,3840]{1,0:T(8,128)(2,1)S(1)}, bf16[24,3840]{1,0:T(8,128)(2,1)S(1)}, u32[]{:S(2)}, u32[]{:S(2)}) collective-permute-start(bf16[24,3840]{1,0:T(8,128)(2,1)S(1)} %constant_dynamic-update-slice_fusion.refs_0_), channel_id=1, source_target_pairs={{0,8},{8,16},{16,24},{24,0},{1,9},{9,17},{17,25},{25,1},{2,10},{10... | collective-permute-start | bytes 552968 | tf_op jit(solution)/shard_map/ppermute | solution.py:451
  42.1 58.7 %collective-permute-start.37 = (bf16[96,2112]{1,0:T(8,128)(2,1)S(1)}, bf16[96,2112]{1,0:T(8,128)(2,1)S(1)}, u32[]{:S(2)}, u32[]{:S(2)}) collective-permute-start(bf16[96,2112]{1,0:T(8,128)(2,1)S(1)} %pad_maximum_fusion.1.refs_0_), channel_id=1, source_target_pairs={{0,8},{8,16},{16,24},{24,0},{1,9},{9,17},{17,25},{25,1},{2,10},{10... | collective-permute-start | bytes 1216520 | tf_op jit(solution)/shard_map/ppermute | solution.py:451
  56.9 45.0 %collective-permute-start.38 = (bf16[96,2112]{1,0:T(8,128)(2,1)S(1)}, bf16[96,2112]{1,0:T(8,128)(2,1)S(1)}, u32[]{:S(2)}, u32[]{:S(2)}) collective-permute-start(bf16[96,2112]{1,0:T(8,128)(2,1)S(1)} %pad_maximum_fusion.1.refs_0_), channel_id=1, source_target_pairs={{0,16},{8,24},{16,0},{24,8},{1,17},{9,25},{17,1},{25,9},{2,18},{10... | collective-permute-start | bytes 1216520 | tf_op jit(solution)/shard_map/ppermute | solution.py:451
  57.0 28.2 %collective-permute-start.11 = (bf16[24,3840]{1,0:T(8,128)(2,1)S(1)}, bf16[24,3840]{1,0:T(8,128)(2,1)S(1)}, u32[]{:S(2)}, u32[]{:S(2)}) collective-permute-start(bf16[24,3840]{1,0:T(8,128)(2,1)S(1)} %constant_dynamic-update-slice_fusion.refs_0_), channel_id=1, source_target_pairs={{0,16},{8,24},{16,0},{24,8},{1,17},{9,25},{17,1},{25,9},{2,18},{10... | collective-permute-start | bytes 552968 | tf_op jit(solution)/shard_map/ppermute | solution.py:451
  59.9 38.8 %collective-permute-start.12 = (bf16[24,3840]{1,0:T(8,128)(2,1)S(1)}, bf16[24,3840]{1,0:T(8,128)(2,1)S(1)}, u32[]{:S(2)}, u32[]{:S(2)}) collective-permute-start(bf16[24,3840]{1,0:T(8,128)(2,1)S(1)} %constant_dynamic-update-slice_fusion.refs_0_), channel_id=1, source_target_pairs={{0,24},{8,0},{16,8},{24,16},{1,25},{9,1},{17,9},{25,17},{2,26},{10... | collective-permute-start | bytes 552968 | tf_op jit(solution)/shard_map/ppermute | solution.py:451
  61.5 47.4 %collective-permute-start.23 = (bf16[4,96,768]{2,1,0:T(8,128)(2,1)S(1)}, bf16[4,96,768]{2,1,0:T(8,128)(2,1)S(1)}, u32[]{:S(2)}, u32[]{:S(2)}) collective-permute-start(bf16[4,96,768]{2,1,0:T(8,128)(2,1)S(1)} %shard_map.293.refs_0_), channel_id=1, source_target_pairs={{0,2},{1,5},{2,0},{3,7},{4,6},{5,1},{6,4},{7,3},{8,10},{9,13},{10,... | collective-permute-start | bytes 1769480 | tf_op jit(solution)/shard_map/ppermute | solution.py:463
  85.1 21.3 %collective-permute-start.39 = (bf16[96,2112]{1,0:T(8,128)(2,1)S(1)}, bf16[96,2112]{1,0:T(8,128)(2,1)S(1)}, u32[]{:S(2)}, u32[]{:S(2)}) collective-permute-start(bf16[96,2112]{1,0:T(8,128)(2,1)S(1)} %pad_maximum_fusion.1.refs_0_), channel_id=1, source_target_pairs={{0,24},{8,0},{16,8},{24,16},{1,25},{9,1},{17,9},{25,17},{2,26},{10... | collective-permute-start | bytes 1216520 | tf_op jit(solution)/shard_map/ppermute | solution.py:451
  106.5 21.7 %collective-permute-start.4 = (bf16[4,24,3200]{2,1,0:T(8,128)(2,1)S(1)}, bf16[4,24,3200]{2,1,0:T(8,128)(2,1)}, u32[]{:S(2)}, u32[]{:S(2)}) collective-permute-start(bf16[4,24,3200]{2,1,0:T(8,128)(2,1)S(1)} %shard_map.289.refs_0_), channel_id=1, source_target_pairs={{0,4},{1,3},{2,6},{3,1},{4,0},{5,7},{6,2},{7,5},{8,12},{9,11},{10,... | collective-permute-start | bytes 1843208 | tf_op jit(solution)/shard_map/ppermute | solution.py:467
  108.9 24.6 %collective-permute-start.13 = (bf16[4,24,3840]{2,1,0:T(8,128)(2,1)}, bf16[4,24,3840]{2,1,0:T(8,128)(2,1)}, u32[]{:S(2)}, u32[]{:S(2)}) collective-permute-start(bf16[4,24,3840]{2,1,0:T(8,128)(2,1)} %shard_map.291.refs_0_), channel_id=1, source_target_pairs={{0,2},{1,5},{2,0},{3,7},{4,6},{5,1},{6,4},{7,3},{8,10},{9,13},{10,... | collective-permute-start | bytes 2211848 | tf_op jit(solution)/shard_map/ppermute | solution.py:463
  140.1 19.8 %collective-permute-start.15 = (bf16[4,24,3840]{2,1,0:T(8,128)(2,1)}, bf16[4,24,3840]{2,1,0:T(8,128)(2,1)}, u32[]{:S(2)}, u32[]{:S(2)}) collective-permute-start(bf16[4,24,3840]{2,1,0:T(8,128)(2,1)} %collective-permute-done.13.refs_1_), channel_id=1, source_target_pairs={{0,4},{1,3},{2,6},{3,1},{4,0},{5,7},{6,2},{7,5},{8,12},{9,11},{10,... | collective-permute-start | bytes 2211848 | tf_op jit(solution)/shard_map/ppermute | solution.py:467
  155.0 29.7 %collective-permute-start.16 = (bf16[4,24,3840]{2,1,0:T(8,128)(2,1)}, bf16[4,24,3840]{2,1,0:T(8,128)(2,1)}, u32[]{:S(2)}, u32[]{:S(2)}) collective-permute-start(bf16[4,24,3840]{2,1,0:T(8,128)(2,1)} %shard_map.291.refs_0_), channel_id=1, source_target_pairs={{0,1},{1,0},{2,3},{3,2},{4,5},{5,4},{6,7},{7,6},{8,9},{9,8},{10,11... | collective-permute-start | bytes 2211848 | tf_op jit(solution)/shard_map/ppermute | solution.py:455
  155.5 29.2 %collective-permute-start.17 = (bf16[4,24,3840]{2,1,0:T(8,128)(2,1)}, bf16[4,24,3840]{2,1,0:T(8,128)(2,1)}, u32[]{:S(2)}, u32[]{:S(2)}) collective-permute-start(bf16[4,24,3840]{2,1,0:T(8,128)(2,1)} %collective-permute-done.13.refs_1_), channel_id=1, source_target_pairs={{0,1},{1,0},{2,3},{3,2},{4,5},{5,4},{6,7},{7,6},{8,9},{9,8},{10,11... | collective-permute-start | bytes 2211848 | tf_op jit(solution)/shard_map/ppermute | solution.py:455
  155.6 29.1 %collective-permute-start.18 = (bf16[4,24,3840]{2,1,0:T(8,128)(2,1)}, bf16[4,24,3840]{2,1,0:T(8,128)(2,1)}, u32[]{:S(2)}, u32[]{:S(2)}) collective-permute-start(bf16[4,24,3840]{2,1,0:T(8,128)(2,1)} %collective-permute-done.14.refs_2_), channel_id=1, source_target_pairs={{0,1},{1,0},{2,3},{3,2},{4,5},{5,4},{6,7},{7,6},{8,9},{9,8},{10,11... | collective-permute-start | bytes 2211848 | tf_op jit(solution)/shard_map/ppermute | solution.py:455
  159.9 24.8 %collective-permute-start.19 = (bf16[4,24,3840]{2,1,0:T(8,128)(2,1)}, bf16[4,24,3840]{2,1,0:T(8,128)(2,1)}, u32[]{:S(2)}, u32[]{:S(2)}) collective-permute-start(bf16[4,24,3840]{2,1,0:T(8,128)(2,1)} %collective-permute-done.15.refs_3_), channel_id=1, source_target_pairs={{0,1},{1,0},{2,3},{3,2},{4,5},{5,4},{6,7},{7,6},{8,9},{9,8},{10,11... | collective-permute-start | bytes 2211848 | tf_op jit(solution)/shard_map/ppermute | solution.py:455
  253.6 51.8 %collective-permute-start.78 = (bf16[42,768]{1,0:T(8,128)(2,1)S(1)}, bf16[42,768]{1,0:T(8,128)(2,1)S(1)}, u32[]{:S(2)}, u32[]{:S(2)}) collective-permute-start(bf16[42,768]{1,0:T(8,128)(2,1)S(1)} %pad.15.refs_0_), channel_id=1, source_target_pairs={{0,8},{8,16},{16,24},{24,0},{1,9},{9,17},{17,25},{25,1},{2,10},{10... | collective-permute-start | bytes 193544 | tf_op jit(solution)/shard_map/ppermute | solution.py:451
  253.6 51.7 %collective-permute-start.79 = (bf16[42,768]{1,0:T(8,128)(2,1)S(1)}, bf16[42,768]{1,0:T(8,128)(2,1)S(1)}, u32[]{:S(2)}, u32[]{:S(2)}) collective-permute-start(bf16[42,768]{1,0:T(8,128)(2,1)S(1)} %pad.15.refs_0_), channel_id=1, source_target_pairs={{0,16},{8,24},{16,0},{24,8},{1,17},{9,25},{17,1},{25,9},{2,18},{10... | collective-permute-start | bytes 193544 | tf_op jit(solution)/shard_map/ppermute | solution.py:451
  253.7 51.6 %collective-permute-start.80 = (bf16[42,768]{1,0:T(8,128)(2,1)S(1)}, bf16[42,768]{1,0:T(8,128)(2,1)S(1)}, u32[]{:S(2)}, u32[]{:S(2)}) collective-permute-start(bf16[42,768]{1,0:T(8,128)(2,1)S(1)} %pad.15.refs_0_), channel_id=1, source_target_pairs={{0,24},{8,0},{16,8},{24,16},{1,25},{9,1},{17,9},{25,17},{2,26},{10... | collective-permute-start | bytes 193544 | tf_op jit(solution)/shard_map/ppermute | solution.py:451
  302.2 55.7 %collective-permute-start.66 = (bf16[4,4,24,3072]{3,2,1,0:T(8,128)(2,1)}, bf16[4,4,24,3072]{3,2,1,0:T(8,128)(2,1)}, u32[]{:S(2)}, u32[]{:S(2)}) collective-permute-start(bf16[4,4,24,3072]{3,2,1,0:T(8,128)(2,1)} %shard_map.303), channel_id=1, source_target_pairs={{0,1},{1,0},{2,3},{3,2},{4,5},{5,4},{6,7},{7,6},{8,9},{9,8},{10,11... | collective-permute-start | bytes 7077896 | tf_op jit(solution)/shard_map/ppermute | solution.py:455
  305.3 60.5 %collective-permute-start.72 = (bf16[4,4,96,768]{3,2,1,0:T(8,128)(2,1)}, bf16[4,4,96,768]{3,2,1,0:T(8,128)(2,1)}, u32[]{:S(2)}, u32[]{:S(2)}) collective-permute-start(bf16[4,4,96,768]{3,2,1,0:T(8,128)(2,1)} %shard_map.307), channel_id=1, source_target_pairs={{0,1},{1,0},{2,3},{3,2},{4,5},{5,4},{6,7},{7,6},{8,9},{9,8},{10,11... | collective-permute-start | bytes 7077896 | tf_op jit(solution)/shard_map/ppermute | solution.py:455
  308.5 22.1 %collective-permute-start.84 = (bf16[4,42,768]{2,1,0:T(8,128)(2,1)S(1)}, bf16[4,42,768]{2,1,0:T(8,128)(2,1)S(1)}, u32[]{:S(2)}, u32[]{:S(2)}) collective-permute-start(bf16[4,42,768]{2,1,0:T(8,128)(2,1)S(1)} %shard_map.311.refs_0_), channel_id=1, source_target_pairs={{0,1},{1,0},{2,3},{3,2},{4,5},{5,4},{6,7},{7,6},{8,9},{9,8},{10,11... | collective-permute-start | bytes 774152 | tf_op jit(solution)/shard_map/ppermute | solution.py:455
  330.6 47.1 %collective-permute-start.60 = (bf16[4,4,24,3200]{3,2,1,0:T(8,128)(2,1)}, bf16[4,4,24,3200]{3,2,1,0:T(8,128)(2,1)}, u32[]{:S(2)}, u32[]{:S(2)}) collective-permute-start(bf16[4,4,24,3200]{3,2,1,0:T(8,128)(2,1)} %shard_map.299), channel_id=1, source_target_pairs={{0,1},{1,0},{2,3},{3,2},{4,5},{5,4},{6,7},{7,6},{8,9},{9,8},{10,11... | collective-permute-start | bytes 7372808 | tf_op jit(solution)/shard_map/ppermute | solution.py:455
  364.2 23.0 %collective-permute-start.67 = (bf16[2,4,24,3072]{3,2,1,0:T(8,128)(2,1)}, bf16[2,4,24,3072]{3,2,1,0:T(8,128)(2,1)}, u32[]{:S(2)}, u32[]{:S(2)}) collective-permute-start(bf16[2,4,24,3072]{3,2,1,0:T(8,128)(2,1)} %shard_map.304), channel_id=1, source_target_pairs={{0,2},{1,5},{2,0},{3,7},{4,6},{5,1},{6,4},{7,3},{8,10},{9,13},{10,... | collective-permute-start | bytes 3538952 | tf_op jit(solution)/shard_map/ppermute | solution.py:463
  372.1 22.0 %collective-permute-start.73 = (bf16[2,4,96,768]{3,2,1,0:T(8,128)(2,1)}, bf16[2,4,96,768]{3,2,1,0:T(8,128)(2,1)S(1)}, u32[]{:S(2)}, u32[]{:S(2)}) collective-permute-start(bf16[2,4,96,768]{3,2,1,0:T(8,128)(2,1)} %shard_map.308), channel_id=1, source_target_pairs={{0,2},{1,5},{2,0},{3,7},{4,6},{5,1},{6,4},{7,3},{8,10},{9,13},{10,... | collective-permute-start | bytes 3538952 | tf_op jit(solution)/shard_map/ppermute | solution.py:463
  384.1 34.7 %collective-permute-start.61 = (bf16[2,4,24,3200]{3,2,1,0:T(8,128)(2,1)}, bf16[2,4,24,3200]{3,2,1,0:T(8,128)(2,1)}, u32[]{:S(2)}, u32[]{:S(2)}) collective-permute-start(bf16[2,4,24,3200]{3,2,1,0:T(8,128)(2,1)} %shard_map.300), channel_id=1, source_target_pairs={{0,2},{1,5},{2,0},{3,7},{4,6},{5,1},{6,4},{7,3},{8,10},{9,13},{10,... | collective-permute-start | bytes 3686408 | tf_op jit(solution)/shard_map/ppermute | solution.py:463
  399.4 25.9 %collective-permute-start.74 = (bf16[4,96,768]{2,1,0:T(8,128)(2,1)}, bf16[4,96,768]{2,1,0:T(8,128)(2,1)S(1)}, u32[]{:S(2)}, u32[]{:S(2)}) collective-permute-start(bf16[4,96,768]{2,1,0:T(8,128)(2,1)} %shard_map.309), channel_id=1, source_target_pairs={{0,4},{1,3},{2,6},{3,1},{4,0},{5,7},{6,2},{7,5},{8,12},{9,11},{10,... | collective-permute-start | bytes 1769480 | tf_op jit(solution)/shard_map/ppermute | solution.py:467
  432.0 19.8 %collective-permute-start.76 = (bf16[96,768]{1,0:T(8,128)(2,1)}, bf16[96,768]{1,0:T(8,128)(2,1)S(1)}, u32[]{:S(2)}, u32[]{:S(2)}) collective-permute-start(bf16[96,768]{1,0:T(8,128)(2,1)} %get-tuple-element.37), channel_id=1, source_target_pairs={{0,16},{8,24},{16,0},{24,8},{1,17},{9,25},{17,1},{25,9},{2,18},{10... | collective-permute-start | bytes 442376 | tf_op jit(solution)/shard_map/ppermute | solution.py:451
  432.5 19.4 %collective-permute-start.75 = (bf16[96,768]{1,0:T(8,128)(2,1)}, bf16[96,768]{1,0:T(8,128)(2,1)S(1)}, u32[]{:S(2)}, u32[]{:S(2)}) collective-permute-start(bf16[96,768]{1,0:T(8,128)(2,1)} %get-tuple-element.36), channel_id=1, source_target_pairs={{0,8},{8,16},{16,24},{24,0},{1,9},{9,17},{17,25},{25,1},{2,10},{10... | collective-permute-start | bytes 442376 | tf_op jit(solution)/shard_map/ppermute | solution.py:451
  (167 other events, 1539.3 us)

commit v2 on v0

--- a/solution.py
+++ b/solution.py
@@ -4,6 +4,8 @@
 import jax
 import jax.numpy as jnp
 from jax import lax
+from jax.experimental import pallas as pl
+from jax.experimental.pallas import tpu as pltpu
 from jax.sharding import PartitionSpec as P
 
 D = 768
@@ -442,9 +444,1111 @@
     return (layer_output, input_gradient) + tuple(summed)
 
 
+def swap_dp(array_in, shift):
+    return lax.ppermute(array_in, "dp", [(i, (i + shift) % 4) for i in range(4)])
+
+
+def swap_core(array_in):
+    return lax.ppermute(array_in, "seq", [(i, i ^ 1) for i in range(8)])
+
+
+def swap_chip(array_in, mask):
+    return lax.ppermute(array_in, "seq", [(i, i ^ (2 * mask)) for i in range(8)])
+
+
+def swap_one(array_in):
+    return lax.ppermute(array_in, "seq", [(i, i ^ (2 if i % 2 == 0 else 4)) for i in range(8)])
+
+
+def swap_two(array_in):
+    return lax.ppermute(array_in, "seq", [(i, i ^ (4 if i % 2 == 0 else 2)) for i in range(8)])
+
+
+def place_in():
+    layer = lax.axis_index("dp")
+    spot = lax.axis_index("seq")
+    return layer, spot // 2, lax.rem(spot, 2)
+
+
+def after(array_in, *before):
+    return lax.optimization_barrier((array_in,) + before)[0]
+
+
+def wide(array_in):
+    return array_in.astype(jnp.float32)
+
+
+def low(array_in):
+    return array_in.astype(jnp.bfloat16)
+
+
+def copies(pieces, shapes, moves):
+    count, made = len(pieces), len(shapes)
+    total = len(moves(0, 0, 0))
+
+    def kernel(*refs):
+        outs, held, sems = refs[count : count + made], refs[count + made : -1], refs[-1]
+        inward = [pltpu.make_async_copy(refs[i], held[i], sems.at[0, i]) for i in range(count)]
+        for copy in inward:
+            copy.start()
+        outward = []
+        for i, (piece, part, out, place) in enumerate(moves(*place_in())):
+            if inward[piece] is not None:
+                inward[piece].wait()
+                inward[piece] = None
+            copy = pltpu.make_async_copy(held[piece].at[part], outs[out].at[place], sems.at[1, i])
+            copy.start()
+            outward.append(copy)
+        for copy in outward:
+            copy.wait()
+
+    size = 2 * sum(math.prod(shape) for shape in shapes) * 2
+    return pl.pallas_call(
+        kernel,
+        out_shape=[jax.ShapeDtypeStruct(shape, pieces[0].dtype) for shape in shapes],
+        in_specs=[pl.BlockSpec(memory_space=pl.ANY)] * count,
+        out_specs=[pl.BlockSpec(memory_space=pl.ANY)] * made,
+        scratch_shapes=[pltpu.VMEM(piece.shape, piece.dtype) for piece in pieces]
+        + [pltpu.SemaphoreType.DMA((2, max(count, total)))],
+        compiler_params=pltpu.CompilerParams(vmem_limit_bytes=24 * 2**20),
+        cost_estimate=pl.CostEstimate(flops=0, bytes_accessed=size, transcendentals=0),
+    )(*pieces)
+
+
+every = slice(None)
+
+
+def gather_dp(shard):
+    pieces = [shard] + [swap_dp(shard, shift) for shift in (1, 2, 3)]
+    return copies(
+        pieces,
+        [(4,) + shard.shape],
+        lambda layer, chip, core: [(i, every, 0, lax.rem(layer + 4 - i, 4)) for i in range(4)],
+    )[0]
+
+
+def plane_moves(column, *before):
+    ready = after(column, *before) if before else column
+    first = swap_one(ready)
+    second = swap_two(ready)
+    return [column, first, second, swap_two(first)]
+
+
+def plane_order(chip, core):
+    near, far = chip ^ (1 + core), chip ^ (2 - core)
+    return (chip, near, far, chip ^ 3), (chip, far, near, chip ^ 3)
+
+
+def gather_plane(mine):
+    def moves(layer, chip, core):
+        own, other = plane_order(chip, core)
+        found = [(i, every, 0, (every, own[i], core)) for i in range(4)]
+        return found + [(4 + i, every, 0, (every, other[i], 1 - core)) for i in range(4)]
+
+    shape = (4, 4, 2) + mine[0].shape[1:]
+    return copies(mine + [swap_core(piece) for piece in mine], [shape], moves)[0]
+
+
+def gather_down(mine):
+    def moves(layer, chip, core):
+        own, other = plane_order(chip, core)
+        found = []
+        for i in range(8):
+            spot, side = (own[i], core) if i < 4 else (other[i - 4], 1 - core)
+            for quarter in range(4):
+                part = (every, every, slice(quarter * D, (quarter + 1) * D))
+                found.append((i, part, 0, (every, spot, side, quarter)))
+        return found
+
+    return copies(mine + [swap_core(piece) for piece in mine], [(4, 4, 2, 4, 24, D)], moves)[0]
+
+
+class Sum:
+    def __init__(self, kept, gone):
+        layer, chip, core = place_in()
+        self.kept = kept
+        self.shape = kept.shape[2:]
+        self.spots = jnp.stack([chip ^ (1 + core), chip ^ 3, chip ^ (2 - core), chip, layer])
+        self.got = swap_core(gone)
+
+    def part(self, take):
+        return pl.BlockSpec((4, None) + self.shape, take)
+
+    def run(self, kernel, grid, in_specs, out_specs, out_shape, *operands):
+        size = sum(math.prod(a.shape) * 2 for a in operands)
+        return pl.pallas_call(
+            kernel,
+            grid_spec=pltpu.PrefetchScalarGridSpec(
+                num_scalar_prefetch=1, grid=grid, in_specs=in_specs, out_specs=out_specs
+            ),
+            out_shape=out_shape,
+            compiler_params=pltpu.CompilerParams(vmem_limit_bytes=32 * 2**20),
+            cost_estimate=pl.CostEstimate(flops=size, bytes_accessed=size, transcendentals=0),
+        )(self.spots, *operands)
+
+    def first(self, *before):
+        def kernel(spots_ref, a_ref, b_ref, o_ref):
+            o_ref[...] = low(wide(a_ref[...]) + wide(b_ref[...]))
+
+        near = self.part(lambda i, s: (0, s[i], 0, 0))
+        out = pl.BlockSpec((None, 4) + self.shape, lambda i, s: (i, 0, 0, 0))
+        got = after(self.got, *before) if before else self.got
+        sent = self.run(kernel, (2,), [near, near], out, half(2, 4, *self.shape), self.kept, got)
+        self.back = swap_one(sent)
+        return sent
+
+    def second(self, *before):
+        def kernel(spots_ref, a_ref, b_ref, c_ref, o_ref):
+            o_ref[...] = low(wide(a_ref[...]) + wide(b_ref[...]) + wide(c_ref[...]))
+
+        pair = (2, None) + self.shape
+        far = pl.BlockSpec(pair, lambda i, s: (i, s[2], 0, 0))
+        moved = pl.BlockSpec((None, 2) + self.shape, lambda i, s: (1, i, 0, 0))
+        out = pl.BlockSpec((2,) + self.shape, lambda i, s: (i, 0, 0))
+        back = after(self.back, *before) if before else self.back
+        onward = self.run(
+            kernel, (2,), [far, far, moved], out, half(4, *self.shape), self.kept, self.got, back
+        )
+        self.last = swap_two(onward)
+        return onward
+
+    def third(self, *before):
+        def kernel(spots_ref, a_ref, b_ref, c_ref, d_ref, own_ref, *outs):
+            for shift in range(4):
+                level = lax.rem(spots_ref[4] + shift, 4)
+                total = wide(a_ref[level]) + wide(b_ref[level]) + wide(c_ref[level])
+                total = total + wide(d_ref[level])
+                if shift:
+                    outs[shift - 1][...] = low(total)
+                else:
+                    own_ref[...] = total
+
+        here = self.part(lambda i, s: (0, s[3], 0, 0))
+        moved = pl.BlockSpec((None, 4) + self.shape, lambda i, s: (0, 0, 0, 0))
+        full = pl.BlockSpec((4,) + self.shape, lambda i, s: (0, 0, 0))
+        flat = pl.BlockSpec(self.shape, lambda i, s: (0, 0))
+        last = after(self.last, *before) if before else self.last
+        self.own, *others = self.run(
+            kernel,
+            (1,),
+            [here, here, moved, full],
+            [flat] * 4,
+            [shape_of(*self.shape)] + [half(*self.shape)] * 3,
+            self.kept,
+            self.got,
+            self.back,
+            last,
+        )
+        self.others = [swap_dp(other, shift) for shift, other in zip((1, 2, 3), others)]
+        return self.own
+
+    def total(self):
+        return self.own + wide(self.others[0]) + wide(self.others[1]) + wide(self.others[2])
+
+
+def norm_parts(values):
+    centered = values - jnp.mean(values, axis=-1, keepdims=True)
+    variance = jnp.mean(centered * centered, axis=-1, keepdims=True)
+    scale = lax.rsqrt(variance + epsilon)
+    return centered * scale, scale
+
+
+def norm_back(grad, normed, scale, gain):
+    scaled = grad * gain
+    return scale * (
+        scaled
+        - jnp.mean(scaled, axis=-1, keepdims=True)
+        - normed * jnp.mean(scaled * normed, axis=-1, keepdims=True)
+    )
+
+
+def gelu_slope(hidden):
+    return 0.5 * (1.0 + lax.erf(hidden * math.sqrt(0.5))) + hidden * jnp.exp(
+        -0.5 * hidden * hidden
+    ) * (1.0 / math.sqrt(2.0 * math.pi))
+
+
+def shape_of(*shape, dtype=jnp.float32):
+    return jax.ShapeDtypeStruct(shape, dtype)
+
+
+def half(*shape):
+    return jax.ShapeDtypeStruct(shape, jnp.bfloat16)
+
+
+def on_core(kernel, out_shape, operands, flops, grid=(), in_specs=None, out_specs=None, scratch=()):
+    arrays = jax.tree.leaves(out_shape) + list(operands)
+    size = sum(math.prod(a.shape) * a.dtype.itemsize for a in arrays)
+    extra = {} if in_specs is None else {"in_specs": in_specs, "out_specs": out_specs}
+    return pl.pallas_call(
+        kernel,
+        out_shape=out_shape,
+        grid=grid,
+        scratch_shapes=scratch,
+        compiler_params=pltpu.CompilerParams(vmem_limit_bytes=52 * 2**20),
+        cost_estimate=pl.CostEstimate(flops=flops, bytes_accessed=size, transcendentals=0),
+        **extra,
+    )(*operands)
+
+
+def column_sum(array_in):
+    return jnp.sum(array_in, axis=0, keepdims=True)
+
+
+def prepare(
+    mix_ref,
+    out_ref,
+    up_ref,
+    down_ref,
+    vectors_ref,
+    bias_ref,
+    cross_mix_ref,
+    cross_out_ref,
+    cross_up_ref,
+    cross_vectors_ref,
+    cross_bias_ref,
+    table_ref,
+    one_ref,
+    two_ref,
+    part_a,
+    part_b,
+    part_c,
+    part_d,
+    small,
+    parts,
+):
+    one_ref[:, 0 : 3 * D] = mix_ref[...]
+    one_ref[:, 3 * D : 4 * D] = out_ref[...]
+    small[...] = jnp.zeros_like(small)
+    small[0:8, 0:24] = wide(vectors_ref[...])
+    small[8:16, 0:24] = wide(cross_vectors_ref[...])
+    small[16:80, 0:24] = wide(table_ref[...])
+    small[80:84, 0:24] = wide(bias_ref[...])
+    small[84:88, 0:24] = wide(cross_bias_ref[...])
+    one_ref[:, 4 * D : 4 * D + 128] = low(small[...].T[0:24, :])
+    two_ref[:, 0 : 4 * D] = up_ref[...]
+    two_ref[:, 4 * D : 5 * D] = cross_out_ref[...]
+    for quarter in range(4):
+        two_ref[:, (5 + quarter) * D : (6 + quarter) * D] = down_ref[quarter]
+    parts[...] = jnp.zeros_like(parts)
+    for spot in range(4):
+        for level in range(4):
+            taken = cross_up_ref[:, 192 * (4 * level + spot) : 192 * (4 * level + spot + 1)]
+            parts[spot, :, 192 * level : 192 * (level + 1)] = taken
+        for third in range(3):
+            taken = cross_mix_ref[:, third * D + 192 * spot : third * D + 192 * (spot + 1)]
+            parts[spot, :, D + 192 * third : D + 192 * (third + 1)] = taken
+    chip = place_in()[1]
+    for mask, ref in enumerate((part_a, part_b, part_c, part_d)):
+        ref[...] = parts[chip ^ mask]
+
+
+def gather_cross(parts, cross_down):
+    pieces = [parts[0]] + [swap_chip(parts[mask], mask) for mask in (1, 2, 3)]
+
+    def moves(layer, chip, core):
+        found = []
+        for mask in range(4):
+            found.append((mask, (every, slice(0, D)), 0, (chip ^ mask, every, slice(0, D))))
+            taken = (every, slice(D, D + 640))
+            found.append((mask, taken, 0, (chip ^ mask, every, slice(2 * D, 2 * D + 640))))
+        found.append((4, every, 0, (every, every, slice(D, 2 * D))))
+        return found
+
+    row = copies(pieces + [cross_down.reshape(4, 24, D)], [(4, 24, 2 * D + 640)], moves)[0]
+    return lax.all_gather(row, "dp")
+
+
+def place_cross(column):
+    other = swap_core(column)
+
+    def moves(layer, chip, core):
+        found = []
+        for piece, side in ((0, core), (1, 1 - core)):
+            lead = (every, every, side, every)
+            source = (every, every, every)
+            found.append((piece, source + (slice(0, D),), 0, lead + (slice(0, D),)))
+            found.append(
+                (piece, source + (slice(2 * D, 2 * D + 640),), 0, lead + (slice(D, D + 640),))
+            )
+            found.append((piece, source + (slice(D, 2 * D),), 1, (every, side)))
+        return found
+
+    up_mix, down = copies(
+        [column, other], [(4, 4, 2, 24, D + 640), (4, 2, 4, 24, D)], moves
+    )
+    return up_mix.reshape(D, D + 640), down.reshape(D, D)
+
+
+def local_attend(tokens_ref, group_ref, docs_ref, docs_column_ref, *outs):
+    mixed_ref, context_ref, probs_ref, n_ref, scale_ref, low_ref, rows_ref = outs
+    rows_ref[...] = wide(group_ref[:, 4 * D : 4 * D + 128]).T
+    tokens = tokens_ref[...]
+    for third in range(3):
+        columns = slice(third * D, (third + 1) * D)
+        mixed = contract(tokens, group_ref[:, columns], 1, 0)
+        if third != 1:
+            mixed = mixed + rows_ref[third // 2 : third // 2 + 1, :]
+        mixed_ref[:, columns] = low(mixed)
+    lane = lax.broadcasted_iota(jnp.int32, (SEG, 128), 1)
+    for segment in range(2):
+        rows = slice(segment * SEG, (segment + 1) * SEG)
+        allowed = docs_column_ref[rows, :] == docs_ref[segment : segment + 1, :]
+        for pair in range(HEADS // 2):
+            query, key, value = (
+                mixed_ref[rows, third * D + pair * 128 : third * D + (pair + 1) * 128]
+                for third in range(3)
+            )
+            found = []
+            for side in range(2):
+                here = (lane < HEAD_DIM) if side == 0 else (lane >= HEAD_DIM)
+                scores = contract(jnp.where(here, query, jnp.zeros_like(query)), key, 1, 1)
+                scores = jnp.where(allowed, scores * HEAD_DIM ** (-0.5), masked_score)
+                powers = jnp.exp(scores - jnp.max(scores, axis=-1, keepdims=True))
+                probs = powers / jnp.sum(powers, axis=-1, keepdims=True)
+                probs_ref[segment * HEADS + 2 * pair + side] = probs
+                found.append(contract(low(probs), value, 1, 0))
+            context = jnp.where(lane < HEAD_DIM, found[0], found[1])
+            context_ref[rows, pair * 128 : (pair + 1) * 128] = low(context)
+    total = wide(tokens) + contract(context_ref[...], group_ref[:, 3 * D : 4 * D], 1, 0)
+    normed, scale = norm_parts(total + rows_ref[2:3, :])
+    n_ref[...] = normed
+    scale_ref[...] = scale
+    low_ref[...] = low(normed * rows_ref[3:4, :] + rows_ref[4:5, :])
+
+
+def local_up_part(low_ref, weight_ref, bias_ref, active_ref, slope_ref):
+    hidden = contract(low_ref[...], weight_ref[...], 1, 0) + wide(bias_ref[...])
+    chance = 0.5 * (1.0 + lax.erf(hidden * math.sqrt(0.5)))
+    density = jnp.exp(-0.5 * hidden * hidden) * (1.0 / math.sqrt(2.0 * math.pi))
+    active_ref[...] = low(hidden * chance)
+    slope_ref[...] = low(chance + hidden * density)
+
+
+def local_down_part(
+    active_ref, weight_ref, first_ref, rows_ref, cot_a, cot_b, places_ref, *outs
+):
+    n_ref, scale_ref, kept_ref, given_ref, total = outs
+    step = pl.program_id(0)
+    part = contract(active_ref[...], weight_ref[...], 1, 0)
+
+    @pl.when(step == 0)
+    def _():
+        first_norm = first_ref[...] * rows_ref[3:4, :] + rows_ref[4:5, :]
+        total[...] = first_norm + rows_ref[5:6, :] + part
+
+    @pl.when(step > 0)
+    def _():
+        total[...] += part
+
+    @pl.when(step == 3)
+    def _():
+        normed, scale = norm_parts(total[...])
+        n_ref[...] = normed
+        scale_ref[...] = scale
+        core = place_in()[2]
+        heads, grads = [], []
+        for place, cot in ((0, cot_a), (1, cot_b)):
+            row = normed[place * SEG : place * SEG + 1] * rows_ref[6:7, :] + rows_ref[7:8, :]
+            heads.append(row + rows_ref[pl.ds(16 + places_ref[place, 0], 1), :])
+            grads.append(wide(cot[...])[0:1])
+        for ref, mine in ((kept_ref, core == 0), (given_ref, core == 1)):
+            ref[...] = jnp.zeros_like(ref)
+            ref[0:1, :] = jnp.where(mine, heads[0], heads[1])
+            ref[1:2, :] = jnp.where(mine, grads[0], grads[1])
+
+
+def join_pair(kept_ref, got_ref, out_ref):
+    core = place_in()[2]
+    out_ref[...] = jnp.zeros_like(out_ref)
+    out_ref[0:2, :] = jnp.where(core == 0, kept_ref[0:2, :], got_ref[0:2, :])
+    out_ref[2:4, :] = jnp.where(core == 0, got_ref[0:2, :], kept_ref[0:2, :])
+
+
+def cross_attend(
+    own_ref, a_ref, b_ref, c_ref, weight_ref, rows_ref, docs_ref, docs_column_ref, *outs
+):
+    in_ref, grad_ref, mixed_ref, probs_ref, context_ref = outs
+    layer, chip, core = place_in()
+    for mask, ref in enumerate((own_ref, a_ref, b_ref, c_ref)):
+        for side in range(2):
+            row = 2 * (chip ^ mask) + side
+            in_ref[pl.ds(row, 1), :] = ref[2 * side : 2 * side + 1, :]
+            grad_ref[pl.ds(row, 1), :] = ref[2 * side + 1 : 2 * side + 2, :]
+    biases = []
+    for vector in (8, 9):
+        row = rows_ref[vector : vector + 1, :]
+        found = row[:, 0:192]
+        for spot in range(1, 4):
+            found = jnp.where(chip == spot, row[:, 192 * spot : 192 * (spot + 1)], found)
+        biases.append(found)
+    bias = jnp.concatenate([biases[0], jnp.zeros_like(biases[0]), biases[1]], axis=1)
+    mixed = low(contract(low(in_ref[...]), weight_ref[:, D : D + 576], 1, 0) + bias)
+    mixed_ref[...] = mixed
+    row_docs = jnp.where(core == 0, docs_ref[0:1, :], docs_ref[1:2, :])
+    column_docs = jnp.where(core == 0, docs_column_ref[:, 0:1], docs_column_ref[:, 1:2])
+    allowed = row_docs == column_docs
+    found = []
+    for head in range(3):
+        query, key, value = (
+            mixed[:, third * 192 + head * HEAD_DIM : third * 192 + (head + 1) * HEAD_DIM]
+            for third in range(3)
+        )
+        scores = contract(query, key, 1, 1) * HEAD_DIM ** (-0.5)
+        scores = jnp.where(allowed, scores, masked_score)
+        powers = jnp.exp(scores - jnp.max(scores, axis=-1, keepdims=True))
+        probs = powers / jnp.sum(powers, axis=-1, keepdims=True)
+        probs_ref[head] = probs
+        found.append(contract(low(probs), value, 1, 0))
+    context_ref[...] = low(jnp.concatenate(found, axis=1))
+
+
+def cross_up_down(
+    own_ref, a_ref, b_ref, c_ref, in_ref, out_weight_ref, rows_ref, up_ref, bias_ref, down_ref, *outs
+):
+    n_ref, scale_ref, low_ref, hidden_ref, active_ref, part_ref = outs
+    chip = place_in()[1]
+    total = in_ref[...] + rows_ref[10:11, :]
+    for mask, ref in enumerate((own_ref, a_ref, b_ref, c_ref)):
+        start = pl.multiple_of(192 * (chip ^ mask), 64)
+        total = total + contract(ref[...], out_weight_ref[pl.ds(start, 192), :], 1, 0)
+    normed, scale = norm_parts(total)
+    n_ref[...] = normed
+    scale_ref[...] = scale
+    first = low(normed * rows_ref[11:12, :] + rows_ref[12:13, :])
+    low_ref[...] = first
+    hidden = contract(first, up_ref[...], 1, 0) + bias_ref[...]
+    hidden_ref[...] = hidden
+    active = low(hidden * (0.5 * (1.0 + lax.erf(hidden * math.sqrt(0.5)))))
+    active_ref[...] = active
+    part_ref[...] = contract(active, down_ref[...], 1, 0)
+
+
+def cross_turn(
+    own_ref, a_ref, b_ref, c_ref, n_ref, rows_ref, grad_ref, hidden_ref, up_ref, down_ref, *outs
+):
+    out_ref, second_ref, hidden_low_ref, part_ref, sums_ref = outs
+    first = n_ref[...] * rows_ref[11:12, :] + rows_ref[12:13, :]
+    total = (own_ref[...] + a_ref[...]) + (b_ref[...] + c_ref[...])
+    normed, scale = norm_parts(first + total + rows_ref[13:14, :])
+    out_ref[...] = normed * rows_ref[14:15, :] + rows_ref[15:16, :]
+    grad = grad_ref[...]
+    second = norm_back(grad, normed, scale, rows_ref[14:15, :])
+    second_ref[...] = second
+    hidden_low = low(contract(low(second), down_ref[...], 1, 1) * gelu_slope(hidden_ref[...]))
+    hidden_low_ref[...] = hidden_low
+    part_ref[...] = contract(hidden_low, up_ref[...], 1, 1)
+    sums_ref[...] = jnp.zeros_like(sums_ref)
+    sums_ref[0:1, :] = column_sum(grad * normed)
+    sums_ref[1:2, :] = column_sum(grad)
+
+
+def cross_attend_back(
+    own_ref,
+    a_ref,
+    b_ref,
+    c_ref,
+    second_ref,
+    n_ref,
+    scale_ref,
+    rows_ref,
+    out_weight_ref,
+    mixed_ref,
+    probs_ref,
+    weight_ref,
+    hidden_low_ref,
+    active_ref,
+    context_ref,
+    in_ref,
+    low_ref,
+    sums_ref,
+    places_ref,
+    total_ref,
+    part_ref,
+    pack_ref,
+    pack,
+    rows,
+):
+    chip = place_in()[1]
+    grad = second_ref[...] + (own_ref[...] + a_ref[...]) + (b_ref[...] + c_ref[...])
+    normed = n_ref[...]
+    total = norm_back(grad, normed, scale_ref[...], rows_ref[11:12, :])
+    total_ref[...] = total
+    branch = low(total)
+    start = pl.multiple_of(192 * chip, 64)
+    context_low = low(contract(branch, out_weight_ref[pl.ds(start, 192), :], 1, 1))
+    mixed = mixed_ref[...]
+    found = [[], [], []]
+    for head in range(3):
+        query, key, value = (
+            mixed[:, third * 192 + head * HEAD_DIM : third * 192 + (head + 1) * HEAD_DIM]
+            for third in range(3)
+        )
+        part = context_low[:, head * HEAD_DIM : (head + 1) * HEAD_DIM]
+        probs = probs_ref[head]
+        prob_grad = contract(part, value, 1, 1)
+        score = low(probs * (prob_grad - jnp.sum(probs * prob_grad, axis=-1, keepdims=True)))
+        found[0].append(contract(score, key, 1, 0) * HEAD_DIM ** (-0.5))
+        found[1].append(contract(score, query, 0, 0) * HEAD_DIM ** (-0.5))
+        found[2].append(contract(low(probs), part, 0, 0))
+    mixed_low = low(jnp.concatenate(found[0] + found[1] + found[2], axis=1))
+    part_ref[...] = contract(mixed_low, weight_ref[:, D : D + 576], 1, 1)
+    pack[...] = jnp.zeros_like(pack)
+    pack[0:8, :] = wide(hidden_low_ref[...])
+    pack[8:16, :] = wide(active_ref[...])
+    pack[16:24, 0:576] = wide(mixed_low)
+    pack[16:24, 576:768] = wide(context_ref[...])
+    for i, value in enumerate(
+        (in_ref[...], wide(low_ref[...]), total, second_ref[...], total)
+    ):
+        rows[...] = value
+        for side in range(2):
+            row = 24 + 2 * i + side
+            pack[row : row + 1, :] = rows[pl.ds(2 * chip + side, 1), :]
+    rows[0:1, :] = column_sum(grad * normed)
+    rows[1:2, :] = column_sum(grad)
+    rows[2:4, :] = sums_ref[0:2, :]
+    pack[34:35, :] = rows[pl.ds(chip, 1), :]
+    for place in range(2):
+        pack[35 + place : 36 + place, :] = jnp.full((1, D), wide(places_ref[place, 0]))
+    pack_ref[...] = low(pack[...])
+
+
+def cross_finish(own_ref, a_ref, b_ref, c_ref, total_ref, out_ref, kept_ref, given_ref, rows):
+    layer, chip, core = place_in()
+    rows[...] = total_ref[...] + (own_ref[...] + a_ref[...]) + (b_ref[...] + c_ref[...])
+    for ref, side in ((kept_ref, core), (given_ref, 1 - core)):
+        ref[...] = jnp.zeros_like(ref)
+        ref[0:1, :] = rows[pl.ds(2 * chip + side, 1), :]
+        ref[1:2, :] = out_ref[pl.ds(2 * chip + side, 1), :]
+
+
+def cross_owner(every_ref, weight_ref, *refs):
+    mix_ref, out_ref, up_ref, down_ref, vectors_ref, bias_ref, table_ref = refs[:7]
+    hidden, mixed, single, active, sums, places = refs[7:]
+    layer, chip, core = place_in()
+    rank = 8 * layer + 2 * chip + core
+    sums[...] = jnp.zeros_like(sums)
+    for level in range(4):
+        for side in range(2):
+            group = 2 * level + side
+            rows = slice(8 * group, 8 * group + 8)
+            for spot in range(4):
+                value = wide(every_ref[8 * level + 2 * spot + side])
+                hidden[spot, rows, :] = value[0:8]
+                mixed[spot, rows, :] = value[16:24]
+                for i in range(5):
+                    start = 8 * group + 2 * spot
+                    single[i, start : start + 2, :] = value[24 + 2 * i : 26 + 2 * i]
+                sums[spot : spot + 1, :] += value[34:35]
+                for sequence in range(2):
+                    row = 16 * level + 8 * sequence + 2 * spot + side
+                    places[row : row + 1, :] = value[35 + sequence : 36 + sequence, 0:128]
+            active[rows, :] = wide(every_ref[8 * level + 2 * chip + side])[8:16]
+
+    def select(count, first):
+        lane = lax.broadcasted_iota(jnp.int32, (count, D), 1)
+        row = lax.broadcasted_iota(jnp.int32, (count, D), 0)
+        return wide(lane == first + row)
+
+    own = select(24, 24 * rank)
+    offset = 24 * (2 * chip + core)
+    units = select(96, 192 * layer + 96 * core)
+    own_low = low(own)
+
+    def columns_of(array_in):
+        return low(contract(own_low, low(array_in), 1, 1))
+
+    inputs = columns_of(single[0])
+    for spot in range(4):
+        part = contract(inputs, low(mixed[spot][:, 0:576]), 1, 0)
+        for third in range(3):
+            start = third * D + 192 * spot
+            mix_ref[:, start : start + 192] = part[:, 192 * third : 192 * (third + 1)]
+    own_mixed = mixed[layer]
+    context = low(contract(low(select(24, 576 + offset)), low(own_mixed), 1, 1))
+    out_ref[...] = contract(context, low(single[2]), 1, 0)
+    first = columns_of(single[1])
+    for spot in range(4):
+        part = contract(first, low(hidden[spot]), 1, 0)
+        for level in range(4):
+            start = 192 * (4 * level + spot)
+            up_ref[:, start : start + 192] = part[:, 192 * level : 192 * (level + 1)]
+    units_low = low(contract(low(units), low(active[...]), 1, 1))
+    down_ref[...] = contract(units_low, low(single[3]), 1, 0)
+    mixed_sum = column_sum(own_mixed)
+    vectors_ref[0:1, :] = contract_exact(mixed_sum, select(24, offset), 1, 1)
+    vectors_ref[1:2, :] = contract_exact(mixed_sum, select(24, 384 + offset), 1, 1)
+    for row, value in (
+        (2, column_sum(single[2])),
+        (3, sums[0:1, :]),
+        (4, sums[1:2, :]),
+        (5, column_sum(single[3])),
+        (6, sums[2:3, :]),
+        (7, sums[3:4, :]),
+    ):
+        vectors_ref[row : row + 1, :] = contract_exact(value, own, 1, 1)
+    bias_ref[...] = contract_exact(column_sum(hidden[chip]), units, 1, 1)
+    grads = contract(low(single[4]), own_low, 1, 1)
+    for spot in range(4):
+        for third in range(3):
+            start = third * D + 192 * spot
+            part = low(mixed[spot][:, 192 * third : 192 * (third + 1)])
+            grads = grads + contract(part, weight_ref[:, start : start + 192], 1, 1)
+    lane = wide(lax.broadcasted_iota(jnp.int32, (64, 64), 1))
+    table_ref[...] = contract_exact(wide(places[:, 0:64] == lane), grads, 0, 0)
+
+
+def split_cores(value, kept_ref, gone_ref):
+    rows = kept_ref.shape[1]
+    core = lax.rem(lax.axis_index("seq"), 2)
+    parts = value.reshape(-1, 2, rows, value.shape[1])
+    kept_ref[...] = low(jnp.where(core == 0, parts[:, 0], parts[:, 1]))
+    gone_ref[...] = low(jnp.where(core == 0, parts[:, 1], parts[:, 0]))
+
+
+def local_down_back(
+    cot_ref, mine_ref, other_ref, n_ref, scale_ref, rows_ref, active_ref, slope_ref, weight_ref, *outs
+):
+    out_ref, second_ref, kept_ref, gone_ref, hidden_ref, sums_ref, bias_ref, second_low_ref = outs
+    step = pl.program_id(0)
+
+    @pl.when(step == 0)
+    def _():
+        core = place_in()[2]
+        row = lax.broadcasted_iota(jnp.int32, (2 * SEG, D), 0)
+        grad = wide(cot_ref[...])
+        normed = n_ref[...]
+        out = normed * rows_ref[6:7, :] + rows_ref[7:8, :]
+        for place in range(2):
+            heads = jnp.where(core == place, mine_ref[...], other_ref[...])
+            grad = jnp.where(row == place * SEG, heads[0:1], grad)
+            out = jnp.where(row == place * SEG, heads[1:2], out)
+        out_ref[...] = low(out)
+        second = norm_back(grad, normed, scale_ref[...], rows_ref[6:7, :])
+        second_ref[...] = second
+        second_low_ref[...] = low(second)
+        sums_ref[0:1, :] = column_sum(wide(low(second)))
+        sums_ref[1:2, :] = column_sum(grad * normed)
+        sums_ref[2:3, :] = column_sum(grad)
+
+    second_low = second_low_ref[...]
+    split_cores(contract(active_ref[...], second_low, 0, 0), kept_ref, gone_ref)
+    hidden = low(contract(second_low, weight_ref[...], 1, 1) * wide(slope_ref[...]))
+    hidden_ref[...] = hidden
+    bias_ref[...] = column_sum(wide(hidden))
+
+
+def local_up_back(low_ref, hidden_ref, weight_ref, second_ref, kept_ref, gone_ref, first_ref):
+    hidden = hidden_ref[...]
+    split_cores(contract(low_ref[...], hidden, 0, 0), kept_ref, gone_ref)
+    part = contract(hidden, weight_ref[...], 1, 1)
+    step = pl.program_id(0)
+
+    @pl.when(step == 0)
+    def _():
+        first_ref[...] = second_ref[...] + part
+
+    @pl.when(step > 0)
+    def _():
+        first_ref[...] += part
+
+
+def local_attend_back(
+    first_ref, n_ref, scale_ref, rows_ref, context_ref, mixed_ref, probs_ref, group_ref, *outs
+):
+    out_ref, total_ref, sums_ref, back_ref, context_low_ref = outs
+    grad, normed = first_ref[...], n_ref[...]
+    total = norm_back(grad, normed, scale_ref[...], rows_ref[3:4, :])
+    total_ref[...] = total
+    branch = low(total)
+    sums_ref[2:3, :] = column_sum(wide(branch))
+    sums_ref[3:4, :] = column_sum(grad * normed)
+    sums_ref[4:5, :] = column_sum(grad)
+    out_ref[...] = contract(context_ref[...], branch, 0, 0)
+    context_low_ref[...] = low(contract(branch, group_ref[...], 1, 1))
+    lane = lax.broadcasted_iota(jnp.int32, (SEG, 128), 1)
+    for segment in range(2):
+        rows = slice(segment * SEG, (segment + 1) * SEG)
+        for pair in range(HEADS // 2):
+            places = [
+                slice(third * D + pair * 128, third * D + (pair + 1) * 128) for third in range(3)
+            ]
+            query, key, value = (mixed_ref[rows, place] for place in places)
+            grad = context_low_ref[rows, places[0]]
+            found = []
+            for side in range(2):
+                here = (lane < HEAD_DIM) if side == 0 else (lane >= HEAD_DIM)
+                probs = probs_ref[segment * HEADS + 2 * pair + side]
+                prob_grad = contract(jnp.where(here, grad, jnp.zeros_like(grad)), value, 1, 1)
+                value_grad = contract(low(probs), grad, 0, 0)
+                score = low(
+                    probs * (prob_grad - jnp.sum(probs * prob_grad, axis=-1, keepdims=True))
+                )
+                found.append(
+                    (contract(score, key, 1, 0), contract(score, query, 0, 0), value_grad)
+                )
+            for third in range(3):
+                merged = jnp.where(lane < HEAD_DIM, found[0][third], found[1][third])
+                if third < 2:
+                    merged = merged * HEAD_DIM ** (-0.5)
+                back_ref[rows, places[third]] = low(merged)
+    for third in (0, 2):
+        columns = slice(third * D, (third + 1) * D)
+        sums_ref[third // 2 : third // 2 + 1, :] = column_sum(wide(back_ref[:, columns]))
+
+
+def local_mix_back(
+    total_ref, back_ref, tokens_ref, group_ref, out_ref, sums_ref, more_ref, bias_ref, *outs
+):
+    input_ref, kept_ref, gone_ref, small_ref = outs
+    tokens, total = tokens_ref[...], total_ref[...]
+    for third in range(3):
+        columns = slice(third * D, (third + 1) * D)
+        back = back_ref[:, columns]
+        grad = contract(tokens, back, 0, 0)
+        split_cores(grad, kept_ref.at[:, :, columns], gone_ref.at[:, :, columns])
+        total = total + contract(back, group_ref[:, columns], 1, 1)
+    input_ref[...] = total
+    columns = slice(3 * D, 4 * D)
+    split_cores(out_ref[...], kept_ref.at[:, :, columns], gone_ref.at[:, :, columns])
+    small_ref[...] = jnp.zeros_like(small_ref)
+    small_ref[0:5, :] = sums_ref[0:5, :]
+    small_ref[5:8, :] = more_ref[0:3, :]
+    small_ref[8:12, :] = bias_ref[...]
+    columns = slice(4 * D, 4 * D + 128)
+    split_cores(small_ref[...].T, kept_ref.at[:, :, columns], gone_ref.at[:, :, columns])
+
+
+def plane_three(array_in):
+    return [array_in] + [swap_chip(array_in, mask) for mask in (1, 2, 3)]
+
+
+def plane_shards(
+    tokens,
+    cotangent,
+    token_docs,
+    segment_docs,
+    segment_positions,
+    local_mix,
+    local_out,
+    local_up,
+    local_down,
+    local_vectors,
+    local_up_bias,
+    cross_mix,
+    cross_out,
+    cross_up,
+    cross_down,
+    cross_vectors,
+    cross_up_bias,
+    position_table,
+):
+    chip = place_in()[1]
+    flat_tokens = tokens.reshape(256, D)
+    flat_cot = cotangent.reshape(256, D)
+    docs_column = token_docs.reshape(256, 1)
+    segment_column = segment_docs.T
+
+    shard_one, shard_two, *cross_pieces = on_core(
+        prepare,
+        [half(24, 3200), half(24, 9 * D)] + [half(24, D + 640)] * 4,
+        (
+            local_mix,
+            local_out,
+            local_up,
+            local_down.reshape(4, 24, D),
+            local_vectors,
+            local_up_bias.reshape(4, 24),
+            cross_mix,
+            cross_out,
+            cross_up,
+            cross_vectors,
+            cross_up_bias.reshape(4, 24),
+            position_table,
+        ),
+        0,
+        scratch=[pltpu.VMEM((128, 128), jnp.float32), pltpu.VMEM((4, 24, D + 640), jnp.bfloat16)],
+    )
+    columns = lax.all_gather(shard_two, "dp")
+    column_one = gather_dp(shard_one)
+    moves_one = plane_moves(column_one)
+    cross_column = gather_cross(after(tuple(cross_pieces), column_one), cross_down)
+    first_group = gather_plane(moves_one).reshape(D, 3200)
+    columns = after(columns, moves_one[1], moves_one[2])
+    moves_two = plane_moves(columns[:, :, : 5 * D])
+    moves_three = plane_moves(columns[:, :, 5 * D :], moves_two[1], moves_two[2])
+
+    mixed_rows, context_rows, probs_kept, normed_one, scale_one, low_one, rows = on_core(
+        local_attend,
+        [
+            half(256, 3 * D),
+            half(256, D),
+            shape_of(24, SEG, SEG),
+            shape_of(256, D),
+            shape_of(256, 1),
+            half(256, D),
+            shape_of(128, D),
+        ],
+        (flat_tokens, first_group, token_docs, docs_column),
+        2 * 256 * D * 5 * D,
+    )
+    up_bias = rows[80:84].reshape(4, 32, 24).transpose(1, 0, 2).reshape(1, 4 * D)
+    cross_bias = rows[84:88].reshape(4, 4, 4, 2, 24)
+    cross_bias = lax.dynamic_index_in_dim(cross_bias, chip, 2, keepdims=False)
+    cross_bias = cross_bias.transpose(1, 2, 0, 3).reshape(1, D)
+    second_group = gather_plane(moves_two).reshape(D, 5 * D)
+    whole = pl.BlockSpec((256, D), lambda j: (0, 0))
+    thin = pl.BlockSpec((256, 1), lambda j: (0, 0))
+    vectors = pl.BlockSpec((128, D), lambda j: (0, 0))
+    eight = pl.BlockSpec((8, D), lambda j: (0, 0))
+    across = pl.BlockSpec((256, D), lambda j: (0, j))
+    tall = pl.BlockSpec((D, D), lambda j: (0, j))
+    deep = pl.BlockSpec((D, D), lambda j: (j, 0))
+    strip = pl.BlockSpec((1, D), lambda j: (0, j))
+    active_rows, slope_rows = on_core(
+        local_up_part,
+        [half(256, 4 * D)] * 2,
+        (low_one, second_group, up_bias),
+        2 * 256 * D * 4 * D,
+        grid=(4,),
+        in_specs=[whole, tall, strip],
+        out_specs=[across, across],
+    )
+    cross_up_mix, cross_down_part = place_cross(after(cross_column, moves_three[1], moves_three[2]))
+    down_weight = gather_down(moves_three).reshape(4 * D, D)
+    normed_two, scale_two, kept, given = on_core(
+        local_down_part,
+        [shape_of(256, D), shape_of(256, 1), shape_of(8, D), shape_of(8, D)],
+        (active_rows, down_weight, normed_one, rows, flat_cot, flat_cot, segment_positions),
+        2 * 256 * D * 4 * D,
+        grid=(4,),
+        in_specs=[
+            across,
+            deep,
+            whole,
+            vectors,
+            pl.BlockSpec((16, D), lambda j: (0, 0)),
+            pl.BlockSpec((16, D), lambda j: (8, 0)),
+            pl.BlockSpec(memory_space=pltpu.SMEM),
+        ],
+        out_specs=[whole, thin, eight, eight],
+        scratch=[pltpu.VMEM((256, D), jnp.float32)],
+    )
+
+    def plain(*shapes):
+        return [pl.BlockSpec(shape, lambda j, n=len(shape): (0,) * n) for shape in shapes]
+
+    row8, mix_share = (8, D), (D, D + 640)
+    out_share = pl.BlockSpec((D, D), lambda j: (0, 4))
+    up_share = pl.BlockSpec((D, D), lambda j: (0, 0))
+    pair = on_core(join_pair, shape_of(8, D), (kept, swap_core(given)), 0)
+    row_in, row_grad, mixed, probs, context = on_core(
+        cross_attend,
+        [shape_of(8, D), shape_of(8, D), half(8, 576), shape_of(3, 8, 8), half(8, 192)],
+        (*plane_three(pair), cross_up_mix, rows, segment_docs, segment_column),
+        0,
+    )
+    row_n, row_scale, row_low, hidden, active, part = on_core(
+        cross_up_down,
+        [shape_of(8, D), shape_of(8, 1), half(8, D), shape_of(8, D), half(8, D), shape_of(8, D)],
+        (
+            *plane_three(context),
+            row_in,
+            second_group,
+            rows,
+            cross_up_mix,
+            cross_bias,
+            cross_down_part,
+        ),
+        0,
+        grid=(1,),
+        in_specs=plain(*[(8, 192)] * 4, row8)
+        + [out_share]
+        + plain((128, D))
+        + [up_share]
+        + plain((1, D), (D, D)),
+        out_specs=plain(row8, (8, 1), row8, row8, row8, row8),
+    )
+    row_out, row_second, hidden_low, part, sums = on_core(
+        cross_turn,
+        [shape_of(8, D), shape_of(8, D), half(8, D), shape_of(8, D), shape_of(8, D)],
+        (*plane_three(part), row_n, rows, row_grad, hidden, cross_up_mix, cross_down_part),
+        0,
+        grid=(1,),
+        in_specs=plain(*[row8] * 4, row8, (128, D), row8, row8) + [up_share] + plain((D, D)),
+        out_specs=plain(*[row8] * 5),
+    )
+    row_total, part, packed = on_core(
+        cross_attend_back,
+        [shape_of(8, D), shape_of(8, D), half(48, D)],
+        (
+            *plane_three(part),
+            row_second,
+            row_n,
+            row_scale,
+            rows,
+            second_group,
+            mixed,
+            probs,
+            cross_up_mix,
+            hidden_low,
+            active,
+            context,
+            row_in,
+            row_low,
+            sums,
+            segment_positions,
+        ),
+        0,
+        grid=(1,),
+        in_specs=plain(*[row8] * 4, row8, row8, (8, 1), (128, D))
+        + [out_share]
+        + plain((8, 576), (3, 8, 8), mix_share, row8, row8, (8, 192), row8, row8, row8)
+        + [pl.BlockSpec(memory_space=pltpu.SMEM)],
+        out_specs=plain(row8, row8, (48, D)),
+        scratch=[pltpu.VMEM((48, D), jnp.float32), pltpu.VMEM((8, D), jnp.float32)],
+    )
+    everyone = lax.all_gather(packed, ("dp", "seq"))
+    kept, given = on_core(
+        cross_finish,
+        [shape_of(8, D), shape_of(8, D)],
+        (*plane_three(part), row_total, row_out),
+        0,
+        scratch=[pltpu.VMEM((8, D), jnp.float32)],
+    )
+    got = swap_core(given)
+
+    fours = pl.BlockSpec((4, 96, D), lambda j: (j, 0, 0))
+    layer_output, second_rows, down_kept, down_gone, hidden_grads, sums_two, bias_grad = on_core(
+        local_down_back,
+        [
+            half(256, D),
+            shape_of(256, D),
+            half(16, 96, D),
+            half(16, 96, D),
+            half(256, 4 * D),
+            shape_of(8, D),
+            shape_of(1, 4 * D),
+        ],
+        (flat_cot, kept, got, normed_two, scale_two, rows, active_rows, slope_rows, down_weight),
+        4 * 256 * D * 4 * D,
+        grid=(4,),
+        in_specs=[whole, eight, eight, whole, thin, vectors, across, across, deep],
+        out_specs=[whole, whole, fours, fours, across, eight, strip],
+        scratch=[pltpu.VMEM((256, D), jnp.bfloat16)],
+    )
+    down_total = Sum(down_kept.reshape(4, 4, 96, D), down_gone.reshape(4, 4, 96, D))
+    sixteens = pl.BlockSpec((16, 24, D), lambda j: (0, 0, j))
+    up_kept, up_gone, first_rows = on_core(
+        local_up_back,
+        [half(16, 24, 4 * D), half(16, 24, 4 * D), shape_of(256, D)],
+        (low_one, hidden_grads, second_group, second_rows),
+        4 * 256 * D * 4 * D,
+        grid=(4,),
+        in_specs=[whole, across, tall, whole],
+        out_specs=[sixteens, sixteens, whole],
+    )
+    up_total = Sum(up_kept.reshape(4, 4, 24, 4 * D), up_gone.reshape(4, 4, 24, 4 * D))
+    down_sent = down_total.first(first_rows)
+    flat = pl.BlockSpec((256, 3 * D), lambda j: (0, 0))
+    out_grad, sum_rows, sums_one, back_rows = on_core(
+        local_attend_back,
+        [shape_of(D, D), shape_of(256, D), shape_of(8, D), half(256, 3 * D)],
+        (
+            after(first_rows, down_sent, up_total.got),
+            normed_one,
+            scale_one,
+            rows,
+            context_rows,
+            mixed_rows,
+            probs_kept,
+            first_group,
+        ),
+        4 * 256 * D * 2 * D,
+        grid=(1,),
+        in_specs=[
+            whole,
+            whole,
+            thin,
+            vectors,
+            whole,
+            flat,
+            pl.BlockSpec((24, SEG, SEG), lambda j: (0, 0, 0)),
+            pl.BlockSpec((D, D), lambda j: (0, 3)),
+        ],
+        out_specs=[pl.BlockSpec((D, D), lambda j: (0, 0)), whole, eight, flat],
+        scratch=[pltpu.VMEM((256, D), jnp.bfloat16)],
+    )
+    up_sent = up_total.first(back_rows)
+    down_onward = down_total.second(up_sent)
+    bias_rows = bias_grad.reshape(32, 4, 24).transpose(1, 0, 2).reshape(4, D)
+    sides = [half(16, 24, 4 * D + 128)] * 2
+    input_grad, mix_kept, mix_gone = on_core(
+        local_mix_back,
+        [shape_of(256, D)] + sides,
+        (
+            sum_rows,
+            after(back_rows, down_onward),
+            flat_tokens,
+            first_group,
+            out_grad,
+            sums_one,
+            sums_two,
+            bias_rows,
+        ),
+        4 * 256 * D * 3 * D,
+        scratch=[pltpu.VMEM((128, D), jnp.float32)],
+    )
+    mix_total = Sum(mix_kept.reshape(4, 4, 24, 3200), mix_gone.reshape(4, 4, 24, 3200))
+    up_onward = up_total.second(input_grad)
+    down_own = down_total.third(up_onward)
+    mix_sent = mix_total.first(down_own)
+    up_own = up_total.third(mix_sent)
+    mix_onward = mix_total.second(up_own)
+    cross_grads = on_core(
+        cross_owner,
+        [
+            shape_of(24, 3 * D),
+            shape_of(24, D),
+            shape_of(24, 4 * D),
+            shape_of(96, D),
+            shape_of(8, 24),
+            shape_of(1, 96),
+            shape_of(64, 24),
+        ],
+        (after(everyone, mix_onward), cross_mix),
+        0,
+        scratch=[
+            pltpu.VMEM((4, 64, D), jnp.float32),
+            pltpu.VMEM((4, 64, D), jnp.float32),
+            pltpu.VMEM((5, 64, D), jnp.float32),
+            pltpu.VMEM((64, D), jnp.float32),
+            pltpu.VMEM((8, D), jnp.float32),
+            pltpu.VMEM((64, 128), jnp.float32),
+        ],
+    )
+    mix_total.third()
+    down_sum, up_sum, mix_sum = down_total.total(), up_total.total(), mix_total.total()
+    return (
+        layer_output.reshape(2, SEG, D),
+        input_grad.reshape(2, SEG, D),
+        mix_sum[:, :2304],
+        mix_sum[:, 2304:3072],
+        up_sum,
+        down_sum,
+        mix_sum[:, 3072:3080].T,
+        mix_sum[:, 3080:3084].T.reshape(96),
+        *cross_grads[:5],
+        cross_grads[5].reshape(96),
+        cross_grads[6],
+    )
+
+
 def solution(mesh):
+    flat = dict(mesh.shape) == {"dp": 4, "seq": 8}
     return jax.shard_map(
-        shards,
+        plane_shards if flat else shards,
         mesh=mesh,
         in_specs=(
             P("dp", "seq", None),

time: 1780 us -> 386 us (0.22)
  waiting for transfers between devices: 1030 us -> 139 us
  local copies, waits for them, and re-layouts: 274 us -> 46.3 us
  blocking collectives: 203 us -> 0 us
  matrix products: 155 us -> 0 us
  Pallas kernels: 0 us -> 102 us
  starting transfers between devices: 0.34 us -> 78.3 us
  other arithmetic: 79.1 us -> 2.31 us
    unnamed x10 -> x3, waiting for transfers between devices: 804 us -> 0.05 us
    all_gather x8 -> x3, waiting for transfers between devices: 223 us -> 0.01 us  [the longest x1 0.01 us: plane_shards(): columns = lax.all_gather(shard_two, 'dp')]
    dot_general x62 -> x0, matrix products: 155 us -> none  [the longest x24 79.8 us: contract(): lax.dot_general(left_side, right_side, (((left_dim,), (right_dim,)), ((),...]
    all_gather x5 -> x0, blocking collectives: 141 us -> none  [the longest x1 44 us: fetch_weights(): lax.all_gather(position_table, ('dp', 'seq'), axis=1, tiled=True)]
    ppermute x0 -> x63, waiting for transfers between devices: none -> 139 us  [the longest x6 68.1 us: swap_one(): lax.ppermute(array_in, 'seq', [(i, i ^ (2 if i % 2 == 0 else 4)) for i in...]
    pallas_call x0 -> x30, Pallas kernels: none -> 102 us  [the longest x15 76 us: on_core(): pl.pallas_call(kernel, out_shape=out_shape, grid=grid, scratch_shapes=scr...]
    unnamed x452 -> x115, local copies, waits for them, and re-layouts: 127 us -> 38.1 us
    ppermute x0 -> x63, starting transfers between devices: none -> 78.2 us  [the longest x12 36.5 us: swap_dp(): lax.ppermute(array_in, 'dp', [(i, (i + shift) % 4) for i in range(4)])]
  transfers between devices with their start and end apart: 9 -> 66, of which waited for: 6 -> 32; matrix products, arithmetic and copies ran while one was open for 5% -> 2% of each run, Pallas kernels for 0% -> 19%
where the time goes in v2:
time: 386 us; the launch traced here: 383 us
  waiting for transfers between devices  139 us (36%)
  Pallas kernels  102 us (26%)
  starting transfers between devices  78.3 us (20%)
  local copies, waits for them, and re-layouts  46.3 us (12%)
  between operations  14.3 us (4%)
    pallas_call x15, Pallas kernels, on_core(): pl.pallas_call(kernel, out_shape=out_shape, grid=grid, scratch_shapes=scr...  76 us
    ppermute x6, waiting for transfers between devices, swap_one(): lax.ppermute(array_in, 'seq', [(i, i ^ (2 if i % 2 == 0 else 4)) for i in...  68.1 us
    unnamed x115, local copies, waits for them, and re-layouts  38.1 us
    ppermute x12, starting transfers between devices, swap_dp(): lax.ppermute(array_in, 'dp', [(i, (i + shift) % 4) for i in range(4)])  36.5 us
    ppermute x9, waiting for transfers between devices, swap_two(): lax.ppermute(array_in, 'seq', [(i, i ^ (4 if i % 2 == 0 else 2)) for i in...  32.2 us
    ppermute x18, starting transfers between devices, swap_chip(): return lax.ppermute(array_in, 'seq', [(i, i ^ 2 * mask) for i in range(8)])  21.2 us
    ppermute x12, waiting for transfers between devices, swap_dp(): lax.ppermute(array_in, 'dp', [(i, (i + shift) % 4) for i in range(4)])  18.9 us
    ppermute x18, waiting for transfers between devices, swap_chip(): return lax.ppermute(array_in, 'seq', [(i, i ^ 2 * mask) for i in range(8)])  17.5 us
  transfers between devices with their start and end apart: 66, of which 32 were waited for; matrix products, arithmetic and copies ran while one was open for 2% of the time, Pallas kernels for 19%

profile of v2, /device:TPU:0, one launch (start us, length us, event | category | flops | bytes accessed | tf_op | source)
XLA Modules:
  0.0 382.7 jit_solution(10104766289972195607)
XLA Ops:
  17.9 3.1 collective-permute-start
  20.9 2.6 collective-permute-start.1
  24.9 3.0 collective-permute-done.refs_1_
  27.9 9.1 %collective-permute-done.1.refs_2_ = bf16[24,3200]{1,0:T(8,128)(2,1)S(1)} collective-permute-done((bf16[24,3200]{1,0:T(8,128)(2,1)S(1)}, bf16[24,3200]{1,0:T(8,128)(2,1)S(1)}, u32[]{:S(2)}, u32[]{:S(2)}) %collective-permute-start.1) | collective-permute-done | bytes 153632 | tf_op jit(solution)/shard_map/ppermute | solution.py:448
  49.5 13.5 %collective-permute-done.3.refs_1_ = bf16[4,24,3200]{2,1,0:T(8,128)(2,1)S(1)} collective-permute-done((bf16[4,24,3200]{2,1,0:T(8,128)(2,1)S(1)}, bf16[4,24,3200]{2,1,0:T(8,128)(2,1)S(1)}, u32[]{:S(2)}, u32[]{:S(2)}) %collective-permute-start.3) | collective-permute-done | bytes 614432 | tf_op jit(solution)/shard_map/ppermute | solution.py:460
  68.6 15.2 %collective-permute-done.10.refs_1_ = bf16[4,24,3840]{2,1,0:T(8,128)(2,1)S(1)} collective-permute-done((bf16[4,24,3840]{2,1,0:T(8,128)(2,1)S(1)}, bf16[4,24,3840]{2,1,0:T(8,128)(2,1)S(1)}, u32[]{:S(2)}, u32[]{:S(2)}) %collective-permute-start.10) | collective-permute-done | bytes 737312 | tf_op jit(solution)/shard_map/ppermute | solution.py:460
  87.7 4.2 %collective-permute-done.5.refs_3_ = bf16[4,24,3200]{2,1,0:T(8,128)(2,1)} collective-permute-done((bf16[4,24,3200]{2,1,0:T(8,128)(2,1)S(1)}, bf16[4,24,3200]{2,1,0:T(8,128)(2,1)}, u32[]{:S(2)}, u32[]{:S(2)}) %collective-permute-start.5) | collective-permute-done | bytes 614432 | tf_op jit(solution)/shard_map/ppermute | solution.py:464
  92.0 8.1 %collective-permute-done.17.refs_1_ = bf16[4,24,3072]{2,1,0:T(8,128)(2,1)S(1)} collective-permute-done((bf16[4,24,3072]{2,1,0:T(8,128)(2,1)S(1)}, bf16[4,24,3072]{2,1,0:T(8,128)(2,1)S(1)}, u32[]{:S(2)}, u32[]{:S(2)}) %collective-permute-start.17) | collective-permute-done | bytes 589856 | tf_op jit(solution)/shard_map/ppermute | solution.py:460
  103.9 4.9 %collective-permute-done.12.refs_3_ = bf16[4,24,3840]{2,1,0:T(8,128)(2,1)} collective-permute-done((bf16[4,24,3840]{2,1,0:T(8,128)(2,1)S(1)}, bf16[4,24,3840]{2,1,0:T(8,128)(2,1)}, u32[]{:S(2)}, u32[]{:S(2)}) %collective-permute-start.12) | collective-permute-done | bytes 737312 | tf_op jit(solution)/shard_map/ppermute | solution.py:464
  113.1 7.2 %collective-permute-done.19.refs_3_ = bf16[4,24,3072]{2,1,0:T(8,128)(2,1)} collective-permute-done((bf16[4,24,3072]{2,1,0:T(8,128)(2,1)}, bf16[4,24,3072]{2,1,0:T(8,128)(2,1)}, u32[]{:S(2)}, u32[]{:S(2)}) %collective-permute-start.19) | collective-permute-done | bytes 589856 | tf_op jit(solution)/shard_map/ppermute | solution.py:464
  129.3 12.6 %shard_map.292 = (bf16[256,2304]{1,0:T(8,128)(2,1)}, bf16[256,768]{1,0:T(8,128)(2,1)S(1)}, f32[24,128,128]{2,1,0:T(8,128)}, f32[256,768]{1,0:T(8,128)}, f32[256,...) custom-call(bf16[256,768]{1,0:T(8,128)(2,1)S(1)} %bitcast.68, bf16[768,3200]{1,0:T(8,128)(2,1)} %bitcast.43, ...), custom_call_target="tpu_custom_call" | custom-call | flops 1509949440 | bytes 10030080 | tf_op jit(solution)/shard_map/pallas_call | solution.py:683
  146.6 2.9 shard_map.293
  152.0 5.7 %shard_map.294 = (bf16[256,3072]{1,0:T(8,128)(2,1)S(1)}, bf16[256,3072]{1,0:T(8,128)(2,1)}) custom-call(bf16[256,768]{1,0:T(8,128)(2,1)S(1)} %get-tuple-element.112.low_ref, bf16[768,3840]{1,0:T(8,128)(2,1)} %bitcast.39, f32[1,3072]{1,0:T(1,128)S(1)} %reshape.123.bias_ref), custom_call_target="tpu_custom_call" | custom-call | flops 1207959552 | bytes 9449472 | tf_op jit(solution)/shard_map/pallas_call | solution.py:683
  157.8 3.1 shard_map.295
  163.0 5.2 %shard_map.296 = (f32[256,768]{1,0:T(8,128)S(1)}, f32[256,1]{1,0:T(8,128)S(1)}, f32[8,768]{1,0:T(8,128)S(1)}, f32[8,768]{1,0:T(8,128)S(1)}) custom-call(bf16[256,3072]{1,0:T(8,128)(2,1)} %copy-done.14, bf16[3072,768]{1,0:T(8,128)(2,1)} %bitcast.46, f32[256,768]{1,0:T(8,128)} %get-tuple-element.118.first_ref.n_ref, ...), custom_call_target="tpu_custom_call" | custom-call | flops 1207959552 | bytes 9094152 | tf_op jit(solution)/shard_map/pallas_call | solution.py:683
  178.8 2.6 shard_map.300
  188.1 2.6 shard_map.301
  206.6 4.1 %shard_map.303 = (f32[8,768]{1,0:T(8,128)S(1)}, f32[8,768]{1,0:T(8,128)S(1)}, bf16[48,768]{1,0:T(8,128)(2,1)}) custom-call(f32[8,768]{1,0:T(8,128)S(1)} %get-tuple-element.138.own_ref, f32[8,768]{1,0:T(8,128)S(1)} %collective-permute-done.38.a_ref, f32[8,768]{1,0:T(8,128)S(1)} %collective-permute-done.39.b_ref, f32[8,768]{1,0:T(8,128)S(1)} %collective-permute-done.40.c_ref, ...), custom_call_target="tpu_custom_call" | custom-call | bytes 8823592 | tf_op jit(solution)/shard_map/pallas_call | solution.py:683
  218.6 8.4 %shard_map.305 = (bf16[256,768]{1,0:T(8,128)(2,1)}, f32[256,768]{1,0:T(8,128)S(1)}, bf16[16,96,768]{2,1,0:T(8,128)(2,1)}, bf16[16,96,768]{2,1,0:T(8,128)(2,1)}, ...) custom-call(bf16[256,768]{1,0:T(8,128)(2,1)S(1)} %bitcast.65, ...), custom_call_target="tpu_custom_call" | custom-call | flops 2415919104 | bytes 16995328 | tf_op jit(solution)/shard_map/pallas_call | solution.py:683
  227.2 7.3 %shard_map.306 = (bf16[16,24,3072]{2,1,0:T(8,128)(2,1)}, bf16[16,24,3072]{2,1,0:T(8,128)(2,1)}, f32[256,768]{1,0:T(8,128)S(1)}) custom-call(bf16[256,768]{1,0:T(8,128)(2,1)S(1)} %copy-done.41, bf16[256,3072]{1,0:T(8,128)(2,1)} %get-tuple-element.156.hidden_ref, bf16[768,3840]{1,0:T(8,128)(2,1)} %bitcast.42, f32[256,768]{1,0:T(8,128)S(1)} %get-tuple-element.157.second_ref), custom_call_target="tpu_custom_call" | custom-call | flops 2415919104 | bytes 14155776 | tf_op jit(solution)/shard_map/pallas_call | solution.py:683
  237.4 2.8 shard_map.307
  243.2 12.1 %shard_map.308 = (f32[768,768]{1,0:T(8,128)}, f32[256,768]{1,0:T(8,128)S(1)}, f32[8,768]{1,0:T(8,128)S(1)}, bf16[256,2304]{1,0:T(8,128)(2,1)}) custom-call(f32[256,768]{1,0:T(8,128)} %copy-done.19, f32[256,768]{1,0:T(8,128)} %get-tuple-element.118.first_ref.n_ref, f32[256,1]{1,0:T(8,128)S(1)} %get-tuple-element.164.scale_ref, ...), custom_call_target="tpu_custom_call" | custom-call | flops 1207959552 | bytes 14377984 | tf_op jit(solution)/shard_map/pallas_call | solution.py:683
  258.9 8.1 %shard_map.311 = (f32[256,768]{1,0:T(8,128)}, bf16[16,24,3200]{2,1,0:T(8,128)(2,1)}, bf16[16,24,3200]{2,1,0:T(8,128)(2,1)}) custom-call(f32[256,768]{1,0:T(8,128)S(1)} %get-tuple-element.168.total_ref, bf16[256,2304]{1,0:T(8,128)(2,1)} %get-tuple-element.173.back_ref, bf16[256,768]{1,0:T(8,128)(2,1)S(1)} %bitcast.69, bf16[768,3200]{1,0:T(8,128)(2,1)} %bitcast.45, ...), custom_call_target="tpu_custom_call" | custom-call | flops 1811939328 | bytes 15396864 | tf_op jit(solution)/shard_map/pallas_call | solution.py:683
  269.2 20.9 %collective-permute-done.50.c_ref = bf16[2,4,24,3072]{3,2,1,0:T(8,128)(2,1)S(1)} collective-permute-done((bf16[2,4,24,3072]{3,2,1,0:T(8,128)(2,1)}, bf16[2,4,24,3072]{3,2,1,0:T(8,128)(2,1)S(1)}, u32[]{:S(2)}, u32[]{:S(2)}) %collective-permute-start.50) | collective-permute-done | bytes 1179680 | tf_op jit(solution)/shard_map/ppermute | solution.py:460
  300.8 15.2 %collective-permute-done.52.d_ref = bf16[4,24,3072]{2,1,0:T(8,128)(2,1)S(1)} collective-permute-done((bf16[4,24,3072]{2,1,0:T(8,128)(2,1)S(1)}, bf16[4,24,3072]{2,1,0:T(8,128)(2,1)S(1)}, u32[]{:S(2)}, u32[]{:S(2)}) %collective-permute-start.52) | collective-permute-done | bytes 589856 | tf_op jit(solution)/shard_map/ppermute | solution.py:464
  317.0 10.1 %collective-permute-done.51.c_ref = bf16[2,4,24,3200]{3,2,1,0:T(8,128)(2,1)S(1)} collective-permute-done((bf16[2,4,24,3200]{3,2,1,0:T(8,128)(2,1)S(1)}, bf16[2,4,24,3200]{3,2,1,0:T(8,128)(2,1)S(1)}, u32[]{:S(2)}, u32[]{:S(2)}) %collective-permute-start.51) | collective-permute-done | bytes 1228832 | tf_op jit(solution)/shard_map/ppermute | solution.py:460
  329.6 9.0 %collective-permute-start.60 = (bf16[96,768]{1,0:T(8,128)(2,1)S(1)}, bf16[96,768]{1,0:T(8,128)(2,1)S(1)}, u32[]{:S(2)}, u32[]{:S(2)}) collective-permute-start(bf16[96,768]{1,0:T(8,128)(2,1)S(1)} %get-tuple-element.195), channel_id=1, source_target_pairs={{0,8},{8,16},{16,24},{24,0},{1,9},{9,17},{17,25},{25,1},{2,10},{10... | collective-permute-start | bytes 442376 | tf_op jit(solution)/shard_map/ppermute | solution.py:448
  342.9 6.8 %collective-permute-start.58 = (bf16[24,3072]{1,0:T(8,128)(2,1)S(1)}, bf16[24,3072]{1,0:T(8,128)(2,1)S(1)}, u32[]{:S(2)}, u32[]{:S(2)}) collective-permute-start(bf16[24,3072]{1,0:T(8,128)(2,1)S(1)} %get-tuple-element.193), channel_id=1, source_target_pairs={{0,16},{8,24},{16,0},{24,8},{1,17},{9,25},{17,1},{25,9},{2,18},{10... | collective-permute-start | bytes 442376 | tf_op jit(solution)/shard_map/ppermute | solution.py:448
  349.7 2.9 collective-permute-done.61
  352.6 7.4 %collective-permute-start.59 = (bf16[24,3072]{1,0:T(8,128)(2,1)S(1)}, bf16[24,3072]{1,0:T(8,128)(2,1)S(1)}, u32[]{:S(2)}, u32[]{:S(2)}) collective-permute-start(bf16[24,3072]{1,0:T(8,128)(2,1)S(1)} %get-tuple-element.194), channel_id=1, source_target_pairs={{0,24},{8,0},{16,8},{24,16},{1,25},{9,1},{17,9},{25,17},{2,26},{10... | collective-permute-start | bytes 442376 | tf_op jit(solution)/shard_map/ppermute | solution.py:448
  362.5 3.3 collective-permute-start.56
  366.6 4.2 %shard_map.318 = (f32[24,2304]{1,0:T(8,128)}, f32[24,768]{1,0:T(8,128)}, f32[24,3072]{1,0:T(8,128)}, f32[96,768]{1,0:T(8,128)}, f32[8,24]{1,0:T(8,128)}, /*index=5*/f32[1,96]{1,0:T(1,128)}, f32[64,24]{1,0:T(8,128)S(1)}) custom-call(bf16[32,48,768]{2,1,0:T(8,128)(2,1)} %bitcast.74, bf16[24,2304]{1,0:T(8,128)(2,1)S(1)} %copy-done.37), custom_call_target="tpu_custom_call" | custom-call | bytes 3361920 | tf_op jit(solution)/shard_map/pallas_call | solution.py:683
  (276 shorter events, 140.4 us)
Async XLA Ops:
  7.2 55.8 %all-gather.7.cloned.1.call-start = ((), (), s32[]{:S(2)}) async-start(), calls=%async_computation | async-start | bytes 1658880 | tf_op jit(solution)/shard_map/all_gather | solution.py:1273
  17.8 85.5 %all-gather.9.cloned.1.call-start = ((), (), s32[]{:S(2)}) async-start(), calls=%async_computation.1 | async-start | bytes 2088960 | tf_op jit(solution)/shard_map/all_gather | solution.py:759
  20.9 16.0 %collective-permute-start.1 = (bf16[24,3200]{1,0:T(8,128)(2,1)S(1)}, bf16[24,3200]{1,0:T(8,128)(2,1)S(1)}, u32[]{:S(2)}, u32[]{:S(2)}) collective-permute-start(bf16[24,3200]{1,0:T(8,128)(2,1)S(1)} %get-tuple-element.111.refs_0_), channel_id=1, source_target_pairs={{0,16},{8,24},{16,0},{24,8},{1,17},{9,25},{17,1},{25,9},{2,18},{10... | collective-permute-start | bytes 460808 | tf_op jit(solution)/shard_map/ppermute | solution.py:448
  23.5 13.4 %collective-permute-start.2 = (bf16[24,3200]{1,0:T(8,128)(2,1)S(1)}, bf16[24,3200]{1,0:T(8,128)(2,1)S(1)}, u32[]{:S(2)}, u32[]{:S(2)}) collective-permute-start(bf16[24,3200]{1,0:T(8,128)(2,1)S(1)} %get-tuple-element.111.refs_0_), channel_id=1, source_target_pairs={{0,24},{8,0},{16,8},{24,16},{1,25},{9,1},{17,9},{25,17},{2,26},{10... | collective-permute-start | bytes 460808 | tf_op jit(solution)/shard_map/ppermute | solution.py:448
  48.4 318.1 %all-gather.11.cloned.1.call-start = ((), (), s32[]{:S(2)}) async-start(), calls=%async_computation.2 | async-start | bytes 2433024 | tf_op jit(solution)/shard_map/all_gather | solution.py:1412
  48.5 14.5 %collective-permute-start.3 = (bf16[4,24,3200]{2,1,0:T(8,128)(2,1)S(1)}, bf16[4,24,3200]{2,1,0:T(8,128)(2,1)S(1)}, u32[]{:S(2)}, u32[]{:S(2)}) collective-permute-start(bf16[4,24,3200]{2,1,0:T(8,128)(2,1)S(1)} %shard_map.290.refs_0_), channel_id=1, source_target_pairs={{0,2},{1,5},{2,0},{3,7},{4,6},{5,1},{6,4},{7,3},{8,10},{9,13},{10,... | collective-permute-start | bytes 1843208 | tf_op jit(solution)/shard_map/ppermute | solution.py:460
  49.1 13.9 %collective-permute-start.4 = (bf16[4,24,3200]{2,1,0:T(8,128)(2,1)S(1)}, bf16[4,24,3200]{2,1,0:T(8,128)(2,1)S(1)}, u32[]{:S(2)}, u32[]{:S(2)}) collective-permute-start(bf16[4,24,3200]{2,1,0:T(8,128)(2,1)S(1)} %shard_map.290.refs_0_), channel_id=1, source_target_pairs={{0,4},{1,3},{2,6},{3,1},{4,0},{5,7},{6,2},{7,5},{8,12},{9,11},{10,... | collective-permute-start | bytes 1843208 | tf_op jit(solution)/shard_map/ppermute | solution.py:464
  64.4 19.4 %collective-permute-start.10 = (bf16[4,24,3840]{2,1,0:T(8,128)(2,1)S(1)}, bf16[4,24,3840]{2,1,0:T(8,128)(2,1)S(1)}, u32[]{:S(2)}, u32[]{:S(2)}) collective-permute-start(bf16[4,24,3840]{2,1,0:T(8,128)(2,1)S(1)} %slice.24.refs_0_), channel_id=1, source_target_pairs={{0,2},{1,5},{2,0},{3,7},{4,6},{5,1},{6,4},{7,3},{8,10},{9,13},{10,... | collective-permute-start | bytes 2211848 | tf_op jit(solution)/shard_map/ppermute | solution.py:460
  65.4 18.4 %collective-permute-start.11 = (bf16[4,24,3840]{2,1,0:T(8,128)(2,1)S(1)}, bf16[4,24,3840]{2,1,0:T(8,128)(2,1)S(1)}, u32[]{:S(2)}, u32[]{:S(2)}) collective-permute-start(bf16[4,24,3840]{2,1,0:T(8,128)(2,1)S(1)} %slice.24.refs_0_), channel_id=1, source_target_pairs={{0,4},{1,3},{2,6},{3,1},{4,0},{5,7},{6,2},{7,5},{8,12},{9,11},{10,... | collective-permute-start | bytes 2211848 | tf_op jit(solution)/shard_map/ppermute | solution.py:464
  67.0 19.4 %collective-permute-start.6 = (bf16[4,24,3200]{2,1,0:T(8,128)(2,1)S(1)}, bf16[4,24,3200]{2,1,0:T(8,128)(2,1)S(1)}, u32[]{:S(2)}, u32[]{:S(2)}) collective-permute-start(bf16[4,24,3200]{2,1,0:T(8,128)(2,1)S(1)} %shard_map.290.refs_0_), channel_id=1, source_target_pairs={{0,1},{1,0},{2,3},{3,2},{4,5},{5,4},{6,7},{7,6},{8,9},{9,8},{10,11... | collective-permute-start | bytes 1843208 | tf_op jit(solution)/shard_map/ppermute | solution.py:452
  67.0 24.9 %collective-permute-start.5 = (bf16[4,24,3200]{2,1,0:T(8,128)(2,1)S(1)}, bf16[4,24,3200]{2,1,0:T(8,128)(2,1)}, u32[]{:S(2)}, u32[]{:S(2)}) collective-permute-start(bf16[4,24,3200]{2,1,0:T(8,128)(2,1)S(1)} %collective-permute-done.3.refs_1_), channel_id=1, source_target_pairs={{0,4},{1,3},{2,6},{3,1},{4,0},{5,7},{6,2},{7,5},{8,12},{9,11},{10,... | collective-permute-start | bytes 1843208 | tf_op jit(solution)/shard_map/ppermute | solution.py:464
  83.8 16.3 %collective-permute-start.17 = (bf16[4,24,3072]{2,1,0:T(8,128)(2,1)S(1)}, bf16[4,24,3072]{2,1,0:T(8,128)(2,1)S(1)}, u32[]{:S(2)}, u32[]{:S(2)}) collective-permute-start(bf16[4,24,3072]{2,1,0:T(8,128)(2,1)S(1)} %slice.26.refs_0_), channel_id=1, source_target_pairs={{0,2},{1,5},{2,0},{3,7},{4,6},{5,1},{6,4},{7,3},{8,10},{9,13},{10,... | collective-permute-start | bytes 1769480 | tf_op jit(solution)/shard_map/ppermute | solution.py:460
  84.8 16.0 %collective-permute-start.18 = (bf16[4,24,3072]{2,1,0:T(8,128)(2,1)S(1)}, bf16[4,24,3072]{2,1,0:T(8,128)(2,1)S(1)}, u32[]{:S(2)}, u32[]{:S(2)}) collective-permute-start(bf16[4,24,3072]{2,1,0:T(8,128)(2,1)S(1)} %slice.26.refs_0_), channel_id=1, source_target_pairs={{0,4},{1,3},{2,6},{3,1},{4,0},{5,7},{6,2},{7,5},{8,12},{9,11},{10,... | collective-permute-start | bytes 1769480 | tf_op jit(solution)/shard_map/ppermute | solution.py:464
  86.4 16.9 %collective-permute-start.7 = (bf16[4,24,3200]{2,1,0:T(8,128)(2,1)S(1)}, bf16[4,24,3200]{2,1,0:T(8,128)(2,1)}, u32[]{:S(2)}, u32[]{:S(2)}) collective-permute-start(bf16[4,24,3200]{2,1,0:T(8,128)(2,1)S(1)} %collective-permute-done.3.refs_1_), channel_id=1, source_target_pairs={{0,1},{1,0},{2,3},{3,2},{4,5},{5,4},{6,7},{7,6},{8,9},{9,8},{10,11... | collective-permute-start | bytes 1843208 | tf_op jit(solution)/shard_map/ppermute | solution.py:452
  87.3 21.5 %collective-permute-start.12 = (bf16[4,24,3840]{2,1,0:T(8,128)(2,1)S(1)}, bf16[4,24,3840]{2,1,0:T(8,128)(2,1)}, u32[]{:S(2)}, u32[]{:S(2)}) collective-permute-start(bf16[4,24,3840]{2,1,0:T(8,128)(2,1)S(1)} %collective-permute-done.10.refs_1_), channel_id=1, source_target_pairs={{0,4},{1,3},{2,6},{3,1},{4,0},{5,7},{6,2},{7,5},{8,12},{9,11},{10,... | collective-permute-start | bytes 2211848 | tf_op jit(solution)/shard_map/ppermute | solution.py:464
  103.3 70.8 %collective-permute-start.31 = (bf16[4,4,24,2176]{3,2,1,0:T(8,128)(2,1)}, bf16[4,4,24,2176]{3,2,1,0:T(8,128)(2,1)}, u32[]{:S(2)}, u32[]{:S(2)}) collective-permute-start(bf16[4,4,24,2176]{3,2,1,0:T(8,128)(2,1)} %bitcast.66), channel_id=1, source_target_pairs={{0,1},{1,0},{2,3},{3,2},{4,5},{5,4},{6,7},{7,6},{8,9},{9,8},{10,11... | collective-permute-start | bytes 5013512 | tf_op jit(solution)/shard_map/ppermute | solution.py:452
  111.5 46.2 %collective-permute-start.20 = (bf16[4,24,3072]{2,1,0:T(8,128)(2,1)S(1)}, bf16[4,24,3072]{2,1,0:T(8,128)(2,1)}, u32[]{:S(2)}, u32[]{:S(2)}) collective-permute-start(bf16[4,24,3072]{2,1,0:T(8,128)(2,1)S(1)} %slice.26.refs_0_), channel_id=1, source_target_pairs={{0,1},{1,0},{2,3},{3,2},{4,5},{5,4},{6,7},{7,6},{8,9},{9,8},{10,11... | collective-permute-start | bytes 1769480 | tf_op jit(solution)/shard_map/ppermute | solution.py:452
  113.1 44.6 %collective-permute-start.21 = (bf16[4,24,3072]{2,1,0:T(8,128)(2,1)}, bf16[4,24,3072]{2,1,0:T(8,128)(2,1)}, u32[]{:S(2)}, u32[]{:S(2)}) collective-permute-start(bf16[4,24,3072]{2,1,0:T(8,128)(2,1)} %copy-done.32), channel_id=1, source_target_pairs={{0,1},{1,0},{2,3},{3,2},{4,5},{5,4},{6,7},{7,6},{8,9},{9,8},{10,11... | collective-permute-start | bytes 1769480 | tf_op jit(solution)/shard_map/ppermute | solution.py:452
  120.3 37.4 %collective-permute-start.22 = (bf16[4,24,3072]{2,1,0:T(8,128)(2,1)}, bf16[4,24,3072]{2,1,0:T(8,128)(2,1)}, u32[]{:S(2)}, u32[]{:S(2)}) collective-permute-start(bf16[4,24,3072]{2,1,0:T(8,128)(2,1)} %copy-done.34), channel_id=1, source_target_pairs={{0,1},{1,0},{2,3},{3,2},{4,5},{5,4},{6,7},{7,6},{8,9},{9,8},{10,11... | collective-permute-start | bytes 1769480 | tf_op jit(solution)/shard_map/ppermute | solution.py:452
  121.2 36.6 %collective-permute-start.23 = (bf16[4,24,3072]{2,1,0:T(8,128)(2,1)}, bf16[4,24,3072]{2,1,0:T(8,128)(2,1)}, u32[]{:S(2)}, u32[]{:S(2)}) collective-permute-start(bf16[4,24,3072]{2,1,0:T(8,128)(2,1)} %collective-permute-done.19.refs_3_), channel_id=1, source_target_pairs={{0,1},{1,0},{2,3},{3,2},{4,5},{5,4},{6,7},{7,6},{8,9},{9,8},{10,11... | collective-permute-start | bytes 1769480 | tf_op jit(solution)/shard_map/ppermute | solution.py:452
  240.2 16.5 %collective-permute-start.47 = (bf16[2,4,96,768]{3,2,1,0:T(8,128)(2,1)}, bf16[2,4,96,768]{3,2,1,0:T(8,128)(2,1)}, u32[]{:S(2)}, u32[]{:S(2)}) collective-permute-start(bf16[2,4,96,768]{3,2,1,0:T(8,128)(2,1)} %shard_map.307), channel_id=1, source_target_pairs={{0,2},{1,5},{2,0},{3,7},{4,6},{5,1},{6,4},{7,3},{8,10},{9,13},{10,... | collective-permute-start | bytes 3538952 | tf_op jit(solution)/shard_map/ppermute | solution.py:460
  267.1 30.1 %collective-permute-start.48 = (bf16[4,4,24,3200]{3,2,1,0:T(8,128)(2,1)}, bf16[4,4,24,3200]{3,2,1,0:T(8,128)(2,1)S(1)}, u32[]{:S(2)}, u32[]{:S(2)}) collective-permute-start(bf16[4,4,24,3200]{3,2,1,0:T(8,128)(2,1)} %bitcast.80), channel_id=1, source_target_pairs={{0,1},{1,0},{2,3},{3,2},{4,5},{5,4},{6,7},{7,6},{8,9},{9,8},{10,11... | collective-permute-start | bytes 7372808 | tf_op jit(solution)/shard_map/ppermute | solution.py:452
  267.1 23.0 %collective-permute-start.50 = (bf16[2,4,24,3072]{3,2,1,0:T(8,128)(2,1)}, bf16[2,4,24,3072]{3,2,1,0:T(8,128)(2,1)S(1)}, u32[]{:S(2)}, u32[]{:S(2)}) collective-permute-start(bf16[2,4,24,3072]{3,2,1,0:T(8,128)(2,1)} %copy-done.17), channel_id=1, source_target_pairs={{0,2},{1,5},{2,0},{3,7},{4,6},{5,1},{6,4},{7,3},{8,10},{9,13},{10,... | collective-permute-start | bytes 3538952 | tf_op jit(solution)/shard_map/ppermute | solution.py:460
  268.5 25.9 %collective-permute-start.49 = (bf16[4,96,768]{2,1,0:T(8,128)(2,1)S(1)}, bf16[4,96,768]{2,1,0:T(8,128)(2,1)S(1)}, u32[]{:S(2)}, u32[]{:S(2)}) collective-permute-start(bf16[4,96,768]{2,1,0:T(8,128)(2,1)S(1)} %shard_map.310), channel_id=1, source_target_pairs={{0,4},{1,3},{2,6},{3,1},{4,0},{5,7},{6,2},{7,5},{8,12},{9,11},{10,... | collective-permute-start | bytes 1769480 | tf_op jit(solution)/shard_map/ppermute | solution.py:464
  298.3 28.8 %collective-permute-start.51 = (bf16[2,4,24,3200]{3,2,1,0:T(8,128)(2,1)S(1)}, bf16[2,4,24,3200]{3,2,1,0:T(8,128)(2,1)S(1)}, u32[]{:S(2)}, u32[]{:S(2)}) collective-permute-start(bf16[2,4,24,3200]{3,2,1,0:T(8,128)(2,1)S(1)} %shard_map.314), channel_id=1, source_target_pairs={{0,2},{1,5},{2,0},{3,7},{4,6},{5,1},{6,4},{7,3},{8,10},{9,13},{10,... | collective-permute-start | bytes 3686408 | tf_op jit(solution)/shard_map/ppermute | solution.py:460
  299.7 16.3 %collective-permute-start.52 = (bf16[4,24,3072]{2,1,0:T(8,128)(2,1)S(1)}, bf16[4,24,3072]{2,1,0:T(8,128)(2,1)S(1)}, u32[]{:S(2)}, u32[]{:S(2)}) collective-permute-start(bf16[4,24,3072]{2,1,0:T(8,128)(2,1)S(1)} %shard_map.312), channel_id=1, source_target_pairs={{0,4},{1,3},{2,6},{3,1},{4,0},{5,7},{6,2},{7,5},{8,12},{9,11},{10,... | collective-permute-start | bytes 1769480 | tf_op jit(solution)/shard_map/ppermute | solution.py:464
  328.1 32.8 %collective-permute-start.53 = (bf16[4,24,3200]{2,1,0:T(8,128)(2,1)S(1)}, bf16[4,24,3200]{2,1,0:T(8,128)(2,1)S(1)}, u32[]{:S(2)}, u32[]{:S(2)}) collective-permute-start(bf16[4,24,3200]{2,1,0:T(8,128)(2,1)S(1)} %shard_map.316), channel_id=1, source_target_pairs={{0,4},{1,3},{2,6},{3,1},{4,0},{5,7},{6,2},{7,5},{8,12},{9,11},{10,... | collective-permute-start | bytes 1843208 | tf_op jit(solution)/shard_map/ppermute | solution.py:464
  329.6 13.3 %collective-permute-start.60 = (bf16[96,768]{1,0:T(8,128)(2,1)S(1)}, bf16[96,768]{1,0:T(8,128)(2,1)S(1)}, u32[]{:S(2)}, u32[]{:S(2)}) collective-permute-start(bf16[96,768]{1,0:T(8,128)(2,1)S(1)} %get-tuple-element.195), channel_id=1, source_target_pairs={{0,8},{8,16},{16,24},{24,0},{1,9},{9,17},{17,25},{25,1},{2,10},{10... | collective-permute-start | bytes 442376 | tf_op jit(solution)/shard_map/ppermute | solution.py:448
  338.6 14.0 %collective-permute-start.61 = (bf16[96,768]{1,0:T(8,128)(2,1)S(1)}, bf16[96,768]{1,0:T(8,128)(2,1)S(1)}, u32[]{:S(2)}, u32[]{:S(2)}) collective-permute-start(bf16[96,768]{1,0:T(8,128)(2,1)S(1)} %get-tuple-element.196), channel_id=1, source_target_pairs={{0,16},{8,24},{16,0},{24,8},{1,17},{9,25},{17,1},{25,9},{2,18},{10... | collective-permute-start | bytes 442376 | tf_op jit(solution)/shard_map/ppermute | solution.py:448
  338.6 21.4 %collective-permute-start.62 = (bf16[96,768]{1,0:T(8,128)(2,1)S(1)}, bf16[96,768]{1,0:T(8,128)(2,1)S(1)}, u32[]{:S(2)}, u32[]{:S(2)}) collective-permute-start(bf16[96,768]{1,0:T(8,128)(2,1)S(1)} %get-tuple-element.197), channel_id=1, source_target_pairs={{0,24},{8,0},{16,8},{24,16},{1,25},{9,1},{17,9},{25,17},{2,26},{10... | collective-permute-start | bytes 442376 | tf_op jit(solution)/shard_map/ppermute | solution.py:448
  341.0 21.6 %collective-permute-start.57 = (bf16[24,3072]{1,0:T(8,128)(2,1)S(1)}, bf16[24,3072]{1,0:T(8,128)(2,1)S(1)}, u32[]{:S(2)}, u32[]{:S(2)}) collective-permute-start(bf16[24,3072]{1,0:T(8,128)(2,1)S(1)} %get-tuple-element.192), channel_id=1, source_target_pairs={{0,8},{8,16},{16,24},{24,0},{1,9},{9,17},{17,25},{25,1},{2,10},{10... | collective-permute-start | bytes 442376 | tf_op jit(solution)/shard_map/ppermute | solution.py:448
  342.9 22.9 %collective-permute-start.58 = (bf16[24,3072]{1,0:T(8,128)(2,1)S(1)}, bf16[24,3072]{1,0:T(8,128)(2,1)S(1)}, u32[]{:S(2)}, u32[]{:S(2)}) collective-permute-start(bf16[24,3072]{1,0:T(8,128)(2,1)S(1)} %get-tuple-element.193), channel_id=1, source_target_pairs={{0,16},{8,24},{16,0},{24,8},{1,17},{9,25},{17,1},{25,9},{2,18},{10... | collective-permute-start | bytes 442376 | tf_op jit(solution)/shard_map/ppermute | solution.py:448
  (89 other events, 590.7 us)
Sparse Core Ops, SparseCore 0:
  17.9 40.5 all-gather.6
  60.1 38.0 all-gather.8
  267.2 67.3 all-gather.10

commit v3 on v2

--- a/solution.py
+++ b/solution.py
@@ -474,6 +474,10 @@
     return lax.optimization_barrier((array_in,) + before)[0]
 
 
+def stage(*values):
+    return lax.optimization_barrier(values)
+
+
 def wide(array_in):
     return array_in.astype(jnp.float32)
 
@@ -482,7 +486,7 @@
     return array_in.astype(jnp.bfloat16)
 
 
-def copies(pieces, shapes, moves):
+def copies(pieces, shapes, moves, room=64):
     count, made = len(pieces), len(shapes)
     total = len(moves(0, 0, 0))
 
@@ -506,32 +510,28 @@
     return pl.pallas_call(
         kernel,
         out_shape=[jax.ShapeDtypeStruct(shape, pieces[0].dtype) for shape in shapes],
-        in_specs=[pl.BlockSpec(memory_space=pl.ANY)] * count,
-        out_specs=[pl.BlockSpec(memory_space=pl.ANY)] * made,
+        in_specs=[pl.BlockSpec(memory_space=pltpu.HBM)] * count,
+        out_specs=[pl.BlockSpec(memory_space=pltpu.HBM)] * made,
         scratch_shapes=[pltpu.VMEM(piece.shape, piece.dtype) for piece in pieces]
         + [pltpu.SemaphoreType.DMA((2, max(count, total)))],
-        compiler_params=pltpu.CompilerParams(vmem_limit_bytes=24 * 2**20),
-        cost_estimate=pl.CostEstimate(flops=0, bytes_accessed=size, transcendentals=0),
+        compiler_params=pltpu.CompilerParams(vmem_limit_bytes=room * 2**20),
+        cost_estimate=pl.CostEstimate(flops=0, bytes_accessed=0, transcendentals=0),
     )(*pieces)
 
 
 every = slice(None)
 
 
-def gather_dp(shard):
-    pieces = [shard] + [swap_dp(shard, shift) for shift in (1, 2, 3)]
+def reach_dp(shard):
+    return [shard] + [swap_dp(shard, shift) for shift in (1, 2, 3)]
+
+
+def join_dp(pieces):
     return copies(
         pieces,
-        [(4,) + shard.shape],
+        [(4,) + pieces[0].shape],
         lambda layer, chip, core: [(i, every, 0, lax.rem(layer + 4 - i, 4)) for i in range(4)],
     )[0]
-
-
-def plane_moves(column, *before):
-    ready = after(column, *before) if before else column
-    first = swap_one(ready)
-    second = swap_two(ready)
-    return [column, first, second, swap_two(first)]
 
 
 def plane_order(chip, core):
@@ -539,17 +539,17 @@
     return (chip, near, far, chip ^ 3), (chip, far, near, chip ^ 3)
 
 
-def gather_plane(mine):
+def gather_plane(mine, others):
     def moves(layer, chip, core):
         own, other = plane_order(chip, core)
         found = [(i, every, 0, (every, own[i], core)) for i in range(4)]
         return found + [(4 + i, every, 0, (every, other[i], 1 - core)) for i in range(4)]
 
     shape = (4, 4, 2) + mine[0].shape[1:]
-    return copies(mine + [swap_core(piece) for piece in mine], [shape], moves)[0]
-
-
-def gather_down(mine):
+    return copies(mine + others, [shape], moves)[0]
+
+
+def gather_down(mine, others):
     def moves(layer, chip, core):
         own, other = plane_order(chip, core)
         found = []
@@ -560,90 +560,105 @@
                 found.append((i, part, 0, (every, spot, side, quarter)))
         return found
 
-    return copies(mine + [swap_core(piece) for piece in mine], [(4, 4, 2, 4, 24, D)], moves)[0]
+    return copies(mine + others, [(4, 4, 2, 4, 24, D)], moves, room=24)[0]
 
 
 class Sum:
-    def __init__(self, kept, gone):
-        layer, chip, core = place_in()
+    def __init__(self, kept):
         self.kept = kept
         self.shape = kept.shape[2:]
-        self.spots = jnp.stack([chip ^ (1 + core), chip ^ 3, chip ^ (2 - core), chip, layer])
-        self.got = swap_core(gone)
-
-    def part(self, take):
-        return pl.BlockSpec((4, None) + self.shape, take)
-
-    def run(self, kernel, grid, in_specs, out_specs, out_shape, *operands):
-        size = sum(math.prod(a.shape) * 2 for a in operands)
+
+    def run(self, operands, out_shapes, plan):
+        shape, count, made = self.shape, len(operands), len(out_shapes)
+        dry = plan(0, 0, 0)
+        pieces = sum(len(sources) for sources, target in dry)
+
+        def kernel(*refs):
+            given, outs = refs[:count], refs[count : count + made]
+            held, built, sems = refs[count + made : -len(dry) - 1], refs[-len(dry) - 1 : -1], refs[-1]
+            inward, outward, steps = [], [], []
+            for sources, target in plan(*place_in()):
+                step = []
+                for operand, index in sources:
+                    spot = len(inward)
+                    source = given[operand].at[index]
+                    copy = pltpu.make_async_copy(source, held[spot], sems.at[0, spot])
+                    copy.start()
+                    inward.append(copy)
+                    step.append(spot)
+                steps.append((step, target))
+            for place, (step, (out, index)) in enumerate(steps):
+                total = None
+                for spot in step:
+                    inward[spot].wait()
+                    value = wide(held[spot][...])
+                    total = value if total is None else total + value
+                built[place][...] = total.astype(built[place].dtype)
+                target = outs[out] if index is None else outs[out].at[index]
+                copy = pltpu.make_async_copy(built[place], target, sems.at[1, place])
+                copy.start()
+                outward.append(copy)
+            for copy in outward:
+                copy.wait()
+
+        far = pl.BlockSpec(memory_space=pltpu.HBM)
         return pl.pallas_call(
             kernel,
-            grid_spec=pltpu.PrefetchScalarGridSpec(
-                num_scalar_prefetch=1, grid=grid, in_specs=in_specs, out_specs=out_specs
-            ),
-            out_shape=out_shape,
-            compiler_params=pltpu.CompilerParams(vmem_limit_bytes=32 * 2**20),
-            cost_estimate=pl.CostEstimate(flops=size, bytes_accessed=size, transcendentals=0),
-        )(self.spots, *operands)
-
-    def first(self, *before):
-        def kernel(spots_ref, a_ref, b_ref, o_ref):
-            o_ref[...] = low(wide(a_ref[...]) + wide(b_ref[...]))
-
-        near = self.part(lambda i, s: (0, s[i], 0, 0))
-        out = pl.BlockSpec((None, 4) + self.shape, lambda i, s: (i, 0, 0, 0))
-        got = after(self.got, *before) if before else self.got
-        sent = self.run(kernel, (2,), [near, near], out, half(2, 4, *self.shape), self.kept, got)
-        self.back = swap_one(sent)
-        return sent
-
-    def second(self, *before):
-        def kernel(spots_ref, a_ref, b_ref, c_ref, o_ref):
-            o_ref[...] = low(wide(a_ref[...]) + wide(b_ref[...]) + wide(c_ref[...]))
-
-        pair = (2, None) + self.shape
-        far = pl.BlockSpec(pair, lambda i, s: (i, s[2], 0, 0))
-        moved = pl.BlockSpec((None, 2) + self.shape, lambda i, s: (1, i, 0, 0))
-        out = pl.BlockSpec((2,) + self.shape, lambda i, s: (i, 0, 0))
-        back = after(self.back, *before) if before else self.back
-        onward = self.run(
-            kernel, (2,), [far, far, moved], out, half(4, *self.shape), self.kept, self.got, back
+            out_shape=out_shapes,
+            in_specs=[far] * count,
+            out_specs=[far] * made,
+            scratch_shapes=[pltpu.VMEM(shape, jnp.bfloat16)] * pieces
+            + [pltpu.VMEM(shape, out_shapes[target[0]].dtype) for sources, target in dry]
+            + [pltpu.SemaphoreType.DMA((2, pieces))],
+            compiler_params=pltpu.CompilerParams(vmem_limit_bytes=64 * 2**20),
+            cost_estimate=pl.CostEstimate(flops=0, bytes_accessed=0, transcendentals=0),
+        )(*operands)
+
+    def first(self, got):
+        self.got = got
+
+        def plan(layer, chip, core):
+            return [
+                ([(0, (z, spot)), (1, (z, spot))], (0, (i, z)))
+                for i, spot in enumerate((chip ^ (1 + core), chip ^ 3))
+                for z in range(4)
+            ]
+
+        return self.run([self.kept, got], [half(2, 4, *self.shape)], plan)[0]
+
+    def second(self, back):
+        self.back = back
+
+        def plan(layer, chip, core):
+            spot = chip ^ (2 - core)
+            return [
+                ([(0, (z, spot)), (1, (z, spot)), (2, (1, z))], (0, z)) for z in range(4)
+            ]
+
+        return self.run([self.kept, self.got, back], [half(4, *self.shape)], plan)[0]
+
+    def third(self, last):
+        def plan(layer, chip, core):
+            found = []
+            for shift in (1, 2, 3, 0):
+                z = lax.rem(layer + shift, 4)
+                sources = [(0, (z, chip)), (1, (z, chip)), (2, (0, z)), (3, z)]
+                found.append((sources, (shift, None)))
+            return found
+
+        self.own, *others = self.run(
+            [self.kept, self.got, self.back, last],
+            [shape_of(*self.shape)] + [half(*self.shape)] * 3,
+            plan,
         )
-        self.last = swap_two(onward)
-        return onward
-
-    def third(self, *before):
-        def kernel(spots_ref, a_ref, b_ref, c_ref, d_ref, own_ref, *outs):
-            for shift in range(4):
-                level = lax.rem(spots_ref[4] + shift, 4)
-                total = wide(a_ref[level]) + wide(b_ref[level]) + wide(c_ref[level])
-                total = total + wide(d_ref[level])
-                if shift:
-                    outs[shift - 1][...] = low(total)
-                else:
-                    own_ref[...] = total
-
-        here = self.part(lambda i, s: (0, s[3], 0, 0))
-        moved = pl.BlockSpec((None, 4) + self.shape, lambda i, s: (0, 0, 0, 0))
-        full = pl.BlockSpec((4,) + self.shape, lambda i, s: (0, 0, 0))
-        flat = pl.BlockSpec(self.shape, lambda i, s: (0, 0))
-        last = after(self.last, *before) if before else self.last
-        self.own, *others = self.run(
-            kernel,
-            (1,),
-            [here, here, moved, full],
-            [flat] * 4,
-            [shape_of(*self.shape)] + [half(*self.shape)] * 3,
-            self.kept,
-            self.got,
-            self.back,
-            last,
-        )
-        self.others = [swap_dp(other, shift) for shift, other in zip((1, 2, 3), others)]
-        return self.own
-
-    def total(self):
-        return self.own + wide(self.others[0]) + wide(self.others[1]) + wide(self.others[2])
+        return others
+
+    def total(self, others):
+        return self.own + wide(others[0]) + wide(others[1]) + wide(others[2])
+
+
+def send_dp(others):
+    return [swap_dp(other, shift) for shift, other in zip((1, 2, 3), others)]
 
 
 def norm_parts(values):
@@ -676,7 +691,7 @@
     return jax.ShapeDtypeStruct(shape, jnp.bfloat16)
 
 
-def on_core(kernel, out_shape, operands, flops, grid=(), in_specs=None, out_specs=None, scratch=()):
+def on_core(kernel, out_shape, operands, flops, room=64, grid=(), in_specs=None, out_specs=None, scratch=()):
     arrays = jax.tree.leaves(out_shape) + list(operands)
     size = sum(math.prod(a.shape) * a.dtype.itemsize for a in arrays)
     extra = {} if in_specs is None else {"in_specs": in_specs, "out_specs": out_specs}
@@ -685,8 +700,8 @@
         out_shape=out_shape,
         grid=grid,
         scratch_shapes=scratch,
-        compiler_params=pltpu.CompilerParams(vmem_limit_bytes=52 * 2**20),
-        cost_estimate=pl.CostEstimate(flops=flops, bytes_accessed=size, transcendentals=0),
+        compiler_params=pltpu.CompilerParams(vmem_limit_bytes=room * 2**20),
+        cost_estimate=pl.CostEstimate(flops=0, bytes_accessed=0, transcendentals=0),
         **extra,
     )(*operands)
 
@@ -695,41 +710,37 @@
     return jnp.sum(array_in, axis=0, keepdims=True)
 
 
-def prepare(
-    mix_ref,
-    out_ref,
-    up_ref,
-    down_ref,
-    vectors_ref,
-    bias_ref,
-    cross_mix_ref,
-    cross_out_ref,
-    cross_up_ref,
-    cross_vectors_ref,
-    cross_bias_ref,
-    table_ref,
-    one_ref,
-    two_ref,
-    part_a,
-    part_b,
-    part_c,
-    part_d,
-    small,
-    parts,
-):
+def prepare(*refs):
+    given, made, held, built = refs[0:12], refs[12:19], refs[19:31], refs[31:38]
+    small, turned, parts, sems = refs[38:]
+    inward = [pltpu.make_async_copy(given[i], held[i], sems.at[0, i]) for i in range(12)]
+    outward = [pltpu.make_async_copy(built[i], made[i], sems.at[1, i]) for i in range(7)]
+    for copy in inward:
+        copy.start()
+    for copy in inward:
+        copy.wait()
+    mix_ref, out_ref, up_ref, down_ref, vectors_ref, bias_ref = held[0:6]
+    cross_mix_ref, cross_out_ref, cross_up_ref, cross_vectors_ref, cross_bias_ref, table_ref = held[6:]
+    one_ref, two_ref, three_ref = built[0:3]
     one_ref[:, 0 : 3 * D] = mix_ref[...]
     one_ref[:, 3 * D : 4 * D] = out_ref[...]
     small[...] = jnp.zeros_like(small)
     small[0:8, 0:24] = wide(vectors_ref[...])
     small[8:16, 0:24] = wide(cross_vectors_ref[...])
-    small[16:80, 0:24] = wide(table_ref[...])
-    small[80:84, 0:24] = wide(bias_ref[...])
-    small[84:88, 0:24] = wide(cross_bias_ref[...])
-    one_ref[:, 4 * D : 4 * D + 128] = low(small[...].T[0:24, :])
+    for row in range(4):
+        lanes = slice(24 * row, 24 * (row + 1))
+        small[80 + row : 81 + row, 0:24] = wide(bias_ref[:, lanes])
+        small[84 + row : 85 + row, 0:24] = wide(cross_bias_ref[:, lanes])
+    turned[...] = small[...].T
+    turned[0:24, 16:80] = wide(table_ref[...])
+    one_ref[:, 4 * D : 4 * D + 128] = low(turned[0:24, :])
+    outward[0].start()
     two_ref[:, 0 : 4 * D] = up_ref[...]
     two_ref[:, 4 * D : 5 * D] = cross_out_ref[...]
     for quarter in range(4):
-        two_ref[:, (5 + quarter) * D : (6 + quarter) * D] = down_ref[quarter]
+        three_ref[:, quarter * D : (quarter + 1) * D] = down_ref[quarter]
+    outward[1].start()
+    outward[2].start()
     parts[...] = jnp.zeros_like(parts)
     for spot in range(4):
         for level in range(4):
@@ -739,13 +750,14 @@
             taken = cross_mix_ref[:, third * D + 192 * spot : third * D + 192 * (spot + 1)]
             parts[spot, :, D + 192 * third : D + 192 * (third + 1)] = taken
     chip = place_in()[1]
-    for mask, ref in enumerate((part_a, part_b, part_c, part_d)):
-        ref[...] = parts[chip ^ mask]
-
-
-def gather_cross(parts, cross_down):
-    pieces = [parts[0]] + [swap_chip(parts[mask], mask) for mask in (1, 2, 3)]
-
+    for mask in range(4):
+        built[3 + mask][...] = parts[chip ^ mask]
+        outward[3 + mask].start()
+    for copy in outward:
+        copy.wait()
+
+
+def join_cross(pieces, cross_down):
     def moves(layer, chip, core):
         found = []
         for mask in range(4):
@@ -755,8 +767,7 @@
         found.append((4, every, 0, (every, every, slice(D, 2 * D))))
         return found
 
-    row = copies(pieces + [cross_down.reshape(4, 24, D)], [(4, 24, 2 * D + 640)], moves)[0]
-    return lax.all_gather(row, "dp")
+    return copies(pieces + [cross_down.reshape(4, 24, D)], [(4, 24, 2 * D + 640)], moves)[0]
 
 
 def place_cross(column):
@@ -775,7 +786,7 @@
         return found
 
     up_mix, down = copies(
-        [column, other], [(4, 4, 2, 24, D + 640), (4, 2, 4, 24, D)], moves
+        [column, other], [(4, 4, 2, 24, D + 640), (4, 2, 4, 24, D)], moves, room=24
     )
     return up_mix.reshape(D, D + 640), down.reshape(D, D)
 
@@ -1250,35 +1261,56 @@
     docs_column = token_docs.reshape(256, 1)
     segment_column = segment_docs.T
 
-    shard_one, shard_two, *cross_pieces = on_core(
+    shards_in = (
+        local_mix,
+        local_out,
+        local_up,
+        local_down.reshape(4, 24, D),
+        local_vectors,
+        local_up_bias.reshape(1, 96),
+        cross_mix,
+        cross_out,
+        cross_up,
+        cross_vectors,
+        cross_up_bias.reshape(1, 96),
+        position_table.T,
+    )
+    made = [half(24, 3200), half(24, 5 * D), half(24, 4 * D)] + [half(24, D + 640)] * 4
+    far = pl.BlockSpec(memory_space=pltpu.HBM)
+    shard_one, shard_two, shard_three, *cross_pieces = on_core(
         prepare,
-        [half(24, 3200), half(24, 9 * D)] + [half(24, D + 640)] * 4,
-        (
-            local_mix,
-            local_out,
-            local_up,
-            local_down.reshape(4, 24, D),
-            local_vectors,
-            local_up_bias.reshape(4, 24),
-            cross_mix,
-            cross_out,
-            cross_up,
-            cross_vectors,
-            cross_up_bias.reshape(4, 24),
-            position_table,
-        ),
+        made,
+        shards_in,
         0,
-        scratch=[pltpu.VMEM((128, 128), jnp.float32), pltpu.VMEM((4, 24, D + 640), jnp.bfloat16)],
-    )
-    columns = lax.all_gather(shard_two, "dp")
-    column_one = gather_dp(shard_one)
-    moves_one = plane_moves(column_one)
-    cross_column = gather_cross(after(tuple(cross_pieces), column_one), cross_down)
-    first_group = gather_plane(moves_one).reshape(D, 3200)
-    columns = after(columns, moves_one[1], moves_one[2])
-    moves_two = plane_moves(columns[:, :, : 5 * D])
-    moves_three = plane_moves(columns[:, :, 5 * D :], moves_two[1], moves_two[2])
-
+        in_specs=[far] * 12,
+        out_specs=[far] * 7,
+        scratch=[pltpu.VMEM(a.shape, a.dtype) for a in list(shards_in) + made]
+        + [
+            pltpu.VMEM((128, 128), jnp.float32),
+            pltpu.VMEM((128, 128), jnp.float32),
+            pltpu.VMEM((4, 24, D + 640), jnp.bfloat16),
+            pltpu.SemaphoreType.DMA((2, 12)),
+        ],
+    )
+    cross_sent = [cross_pieces[0]] + [swap_chip(cross_pieces[mask], mask) for mask in (1, 2, 3)]
+    z_one = reach_dp(shard_one)
+    cross_row = join_cross(cross_sent, cross_down)
+    *z_one, cross_row, shard_two = stage(*z_one, cross_row, shard_two)
+    column_one = join_dp(z_one)
+    column_one, shard_two = stage(column_one, shard_two)
+
+    first, second = swap_one(column_one), swap_two(column_one)
+    *z_two, first, second, column_one = stage(*reach_dp(shard_two), first, second, column_one)
+
+    third = swap_two(first)
+    others = [swap_core(piece) for piece in (column_one, first, second)]
+    third, *z_two = stage(third, *others, *z_two)
+    others, z_two = z_two[:3], z_two[3:]
+    column_two = join_dp(z_two)
+    others.append(swap_core(third))
+    column_two, shard_three, *others = stage(column_two, shard_three, *others)
+
+    first_group = gather_plane([column_one, first, second, third], others).reshape(D, 3200)
     mixed_rows, context_rows, probs_kept, normed_one, scale_one, low_one, rows = on_core(
         local_attend,
         [
@@ -1293,11 +1325,25 @@
         (flat_tokens, first_group, token_docs, docs_column),
         2 * 256 * D * 5 * D,
     )
+    first_two, second_two = swap_one(column_two), swap_two(column_two)
+    *z_three, low_one, first_two, second_two, column_two = stage(
+        *reach_dp(shard_three), low_one, first_two, second_two, column_two
+    )
+
+    third_two = swap_two(first_two)
+    others = [swap_core(piece) for piece in (column_two, first_two, second_two)]
+    column_three = join_dp(z_three)
+    third_two, column_three, cross_row, *others = stage(third_two, column_three, cross_row, *others)
+
+    cross_column = lax.all_gather(cross_row, "dp")
+    first_three, second_three = swap_one(column_three), swap_two(column_three)
+    others.append(swap_core(third_two))
     up_bias = rows[80:84].reshape(4, 32, 24).transpose(1, 0, 2).reshape(1, 4 * D)
     cross_bias = rows[84:88].reshape(4, 4, 4, 2, 24)
     cross_bias = lax.dynamic_index_in_dim(cross_bias, chip, 2, keepdims=False)
     cross_bias = cross_bias.transpose(1, 2, 0, 3).reshape(1, D)
-    second_group = gather_plane(moves_two).reshape(D, 5 * D)
+    second_group = gather_plane([column_two, first_two, second_two, third_two], others)
+    second_group = second_group.reshape(D, 5 * D)
     whole = pl.BlockSpec((256, D), lambda j: (0, 0))
     thin = pl.BlockSpec((256, 1), lambda j: (0, 0))
     vectors = pl.BlockSpec((128, D), lambda j: (0, 0))
@@ -1315,13 +1361,24 @@
         in_specs=[whole, tall, strip],
         out_specs=[across, across],
     )
-    cross_up_mix, cross_down_part = place_cross(after(cross_column, moves_three[1], moves_three[2]))
-    down_weight = gather_down(moves_three).reshape(4 * D, D)
+    active_rows, first_three, second_three, column_three = stage(
+        active_rows, first_three, second_three, column_three
+    )
+
+    third_three = swap_two(first_three)
+    others = [swap_core(piece) for piece in (column_three, first_three, second_three)]
+    third_three, *others = stage(third_three, *others)
+
+    others.append(swap_core(third_three))
+    down_weight = gather_down([column_three, first_three, second_three, third_three], others)
+    down_weight = down_weight.reshape(4 * D, D)
+    cross_up_mix, cross_down_part = place_cross(after(cross_column, down_weight))
     normed_two, scale_two, kept, given = on_core(
         local_down_part,
         [shape_of(256, D), shape_of(256, 1), shape_of(8, D), shape_of(8, D)],
         (active_rows, down_weight, normed_one, rows, flat_cot, flat_cot, segment_positions),
         2 * 256 * D * 4 * D,
+        room=40,
         grid=(4,),
         in_specs=[
             across,
@@ -1342,12 +1399,13 @@
     row8, mix_share = (8, D), (D, D + 640)
     out_share = pl.BlockSpec((D, D), lambda j: (0, 4))
     up_share = pl.BlockSpec((D, D), lambda j: (0, 0))
-    pair = on_core(join_pair, shape_of(8, D), (kept, swap_core(given)), 0)
+    pair = on_core(join_pair, shape_of(8, D), (kept, swap_core(given)), 0, room=12)
     row_in, row_grad, mixed, probs, context = on_core(
         cross_attend,
         [shape_of(8, D), shape_of(8, D), half(8, 576), shape_of(3, 8, 8), half(8, 192)],
         (*plane_three(pair), cross_up_mix, rows, segment_docs, segment_column),
         0,
+        room=12,
     )
     row_n, row_scale, row_low, hidden, active, part = on_core(
         cross_up_down,
@@ -1369,6 +1427,7 @@
         + [up_share]
         + plain((1, D), (D, D)),
         out_specs=plain(row8, (8, 1), row8, row8, row8, row8),
+        room=12,
     )
     row_out, row_second, hidden_low, part, sums = on_core(
         cross_turn,
@@ -1378,6 +1437,7 @@
         grid=(1,),
         in_specs=plain(*[row8] * 4, row8, (128, D), row8, row8) + [up_share] + plain((D, D)),
         out_specs=plain(*[row8] * 5),
+        room=12,
     )
     row_total, part, packed = on_core(
         cross_attend_back,
@@ -1408,6 +1468,7 @@
         + [pl.BlockSpec(memory_space=pltpu.SMEM)],
         out_specs=plain(row8, row8, (48, D)),
         scratch=[pltpu.VMEM((48, D), jnp.float32), pltpu.VMEM((8, D), jnp.float32)],
+        room=12,
     )
     everyone = lax.all_gather(packed, ("dp", "seq"))
     kept, given = on_core(
@@ -1416,6 +1477,7 @@
         (*plane_three(part), row_total, row_out),
         0,
         scratch=[pltpu.VMEM((8, D), jnp.float32)],
+        room=12,
     )
     got = swap_core(given)
 
@@ -1438,7 +1500,10 @@
         out_specs=[whole, whole, fours, fours, across, eight, strip],
         scratch=[pltpu.VMEM((256, D), jnp.bfloat16)],
     )
-    down_total = Sum(down_kept.reshape(4, 4, 96, D), down_gone.reshape(4, 4, 96, D))
+    down_total = Sum(down_kept.reshape(4, 4, 96, D))
+    hidden_grads, down_gone = stage(hidden_grads, down_gone.reshape(4, 4, 96, D))
+
+    down_got = swap_core(down_gone)
     sixteens = pl.BlockSpec((16, 24, D), lambda j: (0, 0, j))
     up_kept, up_gone, first_rows = on_core(
         local_up_back,
@@ -1449,14 +1514,20 @@
         in_specs=[whole, across, tall, whole],
         out_specs=[sixteens, sixteens, whole],
     )
-    up_total = Sum(up_kept.reshape(4, 4, 24, 4 * D), up_gone.reshape(4, 4, 24, 4 * D))
-    down_sent = down_total.first(first_rows)
+    up_total = Sum(up_kept.reshape(4, 4, 24, 4 * D))
+    down_got, first_rows, up_gone = stage(down_got, first_rows, up_gone.reshape(4, 4, 24, 4 * D))
+
+    up_got = swap_core(up_gone)
+    down_sent = down_total.first(down_got)
+    up_got, down_sent, first_rows = stage(up_got, down_sent, first_rows)
+
+    down_back = swap_one(down_sent)
     flat = pl.BlockSpec((256, 3 * D), lambda j: (0, 0))
     out_grad, sum_rows, sums_one, back_rows = on_core(
         local_attend_back,
         [shape_of(D, D), shape_of(256, D), shape_of(8, D), half(256, 3 * D)],
         (
-            after(first_rows, down_sent, up_total.got),
+            first_rows,
             normed_one,
             scale_one,
             rows,
@@ -1480,8 +1551,11 @@
         out_specs=[pl.BlockSpec((D, D), lambda j: (0, 0)), whole, eight, flat],
         scratch=[pltpu.VMEM((256, D), jnp.bfloat16)],
     )
-    up_sent = up_total.first(back_rows)
-    down_onward = down_total.second(up_sent)
+    up_sent = up_total.first(up_got)
+    down_back, back_rows, up_sent = stage(down_back, back_rows, up_sent)
+
+    up_back = swap_one(up_sent)
+    down_onward = down_total.second(down_back)
     bias_rows = bias_grad.reshape(32, 4, 24).transpose(1, 0, 2).reshape(4, D)
     sides = [half(16, 24, 4 * D + 128)] * 2
     input_grad, mix_kept, mix_gone = on_core(
@@ -1489,7 +1563,7 @@
         [shape_of(256, D)] + sides,
         (
             sum_rows,
-            after(back_rows, down_onward),
+            back_rows,
             flat_tokens,
             first_group,
             out_grad,
@@ -1500,12 +1574,30 @@
         4 * 256 * D * 3 * D,
         scratch=[pltpu.VMEM((128, D), jnp.float32)],
     )
-    mix_total = Sum(mix_kept.reshape(4, 4, 24, 3200), mix_gone.reshape(4, 4, 24, 3200))
-    up_onward = up_total.second(input_grad)
-    down_own = down_total.third(up_onward)
-    mix_sent = mix_total.first(down_own)
-    up_own = up_total.third(mix_sent)
-    mix_onward = mix_total.second(up_own)
+    mix_total = Sum(mix_kept.reshape(4, 4, 24, 3200))
+    up_back, down_onward, mix_gone = stage(up_back, down_onward, mix_gone.reshape(4, 4, 24, 3200))
+
+    mix_got, down_last = swap_core(mix_gone), swap_two(down_onward)
+    up_onward = up_total.second(up_back)
+    mix_got, down_last, up_onward = stage(mix_got, down_last, up_onward)
+
+    up_last = swap_two(up_onward)
+    mix_sent = mix_total.first(mix_got)
+    down_others = down_total.third(down_last)
+    up_last, mix_sent, *down_others = stage(up_last, mix_sent, *down_others)
+
+    mix_back, down_others = swap_one(mix_sent), send_dp(down_others)
+    up_others = up_total.third(up_last)
+    mix_back, *others = stage(mix_back, *down_others, *up_others)
+    down_others, up_others = others[:3], others[3:]
+
+    up_others = send_dp(up_others)
+    mix_last = swap_two(mix_total.second(mix_back))
+    down_sum = down_total.total(down_others)
+    mix_last, down_sum, *up_others = stage(mix_last, down_sum, *up_others)
+
+    mix_others = send_dp(mix_total.third(mix_last))
+    up_sum = up_total.total(up_others)
     cross_grads = on_core(
         cross_owner,
         [
@@ -1517,7 +1609,7 @@
             shape_of(1, 96),
             shape_of(64, 24),
         ],
-        (after(everyone, mix_onward), cross_mix),
+        (after(everyone, mix_last), cross_mix),
         0,
         scratch=[
             pltpu.VMEM((4, 64, D), jnp.float32),
@@ -1528,8 +1620,7 @@
             pltpu.VMEM((64, 128), jnp.float32),
         ],
     )
-    mix_total.third()
-    down_sum, up_sum, mix_sum = down_total.total(), up_total.total(), mix_total.total()
+    mix_sum = mix_total.total(mix_others)
     return (
         layer_output.reshape(2, SEG, D),
         input_grad.reshape(2, SEG, D),

time: 386 us -> 343 us (0.89)
  waiting for transfers between devices: 139 us -> 98.6 us
  local copies, waits for them, and re-layouts: 46.3 us -> 27.7 us
  Pallas kernels: 102 us -> 117 us
  other arithmetic: 2.31 us -> 6.45 us
    ppermute x6, waiting for transfers between devices: 68.1 us -> 5.4 us  [swap_one(): lax.ppermute(array_in, 'seq', [(i, i ^ (2 if i % 2 == 0 else 4)) for i in...]
    unnamed x115 -> x64, local copies, waits for them, and re-layouts: 38.1 us -> 20.2 us
    ppermute x12 -> x18, waiting for transfers between devices: 18.9 us -> 30.8 us  [swap_dp(): lax.ppermute(array_in, 'dp', [(i, (i + shift) % 4) for i in range(4)])]
    pallas_call x9, Pallas kernels: 13 us -> 23.4 us  [run(): pl.pallas_call(kernel, out_shape=out_shapes, in_specs=[far] * count, out_...]
    pallas_call x6 -> x8, Pallas kernels: 13.3 us -> 21.6 us  [copies(): pl.pallas_call(kernel, out_shape=[jax.ShapeDtypeStruct(shape, pieces[0].d...]
    ppermute x12 -> x18, starting transfers between devices: 36.5 us -> 31.5 us  [swap_dp(): lax.ppermute(array_in, 'dp', [(i, (i + shift) % 4) for i in range(4)])]
    pallas_call x15, Pallas kernels: 76 us -> 71.8 us  [on_core(): pl.pallas_call(kernel, out_shape=out_shape, grid=grid, scratch_shapes=scr...]
    ppermute x18, waiting for transfers between devices: 2.41 us -> 6.35 us  [swap_core(): return lax.ppermute(array_in, 'seq', [(i, i ^ 1) for i in range(8)])]
  transfers between devices with their start and end apart: 66 -> 71, of which waited for: 32 -> 35; matrix products, arithmetic and copies ran while one was open for 2% -> 4% of each run, Pallas kernels for 19% -> 29%
where the time goes in v3:
time: 343 us; the launch traced here: 341 us
  Pallas kernels  117 us (34%)
  waiting for transfers between devices  98.6 us (29%)
  starting transfers between devices  76.8 us (22%)
  local copies, waits for them, and re-layouts  27.7 us (8%)
  between operations  14.6 us (4%)
  other arithmetic  6.45 us (2%)
    pallas_call x15, Pallas kernels, on_core(): pl.pallas_call(kernel, out_shape=out_shape, grid=grid, scratch_shapes=scr...  71.8 us
    ppermute x9, waiting for transfers between devices, swap_two(): lax.ppermute(array_in, 'seq', [(i, i ^ (4 if i % 2 == 0 else 2)) for i in...  35.1 us
    ppermute x18, starting transfers between devices, swap_dp(): lax.ppermute(array_in, 'dp', [(i, (i + shift) % 4) for i in range(4)])  31.5 us
    ppermute x18, waiting for transfers between devices, swap_dp(): lax.ppermute(array_in, 'dp', [(i, (i + shift) % 4) for i in range(4)])  30.8 us
    pallas_call x9, Pallas kernels, run(): pl.pallas_call(kernel, out_shape=out_shapes, in_specs=[far] * count, out_...  23.4 us
    ppermute x18, starting transfers between devices, swap_chip(): return lax.ppermute(array_in, 'seq', [(i, i ^ 2 * mask) for i in range(8)])  23 us
    pallas_call x8, Pallas kernels, copies(): pl.pallas_call(kernel, out_shape=[jax.ShapeDtypeStruct(shape, pieces[0].d...  21.6 us
    unnamed x64, local copies, waits for them, and re-layouts  20.2 us
  transfers between devices with their start and end apart: 71, of which 35 were waited for; matrix products, arithmetic and copies ran while one was open for 4% of the time, Pallas kernels for 29%

profile of v3, /device:TPU:0, one launch (start us, length us, event | category | flops | bytes accessed | tf_op | source)
XLA Modules:
  0.0 341.0 jit_solution(1170606114322736879)
XLA Ops:
  9.7 3.1 collective-permute-start
  23.8 3.1 collective-permute-done.5.refs_3_
  37.5 5.6 %collective-permute-done.6.refs_1_ = bf16[24,3840]{1,0:T(8,128)(2,1)S(1)} collective-permute-done((bf16[24,3840]{1,0:T(8,128)(2,1)}, bf16[24,3840]{1,0:T(8,128)(2,1)S(1)}, u32[]{:S(2)}, u32[]{:S(2)}) %collective-permute-start.6) | collective-permute-done | bytes 184352 | tf_op jit(solution)/shard_map/ppermute | solution.py:448
  43.1 4.0 %collective-permute-done.7.refs_2_ = bf16[24,3840]{1,0:T(8,128)(2,1)S(1)} collective-permute-done((bf16[24,3840]{1,0:T(8,128)(2,1)}, bf16[24,3840]{1,0:T(8,128)(2,1)S(1)}, u32[]{:S(2)}, u32[]{:S(2)}) %collective-permute-start.7) | collective-permute-done | bytes 184352 | tf_op jit(solution)/shard_map/ppermute | solution.py:448
  48.9 9.2 %collective-permute-done.11.refs_3_ = bf16[4,24,3200]{2,1,0:T(8,128)(2,1)} collective-permute-done((bf16[4,24,3200]{2,1,0:T(8,128)(2,1)S(1)}, bf16[4,24,3200]{2,1,0:T(8,128)(2,1)}, u32[]{:S(2)}, u32[]{:S(2)}) %collective-permute-start.11) | collective-permute-done | bytes 614432 | tf_op jit(solution)/shard_map/ppermute | solution.py:464
  63.4 4.4 %collective-permute-start.16 = (bf16[24,3072]{1,0:T(8,128)(2,1)}, bf16[24,3072]{1,0:T(8,128)(2,1)}, u32[]{:S(2)}, u32[]{:S(2)}) collective-permute-start(bf16[24,3072]{1,0:T(8,128)(2,1)} %get-tuple-element.221.refs_0_), channel_id=1, source_target_pairs={{0,8},{8,16},{16,24},{24,0},{1,9},{9,17},{17,25},{25,1},{2,10},{10... | collective-permute-start | bytes 442376 | tf_op jit(solution)/shard_map/ppermute | solution.py:448
  71.6 4.3 %shard_map.293 = bf16[4,4,2,24,3200]{4,3,2,1,0:T(8,128)(2,1)} custom-call(bf16[4,24,3200]{2,1,0:T(8,128)(2,1)} %shard_map.291.refs_0_, bf16[4,24,3200]{2,1,0:T(8,128)(2,1)} %copy-done.18, bf16[4,24,3200]{2,1,0:T(8,128)(2,1)} %copy-done.17, bf16[4,24,3200]{2,1,0:T(8,128)(2,1)} %collective-permute-done.11.refs_3_, bf16[4,24,3200]{2,1,0:T(8,128)(2,1)} %copy-done.20, ...), custom_call_target="tpu_custom_call" | custom-call | tf_op jit(solution)/shard_map/pallas_call | solution.py:510
  75.9 13.3 %shard_map.294 = (bf16[256,2304]{1,0:T(8,128)(2,1)}, bf16[256,768]{1,0:T(8,128)(2,1)}, f32[24,128,128]{2,1,0:T(8,128)}, f32[256,768]{1,0:T(8,128)}, f32[256,1]{1...) custom-call(bf16[256,768]{1,0:T(8,128)(2,1)} %bitcast.69, bf16[768,3200]{1,0:T(8,128)(2,1)} %bitcast.56, ...), custom_call_target="tpu_custom_call" | custom-call | tf_op jit(solution)/shard_map/pallas_call | solution.py:698
  93.2 7.8 %collective-permute-done.21.refs_3_ = bf16[4,24,3840]{2,1,0:T(8,128)(2,1)} collective-permute-done((bf16[4,24,3840]{2,1,0:T(8,128)(2,1)}, bf16[4,24,3840]{2,1,0:T(8,128)(2,1)}, u32[]{:S(2)}, u32[]{:S(2)}) %collective-permute-start.21) | collective-permute-done | bytes 737312 | tf_op jit(solution)/shard_map/ppermute | solution.py:464
  106.8 5.3 %shard_map.296 = bf16[4,4,2,24,3840]{4,3,2,1,0:T(8,128)(2,1)} custom-call(bf16[4,24,3840]{2,1,0:T(8,128)(2,1)} %shard_map.292.refs_0_, bf16[4,24,3840]{2,1,0:T(8,128)(2,1)} %collective-permute-done.19.refs_1_, bf16[4,24,3840]{2,1,0:T(8,128)(2,1)} %collective-permute-done.20.refs_2_, bf16[4,24,3840]{2,1,0:T(8,128)(2,1)} %collective-permute-done.21.refs_3_, ...), custom_call_target="tpu_custom_call" | custom-call | tf_op jit(solution)/shard_map/pallas_call | solution.py:510
  112.1 6.4 %shard_map.297 = (bf16[256,3072]{1,0:T(8,128)(2,1)}, bf16[256,3072]{1,0:T(8,128)(2,1)}) custom-call(bf16[256,768]{1,0:T(8,128)(2,1)} %get-tuple-element.217.low_ref, bf16[768,3840]{1,0:T(8,128)(2,1)} %bitcast.36, f32[1,3072]{1,0:T(1,128)} %reshape.124.bias_ref), custom_call_target="tpu_custom_call" | custom-call | tf_op jit(solution)/shard_map/pallas_call | solution.py:698
  119.9 8.8 %collective-permute-done.28.refs_3_ = bf16[4,24,3072]{2,1,0:T(8,128)(2,1)S(1)} collective-permute-done((bf16[4,24,3072]{2,1,0:T(8,128)(2,1)}, bf16[4,24,3072]{2,1,0:T(8,128)(2,1)S(1)}, u32[]{:S(2)}, u32[]{:S(2)}) %collective-permute-start.28) | collective-permute-done | bytes 589856 | tf_op jit(solution)/shard_map/ppermute | solution.py:464
  136.5 3.2 all-gather.5.cloned.1.call-done
  142.1 3.3 shard_map.299
  164.9 2.7 copy-done
  182.4 2.7 collective-permute-done.46.c_ref
  196.3 9.1 %shard_map.307 = (bf16[256,768]{1,0:T(8,128)(2,1)}, f32[256,768]{1,0:T(8,128)}, bf16[16,96,768]{2,1,0:T(8,128)(2,1)}, bf16[16,96,768]{2,1,0:T(8,128)(2,1)}, bf16...) custom-call(bf16[256,768]{1,0:T(8,128)(2,1)} %bitcast.50, f32[8,768]{1,0:T(8,128)} %copy-done.15, ...), custom_call_target="tpu_custom_call" | custom-call | tf_op jit(solution)/shard_map/pallas_call | solution.py:698
  205.6 7.7 %shard_map.308 = (bf16[16,24,3072]{2,1,0:T(8,128)(2,1)}, bf16[16,24,3072]{2,1,0:T(8,128)(2,1)}, f32[256,768]{1,0:T(8,128)}) custom-call(bf16[256,768]{1,0:T(8,128)(2,1)} %get-tuple-element.217.low_ref, bf16[256,3072]{1,0:T(8,128)(2,1)} %get-tuple-element.275.hidden_ref, bf16[768,3840]{1,0:T(8,128)(2,1)} %bitcast.37, f32[256,768]{1,0:T(8,128)} %get-tuple-element.276.second_ref), custom_call_target="tpu_custom_call" | custom-call | tf_op jit(solution)/shard_map/pallas_call | solution.py:698
  222.0 11.5 %shard_map.310 = (f32[768,768]{1,0:T(8,128)}, f32[256,768]{1,0:T(8,128)}, f32[8,768]{1,0:T(8,128)}, bf16[256,2304]{1,0:T(8,128)(2,1)}) custom-call(f32[256,768]{1,0:T(8,128)} %get-tuple-element.283.first_ref, f32[256,768]{1,0:T(8,128)} %get-tuple-element.241.first_ref.n_ref, f32[256,1]{1,0:T(8,128)} %get-tuple-element.284.scale_ref, ...), custom_call_target="tpu_custom_call" | custom-call | tf_op jit(solution)/shard_map/pallas_call | solution.py:698
  241.0 8.4 %shard_map.312 = (f32[256,768]{1,0:T(8,128)}, bf16[16,24,3200]{2,1,0:T(8,128)(2,1)}, bf16[16,24,3200]{2,1,0:T(8,128)(2,1)}) custom-call(f32[256,768]{1,0:T(8,128)} %get-tuple-element.288.total_ref, bf16[256,2304]{1,0:T(8,128)(2,1)} %get-tuple-element.293.back_ref, bf16[256,768]{1,0:T(8,128)(2,1)} %bitcast.70, bf16[768,3200]{1,0:T(8,128)(2,1)} %bitcast.58, ...), custom_call_target="tpu_custom_call" | custom-call | tf_op jit(solution)/shard_map/pallas_call | solution.py:698
  255.2 6.4 %collective-permute-done.56.refs_3_ = bf16[4,96,768]{2,1,0:T(8,128)(2,1)} collective-permute-done((bf16[4,96,768]{2,1,0:T(8,128)(2,1)}, bf16[4,96,768]{2,1,0:T(8,128)(2,1)}, u32[]{:S(2)}, u32[]{:S(2)}) %collective-permute-start.56) | collective-permute-done | bytes 589856 | tf_op jit(solution)/shard_map/ppermute | solution.py:464
  263.6 2.7 shard_map.316
  266.3 2.7 shard_map.315
  269.0 2.8 collective-permute-done.57.refs_3_
  277.1 2.7 shard_map.317
  279.8 3.6 %collective-permute-done.59 = bf16[96,768]{1,0:T(8,128)(2,1)} collective-permute-done((bf16[96,768]{1,0:T(8,128)(2,1)}, bf16[96,768]{1,0:T(8,128)(2,1)}, u32[]{:S(2)}, u32[]{:S(2)}) %collective-permute-start.59) | collective-permute-done | bytes 147488 | tf_op jit(solution)/shard_map/ppermute | solution.py:448
  283.4 5.4 %collective-permute-done.60 = bf16[96,768]{1,0:T(8,128)(2,1)} collective-permute-done((bf16[96,768]{1,0:T(8,128)(2,1)}, bf16[96,768]{1,0:T(8,128)(2,1)}, u32[]{:S(2)}, u32[]{:S(2)}) %collective-permute-start.60) | collective-permute-done | bytes 147488 | tf_op jit(solution)/shard_map/ppermute | solution.py:448
  301.2 5.2 %collective-permute-done.63 = bf16[24,3072]{1,0:T(8,128)(2,1)} collective-permute-done((bf16[24,3072]{1,0:T(8,128)(2,1)}, bf16[24,3072]{1,0:T(8,128)(2,1)}, u32[]{:S(2)}, u32[]{:S(2)}) %collective-permute-start.63) | collective-permute-done | bytes 147488 | tf_op jit(solution)/shard_map/ppermute | solution.py:448
  306.4 5.7 %collective-permute-done.64 = bf16[24,3072]{1,0:T(8,128)(2,1)} collective-permute-done((bf16[24,3072]{1,0:T(8,128)(2,1)}, bf16[24,3072]{1,0:T(8,128)(2,1)}, u32[]{:S(2)}, u32[]{:S(2)}) %collective-permute-start.64) | collective-permute-done | bytes 147488 | tf_op jit(solution)/shard_map/ppermute | solution.py:448
  312.1 2.8 shard_map.319
  314.9 3.8 %collective-permute-start.66 = (bf16[24,3200]{1,0:T(8,128)(2,1)}, bf16[24,3200]{1,0:T(8,128)(2,1)}, u32[]{:S(2)}, u32[]{:S(2)}) collective-permute-start(bf16[24,3200]{1,0:T(8,128)(2,1)} %get-tuple-element.330), channel_id=1, source_target_pairs={{0,8},{8,16},{16,24},{24,0},{1,9},{9,17},{17,25},{25,1},{2,10},{10... | collective-permute-start | bytes 460808 | tf_op jit(solution)/shard_map/ppermute | solution.py:448
  323.0 4.4 %shard_map.320 = (f32[24,2304]{1,0:T(8,128)}, f32[24,768]{1,0:T(8,128)}, f32[24,3072]{1,0:T(8,128)}, f32[96,768]{1,0:T(8,128)}, f32[8,24]{1,0:T(8,128)}, /*index=5*/f32[1,96]{1,0:T(1,128)}, f32[64,24]{1,0:T(8,128)}) custom-call(bf16[32,48,768]{2,1,0:T(8,128)(2,1)} %bitcast.68, bf16[24,2304]{1,0:T(8,128)(2,1)} %weight_ref.1), custom_call_target="tpu_custom_call" | custom-call | tf_op jit(solution)/shard_map/pallas_call | solution.py:698
  (232 shorter events, 154.4 us)
Async XLA Ops:
  7.2 132.5 %all-gather.5.cloned.1.call-start = ((), (), s32[]{:S(2)}) async-start(), calls=%async_computation | async-start | bytes 2088960 | tf_op jit(solution)/shard_map/all_gather | solution.py:1338
  9.7 19.0 %collective-permute-start = (bf16[24,3200]{1,0:T(8,128)(2,1)}, bf16[24,3200]{1,0:T(8,128)(2,1)}, u32[]{:S(2)}, u32[]{:S(2)}) collective-permute-start(bf16[24,3200]{1,0:T(8,128)(2,1)} %get-tuple-element.187.refs_0_), channel_id=1, source_target_pairs={{0,8},{8,16},{16,24},{24,0},{1,9},{9,17},{17,25},{25,1},{2,10},{10... | collective-permute-start | bytes 460808 | tf_op jit(solution)/shard_map/ppermute | solution.py:448
  12.8 15.9 %collective-permute-start.1 = (bf16[24,3200]{1,0:T(8,128)(2,1)}, bf16[24,3200]{1,0:T(8,128)(2,1)}, u32[]{:S(2)}, u32[]{:S(2)}) collective-permute-start(bf16[24,3200]{1,0:T(8,128)(2,1)} %get-tuple-element.187.refs_0_), channel_id=1, source_target_pairs={{0,16},{8,24},{16,0},{24,8},{1,17},{9,25},{17,1},{25,9},{2,18},{10... | collective-permute-start | bytes 460808 | tf_op jit(solution)/shard_map/ppermute | solution.py:448
  15.4 13.4 %collective-permute-start.2 = (bf16[24,3200]{1,0:T(8,128)(2,1)}, bf16[24,3200]{1,0:T(8,128)(2,1)}, u32[]{:S(2)}, u32[]{:S(2)}) collective-permute-start(bf16[24,3200]{1,0:T(8,128)(2,1)} %get-tuple-element.187.refs_0_), channel_id=1, source_target_pairs={{0,24},{8,0},{16,8},{24,16},{1,25},{9,1},{17,9},{25,17},{2,26},{10... | collective-permute-start | bytes 460808 | tf_op jit(solution)/shard_map/ppermute | solution.py:448
  30.6 16.5 %collective-permute-start.10 = (bf16[4,24,3200]{2,1,0:T(8,128)(2,1)}, bf16[4,24,3200]{2,1,0:T(8,128)(2,1)S(1)}, u32[]{:S(2)}, u32[]{:S(2)}) collective-permute-start(bf16[4,24,3200]{2,1,0:T(8,128)(2,1)} %shard_map.291.refs_0_), channel_id=1, source_target_pairs={{0,4},{1,3},{2,6},{3,1},{4,0},{5,7},{6,2},{7,5},{8,12},{9,11},{10,... | collective-permute-start | bytes 1843208 | tf_op jit(solution)/shard_map/ppermute | solution.py:464
  32.2 14.9 %collective-permute-start.9 = (bf16[4,24,3200]{2,1,0:T(8,128)(2,1)}, bf16[4,24,3200]{2,1,0:T(8,128)(2,1)S(1)}, u32[]{:S(2)}, u32[]{:S(2)}) collective-permute-start(bf16[4,24,3200]{2,1,0:T(8,128)(2,1)} %shard_map.291.refs_0_), channel_id=1, source_target_pairs={{0,2},{1,5},{2,0},{3,7},{4,6},{5,1},{6,4},{7,3},{8,10},{9,13},{10,... | collective-permute-start | bytes 1843208 | tf_op jit(solution)/shard_map/ppermute | solution.py:460
  34.5 12.6 %collective-permute-start.7 = (bf16[24,3840]{1,0:T(8,128)(2,1)}, bf16[24,3840]{1,0:T(8,128)(2,1)S(1)}, u32[]{:S(2)}, u32[]{:S(2)}) collective-permute-start(bf16[24,3840]{1,0:T(8,128)(2,1)} %get-tuple-element.201.refs_0_), channel_id=1, source_target_pairs={{0,16},{8,24},{16,0},{24,8},{1,17},{9,25},{17,1},{25,9},{2,18},{10... | collective-permute-start | bytes 552968 | tf_op jit(solution)/shard_map/ppermute | solution.py:448
  36.1 11.0 %collective-permute-start.8 = (bf16[24,3840]{1,0:T(8,128)(2,1)}, bf16[24,3840]{1,0:T(8,128)(2,1)S(1)}, u32[]{:S(2)}, u32[]{:S(2)}) collective-permute-start(bf16[24,3840]{1,0:T(8,128)(2,1)} %get-tuple-element.201.refs_0_), channel_id=1, source_target_pairs={{0,24},{8,0},{16,8},{24,16},{1,25},{9,1},{17,9},{25,17},{2,26},{10... | collective-permute-start | bytes 552968 | tf_op jit(solution)/shard_map/ppermute | solution.py:448
  47.8 10.3 %collective-permute-start.11 = (bf16[4,24,3200]{2,1,0:T(8,128)(2,1)S(1)}, bf16[4,24,3200]{2,1,0:T(8,128)(2,1)}, u32[]{:S(2)}, u32[]{:S(2)}) collective-permute-start(bf16[4,24,3200]{2,1,0:T(8,128)(2,1)S(1)} %collective-permute-done.9.refs_1_), channel_id=1, source_target_pairs={{0,4},{1,3},{2,6},{3,1},{4,0},{5,7},{6,2},{7,5},{8,12},{9,11},{10,... | collective-permute-start | bytes 1843208 | tf_op jit(solution)/shard_map/ppermute | solution.py:464
  62.4 26.8 %collective-permute-start.19 = (bf16[4,24,3840]{2,1,0:T(8,128)(2,1)}, bf16[4,24,3840]{2,1,0:T(8,128)(2,1)}, u32[]{:S(2)}, u32[]{:S(2)}) collective-permute-start(bf16[4,24,3840]{2,1,0:T(8,128)(2,1)} %shard_map.292.refs_0_), channel_id=1, source_target_pairs={{0,2},{1,5},{2,0},{3,7},{4,6},{5,1},{6,4},{7,3},{8,10},{9,13},{10,... | collective-permute-start | bytes 2211848 | tf_op jit(solution)/shard_map/ppermute | solution.py:460
  62.9 26.3 %collective-permute-start.20 = (bf16[4,24,3840]{2,1,0:T(8,128)(2,1)}, bf16[4,24,3840]{2,1,0:T(8,128)(2,1)}, u32[]{:S(2)}, u32[]{:S(2)}) collective-permute-start(bf16[4,24,3840]{2,1,0:T(8,128)(2,1)} %shard_map.292.refs_0_), channel_id=1, source_target_pairs={{0,4},{1,3},{2,6},{3,1},{4,0},{5,7},{6,2},{7,5},{8,12},{9,11},{10,... | collective-permute-start | bytes 2211848 | tf_op jit(solution)/shard_map/ppermute | solution.py:464
  63.4 25.8 %collective-permute-start.16 = (bf16[24,3072]{1,0:T(8,128)(2,1)}, bf16[24,3072]{1,0:T(8,128)(2,1)}, u32[]{:S(2)}, u32[]{:S(2)}) collective-permute-start(bf16[24,3072]{1,0:T(8,128)(2,1)} %get-tuple-element.221.refs_0_), channel_id=1, source_target_pairs={{0,8},{8,16},{16,24},{24,0},{1,9},{9,17},{17,25},{25,1},{2,10},{10... | collective-permute-start | bytes 442376 | tf_op jit(solution)/shard_map/ppermute | solution.py:448
  67.8 21.4 %collective-permute-start.17 = (bf16[24,3072]{1,0:T(8,128)(2,1)}, bf16[24,3072]{1,0:T(8,128)(2,1)}, u32[]{:S(2)}, u32[]{:S(2)}) collective-permute-start(bf16[24,3072]{1,0:T(8,128)(2,1)} %get-tuple-element.221.refs_0_), channel_id=1, source_target_pairs={{0,16},{8,24},{16,0},{24,8},{1,17},{9,25},{17,1},{25,9},{2,18},{10... | collective-permute-start | bytes 442376 | tf_op jit(solution)/shard_map/ppermute | solution.py:448
  70.0 19.2 %collective-permute-start.18 = (bf16[24,3072]{1,0:T(8,128)(2,1)}, bf16[24,3072]{1,0:T(8,128)(2,1)}, u32[]{:S(2)}, u32[]{:S(2)}) collective-permute-start(bf16[24,3072]{1,0:T(8,128)(2,1)} %get-tuple-element.221.refs_0_), channel_id=1, source_target_pairs={{0,24},{8,0},{16,8},{24,16},{1,25},{9,1},{17,9},{25,17},{2,26},{10... | collective-permute-start | bytes 442376 | tf_op jit(solution)/shard_map/ppermute | solution.py:448
  89.2 11.8 %collective-permute-start.21 = (bf16[4,24,3840]{2,1,0:T(8,128)(2,1)}, bf16[4,24,3840]{2,1,0:T(8,128)(2,1)}, u32[]{:S(2)}, u32[]{:S(2)}) collective-permute-start(bf16[4,24,3840]{2,1,0:T(8,128)(2,1)} %collective-permute-done.19.refs_1_), channel_id=1, source_target_pairs={{0,4},{1,3},{2,6},{3,1},{4,0},{5,7},{6,2},{7,5},{8,12},{9,11},{10,... | collective-permute-start | bytes 2211848 | tf_op jit(solution)/shard_map/ppermute | solution.py:464
  101.1 221.9 %all-gather.7.cloned.1.call-start = ((), (), s32[]{:S(2)}) async-start(), calls=%async_computation.1 | async-start | bytes 2433024 | tf_op jit(solution)/shard_map/all_gather | solution.py:1473
  101.4 17.1 %collective-permute-start.26 = (bf16[4,24,3072]{2,1,0:T(8,128)(2,1)}, bf16[4,24,3072]{2,1,0:T(8,128)(2,1)}, u32[]{:S(2)}, u32[]{:S(2)}) collective-permute-start(bf16[4,24,3072]{2,1,0:T(8,128)(2,1)} %shard_map.295.refs_0_), channel_id=1, source_target_pairs={{0,2},{1,5},{2,0},{3,7},{4,6},{5,1},{6,4},{7,3},{8,10},{9,13},{10,... | collective-permute-start | bytes 1769480 | tf_op jit(solution)/shard_map/ppermute | solution.py:460
  103.0 15.6 %collective-permute-start.27 = (bf16[4,24,3072]{2,1,0:T(8,128)(2,1)}, bf16[4,24,3072]{2,1,0:T(8,128)(2,1)}, u32[]{:S(2)}, u32[]{:S(2)}) collective-permute-start(bf16[4,24,3072]{2,1,0:T(8,128)(2,1)} %shard_map.295.refs_0_), channel_id=1, source_target_pairs={{0,4},{1,3},{2,6},{3,1},{4,0},{5,7},{6,2},{7,5},{8,12},{9,11},{10,... | collective-permute-start | bytes 1769480 | tf_op jit(solution)/shard_map/ppermute | solution.py:464
  139.7 11.8 %collective-permute-start.37 = (bf16[4,4,24,2176]{3,2,1,0:T(8,128)(2,1)}, bf16[4,4,24,2176]{3,2,1,0:T(8,128)(2,1)}, u32[]{:S(2)}, u32[]{:S(2)}) collective-permute-start(bf16[4,4,24,2176]{3,2,1,0:T(8,128)(2,1)} %bitcast.53), channel_id=1, source_target_pairs={{0,1},{1,0},{2,3},{3,2},{4,5},{5,4},{6,7},{7,6},{8,9},{9,8},{10,11... | collective-permute-start | bytes 5013512 | tf_op jit(solution)/shard_map/ppermute | solution.py:452
  218.3 16.5 %collective-permute-start.53 = (bf16[2,4,96,768]{3,2,1,0:T(8,128)(2,1)}, bf16[2,4,96,768]{3,2,1,0:T(8,128)(2,1)}, u32[]{:S(2)}, u32[]{:S(2)}) collective-permute-start(bf16[2,4,96,768]{3,2,1,0:T(8,128)(2,1)} %shard_map.309), channel_id=1, source_target_pairs={{0,2},{1,5},{2,0},{3,7},{4,6},{5,1},{6,4},{7,3},{8,10},{9,13},{10,... | collective-permute-start | bytes 3538952 | tf_op jit(solution)/shard_map/ppermute | solution.py:460
  234.8 16.5 %collective-permute-start.54 = (bf16[2,4,24,3072]{3,2,1,0:T(8,128)(2,1)}, bf16[2,4,24,3072]{3,2,1,0:T(8,128)(2,1)}, u32[]{:S(2)}, u32[]{:S(2)}) collective-permute-start(bf16[2,4,24,3072]{3,2,1,0:T(8,128)(2,1)} %shard_map.311), channel_id=1, source_target_pairs={{0,2},{1,5},{2,0},{3,7},{4,6},{5,1},{6,4},{7,3},{8,10},{9,13},{10,... | collective-permute-start | bytes 3538952 | tf_op jit(solution)/shard_map/ppermute | solution.py:460
  251.3 10.3 %collective-permute-start.55 = (bf16[4,4,24,3200]{3,2,1,0:T(8,128)(2,1)}, bf16[4,4,24,3200]{3,2,1,0:T(8,128)(2,1)}, u32[]{:S(2)}, u32[]{:S(2)}) collective-permute-start(bf16[4,4,24,3200]{3,2,1,0:T(8,128)(2,1)} %bitcast.80), channel_id=1, source_target_pairs={{0,1},{1,0},{2,3},{3,2},{4,5},{5,4},{6,7},{7,6},{8,9},{9,8},{10,11... | collective-permute-start | bytes 7372808 | tf_op jit(solution)/shard_map/ppermute | solution.py:452
  251.3 10.3 %collective-permute-start.56 = (bf16[4,96,768]{2,1,0:T(8,128)(2,1)}, bf16[4,96,768]{2,1,0:T(8,128)(2,1)}, u32[]{:S(2)}, u32[]{:S(2)}) collective-permute-start(bf16[4,96,768]{2,1,0:T(8,128)(2,1)} %shard_map.313), channel_id=1, source_target_pairs={{0,4},{1,3},{2,6},{3,1},{4,0},{5,7},{6,2},{7,5},{8,12},{9,11},{10,... | collective-permute-start | bytes 1769480 | tf_op jit(solution)/shard_map/ppermute | solution.py:464
  271.8 19.2 %collective-permute-start.58 = (bf16[2,4,24,3200]{3,2,1,0:T(8,128)(2,1)}, bf16[2,4,24,3200]{3,2,1,0:T(8,128)(2,1)}, u32[]{:S(2)}, u32[]{:S(2)}) collective-permute-start(bf16[2,4,24,3200]{3,2,1,0:T(8,128)(2,1)} %shard_map.315), channel_id=1, source_target_pairs={{0,2},{1,5},{2,0},{3,7},{4,6},{5,1},{6,4},{7,3},{8,10},{9,13},{10,... | collective-permute-start | bytes 3686408 | tf_op jit(solution)/shard_map/ppermute | solution.py:460
  273.3 15.5 %collective-permute-start.60 = (bf16[96,768]{1,0:T(8,128)(2,1)}, bf16[96,768]{1,0:T(8,128)(2,1)}, u32[]{:S(2)}, u32[]{:S(2)}) collective-permute-start(bf16[96,768]{1,0:T(8,128)(2,1)} %get-tuple-element.314), channel_id=1, source_target_pairs={{0,16},{8,24},{16,0},{24,8},{1,17},{9,25},{17,1},{25,9},{2,18},{10... | collective-permute-start | bytes 442376 | tf_op jit(solution)/shard_map/ppermute | solution.py:448
  274.7 14.0 %collective-permute-start.61 = (bf16[96,768]{1,0:T(8,128)(2,1)}, bf16[96,768]{1,0:T(8,128)(2,1)}, u32[]{:S(2)}, u32[]{:S(2)}) collective-permute-start(bf16[96,768]{1,0:T(8,128)(2,1)} %get-tuple-element.315), channel_id=1, source_target_pairs={{0,24},{8,0},{16,8},{24,16},{1,25},{9,1},{17,9},{25,17},{2,26},{10... | collective-permute-start | bytes 442376 | tf_op jit(solution)/shard_map/ppermute | solution.py:448
  293.4 18.7 %collective-permute-start.62 = (bf16[4,24,3200]{2,1,0:T(8,128)(2,1)}, bf16[4,24,3200]{2,1,0:T(8,128)(2,1)}, u32[]{:S(2)}, u32[]{:S(2)}) collective-permute-start(bf16[4,24,3200]{2,1,0:T(8,128)(2,1)} %shard_map.318), channel_id=1, source_target_pairs={{0,4},{1,3},{2,6},{3,1},{4,0},{5,7},{6,2},{7,5},{8,12},{9,11},{10,... | collective-permute-start | bytes 1843208 | tf_op jit(solution)/shard_map/ppermute | solution.py:464
  295.4 11.0 %collective-permute-start.63 = (bf16[24,3072]{1,0:T(8,128)(2,1)}, bf16[24,3072]{1,0:T(8,128)(2,1)}, u32[]{:S(2)}, u32[]{:S(2)}) collective-permute-start(bf16[24,3072]{1,0:T(8,128)(2,1)} %get-tuple-element.325), channel_id=1, source_target_pairs={{0,8},{8,16},{16,24},{24,0},{1,9},{9,17},{17,25},{25,1},{2,10},{10... | collective-permute-start | bytes 442376 | tf_op jit(solution)/shard_map/ppermute | solution.py:448
  295.4 16.7 %collective-permute-start.64 = (bf16[24,3072]{1,0:T(8,128)(2,1)}, bf16[24,3072]{1,0:T(8,128)(2,1)}, u32[]{:S(2)}, u32[]{:S(2)}) collective-permute-start(bf16[24,3072]{1,0:T(8,128)(2,1)} %get-tuple-element.326), channel_id=1, source_target_pairs={{0,16},{8,24},{16,0},{24,8},{1,17},{9,25},{17,1},{25,9},{2,18},{10... | collective-permute-start | bytes 442376 | tf_op jit(solution)/shard_map/ppermute | solution.py:448
  296.7 15.4 %collective-permute-start.65 = (bf16[24,3072]{1,0:T(8,128)(2,1)}, bf16[24,3072]{1,0:T(8,128)(2,1)}, u32[]{:S(2)}, u32[]{:S(2)}) collective-permute-start(bf16[24,3072]{1,0:T(8,128)(2,1)} %get-tuple-element.327), channel_id=1, source_target_pairs={{0,24},{8,0},{16,8},{24,16},{1,25},{9,1},{17,9},{25,17},{2,26},{10... | collective-permute-start | bytes 442376 | tf_op jit(solution)/shard_map/ppermute | solution.py:448
  314.9 14.0 %collective-permute-start.66 = (bf16[24,3200]{1,0:T(8,128)(2,1)}, bf16[24,3200]{1,0:T(8,128)(2,1)}, u32[]{:S(2)}, u32[]{:S(2)}) collective-permute-start(bf16[24,3200]{1,0:T(8,128)(2,1)} %get-tuple-element.330), channel_id=1, source_target_pairs={{0,8},{8,16},{16,24},{24,0},{1,9},{9,17},{17,25},{25,1},{2,10},{10... | collective-permute-start | bytes 460808 | tf_op jit(solution)/shard_map/ppermute | solution.py:448
  318.7 11.5 %collective-permute-start.67 = (bf16[24,3200]{1,0:T(8,128)(2,1)}, bf16[24,3200]{1,0:T(8,128)(2,1)}, u32[]{:S(2)}, u32[]{:S(2)}) collective-permute-start(bf16[24,3200]{1,0:T(8,128)(2,1)} %get-tuple-element.331), channel_id=1, source_target_pairs={{0,16},{8,24},{16,0},{24,8},{1,17},{9,25},{17,1},{25,9},{2,18},{10... | collective-permute-start | bytes 460808 | tf_op jit(solution)/shard_map/ppermute | solution.py:448
  (69 other events, 472.3 us)
Sparse Core Ops, SparseCore 0:
  101.2 38.4 all-gather.4
  251.5 62.1 all-gather.6

commit v4 on v3

--- a/solution.py
+++ b/solution.py
@@ -539,6 +539,13 @@
     return (chip, near, far, chip ^ 3), (chip, far, near, chip ^ 3)
 
 
+def join_chips(pieces):
+    def moves(layer, chip, core):
+        return [(i, every, 0, spot) for i, spot in enumerate(plane_order(chip, core)[0])]
+
+    return copies(pieces, [(4,) + pieces[0].shape], moves)[0]
+
+
 def gather_plane(mine, others):
     def moves(layer, chip, core):
         own, other = plane_order(chip, core)
@@ -547,6 +554,20 @@
 
     shape = (4, 4, 2) + mine[0].shape[1:]
     return copies(mine + others, [shape], moves)[0]
+
+
+def gather_up(mine, others):
+    def moves(layer, chip, core):
+        own, other = plane_order(chip, core)
+        found = []
+        for i in range(8):
+            spot, side = (own[i], core) if i < 4 else (other[i - 4], 1 - core)
+            for out, lanes in enumerate((slice(0, 4 * D), slice(4 * D, 5 * D))):
+                found.append((i, (every, every, lanes), out, (every, spot, side)))
+        return found
+
+    up, out = copies(mine + others, [(4, 4, 2, 24, 4 * D), (4, 4, 2, 24, D)], moves)
+    return up.reshape(D, 4 * D), out.reshape(D, D)
 
 
 def gather_down(mine, others):
@@ -560,7 +581,7 @@
                 found.append((i, part, 0, (every, spot, side, quarter)))
         return found
 
-    return copies(mine + others, [(4, 4, 2, 4, 24, D)], moves, room=24)[0]
+    return copies(mine + others, [(4, 4, 2, 4, 24, D)], moves)[0]
 
 
 class Sum:
@@ -770,30 +791,49 @@
     return copies(pieces + [cross_down.reshape(4, 24, D)], [(4, 24, 2 * D + 640)], moves)[0]
 
 
-def place_cross(column):
-    other = swap_core(column)
-
+def place_cross(column, other):
     def moves(layer, chip, core):
         found = []
         for piece, side in ((0, core), (1, 1 - core)):
-            lead = (every, every, side, every)
-            source = (every, every, every)
-            found.append((piece, source + (slice(0, D),), 0, lead + (slice(0, D),)))
-            found.append(
-                (piece, source + (slice(2 * D, 2 * D + 640),), 0, lead + (slice(D, D + 640),))
-            )
-            found.append((piece, source + (slice(D, 2 * D),), 1, (every, side)))
+            source, lead = (every, every, every), (every, every, side)
+            found.append((piece, source + (slice(0, D),), 0, lead))
+            found.append((piece, source + (slice(2 * D, 2 * D + 640),), 1, lead))
+            found.append((piece, source + (slice(D, 2 * D),), 2, (every, side)))
         return found
 
-    up_mix, down = copies(
-        [column, other], [(4, 4, 2, 24, D + 640), (4, 2, 4, 24, D)], moves, room=24
-    )
-    return up_mix.reshape(D, D + 640), down.reshape(D, D)
-
-
-def local_attend(tokens_ref, group_ref, docs_ref, docs_column_ref, *outs):
-    mixed_ref, context_ref, probs_ref, n_ref, scale_ref, low_ref, rows_ref = outs
+    up, mix, down = copies(
+        [column, other], [(4, 4, 2, 24, D), (4, 4, 2, 24, 640), (4, 2, 4, 24, D)], moves
+    )
+    return up.reshape(D, D), mix.reshape(D, 640), down.reshape(D, D)
+
+
+def segment_heads(segment, mixed_ref, docs_ref, docs_column_ref, probs_ref, context_ref):
+    lane = lax.broadcasted_iota(jnp.int32, (SEG, 128), 1)
+    rows = slice(segment * SEG, (segment + 1) * SEG)
+    allowed = docs_column_ref[rows, :] == docs_ref[segment : segment + 1, :]
+    for pair in range(HEADS // 2):
+        query, key, value = (
+            mixed_ref[rows, third * D + pair * 128 : third * D + (pair + 1) * 128]
+            for third in range(3)
+        )
+        found = []
+        for side in range(2):
+            here = (lane < HEAD_DIM) if side == 0 else (lane >= HEAD_DIM)
+            scores = contract(key, jnp.where(here, query, jnp.zeros_like(query)), 1, 1)
+            scores = jnp.where(allowed, scores * HEAD_DIM ** (-0.5), masked_score)
+            powers = jnp.exp(scores - jnp.max(scores, axis=0, keepdims=True))
+            probs = powers / jnp.sum(powers, axis=0, keepdims=True)
+            probs_ref[2 * pair + side] = probs
+            found.append(contract(low(probs), value, 0, 0))
+        context = jnp.where(lane < HEAD_DIM, found[0], found[1])
+        context_ref[:, pair * 128 : (pair + 1) * 128] = low(context)
+
+
+def local_attend(tokens_ref, group_ref, docs_ref, docs_column_ref, places_ref, *outs):
+    mixed_ref, context_ref, probs_ref, rows_ref, places_out = outs
     rows_ref[...] = wide(group_ref[:, 4 * D : 4 * D + 128]).T
+    lane = lax.broadcasted_iota(jnp.int32, (2, 64), 1)
+    places_out[...] = contract_exact(wide(places_ref[...] == lane), rows_ref[16:80, :], 1, 0)
     tokens = tokens_ref[...]
     for third in range(3):
         columns = slice(third * D, (third + 1) * D)
@@ -801,27 +841,17 @@
         if third != 1:
             mixed = mixed + rows_ref[third // 2 : third // 2 + 1, :]
         mixed_ref[:, columns] = low(mixed)
-    lane = lax.broadcasted_iota(jnp.int32, (SEG, 128), 1)
-    for segment in range(2):
-        rows = slice(segment * SEG, (segment + 1) * SEG)
-        allowed = docs_column_ref[rows, :] == docs_ref[segment : segment + 1, :]
-        for pair in range(HEADS // 2):
-            query, key, value = (
-                mixed_ref[rows, third * D + pair * 128 : third * D + (pair + 1) * 128]
-                for third in range(3)
-            )
-            found = []
-            for side in range(2):
-                here = (lane < HEAD_DIM) if side == 0 else (lane >= HEAD_DIM)
-                scores = contract(jnp.where(here, query, jnp.zeros_like(query)), key, 1, 1)
-                scores = jnp.where(allowed, scores * HEAD_DIM ** (-0.5), masked_score)
-                powers = jnp.exp(scores - jnp.max(scores, axis=-1, keepdims=True))
-                probs = powers / jnp.sum(powers, axis=-1, keepdims=True)
-                probs_ref[segment * HEADS + 2 * pair + side] = probs
-                found.append(contract(low(probs), value, 1, 0))
-            context = jnp.where(lane < HEAD_DIM, found[0], found[1])
-            context_ref[rows, pair * 128 : (pair + 1) * 128] = low(context)
-    total = wide(tokens) + contract(context_ref[...], group_ref[:, 3 * D : 4 * D], 1, 0)
+    segment_heads(0, mixed_ref, docs_ref, docs_column_ref, probs_ref, context_ref)
+
+
+def local_attend_more(
+    tokens_ref, mixed_ref, before_ref, weight_ref, rows_ref, docs_ref, docs_column_ref, *outs
+):
+    context_ref, probs_ref, n_ref, scale_ref, low_ref, here = outs
+    segment_heads(1, mixed_ref, docs_ref, docs_column_ref, probs_ref, here)
+    context_ref[0:SEG, :] = before_ref[...]
+    context_ref[SEG : 2 * SEG, :] = here[...]
+    total = wide(tokens_ref[...]) + contract(context_ref[...], weight_ref[...], 1, 0)
     normed, scale = norm_parts(total + rows_ref[2:3, :])
     n_ref[...] = normed
     scale_ref[...] = scale
@@ -861,7 +891,7 @@
         heads, grads = [], []
         for place, cot in ((0, cot_a), (1, cot_b)):
             row = normed[place * SEG : place * SEG + 1] * rows_ref[6:7, :] + rows_ref[7:8, :]
-            heads.append(row + rows_ref[pl.ds(16 + places_ref[place, 0], 1), :])
+            heads.append(row + places_ref[place : place + 1, :])
             grads.append(wide(cot[...])[0:1])
         for ref, mine in ((kept_ref, core == 0), (given_ref, core == 1)):
             ref[...] = jnp.zeros_like(ref)
@@ -894,7 +924,7 @@
             found = jnp.where(chip == spot, row[:, 192 * spot : 192 * (spot + 1)], found)
         biases.append(found)
     bias = jnp.concatenate([biases[0], jnp.zeros_like(biases[0]), biases[1]], axis=1)
-    mixed = low(contract(low(in_ref[...]), weight_ref[:, D : D + 576], 1, 0) + bias)
+    mixed = low(contract(low(in_ref[...]), weight_ref[:, 0:576], 1, 0) + bias)
     mixed_ref[...] = mixed
     row_docs = jnp.where(core == 0, docs_ref[0:1, :], docs_ref[1:2, :])
     column_docs = jnp.where(core == 0, docs_column_ref[:, 0:1], docs_column_ref[:, 1:2])
@@ -1003,7 +1033,7 @@
         found[1].append(contract(score, query, 0, 0) * HEAD_DIM ** (-0.5))
         found[2].append(contract(low(probs), part, 0, 0))
     mixed_low = low(jnp.concatenate(found[0] + found[1] + found[2], axis=1))
-    part_ref[...] = contract(mixed_low, weight_ref[:, D : D + 576], 1, 1)
+    part_ref[...] = contract(mixed_low, weight_ref[:, 0:576], 1, 1)
     pack[...] = jnp.zeros_like(pack)
     pack[0:8, :] = wide(hidden_low_ref[...])
     pack[8:16, :] = wide(active_ref[...])
@@ -1021,7 +1051,8 @@
     rows[2:4, :] = sums_ref[0:2, :]
     pack[34:35, :] = rows[pl.ds(chip, 1), :]
     for place in range(2):
-        pack[35 + place : 36 + place, :] = jnp.full((1, D), wide(places_ref[place, 0]))
+        spot = wide(places_ref[place : place + 1, :])
+        pack[35 + place : 36 + place, :] = jnp.broadcast_to(spot, (1, D))
     pack_ref[...] = low(pack[...])
 
 
@@ -1034,7 +1065,7 @@
         ref[1:2, :] = out_ref[pl.ds(2 * chip + side, 1), :]
 
 
-def cross_owner(every_ref, weight_ref, *refs):
+def cross_owner(mine_ref, other_ref, weight_ref, *refs):
     mix_ref, out_ref, up_ref, down_ref, vectors_ref, bias_ref, table_ref = refs[:7]
     hidden, mixed, single, active, sums, places = refs[7:]
     layer, chip, core = place_in()
@@ -1045,7 +1076,9 @@
             group = 2 * level + side
             rows = slice(8 * group, 8 * group + 8)
             for spot in range(4):
-                value = wide(every_ref[8 * level + 2 * spot + side])
+                value = wide(
+                    jnp.where(core == side, mine_ref[level, spot], other_ref[level, spot])
+                )
                 hidden[spot, rows, :] = value[0:8]
                 mixed[spot, rows, :] = value[16:24]
                 for i in range(5):
@@ -1055,7 +1088,8 @@
                 for sequence in range(2):
                     row = 16 * level + 8 * sequence + 2 * spot + side
                     places[row : row + 1, :] = value[35 + sequence : 36 + sequence, 0:128]
-            active[rows, :] = wide(every_ref[8 * level + 2 * chip + side])[8:16]
+            value = jnp.where(core == side, mine_ref[level, chip], other_ref[level, chip])
+            active[rows, :] = wide(value)[8:16]
 
     def select(count, first):
         lane = lax.broadcasted_iota(jnp.int32, (count, D), 1)
@@ -1166,7 +1200,7 @@
 
 
 def local_attend_back(
-    first_ref, n_ref, scale_ref, rows_ref, context_ref, mixed_ref, probs_ref, group_ref, *outs
+    first_ref, n_ref, scale_ref, rows_ref, context_ref, mixed_ref, probs_a, probs_b, group_ref, *outs
 ):
     out_ref, total_ref, sums_ref, back_ref, context_low_ref = outs
     grad, normed = first_ref[...], n_ref[...]
@@ -1190,14 +1224,14 @@
             found = []
             for side in range(2):
                 here = (lane < HEAD_DIM) if side == 0 else (lane >= HEAD_DIM)
-                probs = probs_ref[segment * HEADS + 2 * pair + side]
-                prob_grad = contract(jnp.where(here, grad, jnp.zeros_like(grad)), value, 1, 1)
-                value_grad = contract(low(probs), grad, 0, 0)
+                probs = (probs_a, probs_b)[segment][2 * pair + side]
+                prob_grad = contract(value, jnp.where(here, grad, jnp.zeros_like(grad)), 1, 1)
+                value_grad = contract(low(probs), grad, 1, 0)
                 score = low(
-                    probs * (prob_grad - jnp.sum(probs * prob_grad, axis=-1, keepdims=True))
+                    probs * (prob_grad - jnp.sum(probs * prob_grad, axis=0, keepdims=True))
                 )
                 found.append(
-                    (contract(score, key, 1, 0), contract(score, query, 0, 0), value_grad)
+                    (contract(score, key, 0, 0), contract(score, query, 1, 0), value_grad)
                 )
             for third in range(3):
                 merged = jnp.where(lane < HEAD_DIM, found[0][third], found[1][third])
@@ -1229,6 +1263,18 @@
     small_ref[8:12, :] = bias_ref[...]
     columns = slice(4 * D, 4 * D + 128)
     split_cores(small_ref[...].T, kept_ref.at[:, :, columns], gone_ref.at[:, :, columns])
+
+
+def finish_mix(own_ref, a_ref, b_ref, c_ref, mix_ref, out_ref, vectors_ref, bias_ref, wide_ref):
+    total = own_ref[...] + wide(a_ref[...]) + wide(b_ref[...]) + wide(c_ref[...])
+    mix_ref[...] = total[:, 0 : 3 * D]
+    out_ref[...] = total[:, 3 * D : 4 * D]
+    wide_ref[...] = jnp.zeros_like(wide_ref)
+    wide_ref[0:24, :] = total[:, 4 * D : 4 * D + 128]
+    turned = wide_ref[...].T
+    vectors_ref[...] = turned[0:8, 0:24]
+    for row in range(4):
+        bias_ref[:, 24 * row : 24 * (row + 1)] = turned[8 + row : 9 + row, 0:24]
 
 
 def plane_three(array_in):
@@ -1294,56 +1340,72 @@
     )
     cross_sent = [cross_pieces[0]] + [swap_chip(cross_pieces[mask], mask) for mask in (1, 2, 3)]
     z_one = reach_dp(shard_one)
-    cross_row = join_cross(cross_sent, cross_down)
-    *z_one, cross_row, shard_two = stage(*z_one, cross_row, shard_two)
+    shard_two, docs_column, segment_column, *z_one = stage(
+        shard_two, docs_column, segment_column, *z_one, *cross_sent
+    )
+    z_one, cross_sent = z_one[:4], z_one[4:]
     column_one = join_dp(z_one)
     column_one, shard_two = stage(column_one, shard_two)
 
     first, second = swap_one(column_one), swap_two(column_one)
-    *z_two, first, second, column_one = stage(*reach_dp(shard_two), first, second, column_one)
+    cross_row = join_cross(cross_sent, after(cross_down, column_one))
+    *z_two, first, second, column_one, cross_row = stage(
+        *reach_dp(shard_two), first, second, column_one, cross_row
+    )
 
     third = swap_two(first)
     others = [swap_core(piece) for piece in (column_one, first, second)]
-    third, *z_two = stage(third, *others, *z_two)
-    others, z_two = z_two[:3], z_two[3:]
     column_two = join_dp(z_two)
+    cross_moved = [cross_row, swap_dp(cross_row, 1)]
+    third, column_two, cross_moved[1], *others = stage(third, column_two, cross_moved[1], *others)
     others.append(swap_core(third))
     column_two, shard_three, *others = stage(column_two, shard_three, *others)
 
     first_group = gather_plane([column_one, first, second, third], others).reshape(D, 3200)
-    mixed_rows, context_rows, probs_kept, normed_one, scale_one, low_one, rows = on_core(
+    mixed_rows, context_first, probs_first, rows, place_rows = on_core(
         local_attend,
-        [
-            half(256, 3 * D),
-            half(256, D),
-            shape_of(24, SEG, SEG),
-            shape_of(256, D),
-            shape_of(256, 1),
-            half(256, D),
-            shape_of(128, D),
-        ],
-        (flat_tokens, first_group, token_docs, docs_column),
-        2 * 256 * D * 5 * D,
+        [half(256, 3 * D), half(SEG, D), shape_of(12, SEG, SEG), shape_of(128, D), shape_of(2, D)],
+        (flat_tokens, first_group, token_docs, docs_column, segment_positions),
+        0,
     )
     first_two, second_two = swap_one(column_two), swap_two(column_two)
-    *z_three, low_one, first_two, second_two, column_two = stage(
-        *reach_dp(shard_three), low_one, first_two, second_two, column_two
-    )
+    *z_three, mixed_rows, first_two, second_two, column_two, cross_moved[1] = stage(
+        *reach_dp(shard_three), mixed_rows, first_two, second_two, column_two, cross_moved[1]
+    )
+    cross_moved.append(swap_dp(cross_moved[1], 1))
 
     third_two = swap_two(first_two)
     others = [swap_core(piece) for piece in (column_two, first_two, second_two)]
     column_three = join_dp(z_three)
-    third_two, column_three, cross_row, *others = stage(third_two, column_three, cross_row, *others)
-
-    cross_column = lax.all_gather(cross_row, "dp")
-    first_three, second_three = swap_one(column_three), swap_two(column_three)
-    others.append(swap_core(third_two))
+    def plain(*shapes):
+        return [pl.BlockSpec(shape, lambda j, n=len(shape): (0,) * n) for shape in shapes]
+
+    context_rows, probs_second, normed_one, scale_one, low_one = on_core(
+        local_attend_more,
+        [half(256, D), shape_of(12, SEG, SEG), shape_of(256, D), shape_of(256, 1), half(256, D)],
+        (flat_tokens, mixed_rows, context_first, first_group, rows, token_docs, docs_column),
+        0,
+        grid=(1,),
+        in_specs=plain((256, D), (256, 3 * D), (SEG, D))
+        + [pl.BlockSpec((D, D), lambda j: (0, 3))]
+        + plain((128, D), (2, SEG), (256, 1)),
+        out_specs=plain((256, D), (12, SEG, SEG), (256, D), (256, 1), (256, D)),
+        scratch=[pltpu.VMEM((SEG, D), jnp.bfloat16)],
+    )
     up_bias = rows[80:84].reshape(4, 32, 24).transpose(1, 0, 2).reshape(1, 4 * D)
     cross_bias = rows[84:88].reshape(4, 4, 4, 2, 24)
     cross_bias = lax.dynamic_index_in_dim(cross_bias, chip, 2, keepdims=False)
     cross_bias = cross_bias.transpose(1, 2, 0, 3).reshape(1, D)
-    second_group = gather_plane([column_two, first_two, second_two, third_two], others)
-    second_group = second_group.reshape(D, 5 * D)
+    cross_moved[2], third_two, column_three, low_one, up_bias, cross_bias, *others = stage(
+        cross_moved[2], third_two, column_three, low_one, up_bias, cross_bias, *others
+    )
+    cross_moved.append(swap_dp(cross_moved[2], 1))
+
+    first_three, second_three = swap_one(column_three), swap_two(column_three)
+    others.append(swap_core(third_two))
+    second_group, cross_out_weight = gather_up(
+        [column_two, first_two, second_two, third_two], others
+    )
     whole = pl.BlockSpec((256, D), lambda j: (0, 0))
     thin = pl.BlockSpec((256, 1), lambda j: (0, 0))
     vectors = pl.BlockSpec((128, D), lambda j: (0, 0))
@@ -1361,24 +1423,23 @@
         in_specs=[whole, tall, strip],
         out_specs=[across, across],
     )
-    active_rows, first_three, second_three, column_three = stage(
-        active_rows, first_three, second_three, column_three
+    active_rows, first_three, second_three, column_three, cross_moved[3] = stage(
+        active_rows, first_three, second_three, column_three, cross_moved[3]
     )
 
     third_three = swap_two(first_three)
     others = [swap_core(piece) for piece in (column_three, first_three, second_three)]
-    third_three, *others = stage(third_three, *others)
+    third_three, cross_column, *others = stage(third_three, join_dp(cross_moved), *others)
 
     others.append(swap_core(third_three))
     down_weight = gather_down([column_three, first_three, second_three, third_three], others)
-    down_weight = down_weight.reshape(4 * D, D)
-    cross_up_mix, cross_down_part = place_cross(after(cross_column, down_weight))
+    down_weight, cross_column = stage(down_weight.reshape(4 * D, D), cross_column)
+    cross_other = swap_core(cross_column)
     normed_two, scale_two, kept, given = on_core(
         local_down_part,
         [shape_of(256, D), shape_of(256, 1), shape_of(8, D), shape_of(8, D)],
-        (active_rows, down_weight, normed_one, rows, flat_cot, flat_cot, segment_positions),
+        (active_rows, down_weight, normed_one, rows, flat_cot, flat_cot, place_rows),
         2 * 256 * D * 4 * D,
-        room=40,
         grid=(4,),
         in_specs=[
             across,
@@ -1387,23 +1448,24 @@
             vectors,
             pl.BlockSpec((16, D), lambda j: (0, 0)),
             pl.BlockSpec((16, D), lambda j: (8, 0)),
-            pl.BlockSpec(memory_space=pltpu.SMEM),
+            pl.BlockSpec((2, D), lambda j: (0, 0)),
         ],
         out_specs=[whole, thin, eight, eight],
         scratch=[pltpu.VMEM((256, D), jnp.float32)],
     )
 
-    def plain(*shapes):
-        return [pl.BlockSpec(shape, lambda j, n=len(shape): (0,) * n) for shape in shapes]
-
-    row8, mix_share = (8, D), (D, D + 640)
-    out_share = pl.BlockSpec((D, D), lambda j: (0, 4))
+    row8, mix_share = (8, D), (D, 640)
+    out_share = pl.BlockSpec((D, D), lambda j: (0, 0))
     up_share = pl.BlockSpec((D, D), lambda j: (0, 0))
-    pair = on_core(join_pair, shape_of(8, D), (kept, swap_core(given)), 0, room=12)
+    given, kept, cross_other = stage(given, kept, cross_other)
+    got = swap_core(given)
+    cross_up_part, cross_mix_part, cross_down_part = place_cross(cross_column, cross_other)
+    kept, got, cross_mix_part = stage(kept, got, cross_mix_part)
+    pair = on_core(join_pair, shape_of(8, D), (kept, got), 0, room=12)
     row_in, row_grad, mixed, probs, context = on_core(
         cross_attend,
         [shape_of(8, D), shape_of(8, D), half(8, 576), shape_of(3, 8, 8), half(8, 192)],
-        (*plane_three(pair), cross_up_mix, rows, segment_docs, segment_column),
+        (*plane_three(pair), cross_mix_part, rows, segment_docs, segment_column),
         0,
         room=12,
     )
@@ -1413,9 +1475,9 @@
         (
             *plane_three(context),
             row_in,
-            second_group,
+            cross_out_weight,
             rows,
-            cross_up_mix,
+            cross_up_part,
             cross_bias,
             cross_down_part,
         ),
@@ -1432,7 +1494,7 @@
     row_out, row_second, hidden_low, part, sums = on_core(
         cross_turn,
         [shape_of(8, D), shape_of(8, D), half(8, D), shape_of(8, D), shape_of(8, D)],
-        (*plane_three(part), row_n, rows, row_grad, hidden, cross_up_mix, cross_down_part),
+        (*plane_three(part), row_n, rows, row_grad, hidden, cross_up_part, cross_down_part),
         0,
         grid=(1,),
         in_specs=plain(*[row8] * 4, row8, (128, D), row8, row8) + [up_share] + plain((D, D)),
@@ -1448,10 +1510,10 @@
             row_n,
             row_scale,
             rows,
-            second_group,
+            cross_out_weight,
             mixed,
             probs,
-            cross_up_mix,
+            cross_mix_part,
             hidden_low,
             active,
             context,
@@ -1464,13 +1526,11 @@
         grid=(1,),
         in_specs=plain(*[row8] * 4, row8, row8, (8, 1), (128, D))
         + [out_share]
-        + plain((8, 576), (3, 8, 8), mix_share, row8, row8, (8, 192), row8, row8, row8)
-        + [pl.BlockSpec(memory_space=pltpu.SMEM)],
+        + plain((8, 576), (3, 8, 8), mix_share, row8, row8, (8, 192), row8, row8, row8, (2, 1)),
         out_specs=plain(row8, row8, (48, D)),
         scratch=[pltpu.VMEM((48, D), jnp.float32), pltpu.VMEM((8, D), jnp.float32)],
         room=12,
     )
-    everyone = lax.all_gather(packed, ("dp", "seq"))
     kept, given = on_core(
         cross_finish,
         [shape_of(8, D), shape_of(8, D)],
@@ -1479,7 +1539,8 @@
         scratch=[pltpu.VMEM((8, D), jnp.float32)],
         room=12,
     )
-    got = swap_core(given)
+    got, kept, packed = stage(swap_core(given), kept, packed)
+    pack_one, pack_two = swap_one(packed), swap_two(packed)
 
     fours = pl.BlockSpec((4, 96, D), lambda j: (j, 0, 0))
     layer_output, second_rows, down_kept, down_gone, hidden_grads, sums_two, bias_grad = on_core(
@@ -1501,7 +1562,10 @@
         scratch=[pltpu.VMEM((256, D), jnp.bfloat16)],
     )
     down_total = Sum(down_kept.reshape(4, 4, 96, D))
-    hidden_grads, down_gone = stage(hidden_grads, down_gone.reshape(4, 4, 96, D))
+    hidden_grads, down_gone, pack_one, pack_two = stage(
+        hidden_grads, down_gone.reshape(4, 4, 96, D), pack_one, pack_two
+    )
+    pack_three = swap_two(pack_one)
 
     down_got = swap_core(down_gone)
     sixteens = pl.BlockSpec((16, 24, D), lambda j: (0, 0, j))
@@ -1515,12 +1579,14 @@
         out_specs=[sixteens, sixteens, whole],
     )
     up_total = Sum(up_kept.reshape(4, 4, 24, 4 * D))
-    down_got, first_rows, up_gone = stage(down_got, first_rows, up_gone.reshape(4, 4, 24, 4 * D))
+    down_got, first_rows, up_gone, pack_three = stage(
+        down_got, first_rows, up_gone.reshape(4, 4, 24, 4 * D), pack_three
+    )
+    plane_pack = join_chips([packed, pack_one, pack_two, pack_three])
+    packs = [plane_pack, swap_dp(plane_pack, 1), swap_dp(plane_pack, 3)]
 
     up_got = swap_core(up_gone)
     down_sent = down_total.first(down_got)
-    up_got, down_sent, first_rows = stage(up_got, down_sent, first_rows)
-
     down_back = swap_one(down_sent)
     flat = pl.BlockSpec((256, 3 * D), lambda j: (0, 0))
     out_grad, sum_rows, sums_one, back_rows = on_core(
@@ -1533,7 +1599,8 @@
             rows,
             context_rows,
             mixed_rows,
-            probs_kept,
+            probs_first,
+            probs_second,
             first_group,
         ),
         4 * 256 * D * 2 * D,
@@ -1545,14 +1612,16 @@
             vectors,
             whole,
             flat,
-            pl.BlockSpec((24, SEG, SEG), lambda j: (0, 0, 0)),
+            pl.BlockSpec((12, SEG, SEG), lambda j: (0, 0, 0)),
+            pl.BlockSpec((12, SEG, SEG), lambda j: (0, 0, 0)),
             pl.BlockSpec((D, D), lambda j: (0, 3)),
         ],
         out_specs=[pl.BlockSpec((D, D), lambda j: (0, 0)), whole, eight, flat],
         scratch=[pltpu.VMEM((256, D), jnp.bfloat16)],
     )
     up_sent = up_total.first(up_got)
-    down_back, back_rows, up_sent = stage(down_back, back_rows, up_sent)
+    down_back, back_rows, up_sent, *packs = stage(down_back, back_rows, up_sent, *packs)
+    packs.insert(2, swap_dp(packs[0], 2))
 
     up_back = swap_one(up_sent)
     down_onward = down_total.second(down_back)
@@ -1575,26 +1644,30 @@
         scratch=[pltpu.VMEM((128, D), jnp.float32)],
     )
     mix_total = Sum(mix_kept.reshape(4, 4, 24, 3200))
-    up_back, down_onward, mix_gone = stage(up_back, down_onward, mix_gone.reshape(4, 4, 24, 3200))
+    up_back, down_onward, mix_gone, packs[2] = stage(
+        up_back, down_onward, mix_gone.reshape(4, 4, 24, 3200), packs[2]
+    )
 
     mix_got, down_last = swap_core(mix_gone), swap_two(down_onward)
     up_onward = up_total.second(up_back)
-    mix_got, down_last, up_onward = stage(mix_got, down_last, up_onward)
+    my_rows = join_dp(packs)
+    mix_got, down_last, up_onward, my_rows = stage(mix_got, down_last, up_onward, my_rows)
 
     up_last = swap_two(up_onward)
     mix_sent = mix_total.first(mix_got)
     down_others = down_total.third(down_last)
-    up_last, mix_sent, *down_others = stage(up_last, mix_sent, *down_others)
+    up_last, mix_sent, my_rows, *down_others = stage(up_last, mix_sent, my_rows, *down_others)
+    other_rows = swap_core(my_rows)
 
     mix_back, down_others = swap_one(mix_sent), send_dp(down_others)
     up_others = up_total.third(up_last)
-    mix_back, *others = stage(mix_back, *down_others, *up_others)
+    mix_back, other_rows, *others = stage(mix_back, other_rows, *down_others, *up_others)
     down_others, up_others = others[:3], others[3:]
 
+    mix_last = swap_two(mix_total.second(mix_back))
     up_others = send_dp(up_others)
-    mix_last = swap_two(mix_total.second(mix_back))
     down_sum = down_total.total(down_others)
-    mix_last, down_sum, *up_others = stage(mix_last, down_sum, *up_others)
+    mix_last, down_sum, other_rows, *up_others = stage(mix_last, down_sum, other_rows, *up_others)
 
     mix_others = send_dp(mix_total.third(mix_last))
     up_sum = up_total.total(up_others)
@@ -1609,7 +1682,7 @@
             shape_of(1, 96),
             shape_of(64, 24),
         ],
-        (after(everyone, mix_last), cross_mix),
+        (my_rows, other_rows, cross_mix),
         0,
         scratch=[
             pltpu.VMEM((4, 64, D), jnp.float32),
@@ -1620,16 +1693,23 @@
             pltpu.VMEM((64, 128), jnp.float32),
         ],
     )
-    mix_sum = mix_total.total(mix_others)
+    mix_sum, out_sum, vectors_sum, bias_sum = on_core(
+        finish_mix,
+        [shape_of(24, 3 * D), shape_of(24, D), shape_of(8, 24), shape_of(1, 96)],
+        (mix_total.own, *mix_others),
+        0,
+        room=12,
+        scratch=[pltpu.VMEM((128, 128), jnp.float32)],
+    )
     return (
         layer_output.reshape(2, SEG, D),
         input_grad.reshape(2, SEG, D),
-        mix_sum[:, :2304],
-        mix_sum[:, 2304:3072],
+        mix_sum,
+        out_sum,
         up_sum,
         down_sum,
-        mix_sum[:, 3072:3080].T,
-        mix_sum[:, 3080:3084].T.reshape(96),
+        vectors_sum,
+        bias_sum.reshape(96),
         *cross_grads[:5],
         cross_grads[5].reshape(96),
         cross_grads[6],

time: 343 us -> 328 us (0.956)
  waiting for transfers between devices: 98.6 us -> 83.2 us
  Pallas kernels: 117 us -> 132 us
  between operations: 14.6 us -> 1.19 us
  local copies, waits for them, and re-layouts: 27.7 us -> 19.7 us
  starting transfers between devices: 76.8 us -> 83.8 us
    ppermute x9 -> x11, waiting for transfers between devices: 35.1 us -> 15.7 us  [swap_two(): lax.ppermute(array_in, 'seq', [(i, i ^ (4 if i % 2 == 0 else 2)) for i in...]
    pallas_call x8 -> x11, Pallas kernels: 21.6 us -> 31.2 us  [copies(): pl.pallas_call(kernel, out_shape=[jax.ShapeDtypeStruct(shape, pieces[0].d...]
    ppermute x18 -> x24, starting transfers between devices: 31.5 us -> 41 us  [swap_dp(): lax.ppermute(array_in, 'dp', [(i, (i + shift) % 4) for i in range(4)])]
    ppermute x18 -> x24, waiting for transfers between devices: 30.8 us -> 37 us  [swap_dp(): lax.ppermute(array_in, 'dp', [(i, (i + shift) % 4) for i in range(4)])]
    pallas_call x15 -> x17, Pallas kernels: 71.8 us -> 77.8 us  [on_core(): pl.pallas_call(kernel, out_shape=out_shape, grid=grid, scratch_shapes=scr...]
    unnamed x64 -> x39, local copies, waits for them, and re-layouts: 20.2 us -> 14.4 us
    ppermute x9 -> x11, starting transfers between devices: 11.9 us -> 10.6 us  [swap_two(): lax.ppermute(array_in, 'seq', [(i, i ^ (4 if i % 2 == 0 else 2)) for i in...]
    ppermute x6 -> x7, starting transfers between devices: 7.17 us -> 6.52 us  [swap_one(): lax.ppermute(array_in, 'seq', [(i, i ^ (2 if i % 2 == 0 else 4)) for i in...]
  transfers between devices with their start and end apart: 71 -> 79, of which waited for: 35 -> 35; matrix products, arithmetic and copies ran while one was open for 4% -> 4% of each run, Pallas kernels for 29% -> 34%
where the time goes in v4:
time: 328 us; the launch traced here: 326 us
  Pallas kernels  132 us (40%)
  starting transfers between devices  83.8 us (26%)
  waiting for transfers between devices  83.2 us (25%)
  local copies, waits for them, and re-layouts  19.7 us (6%)
  other arithmetic  5.23 us (2%)
    pallas_call x17, Pallas kernels, on_core(): pl.pallas_call(kernel, out_shape=out_shape, grid=grid, scratch_shapes=scr...  77.8 us
    ppermute x24, starting transfers between devices, swap_dp(): lax.ppermute(array_in, 'dp', [(i, (i + shift) % 4) for i in range(4)])  41 us
    ppermute x24, waiting for transfers between devices, swap_dp(): lax.ppermute(array_in, 'dp', [(i, (i + shift) % 4) for i in range(4)])  37 us
    pallas_call x11, Pallas kernels, copies(): pl.pallas_call(kernel, out_shape=[jax.ShapeDtypeStruct(shape, pieces[0].d...  31.2 us
    pallas_call x9, Pallas kernels, run(): pl.pallas_call(kernel, out_shape=out_shapes, in_specs=[far] * count, out_...  23.4 us
    ppermute x18, starting transfers between devices, swap_chip(): return lax.ppermute(array_in, 'seq', [(i, i ^ 2 * mask) for i in range(8)])  23.1 us
    ppermute x18, waiting for transfers between devices, swap_chip(): return lax.ppermute(array_in, 'seq', [(i, i ^ 2 * mask) for i in range(8)])  20.2 us
    ppermute x11, waiting for transfers between devices, swap_two(): lax.ppermute(array_in, 'seq', [(i, i ^ (4 if i % 2 == 0 else 2)) for i in...  15.7 us
  transfers between devices with their start and end apart: 79, of which 35 were waited for; matrix products, arithmetic and copies ran while one was open for 4% of the time, Pallas kernels for 34%

profile of v4, /device:TPU:0, one launch (start us, length us, event | category | flops | bytes accessed | tf_op | source)
XLA Modules:
  0.0 325.5 jit_solution(13612364124391753283)
XLA Ops:
  3.1 3.1 collective-permute-start
  25.2 2.7 collective-permute-start.6
  32.1 2.8 collective-permute-done.6.refs_1_
  34.9 5.7 %collective-permute-done.7.refs_2_ = bf16[24,3840]{1,0:T(8,128)(2,1)} collective-permute-done((bf16[24,3840]{1,0:T(8,128)(2,1)}, bf16[24,3840]{1,0:T(8,128)(2,1)}, u32[]{:S(2)}, u32[]{:S(2)}) %collective-permute-start.7) | collective-permute-done | bytes 184352 | tf_op jit(solution)/shard_map/ppermute | solution.py:448
  41.7 4.4 %collective-permute-start.12 = (bf16[4,24,2176]{2,1,0:T(8,128)(2,1)}, bf16[4,24,2176]{2,1,0:T(8,128)(2,1)}, u32[]{:S(2)}, u32[]{:S(2)}) collective-permute-start(bf16[4,24,2176]{2,1,0:T(8,128)(2,1)} %shard_map.291.refs_0_), channel_id=1, source_target_pairs={{0,8},{8,16},{16,24},{24,0},{1,9},{9,17},{17,25},{25,1},{2,10},{10... | collective-permute-start | bytes 1253384 | tf_op jit(solution)/shard_map/ppermute | solution.py:448
  48.0 10.4 %collective-permute-done.12.refs_1_ = bf16[4,24,2176]{2,1,0:T(8,128)(2,1)} collective-permute-done((bf16[4,24,2176]{2,1,0:T(8,128)(2,1)}, bf16[4,24,2176]{2,1,0:T(8,128)(2,1)}, u32[]{:S(2)}, u32[]{:S(2)}) %collective-permute-start.12) | collective-permute-done | bytes 417824 | tf_op jit(solution)/shard_map/ppermute | solution.py:448
  69.5 4.3 %shard_map.293 = bf16[4,4,2,24,3200]{4,3,2,1,0:T(8,128)(2,1)} custom-call(bf16[4,24,3200]{2,1,0:T(8,128)(2,1)} %shard_map.290.refs_0_, bf16[4,24,3200]{2,1,0:T(8,128)(2,1)} %collective-permute-done.9.refs_1_, bf16[4,24,3200]{2,1,0:T(8,128)(2,1)} %collective-permute-done.10.refs_2_, bf16[4,24,3200]{2,1,0:T(8,128)(2,1)} %collective-permute-done.11.refs_3_, ...), custom_call_target="tpu_custom_call" | custom-call | tf_op jit(solution)/shard_map/pallas_call | solution.py:510
  73.9 7.7 %shard_map.294 = (bf16[256,2304]{1,0:T(8,128)(2,1)}, bf16[128,768]{1,0:T(8,128)(2,1)}, f32[12,128,128]{2,1,0:T(8,128)}, f32[128,768]{1,0:T(8,128)}, f32[2,768]{1,0:T(2,128)}) custom-call(bf16[256,768]{1,0:T(8,128)(2,1)} %bitcast.62, bf16[768,3200]{1,0:T(8,128)(2,1)} %bitcast.42, s32[2,128]{1,0:T(2,128)} %docs_ref.4, s32[256,1]{1,0:T(8,128)} %copy.41.docs_column_ref, ...), custom_call_target="tpu_custom_call" | custom-call | tf_op jit(solution)/shard_map/pallas_call | solution.py:719
  85.8 6.9 %shard_map.296 = (bf16[256,768]{1,0:T(8,128)(2,1)}, f32[12,128,128]{2,1,0:T(8,128)}, f32[256,768]{1,0:T(8,128)}, f32[256,1]{1,0:T(8,128)}, bf16[256,768]{1,0:T(8,128)(2,1)}) custom-call(bf16[256,768]{1,0:T(8,128)(2,1)} %bitcast.63, bf16[256,2304]{1,0:T(8,128)(2,1)} %get-tuple-element.266.mixed_ref, bf16[128,768]{1,0:T(8,128)(2,1)} %get-tuple-element.267.before_ref, ...), custom_call_target="tpu_custom_call" | custom-call | tf_op jit(solution)/shard_map/pallas_call | solution.py:719
  100.0 5.4 %shard_map.297 = (bf16[4,4,2,24,3072]{4,3,2,1,0:T(8,128)(2,1)}, bf16[4,4,2,24,768]{4,3,2,1,0:T(8,128)(2,1)}) custom-call(bf16[4,24,3840]{2,1,0:T(8,128)(2,1)} %shard_map.292.refs_0_, bf16[4,24,3840]{2,1,0:T(8,128)(2,1)} %collective-permute-done.20.refs_1_, bf16[4,24,3840]{2,1,0:T(8,128)(2,1)} %collective-permute-done.21.refs_2_, ...), custom_call_target="tpu_custom_call" | custom-call | tf_op jit(solution)/shard_map/pallas_call | solution.py:510
  105.4 6.4 %shard_map.298 = (bf16[256,3072]{1,0:T(8,128)(2,1)}, bf16[256,3072]{1,0:T(8,128)(2,1)}) custom-call(bf16[256,768]{1,0:T(8,128)(2,1)} %get-tuple-element.272.low_ref, bf16[768,3072]{1,0:T(8,128)(2,1)} %bitcast.57, f32[1,3072]{1,0:T(1,128)} %reshape.129.bias_ref), custom_call_target="tpu_custom_call" | custom-call | tf_op jit(solution)/shard_map/pallas_call | solution.py:719
  117.5 6.2 %collective-permute-done.31.refs_3_ = bf16[4,24,3072]{2,1,0:T(8,128)(2,1)} collective-permute-done((bf16[4,24,3072]{2,1,0:T(8,128)(2,1)}, bf16[4,24,3072]{2,1,0:T(8,128)(2,1)}, u32[]{:S(2)}, u32[]{:S(2)}) %collective-permute-start.31) | collective-permute-done | bytes 589856 | tf_op jit(solution)/shard_map/ppermute | solution.py:464
  126.2 4.6 %shard_map.300 = bf16[4,4,2,4,24,768]{5,4,3,2,1,0:T(8,128)(2,1)} custom-call(bf16[4,24,3072]{2,1,0:T(8,128)(2,1)} %shard_map.295.refs_0_, bf16[4,24,3072]{2,1,0:T(8,128)(2,1)} %collective-permute-done.28.refs_1_, bf16[4,24,3072]{2,1,0:T(8,128)(2,1)} %collective-permute-done.29.refs_2_, bf16[4,24,3072]{2,1,0:T(8,128)(2,1)} %collective-permute-done.31.refs_3_, ...), custom_call_target="tpu_custom_call" | custom-call | tf_op jit(solution)/shard_map/pallas_call | solution.py:510
  131.0 6.3 %shard_map.301 = (f32[256,768]{1,0:T(8,128)}, f32[256,1]{1,0:T(8,128)}, f32[8,768]{1,0:T(8,128)}, f32[8,768]{1,0:T(8,128)}) custom-call(bf16[256,3072]{1,0:T(8,128)(2,1)} %get-tuple-element.282.active_ref, bf16[3072,768]{1,0:T(8,128)(2,1)} %bitcast.46, f32[256,768]{1,0:T(8,128)} %get-tuple-element.293.first_ref.n_ref, ...), custom_call_target="tpu_custom_call" | custom-call | tf_op jit(solution)/shard_map/pallas_call | solution.py:719
  137.7 3.4 %shard_map.302 = (bf16[4,4,2,24,768]{4,3,2,1,0:T(8,128)(2,1)}, bf16[4,4,2,24,640]{4,3,2,1,0:T(8,128)(2,1)}, bf16[4,2,4,24,768]{4,3,2,1,0:T(8,128)(2,1)}) custom-call(bf16[4,4,24,2176]{3,2,1,0:T(8,128)(2,1)} %shard_map.299.refs_0_, bf16[4,4,24,2176]{3,2,1,0:T(8,128)(2,1)} %collective-permute-done.36.refs_1_), custom_call_target="tpu_custom_call" | custom-call | tf_op jit(solution)/shard_map/pallas_call | solution.py:510
  186.9 2.7 collective-permute-done.52.c_ref
  193.3 9.1 %shard_map.309 = (bf16[256,768]{1,0:T(8,128)(2,1)}, f32[256,768]{1,0:T(8,128)}, bf16[16,96,768]{2,1,0:T(8,128)(2,1)}, bf16[16,96,768]{2,1,0:T(8,128)(2,1)}, bf16...) custom-call(bf16[256,768]{1,0:T(8,128)(2,1)} %bitcast.61, f32[8,768]{1,0:T(8,128)} %copy-done.11, ...), custom_call_target="tpu_custom_call" | custom-call | tf_op jit(solution)/shard_map/pallas_call | solution.py:719
  203.8 7.7 %shard_map.310 = (bf16[16,24,3072]{2,1,0:T(8,128)(2,1)}, bf16[16,24,3072]{2,1,0:T(8,128)(2,1)}, f32[256,768]{1,0:T(8,128)}) custom-call(bf16[256,768]{1,0:T(8,128)(2,1)} %get-tuple-element.272.low_ref, bf16[256,3072]{1,0:T(8,128)(2,1)} %get-tuple-element.341.hidden_ref, bf16[768,3072]{1,0:T(8,128)(2,1)} %bitcast.58, f32[256,768]{1,0:T(8,128)} %get-tuple-element.342.second_ref), custom_call_target="tpu_custom_call" | custom-call | tf_op jit(solution)/shard_map/pallas_call | solution.py:719
  217.7 3.8 %collective-permute-start.61 = (bf16[4,48,768]{2,1,0:T(8,128)(2,1)}, bf16[4,48,768]{2,1,0:T(8,128)(2,1)}, u32[]{:S(2)}, u32[]{:S(2)}) collective-permute-start(bf16[4,48,768]{2,1,0:T(8,128)(2,1)} %shard_map.314.refs_0_), channel_id=1, source_target_pairs={{0,24},{8,0},{16,8},{24,16},{1,25},{9,1},{17,9},{25,17},{2,26},{10... | collective-permute-start | bytes 884744 | tf_op jit(solution)/shard_map/ppermute | solution.py:448
  221.5 10.7 %shard_map.311 = (f32[768,768]{1,0:T(8,128)}, f32[256,768]{1,0:T(8,128)}, f32[8,768]{1,0:T(8,128)}, bf16[256,2304]{1,0:T(8,128)(2,1)}) custom-call(f32[256,768]{1,0:T(8,128)} %get-tuple-element.346.first_ref, f32[256,768]{1,0:T(8,128)} %get-tuple-element.293.first_ref.n_ref, f32[256,1]{1,0:T(8,128)} %get-tuple-element.347.scale_ref, ...), custom_call_target="tpu_custom_call" | custom-call | tf_op jit(solution)/shard_map/pallas_call | solution.py:719
  241.3 8.4 %shard_map.315 = (f32[256,768]{1,0:T(8,128)}, bf16[16,24,3200]{2,1,0:T(8,128)(2,1)}, bf16[16,24,3200]{2,1,0:T(8,128)(2,1)}) custom-call(f32[256,768]{1,0:T(8,128)} %get-tuple-element.351.total_ref, bf16[256,2304]{1,0:T(8,128)(2,1)} %get-tuple-element.359.back_ref, bf16[256,768]{1,0:T(8,128)(2,1)} %bitcast.64, bf16[768,3200]{1,0:T(8,128)(2,1)} %bitcast.45, ...), custom_call_target="tpu_custom_call" | custom-call | tf_op jit(solution)/shard_map/pallas_call | solution.py:719
  256.5 5.2 %collective-permute-done.65.refs_3_ = bf16[4,96,768]{2,1,0:T(8,128)(2,1)} collective-permute-done((bf16[4,96,768]{2,1,0:T(8,128)(2,1)}, bf16[4,96,768]{2,1,0:T(8,128)(2,1)}, u32[]{:S(2)}, u32[]{:S(2)}) %collective-permute-start.65) | collective-permute-done | bytes 589856 | tf_op jit(solution)/shard_map/ppermute | solution.py:464
  262.3 2.7 shard_map.320
  265.0 2.7 shard_map.319
  267.7 4.3 %collective-permute-done.66.refs_3_ = bf16[4,24,3072]{2,1,0:T(8,128)(2,1)} collective-permute-done((bf16[4,24,3072]{2,1,0:T(8,128)(2,1)}, bf16[4,24,3072]{2,1,0:T(8,128)(2,1)}, u32[]{:S(2)}, u32[]{:S(2)}) %collective-permute-start.66) | collective-permute-done | bytes 589856 | tf_op jit(solution)/shard_map/ppermute | solution.py:464
  274.3 2.8 collective-permute-start.71
  277.0 2.7 shard_map.321
  281.2 5.3 %collective-permute-done.70 = bf16[96,768]{1,0:T(8,128)(2,1)} collective-permute-done((bf16[96,768]{1,0:T(8,128)(2,1)}, bf16[96,768]{1,0:T(8,128)(2,1)}, u32[]{:S(2)}, u32[]{:S(2)}) %collective-permute-start.70) | collective-permute-done | bytes 147488 | tf_op jit(solution)/shard_map/ppermute | solution.py:448
  300.9 3.8 %collective-permute-done.74 = bf16[24,3072]{1,0:T(8,128)(2,1)} collective-permute-done((bf16[24,3072]{1,0:T(8,128)(2,1)}, bf16[24,3072]{1,0:T(8,128)(2,1)}, u32[]{:S(2)}, u32[]{:S(2)}) %collective-permute-start.74) | collective-permute-done | bytes 147488 | tf_op jit(solution)/shard_map/ppermute | solution.py:448
  304.7 2.8 shard_map.323
  307.5 3.7 %collective-permute-start.76 = (bf16[24,3200]{1,0:T(8,128)(2,1)}, bf16[24,3200]{1,0:T(8,128)(2,1)}, u32[]{:S(2)}, u32[]{:S(2)}) collective-permute-start(bf16[24,3200]{1,0:T(8,128)(2,1)} %get-tuple-element.403), channel_id=1, source_target_pairs={{0,8},{8,16},{16,24},{24,0},{1,9},{9,17},{17,25},{25,1},{2,10},{10... | collective-permute-start | bytes 460808 | tf_op jit(solution)/shard_map/ppermute | solution.py:448
  315.6 4.4 %shard_map.325 = (f32[24,2304]{1,0:T(8,128)}, f32[24,768]{1,0:T(8,128)}, f32[24,3072]{1,0:T(8,128)}, f32[96,768]{1,0:T(8,128)}, f32[8,24]{1,0:T(8,128)}, /*index=5*/f32[1,96]{1,0:T(1,128)}, f32[64,24]{1,0:T(8,128)}) custom-call(bf16[4,4,48,768]{3,2,1,0:T(8,128)(2,1)} %shard_map.318.mine_ref, bf16[4,4,48,768]{3,2,1,0:T(8,128)(2,1)} %collective-permute-done.68.other_ref, ...), custom_call_target="tpu_custom_call" | custom-call | tf_op jit(solution)/shard_map/pallas_call | solution.py:719
  (218 shorter events, 161.3 us)
Async XLA Ops:
  3.1 17.1 %collective-permute-start = (bf16[24,3200]{1,0:T(8,128)(2,1)}, bf16[24,3200]{1,0:T(8,128)(2,1)}, u32[]{:S(2)}, u32[]{:S(2)}) collective-permute-start(bf16[24,3200]{1,0:T(8,128)(2,1)} %get-tuple-element.225.refs_0_), channel_id=1, source_target_pairs={{0,8},{8,16},{16,24},{24,0},{1,9},{9,17},{17,25},{25,1},{2,10},{10... | collective-permute-start | bytes 460808 | tf_op jit(solution)/shard_map/ppermute | solution.py:448
  6.2 14.1 %collective-permute-start.1 = (bf16[24,3200]{1,0:T(8,128)(2,1)}, bf16[24,3200]{1,0:T(8,128)(2,1)}, u32[]{:S(2)}, u32[]{:S(2)}) collective-permute-start(bf16[24,3200]{1,0:T(8,128)(2,1)} %get-tuple-element.225.refs_0_), channel_id=1, source_target_pairs={{0,16},{8,24},{16,0},{24,8},{1,17},{9,25},{17,1},{25,9},{2,18},{10... | collective-permute-start | bytes 460808 | tf_op jit(solution)/shard_map/ppermute | solution.py:448
  22.1 18.5 %collective-permute-start.9 = (bf16[4,24,3200]{2,1,0:T(8,128)(2,1)}, bf16[4,24,3200]{2,1,0:T(8,128)(2,1)}, u32[]{:S(2)}, u32[]{:S(2)}) collective-permute-start(bf16[4,24,3200]{2,1,0:T(8,128)(2,1)} %shard_map.290.refs_0_), channel_id=1, source_target_pairs={{0,2},{1,5},{2,0},{3,7},{4,6},{5,1},{6,4},{7,3},{8,10},{9,13},{10,... | collective-permute-start | bytes 1843208 | tf_op jit(solution)/shard_map/ppermute | solution.py:460
  23.7 16.9 %collective-permute-start.10 = (bf16[4,24,3200]{2,1,0:T(8,128)(2,1)}, bf16[4,24,3200]{2,1,0:T(8,128)(2,1)}, u32[]{:S(2)}, u32[]{:S(2)}) collective-permute-start(bf16[4,24,3200]{2,1,0:T(8,128)(2,1)} %shard_map.290.refs_0_), channel_id=1, source_target_pairs={{0,4},{1,3},{2,6},{3,1},{4,0},{5,7},{6,2},{7,5},{8,12},{9,11},{10,... | collective-permute-start | bytes 1843208 | tf_op jit(solution)/shard_map/ppermute | solution.py:464
  40.6 17.8 %collective-permute-start.11 = (bf16[4,24,3200]{2,1,0:T(8,128)(2,1)}, bf16[4,24,3200]{2,1,0:T(8,128)(2,1)}, u32[]{:S(2)}, u32[]{:S(2)}) collective-permute-start(bf16[4,24,3200]{2,1,0:T(8,128)(2,1)} %collective-permute-done.9.refs_1_), channel_id=1, source_target_pairs={{0,4},{1,3},{2,6},{3,1},{4,0},{5,7},{6,2},{7,5},{8,12},{9,11},{10,... | collective-permute-start | bytes 1843208 | tf_op jit(solution)/shard_map/ppermute | solution.py:464
  41.2 17.3 %collective-permute-start.14 = (bf16[4,24,3200]{2,1,0:T(8,128)(2,1)}, bf16[4,24,3200]{2,1,0:T(8,128)(2,1)}, u32[]{:S(2)}, u32[]{:S(2)}) collective-permute-start(bf16[4,24,3200]{2,1,0:T(8,128)(2,1)} %collective-permute-done.9.refs_1_), channel_id=1, source_target_pairs={{0,1},{1,0},{2,3},{3,2},{4,5},{5,4},{6,7},{7,6},{8,9},{9,8},{10,11... | collective-permute-start | bytes 1843208 | tf_op jit(solution)/shard_map/ppermute | solution.py:452
  41.2 17.3 %collective-permute-start.13 = (bf16[4,24,3200]{2,1,0:T(8,128)(2,1)}, bf16[4,24,3200]{2,1,0:T(8,128)(2,1)}, u32[]{:S(2)}, u32[]{:S(2)}) collective-permute-start(bf16[4,24,3200]{2,1,0:T(8,128)(2,1)} %shard_map.290.refs_0_), channel_id=1, source_target_pairs={{0,1},{1,0},{2,3},{3,2},{4,5},{5,4},{6,7},{7,6},{8,9},{9,8},{10,11... | collective-permute-start | bytes 1843208 | tf_op jit(solution)/shard_map/ppermute | solution.py:452
  41.7 16.8 %collective-permute-start.15 = (bf16[4,24,3200]{2,1,0:T(8,128)(2,1)}, bf16[4,24,3200]{2,1,0:T(8,128)(2,1)}, u32[]{:S(2)}, u32[]{:S(2)}) collective-permute-start(bf16[4,24,3200]{2,1,0:T(8,128)(2,1)} %collective-permute-done.10.refs_2_), channel_id=1, source_target_pairs={{0,1},{1,0},{2,3},{3,2},{4,5},{5,4},{6,7},{7,6},{8,9},{9,8},{10,11... | collective-permute-start | bytes 1843208 | tf_op jit(solution)/shard_map/ppermute | solution.py:452
  41.7 16.7 %collective-permute-start.12 = (bf16[4,24,2176]{2,1,0:T(8,128)(2,1)}, bf16[4,24,2176]{2,1,0:T(8,128)(2,1)}, u32[]{:S(2)}, u32[]{:S(2)}) collective-permute-start(bf16[4,24,2176]{2,1,0:T(8,128)(2,1)} %shard_map.291.refs_0_), channel_id=1, source_target_pairs={{0,8},{8,16},{16,24},{24,0},{1,9},{9,17},{17,25},{25,1},{2,10},{10... | collective-permute-start | bytes 1253384 | tf_op jit(solution)/shard_map/ppermute | solution.py:448
  60.9 20.7 %collective-permute-start.20 = (bf16[4,24,3840]{2,1,0:T(8,128)(2,1)}, bf16[4,24,3840]{2,1,0:T(8,128)(2,1)}, u32[]{:S(2)}, u32[]{:S(2)}) collective-permute-start(bf16[4,24,3840]{2,1,0:T(8,128)(2,1)} %shard_map.292.refs_0_), channel_id=1, source_target_pairs={{0,2},{1,5},{2,0},{3,7},{4,6},{5,1},{6,4},{7,3},{8,10},{9,13},{10,... | collective-permute-start | bytes 2211848 | tf_op jit(solution)/shard_map/ppermute | solution.py:460
  61.4 20.2 %collective-permute-start.21 = (bf16[4,24,3840]{2,1,0:T(8,128)(2,1)}, bf16[4,24,3840]{2,1,0:T(8,128)(2,1)}, u32[]{:S(2)}, u32[]{:S(2)}) collective-permute-start(bf16[4,24,3840]{2,1,0:T(8,128)(2,1)} %shard_map.292.refs_0_), channel_id=1, source_target_pairs={{0,4},{1,3},{2,6},{3,1},{4,0},{5,7},{6,2},{7,5},{8,12},{9,11},{10,... | collective-permute-start | bytes 2211848 | tf_op jit(solution)/shard_map/ppermute | solution.py:464
  62.9 18.6 %collective-permute-start.17 = (bf16[24,3072]{1,0:T(8,128)(2,1)}, bf16[24,3072]{1,0:T(8,128)(2,1)}, u32[]{:S(2)}, u32[]{:S(2)}) collective-permute-start(bf16[24,3072]{1,0:T(8,128)(2,1)} %get-tuple-element.262.refs_0_), channel_id=1, source_target_pairs={{0,8},{8,16},{16,24},{24,0},{1,9},{9,17},{17,25},{25,1},{2,10},{10... | collective-permute-start | bytes 442376 | tf_op jit(solution)/shard_map/ppermute | solution.py:448
  63.0 18.6 %collective-permute-start.18 = (bf16[24,3072]{1,0:T(8,128)(2,1)}, bf16[24,3072]{1,0:T(8,128)(2,1)}, u32[]{:S(2)}, u32[]{:S(2)}) collective-permute-start(bf16[24,3072]{1,0:T(8,128)(2,1)} %get-tuple-element.262.refs_0_), channel_id=1, source_target_pairs={{0,16},{8,24},{16,0},{24,8},{1,17},{9,25},{17,1},{25,9},{2,18},{10... | collective-permute-start | bytes 442376 | tf_op jit(solution)/shard_map/ppermute | solution.py:448
  65.3 16.3 %collective-permute-start.19 = (bf16[24,3072]{1,0:T(8,128)(2,1)}, bf16[24,3072]{1,0:T(8,128)(2,1)}, u32[]{:S(2)}, u32[]{:S(2)}) collective-permute-start(bf16[24,3072]{1,0:T(8,128)(2,1)} %get-tuple-element.262.refs_0_), channel_id=1, source_target_pairs={{0,24},{8,0},{16,8},{24,16},{1,25},{9,1},{17,9},{25,17},{2,26},{10... | collective-permute-start | bytes 442376 | tf_op jit(solution)/shard_map/ppermute | solution.py:448
  81.6 15.3 %collective-permute-start.23 = (bf16[4,24,3840]{2,1,0:T(8,128)(2,1)}, bf16[4,24,3840]{2,1,0:T(8,128)(2,1)}, u32[]{:S(2)}, u32[]{:S(2)}) collective-permute-start(bf16[4,24,3840]{2,1,0:T(8,128)(2,1)} %collective-permute-done.20.refs_1_), channel_id=1, source_target_pairs={{0,4},{1,3},{2,6},{3,1},{4,0},{5,7},{6,2},{7,5},{8,12},{9,11},{10,... | collective-permute-start | bytes 2211848 | tf_op jit(solution)/shard_map/ppermute | solution.py:464
  82.2 14.7 %collective-permute-start.25 = (bf16[4,24,3840]{2,1,0:T(8,128)(2,1)}, bf16[4,24,3840]{2,1,0:T(8,128)(2,1)}, u32[]{:S(2)}, u32[]{:S(2)}) collective-permute-start(bf16[4,24,3840]{2,1,0:T(8,128)(2,1)} %collective-permute-done.20.refs_1_), channel_id=1, source_target_pairs={{0,1},{1,0},{2,3},{3,2},{4,5},{5,4},{6,7},{7,6},{8,9},{9,8},{10,11... | collective-permute-start | bytes 2211848 | tf_op jit(solution)/shard_map/ppermute | solution.py:452
  82.2 14.7 %collective-permute-start.24 = (bf16[4,24,3840]{2,1,0:T(8,128)(2,1)}, bf16[4,24,3840]{2,1,0:T(8,128)(2,1)}, u32[]{:S(2)}, u32[]{:S(2)}) collective-permute-start(bf16[4,24,3840]{2,1,0:T(8,128)(2,1)} %shard_map.292.refs_0_), channel_id=1, source_target_pairs={{0,1},{1,0},{2,3},{3,2},{4,5},{5,4},{6,7},{7,6},{8,9},{9,8},{10,11... | collective-permute-start | bytes 2211848 | tf_op jit(solution)/shard_map/ppermute | solution.py:452
  82.7 14.2 %collective-permute-start.26 = (bf16[4,24,3840]{2,1,0:T(8,128)(2,1)}, bf16[4,24,3840]{2,1,0:T(8,128)(2,1)}, u32[]{:S(2)}, u32[]{:S(2)}) collective-permute-start(bf16[4,24,3840]{2,1,0:T(8,128)(2,1)} %collective-permute-done.21.refs_2_), channel_id=1, source_target_pairs={{0,1},{1,0},{2,3},{3,2},{4,5},{5,4},{6,7},{7,6},{8,9},{9,8},{10,11... | collective-permute-start | bytes 2211848 | tf_op jit(solution)/shard_map/ppermute | solution.py:452
  82.7 14.2 %collective-permute-start.22 = (bf16[4,24,2176]{2,1,0:T(8,128)(2,1)}, bf16[4,24,2176]{2,1,0:T(8,128)(2,1)}, u32[]{:S(2)}, u32[]{:S(2)}) collective-permute-start(bf16[4,24,2176]{2,1,0:T(8,128)(2,1)} %collective-permute-done.12.refs_1_), channel_id=1, source_target_pairs={{0,8},{8,16},{16,24},{24,0},{1,9},{9,17},{17,25},{25,1},{2,10},{10... | collective-permute-start | bytes 1253384 | tf_op jit(solution)/shard_map/ppermute | solution.py:448
  96.9 16.6 %collective-permute-start.28 = (bf16[4,24,3072]{2,1,0:T(8,128)(2,1)}, bf16[4,24,3072]{2,1,0:T(8,128)(2,1)}, u32[]{:S(2)}, u32[]{:S(2)}) collective-permute-start(bf16[4,24,3072]{2,1,0:T(8,128)(2,1)} %shard_map.295.refs_0_), channel_id=1, source_target_pairs={{0,2},{1,5},{2,0},{3,7},{4,6},{5,1},{6,4},{7,3},{8,10},{9,13},{10,... | collective-permute-start | bytes 1769480 | tf_op jit(solution)/shard_map/ppermute | solution.py:460
  98.5 15.1 %collective-permute-start.29 = (bf16[4,24,3072]{2,1,0:T(8,128)(2,1)}, bf16[4,24,3072]{2,1,0:T(8,128)(2,1)}, u32[]{:S(2)}, u32[]{:S(2)}) collective-permute-start(bf16[4,24,3072]{2,1,0:T(8,128)(2,1)} %shard_map.295.refs_0_), channel_id=1, source_target_pairs={{0,4},{1,3},{2,6},{3,1},{4,0},{5,7},{6,2},{7,5},{8,12},{9,11},{10,... | collective-permute-start | bytes 1769480 | tf_op jit(solution)/shard_map/ppermute | solution.py:464
  100.0 13.5 %collective-permute-start.30 = (bf16[4,24,2176]{2,1,0:T(8,128)(2,1)}, bf16[4,24,2176]{2,1,0:T(8,128)(2,1)}, u32[]{:S(2)}, u32[]{:S(2)}) collective-permute-start(bf16[4,24,2176]{2,1,0:T(8,128)(2,1)} %collective-permute-done.22.refs_2_), channel_id=1, source_target_pairs={{0,8},{8,16},{16,24},{24,0},{1,9},{9,17},{17,25},{25,1},{2,10},{10... | collective-permute-start | bytes 1253384 | tf_op jit(solution)/shard_map/ppermute | solution.py:448
  211.5 20.8 %collective-permute-start.59 = (bf16[4,4,24,3072]{3,2,1,0:T(8,128)(2,1)}, bf16[4,4,24,3072]{3,2,1,0:T(8,128)(2,1)}, u32[]{:S(2)}, u32[]{:S(2)}) collective-permute-start(bf16[4,4,24,3072]{3,2,1,0:T(8,128)(2,1)} %bitcast.75), channel_id=1, source_target_pairs={{0,1},{1,0},{2,3},{3,2},{4,5},{5,4},{6,7},{7,6},{8,9},{9,8},{10,11... | collective-permute-start | bytes 7077896 | tf_op jit(solution)/shard_map/ppermute | solution.py:452
  214.2 20.7 %collective-permute-start.58 = (bf16[2,4,96,768]{3,2,1,0:T(8,128)(2,1)}, bf16[2,4,96,768]{3,2,1,0:T(8,128)(2,1)}, u32[]{:S(2)}, u32[]{:S(2)}) collective-permute-start(bf16[2,4,96,768]{3,2,1,0:T(8,128)(2,1)} %shard_map.312), channel_id=1, source_target_pairs={{0,2},{1,5},{2,0},{3,7},{4,6},{5,1},{6,4},{7,3},{8,10},{9,13},{10,... | collective-permute-start | bytes 3538952 | tf_op jit(solution)/shard_map/ppermute | solution.py:460
  217.7 17.3 %collective-permute-start.60 = (bf16[4,48,768]{2,1,0:T(8,128)(2,1)}, bf16[4,48,768]{2,1,0:T(8,128)(2,1)}, u32[]{:S(2)}, u32[]{:S(2)}) collective-permute-start(bf16[4,48,768]{2,1,0:T(8,128)(2,1)} %shard_map.314.refs_0_), channel_id=1, source_target_pairs={{0,8},{8,16},{16,24},{24,0},{1,9},{9,17},{17,25},{25,1},{2,10},{10... | collective-permute-start | bytes 884744 | tf_op jit(solution)/shard_map/ppermute | solution.py:448
  217.7 17.2 %collective-permute-start.61 = (bf16[4,48,768]{2,1,0:T(8,128)(2,1)}, bf16[4,48,768]{2,1,0:T(8,128)(2,1)}, u32[]{:S(2)}, u32[]{:S(2)}) collective-permute-start(bf16[4,48,768]{2,1,0:T(8,128)(2,1)} %shard_map.314.refs_0_), channel_id=1, source_target_pairs={{0,24},{8,0},{16,8},{24,16},{1,25},{9,1},{17,9},{25,17},{2,26},{10... | collective-permute-start | bytes 884744 | tf_op jit(solution)/shard_map/ppermute | solution.py:448
  235.0 16.6 %collective-permute-start.62 = (bf16[2,4,24,3072]{3,2,1,0:T(8,128)(2,1)}, bf16[2,4,24,3072]{3,2,1,0:T(8,128)(2,1)}, u32[]{:S(2)}, u32[]{:S(2)}) collective-permute-start(bf16[2,4,24,3072]{3,2,1,0:T(8,128)(2,1)} %shard_map.313), channel_id=1, source_target_pairs={{0,2},{1,5},{2,0},{3,7},{4,6},{5,1},{6,4},{7,3},{8,10},{9,13},{10,... | collective-permute-start | bytes 3538952 | tf_op jit(solution)/shard_map/ppermute | solution.py:460
  235.4 14.3 %collective-permute-start.63 = (bf16[4,48,768]{2,1,0:T(8,128)(2,1)}, bf16[4,48,768]{2,1,0:T(8,128)(2,1)}, u32[]{:S(2)}, u32[]{:S(2)}) collective-permute-start(bf16[4,48,768]{2,1,0:T(8,128)(2,1)} %shard_map.314.refs_0_), channel_id=1, source_target_pairs={{0,16},{8,24},{16,0},{24,8},{1,17},{9,25},{17,1},{25,9},{2,18},{10... | collective-permute-start | bytes 884744 | tf_op jit(solution)/shard_map/ppermute | solution.py:448
  271.9 17.0 %collective-permute-start.67 = (bf16[2,4,24,3200]{3,2,1,0:T(8,128)(2,1)}, bf16[2,4,24,3200]{3,2,1,0:T(8,128)(2,1)}, u32[]{:S(2)}, u32[]{:S(2)}) collective-permute-start(bf16[2,4,24,3200]{3,2,1,0:T(8,128)(2,1)} %shard_map.319), channel_id=1, source_target_pairs={{0,2},{1,5},{2,0},{3,7},{4,6},{5,1},{6,4},{7,3},{8,10},{9,13},{10,... | collective-permute-start | bytes 3686408 | tf_op jit(solution)/shard_map/ppermute | solution.py:460
  272.3 14.2 %collective-permute-start.68 = (bf16[4,4,48,768]{3,2,1,0:T(8,128)(2,1)}, bf16[4,4,48,768]{3,2,1,0:T(8,128)(2,1)}, u32[]{:S(2)}, u32[]{:S(2)}) collective-permute-start(bf16[4,4,48,768]{3,2,1,0:T(8,128)(2,1)} %shard_map.318.mine_ref), channel_id=1, source_target_pairs={{0,1},{1,0},{2,3},{3,2},{4,5},{5,4},{6,7},{7,6},{8,9},{9,8},{10,11... | collective-permute-start | bytes 3538952 | tf_op jit(solution)/shard_map/ppermute | solution.py:452
  272.3 14.2 %collective-permute-start.70 = (bf16[96,768]{1,0:T(8,128)(2,1)}, bf16[96,768]{1,0:T(8,128)(2,1)}, u32[]{:S(2)}, u32[]{:S(2)}) collective-permute-start(bf16[96,768]{1,0:T(8,128)(2,1)} %get-tuple-element.386), channel_id=1, source_target_pairs={{0,16},{8,24},{16,0},{24,8},{1,17},{9,25},{17,1},{25,9},{2,18},{10... | collective-permute-start | bytes 442376 | tf_op jit(solution)/shard_map/ppermute | solution.py:448
  307.5 13.9 %collective-permute-start.76 = (bf16[24,3200]{1,0:T(8,128)(2,1)}, bf16[24,3200]{1,0:T(8,128)(2,1)}, u32[]{:S(2)}, u32[]{:S(2)}) collective-permute-start(bf16[24,3200]{1,0:T(8,128)(2,1)} %get-tuple-element.403), channel_id=1, source_target_pairs={{0,8},{8,16},{16,24},{24,0},{1,9},{9,17},{17,25},{25,1},{2,10},{10... | collective-permute-start | bytes 460808 | tf_op jit(solution)/shard_map/ppermute | solution.py:448
  (65 other events, 430.9 us)

commit v5 on v4

--- a/solution.py
+++ b/solution.py
@@ -807,10 +807,11 @@
     return up.reshape(D, D), mix.reshape(D, 640), down.reshape(D, D)
 
 
-def segment_heads(segment, mixed_ref, docs_ref, docs_column_ref, probs_ref, context_ref):
+def segment_heads(segment, mixed_ref, docs_ref, probs_ref, context_ref):
     lane = lax.broadcasted_iota(jnp.int32, (SEG, 128), 1)
     rows = slice(segment * SEG, (segment + 1) * SEG)
-    allowed = docs_column_ref[rows, :] == docs_ref[segment : segment + 1, :]
+    docs = jnp.broadcast_to(wide(docs_ref[segment : segment + 1, :]), (SEG, SEG))
+    allowed = docs == docs.T
     for pair in range(HEADS // 2):
         query, key, value = (
             mixed_ref[rows, third * D + pair * 128 : third * D + (pair + 1) * 128]
@@ -829,11 +830,13 @@
         context_ref[:, pair * 128 : (pair + 1) * 128] = low(context)
 
 
-def local_attend(tokens_ref, group_ref, docs_ref, docs_column_ref, places_ref, *outs):
+def local_attend(tokens_ref, group_ref, docs_ref, places_ref, *outs):
     mixed_ref, context_ref, probs_ref, rows_ref, places_out = outs
     rows_ref[...] = wide(group_ref[:, 4 * D : 4 * D + 128]).T
-    lane = lax.broadcasted_iota(jnp.int32, (2, 64), 1)
-    places_out[...] = contract_exact(wide(places_ref[...] == lane), rows_ref[16:80, :], 1, 0)
+    lane = lax.broadcasted_iota(jnp.int32, (1, 64), 1)
+    for place in range(2):
+        picked = wide(places_ref[:, place : place + 1] == lane)
+        places_out[place : place + 1, :] = contract_exact(picked, rows_ref[16:80, :], 1, 0)
     tokens = tokens_ref[...]
     for third in range(3):
         columns = slice(third * D, (third + 1) * D)
@@ -841,14 +844,14 @@
         if third != 1:
             mixed = mixed + rows_ref[third // 2 : third // 2 + 1, :]
         mixed_ref[:, columns] = low(mixed)
-    segment_heads(0, mixed_ref, docs_ref, docs_column_ref, probs_ref, context_ref)
+    segment_heads(0, mixed_ref, docs_ref, probs_ref, context_ref)
 
 
 def local_attend_more(
-    tokens_ref, mixed_ref, before_ref, weight_ref, rows_ref, docs_ref, docs_column_ref, *outs
+    tokens_ref, mixed_ref, before_ref, weight_ref, rows_ref, docs_ref, *outs
 ):
     context_ref, probs_ref, n_ref, scale_ref, low_ref, here = outs
-    segment_heads(1, mixed_ref, docs_ref, docs_column_ref, probs_ref, here)
+    segment_heads(1, mixed_ref, docs_ref, probs_ref, here)
     context_ref[0:SEG, :] = before_ref[...]
     context_ref[SEG : 2 * SEG, :] = here[...]
     total = wide(tokens_ref[...]) + contract(context_ref[...], weight_ref[...], 1, 0)
@@ -882,7 +885,7 @@
     def _():
         total[...] += part
 
-    @pl.when(step == 3)
+    @pl.when(step == 1)
     def _():
         normed, scale = norm_parts(total[...])
         n_ref[...] = normed
@@ -907,7 +910,7 @@
 
 
 def cross_attend(
-    own_ref, a_ref, b_ref, c_ref, weight_ref, rows_ref, docs_ref, docs_column_ref, *outs
+    own_ref, a_ref, b_ref, c_ref, weight_ref, rows_ref, docs_ref, *outs
 ):
     in_ref, grad_ref, mixed_ref, probs_ref, context_ref = outs
     layer, chip, core = place_in()
@@ -926,8 +929,11 @@
     bias = jnp.concatenate([biases[0], jnp.zeros_like(biases[0]), biases[1]], axis=1)
     mixed = low(contract(low(in_ref[...]), weight_ref[:, 0:576], 1, 0) + bias)
     mixed_ref[...] = mixed
-    row_docs = jnp.where(core == 0, docs_ref[0:1, :], docs_ref[1:2, :])
-    column_docs = jnp.where(core == 0, docs_column_ref[:, 0:1], docs_column_ref[:, 1:2])
+    row_docs = wide(jnp.where(core == 0, docs_ref[0:1, :], docs_ref[1:2, :]))
+    count = row_docs.shape[1]
+    lane = lax.broadcasted_iota(jnp.int32, (count, count), 1)
+    line = lax.broadcasted_iota(jnp.int32, (count, count), 0)
+    column_docs = jnp.sum(jnp.where(lane == line, row_docs, 0.0), axis=1, keepdims=True)
     allowed = row_docs == column_docs
     found = []
     for head in range(3):
@@ -1051,7 +1057,7 @@
     rows[2:4, :] = sums_ref[0:2, :]
     pack[34:35, :] = rows[pl.ds(chip, 1), :]
     for place in range(2):
-        spot = wide(places_ref[place : place + 1, :])
+        spot = wide(places_ref[:, place : place + 1])
         pack[35 + place : 36 + place, :] = jnp.broadcast_to(spot, (1, D))
     pack_ref[...] = low(pack[...])
 
@@ -1210,7 +1216,7 @@
     sums_ref[2:3, :] = column_sum(wide(branch))
     sums_ref[3:4, :] = column_sum(grad * normed)
     sums_ref[4:5, :] = column_sum(grad)
-    out_ref[...] = contract(context_ref[...], branch, 0, 0)
+    out_ref[...] = low(contract(context_ref[...], branch, 0, 0))
     context_low_ref[...] = low(contract(branch, group_ref[...], 1, 1))
     lane = lax.broadcasted_iota(jnp.int32, (SEG, 128), 1)
     for segment in range(2):
@@ -1256,11 +1262,14 @@
         total = total + contract(back, group_ref[:, columns], 1, 1)
     input_ref[...] = total
     columns = slice(3 * D, 4 * D)
-    split_cores(out_ref[...], kept_ref.at[:, :, columns], gone_ref.at[:, :, columns])
+    split_cores(wide(out_ref[...]), kept_ref.at[:, :, columns], gone_ref.at[:, :, columns])
     small_ref[...] = jnp.zeros_like(small_ref)
     small_ref[0:5, :] = sums_ref[0:5, :]
     small_ref[5:8, :] = more_ref[0:3, :]
-    small_ref[8:12, :] = bias_ref[...]
+    for owner in range(32):
+        for row in range(4):
+            taken = bias_ref[:, 96 * owner + 24 * row : 96 * owner + 24 * (row + 1)]
+            small_ref[8 + row : 9 + row, 24 * owner : 24 * (owner + 1)] = taken
     columns = slice(4 * D, 4 * D + 128)
     split_cores(small_ref[...].T, kept_ref.at[:, :, columns], gone_ref.at[:, :, columns])
 
@@ -1304,8 +1313,7 @@
     chip = place_in()[1]
     flat_tokens = tokens.reshape(256, D)
     flat_cot = cotangent.reshape(256, D)
-    docs_column = token_docs.reshape(256, 1)
-    segment_column = segment_docs.T
+    places_in = segment_positions.T
 
     shards_in = (
         local_mix,
@@ -1340,9 +1348,7 @@
     )
     cross_sent = [cross_pieces[0]] + [swap_chip(cross_pieces[mask], mask) for mask in (1, 2, 3)]
     z_one = reach_dp(shard_one)
-    shard_two, docs_column, segment_column, *z_one = stage(
-        shard_two, docs_column, segment_column, *z_one, *cross_sent
-    )
+    shard_two, *z_one = stage(shard_two, *z_one, *cross_sent)
     z_one, cross_sent = z_one[:4], z_one[4:]
     column_one = join_dp(z_one)
     column_one, shard_two = stage(column_one, shard_two)
@@ -1365,7 +1371,7 @@
     mixed_rows, context_first, probs_first, rows, place_rows = on_core(
         local_attend,
         [half(256, 3 * D), half(SEG, D), shape_of(12, SEG, SEG), shape_of(128, D), shape_of(2, D)],
-        (flat_tokens, first_group, token_docs, docs_column, segment_positions),
+        (flat_tokens, first_group, token_docs, places_in),
         0,
     )
     first_two, second_two = swap_one(column_two), swap_two(column_two)
@@ -1383,21 +1389,18 @@
     context_rows, probs_second, normed_one, scale_one, low_one = on_core(
         local_attend_more,
         [half(256, D), shape_of(12, SEG, SEG), shape_of(256, D), shape_of(256, 1), half(256, D)],
-        (flat_tokens, mixed_rows, context_first, first_group, rows, token_docs, docs_column),
+        (flat_tokens, mixed_rows, context_first, first_group, rows, token_docs),
         0,
         grid=(1,),
         in_specs=plain((256, D), (256, 3 * D), (SEG, D))
         + [pl.BlockSpec((D, D), lambda j: (0, 3))]
-        + plain((128, D), (2, SEG), (256, 1)),
+        + plain((128, D), (2, SEG)),
         out_specs=plain((256, D), (12, SEG, SEG), (256, D), (256, 1), (256, D)),
         scratch=[pltpu.VMEM((SEG, D), jnp.bfloat16)],
     )
     up_bias = rows[80:84].reshape(4, 32, 24).transpose(1, 0, 2).reshape(1, 4 * D)
-    cross_bias = rows[84:88].reshape(4, 4, 4, 2, 24)
-    cross_bias = lax.dynamic_index_in_dim(cross_bias, chip, 2, keepdims=False)
-    cross_bias = cross_bias.transpose(1, 2, 0, 3).reshape(1, D)
-    cross_moved[2], third_two, column_three, low_one, up_bias, cross_bias, *others = stage(
-        cross_moved[2], third_two, column_three, low_one, up_bias, cross_bias, *others
+    cross_moved[2], third_two, column_three, low_one, up_bias, rows_later, *others = stage(
+        cross_moved[2], third_two, column_three, low_one, up_bias, rows[84:88], *others
     )
     cross_moved.append(swap_dp(cross_moved[2], 1))
 
@@ -1414,6 +1417,10 @@
     tall = pl.BlockSpec((D, D), lambda j: (0, j))
     deep = pl.BlockSpec((D, D), lambda j: (j, 0))
     strip = pl.BlockSpec((1, D), lambda j: (0, j))
+    across_half = pl.BlockSpec((256, 2 * D), lambda j: (0, j))
+    tall_half = pl.BlockSpec((D, 2 * D), lambda j: (0, j))
+    deep_half = pl.BlockSpec((2 * D, D), lambda j: (j, 0))
+    strip_half = pl.BlockSpec((1, 2 * D), lambda j: (0, j))
     active_rows, slope_rows = on_core(
         local_up_part,
         [half(256, 4 * D)] * 2,
@@ -1423,13 +1430,18 @@
         in_specs=[whole, tall, strip],
         out_specs=[across, across],
     )
-    active_rows, first_three, second_three, column_three, cross_moved[3] = stage(
-        active_rows, first_three, second_three, column_three, cross_moved[3]
+    active_rows, first_three, second_three, column_three, cross_moved[3], rows_later = stage(
+        active_rows, first_three, second_three, column_three, cross_moved[3], rows_later
     )
 
     third_three = swap_two(first_three)
     others = [swap_core(piece) for piece in (column_three, first_three, second_three)]
-    third_three, cross_column, *others = stage(third_three, join_dp(cross_moved), *others)
+    cross_bias = rows_later.reshape(4, 4, 4, 2, 24)
+    cross_bias = lax.dynamic_index_in_dim(cross_bias, chip, 2, keepdims=False)
+    cross_bias = cross_bias.transpose(1, 2, 0, 3).reshape(1, D)
+    third_three, cross_column, cross_bias, *others = stage(
+        third_three, join_dp(cross_moved), cross_bias, *others
+    )
 
     others.append(swap_core(third_three))
     down_weight = gather_down([column_three, first_three, second_three, third_three], others)
@@ -1440,10 +1452,10 @@
         [shape_of(256, D), shape_of(256, 1), shape_of(8, D), shape_of(8, D)],
         (active_rows, down_weight, normed_one, rows, flat_cot, flat_cot, place_rows),
         2 * 256 * D * 4 * D,
-        grid=(4,),
+        grid=(2,),
         in_specs=[
-            across,
-            deep,
+            across_half,
+            deep_half,
             whole,
             vectors,
             pl.BlockSpec((16, D), lambda j: (0, 0)),
@@ -1465,7 +1477,7 @@
     row_in, row_grad, mixed, probs, context = on_core(
         cross_attend,
         [shape_of(8, D), shape_of(8, D), half(8, 576), shape_of(3, 8, 8), half(8, 192)],
-        (*plane_three(pair), cross_mix_part, rows, segment_docs, segment_column),
+        (*plane_three(pair), cross_mix_part, rows, segment_docs),
         0,
         room=12,
     )
@@ -1520,13 +1532,13 @@
             row_in,
             row_low,
             sums,
-            segment_positions,
+            places_in,
         ),
         0,
         grid=(1,),
         in_specs=plain(*[row8] * 4, row8, row8, (8, 1), (128, D))
         + [out_share]
-        + plain((8, 576), (3, 8, 8), mix_share, row8, row8, (8, 192), row8, row8, row8, (2, 1)),
+        + plain((8, 576), (3, 8, 8), mix_share, row8, row8, (8, 192), row8, row8, row8, (1, 2)),
         out_specs=plain(row8, row8, (48, D)),
         scratch=[pltpu.VMEM((48, D), jnp.float32), pltpu.VMEM((8, D), jnp.float32)],
         room=12,
@@ -1542,7 +1554,7 @@
     got, kept, packed = stage(swap_core(given), kept, packed)
     pack_one, pack_two = swap_one(packed), swap_two(packed)
 
-    fours = pl.BlockSpec((4, 96, D), lambda j: (j, 0, 0))
+    twos = pl.BlockSpec((8, 96, D), lambda j: (j, 0, 0))
     layer_output, second_rows, down_kept, down_gone, hidden_grads, sums_two, bias_grad = on_core(
         local_down_back,
         [
@@ -1556,9 +1568,9 @@
         ],
         (flat_cot, kept, got, normed_two, scale_two, rows, active_rows, slope_rows, down_weight),
         4 * 256 * D * 4 * D,
-        grid=(4,),
-        in_specs=[whole, eight, eight, whole, thin, vectors, across, across, deep],
-        out_specs=[whole, whole, fours, fours, across, eight, strip],
+        grid=(2,),
+        in_specs=[whole, eight, eight, whole, thin, vectors, across_half, across_half, deep_half],
+        out_specs=[whole, whole, twos, twos, across_half, eight, strip_half],
         scratch=[pltpu.VMEM((256, D), jnp.bfloat16)],
     )
     down_total = Sum(down_kept.reshape(4, 4, 96, D))
@@ -1568,14 +1580,14 @@
     pack_three = swap_two(pack_one)
 
     down_got = swap_core(down_gone)
-    sixteens = pl.BlockSpec((16, 24, D), lambda j: (0, 0, j))
+    sixteens = pl.BlockSpec((16, 24, 2 * D), lambda j: (0, 0, j))
     up_kept, up_gone, first_rows = on_core(
         local_up_back,
         [half(16, 24, 4 * D), half(16, 24, 4 * D), shape_of(256, D)],
         (low_one, hidden_grads, second_group, second_rows),
         4 * 256 * D * 4 * D,
-        grid=(4,),
-        in_specs=[whole, across, tall, whole],
+        grid=(2,),
+        in_specs=[whole, across_half, tall_half, whole],
         out_specs=[sixteens, sixteens, whole],
     )
     up_total = Sum(up_kept.reshape(4, 4, 24, 4 * D))
@@ -1591,7 +1603,7 @@
     flat = pl.BlockSpec((256, 3 * D), lambda j: (0, 0))
     out_grad, sum_rows, sums_one, back_rows = on_core(
         local_attend_back,
-        [shape_of(D, D), shape_of(256, D), shape_of(8, D), half(256, 3 * D)],
+        [half(D, D), shape_of(256, D), shape_of(8, D), half(256, 3 * D)],
         (
             first_rows,
             normed_one,
@@ -1625,7 +1637,6 @@
 
     up_back = swap_one(up_sent)
     down_onward = down_total.second(down_back)
-    bias_rows = bias_grad.reshape(32, 4, 24).transpose(1, 0, 2).reshape(4, D)
     sides = [half(16, 24, 4 * D + 128)] * 2
     input_grad, mix_kept, mix_gone = on_core(
         local_mix_back,
@@ -1638,7 +1649,7 @@
             out_grad,
             sums_one,
             sums_two,
-            bias_rows,
+            bias_grad,
         ),
         4 * 256 * D * 3 * D,
         scratch=[pltpu.VMEM((128, D), jnp.float32)],
@@ -1698,7 +1709,9 @@
         [shape_of(24, 3 * D), shape_of(24, D), shape_of(8, 24), shape_of(1, 96)],
         (mix_total.own, *mix_others),
         0,
-        room=12,
+        grid=(1,),
+        in_specs=plain(*[(24, 4 * D + 128)] * 4),
+        out_specs=plain((24, 3 * D), (24, D), (8, 24), (1, 96)),
         scratch=[pltpu.VMEM((128, 128), jnp.float32)],
     )
     return (

time: 328 us -> 322 us (0.982)
  waiting for transfers between devices: 83.2 us -> 96.3 us
  starting transfers between devices: 83.8 us -> 74.4 us
  local copies, waits for them, and re-layouts: 19.7 us -> 14.6 us
    ppermute x24, waiting for transfers between devices: 37 us -> 50.4 us  [swap_dp(): lax.ppermute(array_in, 'dp', [(i, (i + shift) % 4) for i in range(4)])]
    ppermute x24, starting transfers between devices: 41 us -> 31.1 us  [swap_dp(): lax.ppermute(array_in, 'dp', [(i, (i + shift) % 4) for i in range(4)])]
    unnamed x39 -> x31, local copies, waits for them, and re-layouts: 14.4 us -> 10.8 us
  transfers between devices with their start and end apart: 79 -> 79, of which waited for: 35 -> 37; matrix products, arithmetic and copies ran while one was open for 4% -> 3% of each run, Pallas kernels for 34% -> 34%
where the time goes in v5:
time: 322 us; the launch traced here: 320 us
  Pallas kernels  129 us (40%)
  waiting for transfers between devices  96.3 us (30%)
  starting transfers between devices  74.4 us (23%)
  local copies, waits for them, and re-layouts  14.6 us (5%)
  other arithmetic  3.84 us (1%)
    pallas_call x17, Pallas kernels, on_core(): pl.pallas_call(kernel, out_shape=out_shape, grid=grid, scratch_shapes=scr...  74.9 us
    ppermute x24, waiting for transfers between devices, swap_dp(): lax.ppermute(array_in, 'dp', [(i, (i + shift) % 4) for i in range(4)])  50.4 us
    ppermute x24, starting transfers between devices, swap_dp(): lax.ppermute(array_in, 'dp', [(i, (i + shift) % 4) for i in range(4)])  31.1 us
    pallas_call x11, Pallas kernels, copies(): pl.pallas_call(kernel, out_shape=[jax.ShapeDtypeStruct(shape, pieces[0].d...  31.1 us
    pallas_call x9, Pallas kernels, run(): pl.pallas_call(kernel, out_shape=out_shapes, in_specs=[far] * count, out_...  23.4 us
    ppermute x18, starting transfers between devices, swap_chip(): return lax.ppermute(array_in, 'seq', [(i, i ^ 2 * mask) for i in range(8)])  23.1 us
    ppermute x11, waiting for transfers between devices, swap_two(): lax.ppermute(array_in, 'seq', [(i, i ^ (4 if i % 2 == 0 else 2)) for i in...  18.9 us
    ppermute x18, waiting for transfers between devices, swap_chip(): return lax.ppermute(array_in, 'seq', [(i, i ^ 2 * mask) for i in range(8)])  18.6 us
  transfers between devices with their start and end apart: 79, of which 37 were waited for; matrix products, arithmetic and copies ran while one was open for 3% of the time, Pallas kernels for 34%

profile of v5, /device:TPU:0, one launch (start us, length us, event | category | flops | bytes accessed | tf_op | source)
XLA Modules:
  0.0 319.7 jit_solution(5974401306143021577)
XLA Ops:
  3.1 5.1 %collective-permute-start.2 = (bf16[24,3200]{1,0:T(8,128)(2,1)}, bf16[24,3200]{1,0:T(8,128)(2,1)}, u32[]{:S(2)}, u32[]{:S(2)}) collective-permute-start(bf16[24,3200]{1,0:T(8,128)(2,1)} %get-tuple-element.225.refs_0_), channel_id=1, source_target_pairs={{0,24},{8,0},{16,8},{24,16},{1,25},{9,1},{17,9},{25,17},{2,26},{10... | collective-permute-start | bytes 460808 | tf_op jit(solution)/shard_map/ppermute | solution.py:448
  16.3 3.1 collective-permute-done.5.refs_3_
  33.2 11.7 %collective-permute-done.7.refs_2_ = bf16[24,3840]{1,0:T(8,128)(2,1)} collective-permute-done((bf16[24,3840]{1,0:T(8,128)(2,1)}, bf16[24,3840]{1,0:T(8,128)(2,1)}, u32[]{:S(2)}, u32[]{:S(2)}) %collective-permute-start.7) | collective-permute-done | bytes 184352 | tf_op jit(solution)/shard_map/ppermute | solution.py:448
  48.0 11.9 %collective-permute-done.12.refs_1_ = bf16[4,24,2176]{2,1,0:T(8,128)(2,1)} collective-permute-done((bf16[4,24,2176]{2,1,0:T(8,128)(2,1)}, bf16[4,24,2176]{2,1,0:T(8,128)(2,1)}, u32[]{:S(2)}, u32[]{:S(2)}) %collective-permute-start.12) | collective-permute-done | bytes 417824 | tf_op jit(solution)/shard_map/ppermute | solution.py:448
  66.5 4.3 %shard_map.293 = bf16[4,4,2,24,3200]{4,3,2,1,0:T(8,128)(2,1)} custom-call(bf16[4,24,3200]{2,1,0:T(8,128)(2,1)} %shard_map.290.refs_0_, bf16[4,24,3200]{2,1,0:T(8,128)(2,1)} %collective-permute-done.9.refs_1_, bf16[4,24,3200]{2,1,0:T(8,128)(2,1)} %collective-permute-done.10.refs_2_, bf16[4,24,3200]{2,1,0:T(8,128)(2,1)} %collective-permute-done.11.refs_3_, ...), custom_call_target="tpu_custom_call" | custom-call | tf_op jit(solution)/shard_map/pallas_call | solution.py:510
  70.8 7.7 %shard_map.294 = (bf16[256,2304]{1,0:T(8,128)(2,1)}, bf16[128,768]{1,0:T(8,128)(2,1)}, f32[12,128,128]{2,1,0:T(8,128)}, f32[128,768]{1,0:T(8,128)}, f32[2,768]{1,0:T(2,128)}) custom-call(bf16[256,768]{1,0:T(8,128)(2,1)} %bitcast.61, bf16[768,3200]{1,0:T(8,128)(2,1)} %bitcast.41, s32[2,128]{1,0:T(2,128)} %docs_ref.4, s32[1,2]{1,0:T(1,128)} %bitcast.39), custom_call_target="tpu_custom_call" | custom-call | tf_op jit(solution)/shard_map/pallas_call | solution.py:719
  78.5 3.5 %collective-permute-done.21.refs_2_ = bf16[4,24,3840]{2,1,0:T(8,128)(2,1)} collective-permute-done((bf16[4,24,3840]{2,1,0:T(8,128)(2,1)}, bf16[4,24,3840]{2,1,0:T(8,128)(2,1)}, u32[]{:S(2)}, u32[]{:S(2)}) %collective-permute-start.21) | collective-permute-done | bytes 737312 | tf_op jit(solution)/shard_map/ppermute | solution.py:464
  85.2 6.9 %shard_map.296 = (bf16[256,768]{1,0:T(8,128)(2,1)}, f32[12,128,128]{2,1,0:T(8,128)}, f32[256,768]{1,0:T(8,128)}, f32[256,1]{1,0:T(8,128)}, bf16[256,768]{1,0:T(8,128)(2,1)}) custom-call(bf16[256,768]{1,0:T(8,128)(2,1)} %bitcast.62, bf16[256,2304]{1,0:T(8,128)(2,1)} %get-tuple-element.265.mixed_ref, bf16[128,768]{1,0:T(8,128)(2,1)} %get-tuple-element.266.before_ref, ...), custom_call_target="tpu_custom_call" | custom-call | tf_op jit(solution)/shard_map/pallas_call | solution.py:719
  94.0 3.4 %collective-permute-done.22.refs_2_ = bf16[4,24,2176]{2,1,0:T(8,128)(2,1)} collective-permute-done((bf16[4,24,2176]{2,1,0:T(8,128)(2,1)}, bf16[4,24,2176]{2,1,0:T(8,128)(2,1)}, u32[]{:S(2)}, u32[]{:S(2)}) %collective-permute-start.22) | collective-permute-done | bytes 417824 | tf_op jit(solution)/shard_map/ppermute | solution.py:448
  100.1 5.4 %shard_map.297 = (bf16[4,4,2,24,3072]{4,3,2,1,0:T(8,128)(2,1)}, bf16[4,4,2,24,768]{4,3,2,1,0:T(8,128)(2,1)}) custom-call(bf16[4,24,3840]{2,1,0:T(8,128)(2,1)} %shard_map.292.refs_0_, bf16[4,24,3840]{2,1,0:T(8,128)(2,1)} %collective-permute-done.20.refs_1_, bf16[4,24,3840]{2,1,0:T(8,128)(2,1)} %collective-permute-done.21.refs_2_, ...), custom_call_target="tpu_custom_call" | custom-call | tf_op jit(solution)/shard_map/pallas_call | solution.py:510
  105.5 6.4 %shard_map.298 = (bf16[256,3072]{1,0:T(8,128)(2,1)}, bf16[256,3072]{1,0:T(8,128)(2,1)}) custom-call(bf16[256,768]{1,0:T(8,128)(2,1)} %get-tuple-element.271.low_ref, bf16[768,3072]{1,0:T(8,128)(2,1)} %bitcast.56, f32[1,3072]{1,0:T(1,128)} %reshape.119.bias_ref), custom_call_target="tpu_custom_call" | custom-call | tf_op jit(solution)/shard_map/pallas_call | solution.py:719
  119.0 5.7 %collective-permute-done.31.refs_3_ = bf16[4,24,3072]{2,1,0:T(8,128)(2,1)} collective-permute-done((bf16[4,24,3072]{2,1,0:T(8,128)(2,1)}, bf16[4,24,3072]{2,1,0:T(8,128)(2,1)}, u32[]{:S(2)}, u32[]{:S(2)}) %collective-permute-start.31) | collective-permute-done | bytes 589856 | tf_op jit(solution)/shard_map/ppermute | solution.py:464
  127.0 4.6 %shard_map.300 = bf16[4,4,2,4,24,768]{5,4,3,2,1,0:T(8,128)(2,1)} custom-call(bf16[4,24,3072]{2,1,0:T(8,128)(2,1)} %shard_map.295.refs_0_, bf16[4,24,3072]{2,1,0:T(8,128)(2,1)} %collective-permute-done.28.refs_1_, bf16[4,24,3072]{2,1,0:T(8,128)(2,1)} %collective-permute-done.29.refs_2_, bf16[4,24,3072]{2,1,0:T(8,128)(2,1)} %collective-permute-done.31.refs_3_, ...), custom_call_target="tpu_custom_call" | custom-call | tf_op jit(solution)/shard_map/pallas_call | solution.py:510
  131.9 5.3 %shard_map.301 = (f32[256,768]{1,0:T(8,128)}, f32[256,1]{1,0:T(8,128)}, f32[8,768]{1,0:T(8,128)}, f32[8,768]{1,0:T(8,128)}) custom-call(bf16[256,3072]{1,0:T(8,128)(2,1)} %get-tuple-element.282.active_ref, bf16[3072,768]{1,0:T(8,128)(2,1)} %bitcast.45, f32[256,768]{1,0:T(8,128)} %get-tuple-element.294.first_ref.n_ref, ...), custom_call_target="tpu_custom_call" | custom-call | tf_op jit(solution)/shard_map/pallas_call | solution.py:719
  137.6 3.3 %shard_map.302 = (bf16[4,4,2,24,768]{4,3,2,1,0:T(8,128)(2,1)}, bf16[4,4,2,24,640]{4,3,2,1,0:T(8,128)(2,1)}, bf16[4,2,4,24,768]{4,3,2,1,0:T(8,128)(2,1)}) custom-call(bf16[4,4,24,2176]{3,2,1,0:T(8,128)(2,1)} %shard_map.299.refs_0_, bf16[4,4,24,2176]{3,2,1,0:T(8,128)(2,1)} %collective-permute-done.36.refs_1_), custom_call_target="tpu_custom_call" | custom-call | tf_op jit(solution)/shard_map/pallas_call | solution.py:510
  190.9 8.3 %shard_map.309 = (bf16[256,768]{1,0:T(8,128)(2,1)}, f32[256,768]{1,0:T(8,128)}, bf16[16,96,768]{2,1,0:T(8,128)(2,1)}, bf16[16,96,768]{2,1,0:T(8,128)(2,1)}, bf16...) custom-call(bf16[256,768]{1,0:T(8,128)(2,1)} %bitcast.60, f32[8,768]{1,0:T(8,128)} %copy-done.9, ...), custom_call_target="tpu_custom_call" | custom-call | tf_op jit(solution)/shard_map/pallas_call | solution.py:719
  200.3 7.0 %shard_map.310 = (bf16[16,24,3072]{2,1,0:T(8,128)(2,1)}, bf16[16,24,3072]{2,1,0:T(8,128)(2,1)}, f32[256,768]{1,0:T(8,128)}) custom-call(bf16[256,768]{1,0:T(8,128)(2,1)} %get-tuple-element.271.low_ref, bf16[256,3072]{1,0:T(8,128)(2,1)} %get-tuple-element.341.hidden_ref, bf16[768,3072]{1,0:T(8,128)(2,1)} %bitcast.57, f32[256,768]{1,0:T(8,128)} %get-tuple-element.342.second_ref), custom_call_target="tpu_custom_call" | custom-call | tf_op jit(solution)/shard_map/pallas_call | solution.py:719
  207.4 2.7 shard_map.312
  215.1 10.7 %shard_map.311 = (bf16[768,768]{1,0:T(8,128)(2,1)}, f32[256,768]{1,0:T(8,128)}, f32[8,768]{1,0:T(8,128)}, bf16[256,2304]{1,0:T(8,128)(2,1)}) custom-call(f32[256,768]{1,0:T(8,128)} %get-tuple-element.346.first_ref, f32[256,768]{1,0:T(8,128)} %get-tuple-element.294.first_ref.n_ref, f32[256,1]{1,0:T(8,128)} %get-tuple-element.347.scale_ref, ...), custom_call_target="tpu_custom_call" | custom-call | tf_op jit(solution)/shard_map/pallas_call | solution.py:719
  225.8 2.6 shard_map.313
  233.2 7.9 %shard_map.315 = (f32[256,768]{1,0:T(8,128)}, bf16[16,24,3200]{2,1,0:T(8,128)(2,1)}, bf16[16,24,3200]{2,1,0:T(8,128)(2,1)}) custom-call(f32[256,768]{1,0:T(8,128)} %get-tuple-element.351.total_ref, bf16[256,2304]{1,0:T(8,128)(2,1)} %get-tuple-element.359.back_ref, bf16[256,768]{1,0:T(8,128)(2,1)} %bitcast.63, bf16[768,3200]{1,0:T(8,128)(2,1)} %bitcast.44, ...), custom_call_target="tpu_custom_call" | custom-call | tf_op jit(solution)/shard_map/pallas_call | solution.py:719
  241.2 4.0 %collective-permute-done.63.refs_2_ = bf16[4,48,768]{2,1,0:T(8,128)(2,1)} collective-permute-done((bf16[4,48,768]{2,1,0:T(8,128)(2,1)}, bf16[4,48,768]{2,1,0:T(8,128)(2,1)}, u32[]{:S(2)}, u32[]{:S(2)}) %collective-permute-start.63) | collective-permute-done | bytes 294944 | tf_op jit(solution)/shard_map/ppermute | solution.py:448
  250.8 4.7 %collective-permute-done.65.refs_3_ = bf16[4,96,768]{2,1,0:T(8,128)(2,1)} collective-permute-done((bf16[4,96,768]{2,1,0:T(8,128)(2,1)}, bf16[4,96,768]{2,1,0:T(8,128)(2,1)}, u32[]{:S(2)}, u32[]{:S(2)}) %collective-permute-start.65) | collective-permute-done | bytes 589856 | tf_op jit(solution)/shard_map/ppermute | solution.py:464
  256.5 2.7 shard_map.320
  259.2 2.7 shard_map.319
  261.9 3.7 %collective-permute-done.66.refs_3_ = bf16[4,24,3072]{2,1,0:T(8,128)(2,1)} collective-permute-done((bf16[4,24,3072]{2,1,0:T(8,128)(2,1)}, bf16[4,24,3072]{2,1,0:T(8,128)(2,1)}, u32[]{:S(2)}, u32[]{:S(2)}) %collective-permute-start.66) | collective-permute-done | bytes 589856 | tf_op jit(solution)/shard_map/ppermute | solution.py:464
  270.6 2.7 shard_map.321
  275.7 5.9 %collective-permute-done.70 = bf16[96,768]{1,0:T(8,128)(2,1)} collective-permute-done((bf16[96,768]{1,0:T(8,128)(2,1)}, bf16[96,768]{1,0:T(8,128)(2,1)}, u32[]{:S(2)}, u32[]{:S(2)}) %collective-permute-start.70) | collective-permute-done | bytes 147488 | tf_op jit(solution)/shard_map/ppermute | solution.py:448
  295.2 4.4 %collective-permute-done.74 = bf16[24,3072]{1,0:T(8,128)(2,1)} collective-permute-done((bf16[24,3072]{1,0:T(8,128)(2,1)}, bf16[24,3072]{1,0:T(8,128)(2,1)}, u32[]{:S(2)}, u32[]{:S(2)}) %collective-permute-start.74) | collective-permute-done | bytes 147488 | tf_op jit(solution)/shard_map/ppermute | solution.py:448
  299.6 2.7 shard_map.323
  302.4 3.7 %collective-permute-start.76 = (bf16[24,3200]{1,0:T(8,128)(2,1)}, bf16[24,3200]{1,0:T(8,128)(2,1)}, u32[]{:S(2)}, u32[]{:S(2)}) collective-permute-start(bf16[24,3200]{1,0:T(8,128)(2,1)} %get-tuple-element.403), channel_id=1, source_target_pairs={{0,8},{8,16},{16,24},{24,0},{1,9},{9,17},{17,25},{25,1},{2,10},{10... | collective-permute-start | bytes 460808 | tf_op jit(solution)/shard_map/ppermute | solution.py:448
  310.4 4.4 %shard_map.325 = (f32[24,2304]{1,0:T(8,128)}, f32[24,768]{1,0:T(8,128)}, f32[24,3072]{1,0:T(8,128)}, f32[96,768]{1,0:T(8,128)}, f32[8,24]{1,0:T(8,128)}, /*index=5*/f32[1,96]{1,0:T(1,128)}, f32[64,24]{1,0:T(8,128)}) custom-call(bf16[4,4,48,768]{3,2,1,0:T(8,128)(2,1)} %shard_map.318.mine_ref, bf16[4,4,48,768]{3,2,1,0:T(8,128)(2,1)} %collective-permute-done.68.other_ref, ...), custom_call_target="tpu_custom_call" | custom-call | tf_op jit(solution)/shard_map/pallas_call | solution.py:719
  (204 shorter events, 149.4 us)
Async XLA Ops:
  3.1 16.2 %collective-permute-start.2 = (bf16[24,3200]{1,0:T(8,128)(2,1)}, bf16[24,3200]{1,0:T(8,128)(2,1)}, u32[]{:S(2)}, u32[]{:S(2)}) collective-permute-start(bf16[24,3200]{1,0:T(8,128)(2,1)} %get-tuple-element.225.refs_0_), channel_id=1, source_target_pairs={{0,24},{8,0},{16,8},{24,16},{1,25},{9,1},{17,9},{25,17},{2,26},{10... | collective-permute-start | bytes 460808 | tf_op jit(solution)/shard_map/ppermute | solution.py:448
  23.4 21.5 %collective-permute-start.10 = (bf16[4,24,3200]{2,1,0:T(8,128)(2,1)}, bf16[4,24,3200]{2,1,0:T(8,128)(2,1)}, u32[]{:S(2)}, u32[]{:S(2)}) collective-permute-start(bf16[4,24,3200]{2,1,0:T(8,128)(2,1)} %shard_map.290.refs_0_), channel_id=1, source_target_pairs={{0,4},{1,3},{2,6},{3,1},{4,0},{5,7},{6,2},{7,5},{8,12},{9,11},{10,... | collective-permute-start | bytes 1843208 | tf_op jit(solution)/shard_map/ppermute | solution.py:464
  25.0 19.9 %collective-permute-start.9 = (bf16[4,24,3200]{2,1,0:T(8,128)(2,1)}, bf16[4,24,3200]{2,1,0:T(8,128)(2,1)}, u32[]{:S(2)}, u32[]{:S(2)}) collective-permute-start(bf16[4,24,3200]{2,1,0:T(8,128)(2,1)} %shard_map.290.refs_0_), channel_id=1, source_target_pairs={{0,2},{1,5},{2,0},{3,7},{4,6},{5,1},{6,4},{7,3},{8,10},{9,13},{10,... | collective-permute-start | bytes 1843208 | tf_op jit(solution)/shard_map/ppermute | solution.py:460
  27.8 17.1 %collective-permute-start.7 = (bf16[24,3840]{1,0:T(8,128)(2,1)}, bf16[24,3840]{1,0:T(8,128)(2,1)}, u32[]{:S(2)}, u32[]{:S(2)}) collective-permute-start(bf16[24,3840]{1,0:T(8,128)(2,1)} %get-tuple-element.238.refs_0_), channel_id=1, source_target_pairs={{0,16},{8,24},{16,0},{24,8},{1,17},{9,25},{17,1},{25,9},{2,18},{10... | collective-permute-start | bytes 552968 | tf_op jit(solution)/shard_map/ppermute | solution.py:448
  29.3 15.6 %collective-permute-start.6 = (bf16[24,3840]{1,0:T(8,128)(2,1)}, bf16[24,3840]{1,0:T(8,128)(2,1)}, u32[]{:S(2)}, u32[]{:S(2)}) collective-permute-start(bf16[24,3840]{1,0:T(8,128)(2,1)} %get-tuple-element.238.refs_0_), channel_id=1, source_target_pairs={{0,8},{8,16},{16,24},{24,0},{1,9},{9,17},{17,25},{25,1},{2,10},{10... | collective-permute-start | bytes 552968 | tf_op jit(solution)/shard_map/ppermute | solution.py:448
  44.9 15.0 %collective-permute-start.13 = (bf16[4,24,3200]{2,1,0:T(8,128)(2,1)}, bf16[4,24,3200]{2,1,0:T(8,128)(2,1)}, u32[]{:S(2)}, u32[]{:S(2)}) collective-permute-start(bf16[4,24,3200]{2,1,0:T(8,128)(2,1)} %shard_map.290.refs_0_), channel_id=1, source_target_pairs={{0,1},{1,0},{2,3},{3,2},{4,5},{5,4},{6,7},{7,6},{8,9},{9,8},{10,11... | collective-permute-start | bytes 1843208 | tf_op jit(solution)/shard_map/ppermute | solution.py:452
  45.0 14.9 %collective-permute-start.15 = (bf16[4,24,3200]{2,1,0:T(8,128)(2,1)}, bf16[4,24,3200]{2,1,0:T(8,128)(2,1)}, u32[]{:S(2)}, u32[]{:S(2)}) collective-permute-start(bf16[4,24,3200]{2,1,0:T(8,128)(2,1)} %collective-permute-done.10.refs_2_), channel_id=1, source_target_pairs={{0,1},{1,0},{2,3},{3,2},{4,5},{5,4},{6,7},{7,6},{8,9},{9,8},{10,11... | collective-permute-start | bytes 1843208 | tf_op jit(solution)/shard_map/ppermute | solution.py:452
  45.5 14.4 %collective-permute-start.14 = (bf16[4,24,3200]{2,1,0:T(8,128)(2,1)}, bf16[4,24,3200]{2,1,0:T(8,128)(2,1)}, u32[]{:S(2)}, u32[]{:S(2)}) collective-permute-start(bf16[4,24,3200]{2,1,0:T(8,128)(2,1)} %collective-permute-done.9.refs_1_), channel_id=1, source_target_pairs={{0,1},{1,0},{2,3},{3,2},{4,5},{5,4},{6,7},{7,6},{8,9},{9,8},{10,11... | collective-permute-start | bytes 1843208 | tf_op jit(solution)/shard_map/ppermute | solution.py:452
  45.6 14.4 %collective-permute-start.11 = (bf16[4,24,3200]{2,1,0:T(8,128)(2,1)}, bf16[4,24,3200]{2,1,0:T(8,128)(2,1)}, u32[]{:S(2)}, u32[]{:S(2)}) collective-permute-start(bf16[4,24,3200]{2,1,0:T(8,128)(2,1)} %collective-permute-done.9.refs_1_), channel_id=1, source_target_pairs={{0,4},{1,3},{2,6},{3,1},{4,0},{5,7},{6,2},{7,5},{8,12},{9,11},{10,... | collective-permute-start | bytes 1843208 | tf_op jit(solution)/shard_map/ppermute | solution.py:464
  46.1 13.8 %collective-permute-start.12 = (bf16[4,24,2176]{2,1,0:T(8,128)(2,1)}, bf16[4,24,2176]{2,1,0:T(8,128)(2,1)}, u32[]{:S(2)}, u32[]{:S(2)}) collective-permute-start(bf16[4,24,2176]{2,1,0:T(8,128)(2,1)} %shard_map.291.refs_0_), channel_id=1, source_target_pairs={{0,8},{8,16},{16,24},{24,0},{1,9},{9,17},{17,25},{25,1},{2,10},{10... | collective-permute-start | bytes 1253384 | tf_op jit(solution)/shard_map/ppermute | solution.py:448
  62.4 19.6 %collective-permute-start.21 = (bf16[4,24,3840]{2,1,0:T(8,128)(2,1)}, bf16[4,24,3840]{2,1,0:T(8,128)(2,1)}, u32[]{:S(2)}, u32[]{:S(2)}) collective-permute-start(bf16[4,24,3840]{2,1,0:T(8,128)(2,1)} %shard_map.292.refs_0_), channel_id=1, source_target_pairs={{0,4},{1,3},{2,6},{3,1},{4,0},{5,7},{6,2},{7,5},{8,12},{9,11},{10,... | collective-permute-start | bytes 2211848 | tf_op jit(solution)/shard_map/ppermute | solution.py:464
  62.9 19.1 %collective-permute-start.20 = (bf16[4,24,3840]{2,1,0:T(8,128)(2,1)}, bf16[4,24,3840]{2,1,0:T(8,128)(2,1)}, u32[]{:S(2)}, u32[]{:S(2)}) collective-permute-start(bf16[4,24,3840]{2,1,0:T(8,128)(2,1)} %shard_map.292.refs_0_), channel_id=1, source_target_pairs={{0,2},{1,5},{2,0},{3,7},{4,6},{5,1},{6,4},{7,3},{8,10},{9,13},{10,... | collective-permute-start | bytes 2211848 | tf_op jit(solution)/shard_map/ppermute | solution.py:460
  64.4 14.0 %collective-permute-start.19 = (bf16[24,3072]{1,0:T(8,128)(2,1)}, bf16[24,3072]{1,0:T(8,128)(2,1)}, u32[]{:S(2)}, u32[]{:S(2)}) collective-permute-start(bf16[24,3072]{1,0:T(8,128)(2,1)} %get-tuple-element.261.refs_0_), channel_id=1, source_target_pairs={{0,24},{8,0},{16,8},{24,16},{1,25},{9,1},{17,9},{25,17},{2,26},{10... | collective-permute-start | bytes 442376 | tf_op jit(solution)/shard_map/ppermute | solution.py:448
  64.4 14.0 %collective-permute-start.18 = (bf16[24,3072]{1,0:T(8,128)(2,1)}, bf16[24,3072]{1,0:T(8,128)(2,1)}, u32[]{:S(2)}, u32[]{:S(2)}) collective-permute-start(bf16[24,3072]{1,0:T(8,128)(2,1)} %get-tuple-element.261.refs_0_), channel_id=1, source_target_pairs={{0,16},{8,24},{16,0},{24,8},{1,17},{9,25},{17,1},{25,9},{2,18},{10... | collective-permute-start | bytes 442376 | tf_op jit(solution)/shard_map/ppermute | solution.py:448
  64.4 14.1 %collective-permute-start.17 = (bf16[24,3072]{1,0:T(8,128)(2,1)}, bf16[24,3072]{1,0:T(8,128)(2,1)}, u32[]{:S(2)}, u32[]{:S(2)}) collective-permute-start(bf16[24,3072]{1,0:T(8,128)(2,1)} %get-tuple-element.261.refs_0_), channel_id=1, source_target_pairs={{0,8},{8,16},{16,24},{24,0},{1,9},{9,17},{17,25},{25,1},{2,10},{10... | collective-permute-start | bytes 442376 | tf_op jit(solution)/shard_map/ppermute | solution.py:448
  82.0 15.4 %collective-permute-start.24 = (bf16[4,24,3840]{2,1,0:T(8,128)(2,1)}, bf16[4,24,3840]{2,1,0:T(8,128)(2,1)}, u32[]{:S(2)}, u32[]{:S(2)}) collective-permute-start(bf16[4,24,3840]{2,1,0:T(8,128)(2,1)} %shard_map.292.refs_0_), channel_id=1, source_target_pairs={{0,1},{1,0},{2,3},{3,2},{4,5},{5,4},{6,7},{7,6},{8,9},{9,8},{10,11... | collective-permute-start | bytes 2211848 | tf_op jit(solution)/shard_map/ppermute | solution.py:452
  82.2 15.3 %collective-permute-start.26 = (bf16[4,24,3840]{2,1,0:T(8,128)(2,1)}, bf16[4,24,3840]{2,1,0:T(8,128)(2,1)}, u32[]{:S(2)}, u32[]{:S(2)}) collective-permute-start(bf16[4,24,3840]{2,1,0:T(8,128)(2,1)} %collective-permute-done.21.refs_2_), channel_id=1, source_target_pairs={{0,1},{1,0},{2,3},{3,2},{4,5},{5,4},{6,7},{7,6},{8,9},{9,8},{10,11... | collective-permute-start | bytes 2211848 | tf_op jit(solution)/shard_map/ppermute | solution.py:452
  82.6 14.9 %collective-permute-start.25 = (bf16[4,24,3840]{2,1,0:T(8,128)(2,1)}, bf16[4,24,3840]{2,1,0:T(8,128)(2,1)}, u32[]{:S(2)}, u32[]{:S(2)}) collective-permute-start(bf16[4,24,3840]{2,1,0:T(8,128)(2,1)} %collective-permute-done.20.refs_1_), channel_id=1, source_target_pairs={{0,1},{1,0},{2,3},{3,2},{4,5},{5,4},{6,7},{7,6},{8,9},{9,8},{10,11... | collective-permute-start | bytes 2211848 | tf_op jit(solution)/shard_map/ppermute | solution.py:452
  82.7 14.8 %collective-permute-start.23 = (bf16[4,24,3840]{2,1,0:T(8,128)(2,1)}, bf16[4,24,3840]{2,1,0:T(8,128)(2,1)}, u32[]{:S(2)}, u32[]{:S(2)}) collective-permute-start(bf16[4,24,3840]{2,1,0:T(8,128)(2,1)} %collective-permute-done.20.refs_1_), channel_id=1, source_target_pairs={{0,4},{1,3},{2,6},{3,1},{4,0},{5,7},{6,2},{7,5},{8,12},{9,11},{10,... | collective-permute-start | bytes 2211848 | tf_op jit(solution)/shard_map/ppermute | solution.py:464
  82.9 14.5 %collective-permute-start.22 = (bf16[4,24,2176]{2,1,0:T(8,128)(2,1)}, bf16[4,24,2176]{2,1,0:T(8,128)(2,1)}, u32[]{:S(2)}, u32[]{:S(2)}) collective-permute-start(bf16[4,24,2176]{2,1,0:T(8,128)(2,1)} %collective-permute-done.12.refs_1_), channel_id=1, source_target_pairs={{0,8},{8,16},{16,24},{24,0},{1,9},{9,17},{17,25},{25,1},{2,10},{10... | collective-permute-start | bytes 1253384 | tf_op jit(solution)/shard_map/ppermute | solution.py:448
  97.5 16.3 %collective-permute-start.29 = (bf16[4,24,3072]{2,1,0:T(8,128)(2,1)}, bf16[4,24,3072]{2,1,0:T(8,128)(2,1)}, u32[]{:S(2)}, u32[]{:S(2)}) collective-permute-start(bf16[4,24,3072]{2,1,0:T(8,128)(2,1)} %shard_map.295.refs_0_), channel_id=1, source_target_pairs={{0,4},{1,3},{2,6},{3,1},{4,0},{5,7},{6,2},{7,5},{8,12},{9,11},{10,... | collective-permute-start | bytes 1769480 | tf_op jit(solution)/shard_map/ppermute | solution.py:464
  98.1 15.8 %collective-permute-start.28 = (bf16[4,24,3072]{2,1,0:T(8,128)(2,1)}, bf16[4,24,3072]{2,1,0:T(8,128)(2,1)}, u32[]{:S(2)}, u32[]{:S(2)}) collective-permute-start(bf16[4,24,3072]{2,1,0:T(8,128)(2,1)} %shard_map.295.refs_0_), channel_id=1, source_target_pairs={{0,2},{1,5},{2,0},{3,7},{4,6},{5,1},{6,4},{7,3},{8,10},{9,13},{10,... | collective-permute-start | bytes 1769480 | tf_op jit(solution)/shard_map/ppermute | solution.py:460
  207.3 18.6 %collective-permute-start.59 = (bf16[4,4,24,3072]{3,2,1,0:T(8,128)(2,1)}, bf16[4,4,24,3072]{3,2,1,0:T(8,128)(2,1)}, u32[]{:S(2)}, u32[]{:S(2)}) collective-permute-start(bf16[4,4,24,3072]{3,2,1,0:T(8,128)(2,1)} %bitcast.72), channel_id=1, source_target_pairs={{0,1},{1,0},{2,3},{3,2},{4,5},{5,4},{6,7},{7,6},{8,9},{9,8},{10,11... | collective-permute-start | bytes 7077896 | tf_op jit(solution)/shard_map/ppermute | solution.py:452
  210.0 18.7 %collective-permute-start.58 = (bf16[2,4,96,768]{3,2,1,0:T(8,128)(2,1)}, bf16[2,4,96,768]{3,2,1,0:T(8,128)(2,1)}, u32[]{:S(2)}, u32[]{:S(2)}) collective-permute-start(bf16[2,4,96,768]{3,2,1,0:T(8,128)(2,1)} %shard_map.312), channel_id=1, source_target_pairs={{0,2},{1,5},{2,0},{3,7},{4,6},{5,1},{6,4},{7,3},{8,10},{9,13},{10,... | collective-permute-start | bytes 3538952 | tf_op jit(solution)/shard_map/ppermute | solution.py:460
  213.0 15.7 %collective-permute-start.61 = (bf16[4,48,768]{2,1,0:T(8,128)(2,1)}, bf16[4,48,768]{2,1,0:T(8,128)(2,1)}, u32[]{:S(2)}, u32[]{:S(2)}) collective-permute-start(bf16[4,48,768]{2,1,0:T(8,128)(2,1)} %shard_map.314.refs_0_), channel_id=1, source_target_pairs={{0,24},{8,0},{16,8},{24,16},{1,25},{9,1},{17,9},{25,17},{2,26},{10... | collective-permute-start | bytes 884744 | tf_op jit(solution)/shard_map/ppermute | solution.py:448
  214.5 14.2 %collective-permute-start.60 = (bf16[4,48,768]{2,1,0:T(8,128)(2,1)}, bf16[4,48,768]{2,1,0:T(8,128)(2,1)}, u32[]{:S(2)}, u32[]{:S(2)}) collective-permute-start(bf16[4,48,768]{2,1,0:T(8,128)(2,1)} %shard_map.314.refs_0_), channel_id=1, source_target_pairs={{0,8},{8,16},{16,24},{24,0},{1,9},{9,17},{17,25},{25,1},{2,10},{10... | collective-permute-start | bytes 884744 | tf_op jit(solution)/shard_map/ppermute | solution.py:448
  228.7 16.5 %collective-permute-start.62 = (bf16[2,4,24,3072]{3,2,1,0:T(8,128)(2,1)}, bf16[2,4,24,3072]{3,2,1,0:T(8,128)(2,1)}, u32[]{:S(2)}, u32[]{:S(2)}) collective-permute-start(bf16[2,4,24,3072]{3,2,1,0:T(8,128)(2,1)} %shard_map.313), channel_id=1, source_target_pairs={{0,2},{1,5},{2,0},{3,7},{4,6},{5,1},{6,4},{7,3},{8,10},{9,13},{10,... | collective-permute-start | bytes 3538952 | tf_op jit(solution)/shard_map/ppermute | solution.py:460
  229.4 15.8 %collective-permute-start.63 = (bf16[4,48,768]{2,1,0:T(8,128)(2,1)}, bf16[4,48,768]{2,1,0:T(8,128)(2,1)}, u32[]{:S(2)}, u32[]{:S(2)}) collective-permute-start(bf16[4,48,768]{2,1,0:T(8,128)(2,1)} %shard_map.314.refs_0_), channel_id=1, source_target_pairs={{0,16},{8,24},{16,0},{24,8},{1,17},{9,25},{17,1},{25,9},{2,18},{10... | collective-permute-start | bytes 884744 | tf_op jit(solution)/shard_map/ppermute | solution.py:448
  265.6 17.0 %collective-permute-start.67 = (bf16[2,4,24,3200]{3,2,1,0:T(8,128)(2,1)}, bf16[2,4,24,3200]{3,2,1,0:T(8,128)(2,1)}, u32[]{:S(2)}, u32[]{:S(2)}) collective-permute-start(bf16[2,4,24,3200]{3,2,1,0:T(8,128)(2,1)} %shard_map.319), channel_id=1, source_target_pairs={{0,2},{1,5},{2,0},{3,7},{4,6},{5,1},{6,4},{7,3},{8,10},{9,13},{10,... | collective-permute-start | bytes 3686408 | tf_op jit(solution)/shard_map/ppermute | solution.py:460
  266.8 14.8 %collective-permute-start.68 = (bf16[4,4,48,768]{3,2,1,0:T(8,128)(2,1)}, bf16[4,4,48,768]{3,2,1,0:T(8,128)(2,1)}, u32[]{:S(2)}, u32[]{:S(2)}) collective-permute-start(bf16[4,4,48,768]{3,2,1,0:T(8,128)(2,1)} %shard_map.318.mine_ref), channel_id=1, source_target_pairs={{0,1},{1,0},{2,3},{3,2},{4,5},{5,4},{6,7},{7,6},{8,9},{9,8},{10,11... | collective-permute-start | bytes 3538952 | tf_op jit(solution)/shard_map/ppermute | solution.py:452
  285.1 14.5 %collective-permute-start.72 = (bf16[4,24,3200]{2,1,0:T(8,128)(2,1)}, bf16[4,24,3200]{2,1,0:T(8,128)(2,1)}, u32[]{:S(2)}, u32[]{:S(2)}) collective-permute-start(bf16[4,24,3200]{2,1,0:T(8,128)(2,1)} %shard_map.322), channel_id=1, source_target_pairs={{0,4},{1,3},{2,6},{3,1},{4,0},{5,7},{6,2},{7,5},{8,12},{9,11},{10,... | collective-permute-start | bytes 1843208 | tf_op jit(solution)/shard_map/ppermute | solution.py:464
  302.4 13.9 %collective-permute-start.76 = (bf16[24,3200]{1,0:T(8,128)(2,1)}, bf16[24,3200]{1,0:T(8,128)(2,1)}, u32[]{:S(2)}, u32[]{:S(2)}) collective-permute-start(bf16[24,3200]{1,0:T(8,128)(2,1)} %get-tuple-element.403), channel_id=1, source_target_pairs={{0,8},{8,16},{16,24},{24,0},{1,9},{9,17},{17,25},{25,1},{2,10},{10... | collective-permute-start | bytes 460808 | tf_op jit(solution)/shard_map/ppermute | solution.py:448
  (62 other events, 378.9 us)

commit v6 on v5

--- a/solution.py
+++ b/solution.py
@@ -1678,7 +1678,7 @@
     mix_last = swap_two(mix_total.second(mix_back))
     up_others = send_dp(up_others)
     down_sum = down_total.total(down_others)
-    mix_last, down_sum, other_rows, *up_others = stage(mix_last, down_sum, other_rows, *up_others)
+    mix_last, down_sum, other_rows = stage(mix_last, down_sum, other_rows)
 
     mix_others = send_dp(mix_total.third(mix_last))
     up_sum = up_total.total(up_others)

time: 322 us -> 317 us (0.984)
  waiting for transfers between devices: 96.3 us -> 92.4 us
    ppermute x24, waiting for transfers between devices: 50.4 us -> 43.7 us  [swap_dp(): lax.ppermute(array_in, 'dp', [(i, (i + shift) % 4) for i in range(4)])]
  transfers between devices with their start and end apart: 79 -> 79, of which waited for: 37 -> 36; matrix products, arithmetic and copies ran while one was open for 3% -> 3% of each run, Pallas kernels for 34% -> 35%
where the time goes in v6:
time: 317 us; the launch traced here: 315 us
  Pallas kernels  129 us (41%)
  waiting for transfers between devices  92.4 us (29%)
  starting transfers between devices  73.3 us (23%)
  local copies, waits for them, and re-layouts  14.6 us (5%)
  other arithmetic  3.85 us (1%)
    pallas_call x17, Pallas kernels, on_core(): pl.pallas_call(kernel, out_shape=out_shape, grid=grid, scratch_shapes=scr...  74.9 us
    ppermute x24, waiting for transfers between devices, swap_dp(): lax.ppermute(array_in, 'dp', [(i, (i + shift) % 4) for i in range(4)])  43.7 us
    pallas_call x11, Pallas kernels, copies(): pl.pallas_call(kernel, out_shape=[jax.ShapeDtypeStruct(shape, pieces[0].d...  31.1 us
    ppermute x24, starting transfers between devices, swap_dp(): lax.ppermute(array_in, 'dp', [(i, (i + shift) % 4) for i in range(4)])  30.1 us
    pallas_call x9, Pallas kernels, run(): pl.pallas_call(kernel, out_shape=out_shapes, in_specs=[far] * count, out_...  23.4 us
    ppermute x18, starting transfers between devices, swap_chip(): return lax.ppermute(array_in, 'seq', [(i, i ^ 2 * mask) for i in range(8)])  23.1 us
    ppermute x11, waiting for transfers between devices, swap_two(): lax.ppermute(array_in, 'seq', [(i, i ^ (4 if i % 2 == 0 else 2)) for i in...  21.7 us
    ppermute x18, waiting for transfers between devices, swap_chip(): return lax.ppermute(array_in, 'seq', [(i, i ^ 2 * mask) for i in range(8)])  18.6 us
  transfers between devices with their start and end apart: 79, of which 36 were waited for; matrix products, arithmetic and copies ran while one was open for 3% of the time, Pallas kernels for 35%

profile of v6, /device:TPU:0, one launch (start us, length us, event | category | flops | bytes accessed | tf_op | source)
XLA Modules:
  0.0 314.6 jit_solution(11028239612807008645)
XLA Ops:
  3.1 5.1 %collective-permute-start.2 = (bf16[24,3200]{1,0:T(8,128)(2,1)}, bf16[24,3200]{1,0:T(8,128)(2,1)}, u32[]{:S(2)}, u32[]{:S(2)}) collective-permute-start(bf16[24,3200]{1,0:T(8,128)(2,1)} %get-tuple-element.222.refs_0_), channel_id=1, source_target_pairs={{0,24},{8,0},{16,8},{24,16},{1,25},{9,1},{17,9},{25,17},{2,26},{10... | collective-permute-start | bytes 460808 | tf_op jit(solution)/shard_map/ppermute | solution.py:448
  16.3 3.1 collective-permute-done.5.refs_3_
  33.2 11.7 %collective-permute-done.7.refs_2_ = bf16[24,3840]{1,0:T(8,128)(2,1)} collective-permute-done((bf16[24,3840]{1,0:T(8,128)(2,1)}, bf16[24,3840]{1,0:T(8,128)(2,1)}, u32[]{:S(2)}, u32[]{:S(2)}) %collective-permute-start.7) | collective-permute-done | bytes 184352 | tf_op jit(solution)/shard_map/ppermute | solution.py:448
  48.0 11.9 %collective-permute-done.12.refs_1_ = bf16[4,24,2176]{2,1,0:T(8,128)(2,1)} collective-permute-done((bf16[4,24,2176]{2,1,0:T(8,128)(2,1)}, bf16[4,24,2176]{2,1,0:T(8,128)(2,1)}, u32[]{:S(2)}, u32[]{:S(2)}) %collective-permute-start.12) | collective-permute-done | bytes 417824 | tf_op jit(solution)/shard_map/ppermute | solution.py:448
  66.5 4.3 %shard_map.293 = bf16[4,4,2,24,3200]{4,3,2,1,0:T(8,128)(2,1)} custom-call(bf16[4,24,3200]{2,1,0:T(8,128)(2,1)} %shard_map.290.refs_0_, bf16[4,24,3200]{2,1,0:T(8,128)(2,1)} %collective-permute-done.9.refs_1_, bf16[4,24,3200]{2,1,0:T(8,128)(2,1)} %collective-permute-done.10.refs_2_, bf16[4,24,3200]{2,1,0:T(8,128)(2,1)} %collective-permute-done.11.refs_3_, ...), custom_call_target="tpu_custom_call" | custom-call | tf_op jit(solution)/shard_map/pallas_call | solution.py:510
  70.8 7.7 %shard_map.294 = (bf16[256,2304]{1,0:T(8,128)(2,1)}, bf16[128,768]{1,0:T(8,128)(2,1)}, f32[12,128,128]{2,1,0:T(8,128)}, f32[128,768]{1,0:T(8,128)}, f32[2,768]{1,0:T(2,128)}) custom-call(bf16[256,768]{1,0:T(8,128)(2,1)} %bitcast.61, bf16[768,3200]{1,0:T(8,128)(2,1)} %bitcast.41, s32[2,128]{1,0:T(2,128)} %docs_ref.4, s32[1,2]{1,0:T(1,128)} %bitcast.39), custom_call_target="tpu_custom_call" | custom-call | tf_op jit(solution)/shard_map/pallas_call | solution.py:719
  78.5 3.5 %collective-permute-done.21.refs_2_ = bf16[4,24,3840]{2,1,0:T(8,128)(2,1)} collective-permute-done((bf16[4,24,3840]{2,1,0:T(8,128)(2,1)}, bf16[4,24,3840]{2,1,0:T(8,128)(2,1)}, u32[]{:S(2)}, u32[]{:S(2)}) %collective-permute-start.21) | collective-permute-done | bytes 737312 | tf_op jit(solution)/shard_map/ppermute | solution.py:464
  85.2 6.9 %shard_map.296 = (bf16[256,768]{1,0:T(8,128)(2,1)}, f32[12,128,128]{2,1,0:T(8,128)}, f32[256,768]{1,0:T(8,128)}, f32[256,1]{1,0:T(8,128)}, bf16[256,768]{1,0:T(8,128)(2,1)}) custom-call(bf16[256,768]{1,0:T(8,128)(2,1)} %bitcast.62, bf16[256,2304]{1,0:T(8,128)(2,1)} %get-tuple-element.262.mixed_ref, bf16[128,768]{1,0:T(8,128)(2,1)} %get-tuple-element.263.before_ref, ...), custom_call_target="tpu_custom_call" | custom-call | tf_op jit(solution)/shard_map/pallas_call | solution.py:719
  94.0 3.4 %collective-permute-done.22.refs_2_ = bf16[4,24,2176]{2,1,0:T(8,128)(2,1)} collective-permute-done((bf16[4,24,2176]{2,1,0:T(8,128)(2,1)}, bf16[4,24,2176]{2,1,0:T(8,128)(2,1)}, u32[]{:S(2)}, u32[]{:S(2)}) %collective-permute-start.22) | collective-permute-done | bytes 417824 | tf_op jit(solution)/shard_map/ppermute | solution.py:448
  100.1 5.4 %shard_map.297 = (bf16[4,4,2,24,3072]{4,3,2,1,0:T(8,128)(2,1)}, bf16[4,4,2,24,768]{4,3,2,1,0:T(8,128)(2,1)}) custom-call(bf16[4,24,3840]{2,1,0:T(8,128)(2,1)} %shard_map.292.refs_0_, bf16[4,24,3840]{2,1,0:T(8,128)(2,1)} %collective-permute-done.20.refs_1_, bf16[4,24,3840]{2,1,0:T(8,128)(2,1)} %collective-permute-done.21.refs_2_, ...), custom_call_target="tpu_custom_call" | custom-call | tf_op jit(solution)/shard_map/pallas_call | solution.py:510
  105.5 6.4 %shard_map.298 = (bf16[256,3072]{1,0:T(8,128)(2,1)}, bf16[256,3072]{1,0:T(8,128)(2,1)}) custom-call(bf16[256,768]{1,0:T(8,128)(2,1)} %get-tuple-element.268.low_ref, bf16[768,3072]{1,0:T(8,128)(2,1)} %bitcast.56, f32[1,3072]{1,0:T(1,128)} %reshape.119.bias_ref), custom_call_target="tpu_custom_call" | custom-call | tf_op jit(solution)/shard_map/pallas_call | solution.py:719
  119.0 5.7 %collective-permute-done.31.refs_3_ = bf16[4,24,3072]{2,1,0:T(8,128)(2,1)} collective-permute-done((bf16[4,24,3072]{2,1,0:T(8,128)(2,1)}, bf16[4,24,3072]{2,1,0:T(8,128)(2,1)}, u32[]{:S(2)}, u32[]{:S(2)}) %collective-permute-start.31) | collective-permute-done | bytes 589856 | tf_op jit(solution)/shard_map/ppermute | solution.py:464
  127.0 4.6 %shard_map.300 = bf16[4,4,2,4,24,768]{5,4,3,2,1,0:T(8,128)(2,1)} custom-call(bf16[4,24,3072]{2,1,0:T(8,128)(2,1)} %shard_map.295.refs_0_, bf16[4,24,3072]{2,1,0:T(8,128)(2,1)} %collective-permute-done.28.refs_1_, bf16[4,24,3072]{2,1,0:T(8,128)(2,1)} %collective-permute-done.29.refs_2_, bf16[4,24,3072]{2,1,0:T(8,128)(2,1)} %collective-permute-done.31.refs_3_, ...), custom_call_target="tpu_custom_call" | custom-call | tf_op jit(solution)/shard_map/pallas_call | solution.py:510
  131.9 5.3 %shard_map.301 = (f32[256,768]{1,0:T(8,128)}, f32[256,1]{1,0:T(8,128)}, f32[8,768]{1,0:T(8,128)}, f32[8,768]{1,0:T(8,128)}) custom-call(bf16[256,3072]{1,0:T(8,128)(2,1)} %get-tuple-element.279.active_ref, bf16[3072,768]{1,0:T(8,128)(2,1)} %bitcast.45, f32[256,768]{1,0:T(8,128)} %get-tuple-element.291.first_ref.n_ref, ...), custom_call_target="tpu_custom_call" | custom-call | tf_op jit(solution)/shard_map/pallas_call | solution.py:719
  137.6 3.3 %shard_map.302 = (bf16[4,4,2,24,768]{4,3,2,1,0:T(8,128)(2,1)}, bf16[4,4,2,24,640]{4,3,2,1,0:T(8,128)(2,1)}, bf16[4,2,4,24,768]{4,3,2,1,0:T(8,128)(2,1)}) custom-call(bf16[4,4,24,2176]{3,2,1,0:T(8,128)(2,1)} %shard_map.299.refs_0_, bf16[4,4,24,2176]{3,2,1,0:T(8,128)(2,1)} %collective-permute-done.36.refs_1_), custom_call_target="tpu_custom_call" | custom-call | tf_op jit(solution)/shard_map/pallas_call | solution.py:510
  190.9 8.3 %shard_map.309 = (bf16[256,768]{1,0:T(8,128)(2,1)}, f32[256,768]{1,0:T(8,128)}, bf16[16,96,768]{2,1,0:T(8,128)(2,1)}, bf16[16,96,768]{2,1,0:T(8,128)(2,1)}, bf16...) custom-call(bf16[256,768]{1,0:T(8,128)(2,1)} %bitcast.60, f32[8,768]{1,0:T(8,128)} %copy-done.9, ...), custom_call_target="tpu_custom_call" | custom-call | tf_op jit(solution)/shard_map/pallas_call | solution.py:719
  200.3 7.0 %shard_map.310 = (bf16[16,24,3072]{2,1,0:T(8,128)(2,1)}, bf16[16,24,3072]{2,1,0:T(8,128)(2,1)}, f32[256,768]{1,0:T(8,128)}) custom-call(bf16[256,768]{1,0:T(8,128)(2,1)} %get-tuple-element.268.low_ref, bf16[256,3072]{1,0:T(8,128)(2,1)} %get-tuple-element.338.hidden_ref, bf16[768,3072]{1,0:T(8,128)(2,1)} %bitcast.57, f32[256,768]{1,0:T(8,128)} %get-tuple-element.339.second_ref), custom_call_target="tpu_custom_call" | custom-call | tf_op jit(solution)/shard_map/pallas_call | solution.py:719
  207.4 2.7 shard_map.312
  215.1 10.7 %shard_map.311 = (bf16[768,768]{1,0:T(8,128)(2,1)}, f32[256,768]{1,0:T(8,128)}, f32[8,768]{1,0:T(8,128)}, bf16[256,2304]{1,0:T(8,128)(2,1)}) custom-call(f32[256,768]{1,0:T(8,128)} %get-tuple-element.343.first_ref, f32[256,768]{1,0:T(8,128)} %get-tuple-element.291.first_ref.n_ref, f32[256,1]{1,0:T(8,128)} %get-tuple-element.344.scale_ref, ...), custom_call_target="tpu_custom_call" | custom-call | tf_op jit(solution)/shard_map/pallas_call | solution.py:719
  225.8 2.6 shard_map.313
  233.2 7.9 %shard_map.315 = (f32[256,768]{1,0:T(8,128)}, bf16[16,24,3200]{2,1,0:T(8,128)(2,1)}, bf16[16,24,3200]{2,1,0:T(8,128)(2,1)}) custom-call(f32[256,768]{1,0:T(8,128)} %get-tuple-element.348.total_ref, bf16[256,2304]{1,0:T(8,128)(2,1)} %get-tuple-element.356.back_ref, bf16[256,768]{1,0:T(8,128)(2,1)} %bitcast.63, bf16[768,3200]{1,0:T(8,128)(2,1)} %bitcast.44, ...), custom_call_target="tpu_custom_call" | custom-call | tf_op jit(solution)/shard_map/pallas_call | solution.py:719
  241.2 4.0 %collective-permute-done.63.refs_2_ = bf16[4,48,768]{2,1,0:T(8,128)(2,1)} collective-permute-done((bf16[4,48,768]{2,1,0:T(8,128)(2,1)}, bf16[4,48,768]{2,1,0:T(8,128)(2,1)}, u32[]{:S(2)}, u32[]{:S(2)}) %collective-permute-start.63) | collective-permute-done | bytes 294944 | tf_op jit(solution)/shard_map/ppermute | solution.py:448
  250.8 4.7 %collective-permute-done.65.refs_3_ = bf16[4,96,768]{2,1,0:T(8,128)(2,1)} collective-permute-done((bf16[4,96,768]{2,1,0:T(8,128)(2,1)}, bf16[4,96,768]{2,1,0:T(8,128)(2,1)}, u32[]{:S(2)}, u32[]{:S(2)}) %collective-permute-start.65) | collective-permute-done | bytes 589856 | tf_op jit(solution)/shard_map/ppermute | solution.py:464
  256.5 2.7 shard_map.320
  259.2 2.7 shard_map.319
  261.9 3.7 %collective-permute-done.66.refs_3_ = bf16[4,24,3072]{2,1,0:T(8,128)(2,1)} collective-permute-done((bf16[4,24,3072]{2,1,0:T(8,128)(2,1)}, bf16[4,24,3072]{2,1,0:T(8,128)(2,1)}, u32[]{:S(2)}, u32[]{:S(2)}) %collective-permute-start.66) | collective-permute-done | bytes 589856 | tf_op jit(solution)/shard_map/ppermute | solution.py:464
  270.6 2.7 shard_map.321
  275.7 5.9 %collective-permute-done.70 = bf16[96,768]{1,0:T(8,128)(2,1)} collective-permute-done((bf16[96,768]{1,0:T(8,128)(2,1)}, bf16[96,768]{1,0:T(8,128)(2,1)}, u32[]{:S(2)}, u32[]{:S(2)}) %collective-permute-start.70) | collective-permute-done | bytes 147488 | tf_op jit(solution)/shard_map/ppermute | solution.py:448
  292.9 2.8 collective-permute-done.72.refs_3_
  295.7 2.7 shard_map.323
  298.4 2.6 collective-permute-start.73
  305.4 4.4 %shard_map.325 = (f32[24,2304]{1,0:T(8,128)}, f32[24,768]{1,0:T(8,128)}, f32[24,3072]{1,0:T(8,128)}, f32[96,768]{1,0:T(8,128)}, f32[8,24]{1,0:T(8,128)}, /*index=5*/f32[1,96]{1,0:T(1,128)}, f32[64,24]{1,0:T(8,128)}) custom-call(bf16[4,4,48,768]{3,2,1,0:T(8,128)(2,1)} %shard_map.318.mine_ref, bf16[4,4,48,768]{3,2,1,0:T(8,128)(2,1)} %collective-permute-done.68.other_ref, ...), custom_call_target="tpu_custom_call" | custom-call | tf_op jit(solution)/shard_map/pallas_call | solution.py:719
  (204 shorter events, 147.1 us)
Async XLA Ops:
  3.1 16.2 %collective-permute-start.2 = (bf16[24,3200]{1,0:T(8,128)(2,1)}, bf16[24,3200]{1,0:T(8,128)(2,1)}, u32[]{:S(2)}, u32[]{:S(2)}) collective-permute-start(bf16[24,3200]{1,0:T(8,128)(2,1)} %get-tuple-element.222.refs_0_), channel_id=1, source_target_pairs={{0,24},{8,0},{16,8},{24,16},{1,25},{9,1},{17,9},{25,17},{2,26},{10... | collective-permute-start | bytes 460808 | tf_op jit(solution)/shard_map/ppermute | solution.py:448
  23.4 21.5 %collective-permute-start.10 = (bf16[4,24,3200]{2,1,0:T(8,128)(2,1)}, bf16[4,24,3200]{2,1,0:T(8,128)(2,1)}, u32[]{:S(2)}, u32[]{:S(2)}) collective-permute-start(bf16[4,24,3200]{2,1,0:T(8,128)(2,1)} %shard_map.290.refs_0_), channel_id=1, source_target_pairs={{0,4},{1,3},{2,6},{3,1},{4,0},{5,7},{6,2},{7,5},{8,12},{9,11},{10,... | collective-permute-start | bytes 1843208 | tf_op jit(solution)/shard_map/ppermute | solution.py:464
  25.0 19.9 %collective-permute-start.9 = (bf16[4,24,3200]{2,1,0:T(8,128)(2,1)}, bf16[4,24,3200]{2,1,0:T(8,128)(2,1)}, u32[]{:S(2)}, u32[]{:S(2)}) collective-permute-start(bf16[4,24,3200]{2,1,0:T(8,128)(2,1)} %shard_map.290.refs_0_), channel_id=1, source_target_pairs={{0,2},{1,5},{2,0},{3,7},{4,6},{5,1},{6,4},{7,3},{8,10},{9,13},{10,... | collective-permute-start | bytes 1843208 | tf_op jit(solution)/shard_map/ppermute | solution.py:460
  27.8 17.1 %collective-permute-start.7 = (bf16[24,3840]{1,0:T(8,128)(2,1)}, bf16[24,3840]{1,0:T(8,128)(2,1)}, u32[]{:S(2)}, u32[]{:S(2)}) collective-permute-start(bf16[24,3840]{1,0:T(8,128)(2,1)} %get-tuple-element.235.refs_0_), channel_id=1, source_target_pairs={{0,16},{8,24},{16,0},{24,8},{1,17},{9,25},{17,1},{25,9},{2,18},{10... | collective-permute-start | bytes 552968 | tf_op jit(solution)/shard_map/ppermute | solution.py:448
  29.3 15.6 %collective-permute-start.6 = (bf16[24,3840]{1,0:T(8,128)(2,1)}, bf16[24,3840]{1,0:T(8,128)(2,1)}, u32[]{:S(2)}, u32[]{:S(2)}) collective-permute-start(bf16[24,3840]{1,0:T(8,128)(2,1)} %get-tuple-element.235.refs_0_), channel_id=1, source_target_pairs={{0,8},{8,16},{16,24},{24,0},{1,9},{9,17},{17,25},{25,1},{2,10},{10... | collective-permute-start | bytes 552968 | tf_op jit(solution)/shard_map/ppermute | solution.py:448
  44.9 15.0 %collective-permute-start.13 = (bf16[4,24,3200]{2,1,0:T(8,128)(2,1)}, bf16[4,24,3200]{2,1,0:T(8,128)(2,1)}, u32[]{:S(2)}, u32[]{:S(2)}) collective-permute-start(bf16[4,24,3200]{2,1,0:T(8,128)(2,1)} %shard_map.290.refs_0_), channel_id=1, source_target_pairs={{0,1},{1,0},{2,3},{3,2},{4,5},{5,4},{6,7},{7,6},{8,9},{9,8},{10,11... | collective-permute-start | bytes 1843208 | tf_op jit(solution)/shard_map/ppermute | solution.py:452
  45.0 14.9 %collective-permute-start.15 = (bf16[4,24,3200]{2,1,0:T(8,128)(2,1)}, bf16[4,24,3200]{2,1,0:T(8,128)(2,1)}, u32[]{:S(2)}, u32[]{:S(2)}) collective-permute-start(bf16[4,24,3200]{2,1,0:T(8,128)(2,1)} %collective-permute-done.10.refs_2_), channel_id=1, source_target_pairs={{0,1},{1,0},{2,3},{3,2},{4,5},{5,4},{6,7},{7,6},{8,9},{9,8},{10,11... | collective-permute-start | bytes 1843208 | tf_op jit(solution)/shard_map/ppermute | solution.py:452
  45.5 14.4 %collective-permute-start.14 = (bf16[4,24,3200]{2,1,0:T(8,128)(2,1)}, bf16[4,24,3200]{2,1,0:T(8,128)(2,1)}, u32[]{:S(2)}, u32[]{:S(2)}) collective-permute-start(bf16[4,24,3200]{2,1,0:T(8,128)(2,1)} %collective-permute-done.9.refs_1_), channel_id=1, source_target_pairs={{0,1},{1,0},{2,3},{3,2},{4,5},{5,4},{6,7},{7,6},{8,9},{9,8},{10,11... | collective-permute-start | bytes 1843208 | tf_op jit(solution)/shard_map/ppermute | solution.py:452
  45.6 14.4 %collective-permute-start.11 = (bf16[4,24,3200]{2,1,0:T(8,128)(2,1)}, bf16[4,24,3200]{2,1,0:T(8,128)(2,1)}, u32[]{:S(2)}, u32[]{:S(2)}) collective-permute-start(bf16[4,24,3200]{2,1,0:T(8,128)(2,1)} %collective-permute-done.9.refs_1_), channel_id=1, source_target_pairs={{0,4},{1,3},{2,6},{3,1},{4,0},{5,7},{6,2},{7,5},{8,12},{9,11},{10,... | collective-permute-start | bytes 1843208 | tf_op jit(solution)/shard_map/ppermute | solution.py:464
  46.1 13.8 %collective-permute-start.12 = (bf16[4,24,2176]{2,1,0:T(8,128)(2,1)}, bf16[4,24,2176]{2,1,0:T(8,128)(2,1)}, u32[]{:S(2)}, u32[]{:S(2)}) collective-permute-start(bf16[4,24,2176]{2,1,0:T(8,128)(2,1)} %shard_map.291.refs_0_), channel_id=1, source_target_pairs={{0,8},{8,16},{16,24},{24,0},{1,9},{9,17},{17,25},{25,1},{2,10},{10... | collective-permute-start | bytes 1253384 | tf_op jit(solution)/shard_map/ppermute | solution.py:448
  62.4 19.6 %collective-permute-start.21 = (bf16[4,24,3840]{2,1,0:T(8,128)(2,1)}, bf16[4,24,3840]{2,1,0:T(8,128)(2,1)}, u32[]{:S(2)}, u32[]{:S(2)}) collective-permute-start(bf16[4,24,3840]{2,1,0:T(8,128)(2,1)} %shard_map.292.refs_0_), channel_id=1, source_target_pairs={{0,4},{1,3},{2,6},{3,1},{4,0},{5,7},{6,2},{7,5},{8,12},{9,11},{10,... | collective-permute-start | bytes 2211848 | tf_op jit(solution)/shard_map/ppermute | solution.py:464
  62.9 19.1 %collective-permute-start.20 = (bf16[4,24,3840]{2,1,0:T(8,128)(2,1)}, bf16[4,24,3840]{2,1,0:T(8,128)(2,1)}, u32[]{:S(2)}, u32[]{:S(2)}) collective-permute-start(bf16[4,24,3840]{2,1,0:T(8,128)(2,1)} %shard_map.292.refs_0_), channel_id=1, source_target_pairs={{0,2},{1,5},{2,0},{3,7},{4,6},{5,1},{6,4},{7,3},{8,10},{9,13},{10,... | collective-permute-start | bytes 2211848 | tf_op jit(solution)/shard_map/ppermute | solution.py:460
  64.4 14.0 %collective-permute-start.19 = (bf16[24,3072]{1,0:T(8,128)(2,1)}, bf16[24,3072]{1,0:T(8,128)(2,1)}, u32[]{:S(2)}, u32[]{:S(2)}) collective-permute-start(bf16[24,3072]{1,0:T(8,128)(2,1)} %get-tuple-element.258.refs_0_), channel_id=1, source_target_pairs={{0,24},{8,0},{16,8},{24,16},{1,25},{9,1},{17,9},{25,17},{2,26},{10... | collective-permute-start | bytes 442376 | tf_op jit(solution)/shard_map/ppermute | solution.py:448
  64.4 14.0 %collective-permute-start.18 = (bf16[24,3072]{1,0:T(8,128)(2,1)}, bf16[24,3072]{1,0:T(8,128)(2,1)}, u32[]{:S(2)}, u32[]{:S(2)}) collective-permute-start(bf16[24,3072]{1,0:T(8,128)(2,1)} %get-tuple-element.258.refs_0_), channel_id=1, source_target_pairs={{0,16},{8,24},{16,0},{24,8},{1,17},{9,25},{17,1},{25,9},{2,18},{10... | collective-permute-start | bytes 442376 | tf_op jit(solution)/shard_map/ppermute | solution.py:448
  64.4 14.1 %collective-permute-start.17 = (bf16[24,3072]{1,0:T(8,128)(2,1)}, bf16[24,3072]{1,0:T(8,128)(2,1)}, u32[]{:S(2)}, u32[]{:S(2)}) collective-permute-start(bf16[24,3072]{1,0:T(8,128)(2,1)} %get-tuple-element.258.refs_0_), channel_id=1, source_target_pairs={{0,8},{8,16},{16,24},{24,0},{1,9},{9,17},{17,25},{25,1},{2,10},{10... | collective-permute-start | bytes 442376 | tf_op jit(solution)/shard_map/ppermute | solution.py:448
  82.0 15.4 %collective-permute-start.24 = (bf16[4,24,3840]{2,1,0:T(8,128)(2,1)}, bf16[4,24,3840]{2,1,0:T(8,128)(2,1)}, u32[]{:S(2)}, u32[]{:S(2)}) collective-permute-start(bf16[4,24,3840]{2,1,0:T(8,128)(2,1)} %shard_map.292.refs_0_), channel_id=1, source_target_pairs={{0,1},{1,0},{2,3},{3,2},{4,5},{5,4},{6,7},{7,6},{8,9},{9,8},{10,11... | collective-permute-start | bytes 2211848 | tf_op jit(solution)/shard_map/ppermute | solution.py:452
  82.2 15.3 %collective-permute-start.26 = (bf16[4,24,3840]{2,1,0:T(8,128)(2,1)}, bf16[4,24,3840]{2,1,0:T(8,128)(2,1)}, u32[]{:S(2)}, u32[]{:S(2)}) collective-permute-start(bf16[4,24,3840]{2,1,0:T(8,128)(2,1)} %collective-permute-done.21.refs_2_), channel_id=1, source_target_pairs={{0,1},{1,0},{2,3},{3,2},{4,5},{5,4},{6,7},{7,6},{8,9},{9,8},{10,11... | collective-permute-start | bytes 2211848 | tf_op jit(solution)/shard_map/ppermute | solution.py:452
  82.6 14.9 %collective-permute-start.25 = (bf16[4,24,3840]{2,1,0:T(8,128)(2,1)}, bf16[4,24,3840]{2,1,0:T(8,128)(2,1)}, u32[]{:S(2)}, u32[]{:S(2)}) collective-permute-start(bf16[4,24,3840]{2,1,0:T(8,128)(2,1)} %collective-permute-done.20.refs_1_), channel_id=1, source_target_pairs={{0,1},{1,0},{2,3},{3,2},{4,5},{5,4},{6,7},{7,6},{8,9},{9,8},{10,11... | collective-permute-start | bytes 2211848 | tf_op jit(solution)/shard_map/ppermute | solution.py:452
  82.7 14.8 %collective-permute-start.23 = (bf16[4,24,3840]{2,1,0:T(8,128)(2,1)}, bf16[4,24,3840]{2,1,0:T(8,128)(2,1)}, u32[]{:S(2)}, u32[]{:S(2)}) collective-permute-start(bf16[4,24,3840]{2,1,0:T(8,128)(2,1)} %collective-permute-done.20.refs_1_), channel_id=1, source_target_pairs={{0,4},{1,3},{2,6},{3,1},{4,0},{5,7},{6,2},{7,5},{8,12},{9,11},{10,... | collective-permute-start | bytes 2211848 | tf_op jit(solution)/shard_map/ppermute | solution.py:464
  82.9 14.5 %collective-permute-start.22 = (bf16[4,24,2176]{2,1,0:T(8,128)(2,1)}, bf16[4,24,2176]{2,1,0:T(8,128)(2,1)}, u32[]{:S(2)}, u32[]{:S(2)}) collective-permute-start(bf16[4,24,2176]{2,1,0:T(8,128)(2,1)} %collective-permute-done.12.refs_1_), channel_id=1, source_target_pairs={{0,8},{8,16},{16,24},{24,0},{1,9},{9,17},{17,25},{25,1},{2,10},{10... | collective-permute-start | bytes 1253384 | tf_op jit(solution)/shard_map/ppermute | solution.py:448
  97.5 16.3 %collective-permute-start.29 = (bf16[4,24,3072]{2,1,0:T(8,128)(2,1)}, bf16[4,24,3072]{2,1,0:T(8,128)(2,1)}, u32[]{:S(2)}, u32[]{:S(2)}) collective-permute-start(bf16[4,24,3072]{2,1,0:T(8,128)(2,1)} %shard_map.295.refs_0_), channel_id=1, source_target_pairs={{0,4},{1,3},{2,6},{3,1},{4,0},{5,7},{6,2},{7,5},{8,12},{9,11},{10,... | collective-permute-start | bytes 1769480 | tf_op jit(solution)/shard_map/ppermute | solution.py:464
  98.1 15.8 %collective-permute-start.28 = (bf16[4,24,3072]{2,1,0:T(8,128)(2,1)}, bf16[4,24,3072]{2,1,0:T(8,128)(2,1)}, u32[]{:S(2)}, u32[]{:S(2)}) collective-permute-start(bf16[4,24,3072]{2,1,0:T(8,128)(2,1)} %shard_map.295.refs_0_), channel_id=1, source_target_pairs={{0,2},{1,5},{2,0},{3,7},{4,6},{5,1},{6,4},{7,3},{8,10},{9,13},{10,... | collective-permute-start | bytes 1769480 | tf_op jit(solution)/shard_map/ppermute | solution.py:460
  207.3 18.6 %collective-permute-start.59 = (bf16[4,4,24,3072]{3,2,1,0:T(8,128)(2,1)}, bf16[4,4,24,3072]{3,2,1,0:T(8,128)(2,1)}, u32[]{:S(2)}, u32[]{:S(2)}) collective-permute-start(bf16[4,4,24,3072]{3,2,1,0:T(8,128)(2,1)} %bitcast.72), channel_id=1, source_target_pairs={{0,1},{1,0},{2,3},{3,2},{4,5},{5,4},{6,7},{7,6},{8,9},{9,8},{10,11... | collective-permute-start | bytes 7077896 | tf_op jit(solution)/shard_map/ppermute | solution.py:452
  210.0 18.7 %collective-permute-start.58 = (bf16[2,4,96,768]{3,2,1,0:T(8,128)(2,1)}, bf16[2,4,96,768]{3,2,1,0:T(8,128)(2,1)}, u32[]{:S(2)}, u32[]{:S(2)}) collective-permute-start(bf16[2,4,96,768]{3,2,1,0:T(8,128)(2,1)} %shard_map.312), channel_id=1, source_target_pairs={{0,2},{1,5},{2,0},{3,7},{4,6},{5,1},{6,4},{7,3},{8,10},{9,13},{10,... | collective-permute-start | bytes 3538952 | tf_op jit(solution)/shard_map/ppermute | solution.py:460
  213.0 15.7 %collective-permute-start.61 = (bf16[4,48,768]{2,1,0:T(8,128)(2,1)}, bf16[4,48,768]{2,1,0:T(8,128)(2,1)}, u32[]{:S(2)}, u32[]{:S(2)}) collective-permute-start(bf16[4,48,768]{2,1,0:T(8,128)(2,1)} %shard_map.314.refs_0_), channel_id=1, source_target_pairs={{0,24},{8,0},{16,8},{24,16},{1,25},{9,1},{17,9},{25,17},{2,26},{10... | collective-permute-start | bytes 884744 | tf_op jit(solution)/shard_map/ppermute | solution.py:448
  214.5 14.2 %collective-permute-start.60 = (bf16[4,48,768]{2,1,0:T(8,128)(2,1)}, bf16[4,48,768]{2,1,0:T(8,128)(2,1)}, u32[]{:S(2)}, u32[]{:S(2)}) collective-permute-start(bf16[4,48,768]{2,1,0:T(8,128)(2,1)} %shard_map.314.refs_0_), channel_id=1, source_target_pairs={{0,8},{8,16},{16,24},{24,0},{1,9},{9,17},{17,25},{25,1},{2,10},{10... | collective-permute-start | bytes 884744 | tf_op jit(solution)/shard_map/ppermute | solution.py:448
  228.7 16.5 %collective-permute-start.62 = (bf16[2,4,24,3072]{3,2,1,0:T(8,128)(2,1)}, bf16[2,4,24,3072]{3,2,1,0:T(8,128)(2,1)}, u32[]{:S(2)}, u32[]{:S(2)}) collective-permute-start(bf16[2,4,24,3072]{3,2,1,0:T(8,128)(2,1)} %shard_map.313), channel_id=1, source_target_pairs={{0,2},{1,5},{2,0},{3,7},{4,6},{5,1},{6,4},{7,3},{8,10},{9,13},{10,... | collective-permute-start | bytes 3538952 | tf_op jit(solution)/shard_map/ppermute | solution.py:460
  229.4 15.8 %collective-permute-start.63 = (bf16[4,48,768]{2,1,0:T(8,128)(2,1)}, bf16[4,48,768]{2,1,0:T(8,128)(2,1)}, u32[]{:S(2)}, u32[]{:S(2)}) collective-permute-start(bf16[4,48,768]{2,1,0:T(8,128)(2,1)} %shard_map.314.refs_0_), channel_id=1, source_target_pairs={{0,16},{8,24},{16,0},{24,8},{1,17},{9,25},{17,1},{25,9},{2,18},{10... | collective-permute-start | bytes 884744 | tf_op jit(solution)/shard_map/ppermute | solution.py:448
  265.6 17.0 %collective-permute-start.67 = (bf16[2,4,24,3200]{3,2,1,0:T(8,128)(2,1)}, bf16[2,4,24,3200]{3,2,1,0:T(8,128)(2,1)}, u32[]{:S(2)}, u32[]{:S(2)}) collective-permute-start(bf16[2,4,24,3200]{3,2,1,0:T(8,128)(2,1)} %shard_map.319), channel_id=1, source_target_pairs={{0,2},{1,5},{2,0},{3,7},{4,6},{5,1},{6,4},{7,3},{8,10},{9,13},{10,... | collective-permute-start | bytes 3686408 | tf_op jit(solution)/shard_map/ppermute | solution.py:460
  266.8 14.8 %collective-permute-start.68 = (bf16[4,4,48,768]{3,2,1,0:T(8,128)(2,1)}, bf16[4,4,48,768]{3,2,1,0:T(8,128)(2,1)}, u32[]{:S(2)}, u32[]{:S(2)}) collective-permute-start(bf16[4,4,48,768]{3,2,1,0:T(8,128)(2,1)} %shard_map.318.mine_ref), channel_id=1, source_target_pairs={{0,1},{1,0},{2,3},{3,2},{4,5},{5,4},{6,7},{7,6},{8,9},{9,8},{10,11... | collective-permute-start | bytes 3538952 | tf_op jit(solution)/shard_map/ppermute | solution.py:452
  286.3 15.9 %collective-permute-start.76 = (bf16[24,3072]{1,0:T(8,128)(2,1)}, bf16[24,3072]{1,0:T(8,128)(2,1)}, u32[]{:S(2)}, u32[]{:S(2)}) collective-permute-start(bf16[24,3072]{1,0:T(8,128)(2,1)} %get-tuple-element.403), channel_id=1, source_target_pairs={{0,8},{8,16},{16,24},{24,0},{1,9},{9,17},{17,25},{25,1},{2,10},{10... | collective-permute-start | bytes 442376 | tf_op jit(solution)/shard_map/ppermute | solution.py:448
  288.6 14.8 %collective-permute-start.77 = (bf16[24,3072]{1,0:T(8,128)(2,1)}, bf16[24,3072]{1,0:T(8,128)(2,1)}, u32[]{:S(2)}, u32[]{:S(2)}) collective-permute-start(bf16[24,3072]{1,0:T(8,128)(2,1)} %get-tuple-element.404), channel_id=1, source_target_pairs={{0,16},{8,24},{16,0},{24,8},{1,17},{9,25},{17,1},{25,9},{2,18},{10... | collective-permute-start | bytes 442376 | tf_op jit(solution)/shard_map/ppermute | solution.py:448
  (62 other events, 386.9 us)

commit v7 on v6

--- a/solution.py
+++ b/solution.py
@@ -1365,7 +1365,6 @@
     cross_moved = [cross_row, swap_dp(cross_row, 1)]
     third, column_two, cross_moved[1], *others = stage(third, column_two, cross_moved[1], *others)
     others.append(swap_core(third))
-    column_two, shard_three, *others = stage(column_two, shard_three, *others)
 
     first_group = gather_plane([column_one, first, second, third], others).reshape(D, 3200)
     mixed_rows, context_first, probs_first, rows, place_rows = on_core(
@@ -1662,7 +1661,6 @@
     mix_got, down_last = swap_core(mix_gone), swap_two(down_onward)
     up_onward = up_total.second(up_back)
     my_rows = join_dp(packs)
-    mix_got, down_last, up_onward, my_rows = stage(mix_got, down_last, up_onward, my_rows)
 
     up_last = swap_two(up_onward)
     mix_sent = mix_total.first(mix_got)

time: 317 us -> 311 us (0.981)
  waiting for transfers between devices: 92.4 us -> 86.6 us
  transfers between devices with their start and end apart: 79 -> 79, of which waited for: 36 -> 35; matrix products, arithmetic and copies ran while one was open for 3% -> 3% of each run, Pallas kernels for 35% -> 36%
where the time goes in v7:
time: 311 us; the launch traced here: 308 us
  Pallas kernels  129 us (41%)
  waiting for transfers between devices  86.6 us (28%)
  starting transfers between devices  72.7 us (23%)
  local copies, waits for them, and re-layouts  14.6 us (5%)
  other arithmetic  3.85 us (1%)
    pallas_call x17, Pallas kernels, on_core(): pl.pallas_call(kernel, out_shape=out_shape, grid=grid, scratch_shapes=scr...  75 us
    ppermute x24, waiting for transfers between devices, swap_dp(): lax.ppermute(array_in, 'dp', [(i, (i + shift) % 4) for i in range(4)])  43.1 us
    pallas_call x11, Pallas kernels, copies(): pl.pallas_call(kernel, out_shape=[jax.ShapeDtypeStruct(shape, pieces[0].d...  31.1 us
    ppermute x24, starting transfers between devices, swap_dp(): lax.ppermute(array_in, 'dp', [(i, (i + shift) % 4) for i in range(4)])  29.7 us
    pallas_call x9, Pallas kernels, run(): pl.pallas_call(kernel, out_shape=out_shapes, in_specs=[far] * count, out_...  23.4 us
    ppermute x18, starting transfers between devices, swap_chip(): return lax.ppermute(array_in, 'seq', [(i, i ^ 2 * mask) for i in range(8)])  23.1 us
    ppermute x11, waiting for transfers between devices, swap_two(): lax.ppermute(array_in, 'seq', [(i, i ^ (4 if i % 2 == 0 else 2)) for i in...  18.7 us
    ppermute x18, waiting for transfers between devices, swap_chip(): return lax.ppermute(array_in, 'seq', [(i, i ^ 2 * mask) for i in range(8)])  18.1 us
  transfers between devices with their start and end apart: 79, of which 35 were waited for; matrix products, arithmetic and copies ran while one was open for 3% of the time, Pallas kernels for 36%

profile of v7, /device:TPU:0, one launch (start us, length us, event | category | flops | bytes accessed | tf_op | source)
XLA Modules:
  0.0 308.4 jit_solution(4151155923745135986)
XLA Ops:
  0.6 2.5 shard_map.289
  3.1 5.1 %collective-permute-start.5 = (bf16[24,3200]{1,0:T(8,128)(2,1)}, bf16[24,3200]{1,0:T(8,128)(2,1)}, u32[]{:S(2)}, u32[]{:S(2)}) collective-permute-start(bf16[24,3200]{1,0:T(8,128)(2,1)} %get-tuple-element.213.refs_0_), channel_id=1, source_target_pairs={{0,24},{8,0},{16,8},{24,16},{1,25},{9,1},{17,9},{25,17},{2,26},{10... | collective-permute-start | bytes 460808 | tf_op jit(solution)/shard_map/ppermute | solution.py:448
  13.8 2.4 collective-permute-start.8
  16.3 3.1 collective-permute-done.8.refs_3_
  33.2 11.7 %collective-permute-done.10.refs_2_ = bf16[24,3840]{1,0:T(8,128)(2,1)} collective-permute-done((bf16[24,3840]{1,0:T(8,128)(2,1)}, bf16[24,3840]{1,0:T(8,128)(2,1)}, u32[]{:S(2)}, u32[]{:S(2)}) %collective-permute-start.10) | collective-permute-done | bytes 184352 | tf_op jit(solution)/shard_map/ppermute | solution.py:448
  48.0 11.9 %collective-permute-done.15.refs_1_ = bf16[4,24,2176]{2,1,0:T(8,128)(2,1)} collective-permute-done((bf16[4,24,2176]{2,1,0:T(8,128)(2,1)}, bf16[4,24,2176]{2,1,0:T(8,128)(2,1)}, u32[]{:S(2)}, u32[]{:S(2)}) %collective-permute-start.15) | collective-permute-done | bytes 417824 | tf_op jit(solution)/shard_map/ppermute | solution.py:448
  64.1 4.3 %shard_map.293 = bf16[4,4,2,24,3200]{4,3,2,1,0:T(8,128)(2,1)} custom-call(bf16[4,24,3200]{2,1,0:T(8,128)(2,1)} %shard_map.290.refs_0_, bf16[4,24,3200]{2,1,0:T(8,128)(2,1)} %collective-permute-done.12.refs_1_, bf16[4,24,3200]{2,1,0:T(8,128)(2,1)} %collective-permute-done.13.refs_2_, bf16[4,24,3200]{2,1,0:T(8,128)(2,1)} %collective-permute-done.14.refs_3_, ...), custom_call_target="tpu_custom_call" | custom-call | tf_op jit(solution)/shard_map/pallas_call | solution.py:510
  68.5 7.7 %shard_map.294 = (bf16[256,2304]{1,0:T(8,128)(2,1)}, bf16[128,768]{1,0:T(8,128)(2,1)}, f32[12,128,128]{2,1,0:T(8,128)}, f32[128,768]{1,0:T(8,128)}, f32[2,768]{1,0:T(2,128)}) custom-call(bf16[256,768]{1,0:T(8,128)(2,1)} %bitcast.61, bf16[768,3200]{1,0:T(8,128)(2,1)} %bitcast.41, s32[2,128]{1,0:T(2,128)} %docs_ref.4, s32[1,2]{1,0:T(1,128)} %bitcast.39), custom_call_target="tpu_custom_call" | custom-call | tf_op jit(solution)/shard_map/pallas_call | solution.py:719
  76.2 3.3 %collective-permute-done.21.refs_2_ = bf16[4,24,3840]{2,1,0:T(8,128)(2,1)} collective-permute-done((bf16[4,24,3840]{2,1,0:T(8,128)(2,1)}, bf16[4,24,3840]{2,1,0:T(8,128)(2,1)}, u32[]{:S(2)}, u32[]{:S(2)}) %collective-permute-start.21) | collective-permute-done | bytes 737312 | tf_op jit(solution)/shard_map/ppermute | solution.py:464
  82.9 6.9 %shard_map.296 = (bf16[256,768]{1,0:T(8,128)(2,1)}, f32[12,128,128]{2,1,0:T(8,128)}, f32[256,768]{1,0:T(8,128)}, f32[256,1]{1,0:T(8,128)}, bf16[256,768]{1,0:T(8,128)(2,1)}) custom-call(bf16[256,768]{1,0:T(8,128)(2,1)} %bitcast.62, bf16[256,2304]{1,0:T(8,128)(2,1)} %get-tuple-element.246.mixed_ref, bf16[128,768]{1,0:T(8,128)(2,1)} %get-tuple-element.247.before_ref, ...), custom_call_target="tpu_custom_call" | custom-call | tf_op jit(solution)/shard_map/pallas_call | solution.py:719
  91.7 3.5 %collective-permute-done.22.refs_2_ = bf16[4,24,2176]{2,1,0:T(8,128)(2,1)} collective-permute-done((bf16[4,24,2176]{2,1,0:T(8,128)(2,1)}, bf16[4,24,2176]{2,1,0:T(8,128)(2,1)}, u32[]{:S(2)}, u32[]{:S(2)}) %collective-permute-start.22) | collective-permute-done | bytes 417824 | tf_op jit(solution)/shard_map/ppermute | solution.py:448
  97.8 5.4 %shard_map.297 = (bf16[4,4,2,24,3072]{4,3,2,1,0:T(8,128)(2,1)}, bf16[4,4,2,24,768]{4,3,2,1,0:T(8,128)(2,1)}) custom-call(bf16[4,24,3840]{2,1,0:T(8,128)(2,1)} %shard_map.292.refs_0_, bf16[4,24,3840]{2,1,0:T(8,128)(2,1)} %collective-permute-done.20.refs_1_, bf16[4,24,3840]{2,1,0:T(8,128)(2,1)} %collective-permute-done.21.refs_2_, ...), custom_call_target="tpu_custom_call" | custom-call | tf_op jit(solution)/shard_map/pallas_call | solution.py:510
  103.2 6.4 %shard_map.298 = (bf16[256,3072]{1,0:T(8,128)(2,1)}, bf16[256,3072]{1,0:T(8,128)(2,1)}) custom-call(bf16[256,768]{1,0:T(8,128)(2,1)} %get-tuple-element.252.low_ref, bf16[768,3072]{1,0:T(8,128)(2,1)} %bitcast.56, f32[1,3072]{1,0:T(1,128)} %reshape.119.bias_ref), custom_call_target="tpu_custom_call" | custom-call | tf_op jit(solution)/shard_map/pallas_call | solution.py:719
  116.5 6.0 %collective-permute-done.31.refs_3_ = bf16[4,24,3072]{2,1,0:T(8,128)(2,1)} collective-permute-done((bf16[4,24,3072]{2,1,0:T(8,128)(2,1)}, bf16[4,24,3072]{2,1,0:T(8,128)(2,1)}, u32[]{:S(2)}, u32[]{:S(2)}) %collective-permute-start.31) | collective-permute-done | bytes 589856 | tf_op jit(solution)/shard_map/ppermute | solution.py:464
  124.8 4.6 %shard_map.300 = bf16[4,4,2,4,24,768]{5,4,3,2,1,0:T(8,128)(2,1)} custom-call(bf16[4,24,3072]{2,1,0:T(8,128)(2,1)} %shard_map.295.refs_0_, bf16[4,24,3072]{2,1,0:T(8,128)(2,1)} %collective-permute-done.28.refs_1_, bf16[4,24,3072]{2,1,0:T(8,128)(2,1)} %collective-permute-done.29.refs_2_, bf16[4,24,3072]{2,1,0:T(8,128)(2,1)} %collective-permute-done.31.refs_3_, ...), custom_call_target="tpu_custom_call" | custom-call | tf_op jit(solution)/shard_map/pallas_call | solution.py:510
  129.6 5.3 %shard_map.301 = (f32[256,768]{1,0:T(8,128)}, f32[256,1]{1,0:T(8,128)}, f32[8,768]{1,0:T(8,128)}, f32[8,768]{1,0:T(8,128)}) custom-call(bf16[256,3072]{1,0:T(8,128)(2,1)} %get-tuple-element.263.active_ref, bf16[3072,768]{1,0:T(8,128)(2,1)} %bitcast.45, f32[256,768]{1,0:T(8,128)} %get-tuple-element.275.first_ref.n_ref, ...), custom_call_target="tpu_custom_call" | custom-call | tf_op jit(solution)/shard_map/pallas_call | solution.py:719
  135.4 3.3 %shard_map.302 = (bf16[4,4,2,24,768]{4,3,2,1,0:T(8,128)(2,1)}, bf16[4,4,2,24,640]{4,3,2,1,0:T(8,128)(2,1)}, bf16[4,2,4,24,768]{4,3,2,1,0:T(8,128)(2,1)}) custom-call(bf16[4,4,24,2176]{3,2,1,0:T(8,128)(2,1)} %shard_map.299.refs_0_, bf16[4,4,24,2176]{3,2,1,0:T(8,128)(2,1)} %collective-permute-done.36.refs_1_), custom_call_target="tpu_custom_call" | custom-call | tf_op jit(solution)/shard_map/pallas_call | solution.py:510
  188.3 8.3 %shard_map.309 = (bf16[256,768]{1,0:T(8,128)(2,1)}, f32[256,768]{1,0:T(8,128)}, bf16[16,96,768]{2,1,0:T(8,128)(2,1)}, bf16[16,96,768]{2,1,0:T(8,128)(2,1)}, bf16...) custom-call(bf16[256,768]{1,0:T(8,128)(2,1)} %bitcast.60, f32[8,768]{1,0:T(8,128)} %copy-done.9, ...), custom_call_target="tpu_custom_call" | custom-call | tf_op jit(solution)/shard_map/pallas_call | solution.py:719
  198.3 7.0 %shard_map.310 = (bf16[16,24,3072]{2,1,0:T(8,128)(2,1)}, bf16[16,24,3072]{2,1,0:T(8,128)(2,1)}, f32[256,768]{1,0:T(8,128)}) custom-call(bf16[256,768]{1,0:T(8,128)(2,1)} %get-tuple-element.252.low_ref, bf16[256,3072]{1,0:T(8,128)(2,1)} %get-tuple-element.322.hidden_ref, bf16[768,3072]{1,0:T(8,128)(2,1)} %bitcast.57, f32[256,768]{1,0:T(8,128)} %get-tuple-element.323.second_ref), custom_call_target="tpu_custom_call" | custom-call | tf_op jit(solution)/shard_map/pallas_call | solution.py:719
  205.3 2.7 shard_map.312
  212.5 10.7 %shard_map.311 = (bf16[768,768]{1,0:T(8,128)(2,1)}, f32[256,768]{1,0:T(8,128)}, f32[8,768]{1,0:T(8,128)}, bf16[256,2304]{1,0:T(8,128)(2,1)}) custom-call(f32[256,768]{1,0:T(8,128)} %get-tuple-element.327.first_ref, f32[256,768]{1,0:T(8,128)} %get-tuple-element.275.first_ref.n_ref, f32[256,1]{1,0:T(8,128)} %get-tuple-element.328.scale_ref, ...), custom_call_target="tpu_custom_call" | custom-call | tf_op jit(solution)/shard_map/pallas_call | solution.py:719
  223.3 2.6 shard_map.313
  231.2 7.9 %shard_map.315 = (f32[256,768]{1,0:T(8,128)}, bf16[16,24,3200]{2,1,0:T(8,128)(2,1)}, bf16[16,24,3200]{2,1,0:T(8,128)(2,1)}) custom-call(f32[256,768]{1,0:T(8,128)} %get-tuple-element.332.total_ref, bf16[256,2304]{1,0:T(8,128)(2,1)} %get-tuple-element.340.back_ref, bf16[256,768]{1,0:T(8,128)(2,1)} %bitcast.63, bf16[768,3200]{1,0:T(8,128)(2,1)} %bitcast.44, ...), custom_call_target="tpu_custom_call" | custom-call | tf_op jit(solution)/shard_map/pallas_call | solution.py:719
  239.1 4.0 %collective-permute-done.63.refs_2_ = bf16[4,48,768]{2,1,0:T(8,128)(2,1)} collective-permute-done((bf16[4,48,768]{2,1,0:T(8,128)(2,1)}, bf16[4,48,768]{2,1,0:T(8,128)(2,1)}, u32[]{:S(2)}, u32[]{:S(2)}) %collective-permute-start.63) | collective-permute-done | bytes 294944 | tf_op jit(solution)/shard_map/ppermute | solution.py:448
  249.7 3.6 %collective-permute-done.66.refs_3_ = bf16[4,96,768]{2,1,0:T(8,128)(2,1)} collective-permute-done((bf16[4,96,768]{2,1,0:T(8,128)(2,1)}, bf16[4,96,768]{2,1,0:T(8,128)(2,1)}, u32[]{:S(2)}, u32[]{:S(2)}) %collective-permute-start.66) | collective-permute-done | bytes 589856 | tf_op jit(solution)/shard_map/ppermute | solution.py:464
  253.4 2.7 shard_map.320
  256.1 2.7 shard_map.318
  264.7 2.7 shard_map.321
  269.4 5.9 %collective-permute-done.70 = bf16[96,768]{1,0:T(8,128)(2,1)} collective-permute-done((bf16[96,768]{1,0:T(8,128)(2,1)}, bf16[96,768]{1,0:T(8,128)(2,1)}, u32[]{:S(2)}, u32[]{:S(2)}) %collective-permute-start.70) | collective-permute-done | bytes 147488 | tf_op jit(solution)/shard_map/ppermute | solution.py:448
  286.7 3.0 collective-permute-done.72.refs_3_
  289.7 2.7 shard_map.323
  299.1 4.4 %shard_map.325 = (f32[24,2304]{1,0:T(8,128)}, f32[24,768]{1,0:T(8,128)}, f32[24,3072]{1,0:T(8,128)}, f32[96,768]{1,0:T(8,128)}, f32[8,24]{1,0:T(8,128)}, /*index=5*/f32[1,96]{1,0:T(1,128)}, f32[64,24]{1,0:T(8,128)}) custom-call(bf16[4,4,48,768]{3,2,1,0:T(8,128)(2,1)} %shard_map.319.mine_ref, bf16[4,4,48,768]{3,2,1,0:T(8,128)(2,1)} %collective-permute-done.68.other_ref, ...), custom_call_target="tpu_custom_call" | custom-call | tf_op jit(solution)/shard_map/pallas_call | solution.py:719
  (204 shorter events, 142.9 us)
Async XLA Ops:
  3.1 16.2 %collective-permute-start.5 = (bf16[24,3200]{1,0:T(8,128)(2,1)}, bf16[24,3200]{1,0:T(8,128)(2,1)}, u32[]{:S(2)}, u32[]{:S(2)}) collective-permute-start(bf16[24,3200]{1,0:T(8,128)(2,1)} %get-tuple-element.213.refs_0_), channel_id=1, source_target_pairs={{0,24},{8,0},{16,8},{24,16},{1,25},{9,1},{17,9},{25,17},{2,26},{10... | collective-permute-start | bytes 460808 | tf_op jit(solution)/shard_map/ppermute | solution.py:448
  23.4 21.5 %collective-permute-start.13 = (bf16[4,24,3200]{2,1,0:T(8,128)(2,1)}, bf16[4,24,3200]{2,1,0:T(8,128)(2,1)}, u32[]{:S(2)}, u32[]{:S(2)}) collective-permute-start(bf16[4,24,3200]{2,1,0:T(8,128)(2,1)} %shard_map.290.refs_0_), channel_id=1, source_target_pairs={{0,4},{1,3},{2,6},{3,1},{4,0},{5,7},{6,2},{7,5},{8,12},{9,11},{10,... | collective-permute-start | bytes 1843208 | tf_op jit(solution)/shard_map/ppermute | solution.py:464
  25.0 19.9 %collective-permute-start.12 = (bf16[4,24,3200]{2,1,0:T(8,128)(2,1)}, bf16[4,24,3200]{2,1,0:T(8,128)(2,1)}, u32[]{:S(2)}, u32[]{:S(2)}) collective-permute-start(bf16[4,24,3200]{2,1,0:T(8,128)(2,1)} %shard_map.290.refs_0_), channel_id=1, source_target_pairs={{0,2},{1,5},{2,0},{3,7},{4,6},{5,1},{6,4},{7,3},{8,10},{9,13},{10,... | collective-permute-start | bytes 1843208 | tf_op jit(solution)/shard_map/ppermute | solution.py:460
  27.8 17.1 %collective-permute-start.10 = (bf16[24,3840]{1,0:T(8,128)(2,1)}, bf16[24,3840]{1,0:T(8,128)(2,1)}, u32[]{:S(2)}, u32[]{:S(2)}) collective-permute-start(bf16[24,3840]{1,0:T(8,128)(2,1)} %get-tuple-element.228.refs_0_), channel_id=1, source_target_pairs={{0,16},{8,24},{16,0},{24,8},{1,17},{9,25},{17,1},{25,9},{2,18},{10... | collective-permute-start | bytes 552968 | tf_op jit(solution)/shard_map/ppermute | solution.py:448
  29.3 15.6 %collective-permute-start.9 = (bf16[24,3840]{1,0:T(8,128)(2,1)}, bf16[24,3840]{1,0:T(8,128)(2,1)}, u32[]{:S(2)}, u32[]{:S(2)}) collective-permute-start(bf16[24,3840]{1,0:T(8,128)(2,1)} %get-tuple-element.228.refs_0_), channel_id=1, source_target_pairs={{0,8},{8,16},{16,24},{24,0},{1,9},{9,17},{17,25},{25,1},{2,10},{10... | collective-permute-start | bytes 552968 | tf_op jit(solution)/shard_map/ppermute | solution.py:448
  44.9 15.0 %collective-permute-start.16 = (bf16[4,24,3200]{2,1,0:T(8,128)(2,1)}, bf16[4,24,3200]{2,1,0:T(8,128)(2,1)}, u32[]{:S(2)}, u32[]{:S(2)}) collective-permute-start(bf16[4,24,3200]{2,1,0:T(8,128)(2,1)} %shard_map.290.refs_0_), channel_id=1, source_target_pairs={{0,1},{1,0},{2,3},{3,2},{4,5},{5,4},{6,7},{7,6},{8,9},{9,8},{10,11... | collective-permute-start | bytes 1843208 | tf_op jit(solution)/shard_map/ppermute | solution.py:452
  45.0 14.9 %collective-permute-start.18 = (bf16[4,24,3200]{2,1,0:T(8,128)(2,1)}, bf16[4,24,3200]{2,1,0:T(8,128)(2,1)}, u32[]{:S(2)}, u32[]{:S(2)}) collective-permute-start(bf16[4,24,3200]{2,1,0:T(8,128)(2,1)} %collective-permute-done.13.refs_2_), channel_id=1, source_target_pairs={{0,1},{1,0},{2,3},{3,2},{4,5},{5,4},{6,7},{7,6},{8,9},{9,8},{10,11... | collective-permute-start | bytes 1843208 | tf_op jit(solution)/shard_map/ppermute | solution.py:452
  45.5 14.4 %collective-permute-start.17 = (bf16[4,24,3200]{2,1,0:T(8,128)(2,1)}, bf16[4,24,3200]{2,1,0:T(8,128)(2,1)}, u32[]{:S(2)}, u32[]{:S(2)}) collective-permute-start(bf16[4,24,3200]{2,1,0:T(8,128)(2,1)} %collective-permute-done.12.refs_1_), channel_id=1, source_target_pairs={{0,1},{1,0},{2,3},{3,2},{4,5},{5,4},{6,7},{7,6},{8,9},{9,8},{10,11... | collective-permute-start | bytes 1843208 | tf_op jit(solution)/shard_map/ppermute | solution.py:452
  45.6 14.4 %collective-permute-start.14 = (bf16[4,24,3200]{2,1,0:T(8,128)(2,1)}, bf16[4,24,3200]{2,1,0:T(8,128)(2,1)}, u32[]{:S(2)}, u32[]{:S(2)}) collective-permute-start(bf16[4,24,3200]{2,1,0:T(8,128)(2,1)} %collective-permute-done.12.refs_1_), channel_id=1, source_target_pairs={{0,4},{1,3},{2,6},{3,1},{4,0},{5,7},{6,2},{7,5},{8,12},{9,11},{10,... | collective-permute-start | bytes 1843208 | tf_op jit(solution)/shard_map/ppermute | solution.py:464
  46.1 13.8 %collective-permute-start.15 = (bf16[4,24,2176]{2,1,0:T(8,128)(2,1)}, bf16[4,24,2176]{2,1,0:T(8,128)(2,1)}, u32[]{:S(2)}, u32[]{:S(2)}) collective-permute-start(bf16[4,24,2176]{2,1,0:T(8,128)(2,1)} %shard_map.291.refs_0_), channel_id=1, source_target_pairs={{0,8},{8,16},{16,24},{24,0},{1,9},{9,17},{17,25},{25,1},{2,10},{10... | collective-permute-start | bytes 1253384 | tf_op jit(solution)/shard_map/ppermute | solution.py:448
  60.0 19.4 %collective-permute-start.21 = (bf16[4,24,3840]{2,1,0:T(8,128)(2,1)}, bf16[4,24,3840]{2,1,0:T(8,128)(2,1)}, u32[]{:S(2)}, u32[]{:S(2)}) collective-permute-start(bf16[4,24,3840]{2,1,0:T(8,128)(2,1)} %shard_map.292.refs_0_), channel_id=1, source_target_pairs={{0,4},{1,3},{2,6},{3,1},{4,0},{5,7},{6,2},{7,5},{8,12},{9,11},{10,... | collective-permute-start | bytes 2211848 | tf_op jit(solution)/shard_map/ppermute | solution.py:464
  60.6 18.8 %collective-permute-start.20 = (bf16[4,24,3840]{2,1,0:T(8,128)(2,1)}, bf16[4,24,3840]{2,1,0:T(8,128)(2,1)}, u32[]{:S(2)}, u32[]{:S(2)}) collective-permute-start(bf16[4,24,3840]{2,1,0:T(8,128)(2,1)} %shard_map.292.refs_0_), channel_id=1, source_target_pairs={{0,2},{1,5},{2,0},{3,7},{4,6},{5,1},{6,4},{7,3},{8,10},{9,13},{10,... | collective-permute-start | bytes 2211848 | tf_op jit(solution)/shard_map/ppermute | solution.py:460
  62.1 14.1 %collective-permute-start.2 = (bf16[24,3072]{1,0:T(8,128)(2,1)}, bf16[24,3072]{1,0:T(8,128)(2,1)}, u32[]{:S(2)}, u32[]{:S(2)}) collective-permute-start(bf16[24,3072]{1,0:T(8,128)(2,1)} %get-tuple-element.242.refs_0_), channel_id=1, source_target_pairs={{0,24},{8,0},{16,8},{24,16},{1,25},{9,1},{17,9},{25,17},{2,26},{10... | collective-permute-start | bytes 442376 | tf_op jit(solution)/shard_map/ppermute | solution.py:448
  62.1 14.1 %collective-permute-start.1 = (bf16[24,3072]{1,0:T(8,128)(2,1)}, bf16[24,3072]{1,0:T(8,128)(2,1)}, u32[]{:S(2)}, u32[]{:S(2)}) collective-permute-start(bf16[24,3072]{1,0:T(8,128)(2,1)} %get-tuple-element.242.refs_0_), channel_id=1, source_target_pairs={{0,16},{8,24},{16,0},{24,8},{1,17},{9,25},{17,1},{25,9},{2,18},{10... | collective-permute-start | bytes 442376 | tf_op jit(solution)/shard_map/ppermute | solution.py:448
  62.4 13.8 %collective-permute-start = (bf16[24,3072]{1,0:T(8,128)(2,1)}, bf16[24,3072]{1,0:T(8,128)(2,1)}, u32[]{:S(2)}, u32[]{:S(2)}) collective-permute-start(bf16[24,3072]{1,0:T(8,128)(2,1)} %get-tuple-element.242.refs_0_), channel_id=1, source_target_pairs={{0,8},{8,16},{16,24},{24,0},{1,9},{9,17},{17,25},{25,1},{2,10},{10... | collective-permute-start | bytes 442376 | tf_op jit(solution)/shard_map/ppermute | solution.py:448
  79.5 15.7 %collective-permute-start.24 = (bf16[4,24,3840]{2,1,0:T(8,128)(2,1)}, bf16[4,24,3840]{2,1,0:T(8,128)(2,1)}, u32[]{:S(2)}, u32[]{:S(2)}) collective-permute-start(bf16[4,24,3840]{2,1,0:T(8,128)(2,1)} %shard_map.292.refs_0_), channel_id=1, source_target_pairs={{0,1},{1,0},{2,3},{3,2},{4,5},{5,4},{6,7},{7,6},{8,9},{9,8},{10,11... | collective-permute-start | bytes 2211848 | tf_op jit(solution)/shard_map/ppermute | solution.py:452
  79.6 15.5 %collective-permute-start.26 = (bf16[4,24,3840]{2,1,0:T(8,128)(2,1)}, bf16[4,24,3840]{2,1,0:T(8,128)(2,1)}, u32[]{:S(2)}, u32[]{:S(2)}) collective-permute-start(bf16[4,24,3840]{2,1,0:T(8,128)(2,1)} %collective-permute-done.21.refs_2_), channel_id=1, source_target_pairs={{0,1},{1,0},{2,3},{3,2},{4,5},{5,4},{6,7},{7,6},{8,9},{9,8},{10,11... | collective-permute-start | bytes 2211848 | tf_op jit(solution)/shard_map/ppermute | solution.py:452
  80.0 15.2 %collective-permute-start.25 = (bf16[4,24,3840]{2,1,0:T(8,128)(2,1)}, bf16[4,24,3840]{2,1,0:T(8,128)(2,1)}, u32[]{:S(2)}, u32[]{:S(2)}) collective-permute-start(bf16[4,24,3840]{2,1,0:T(8,128)(2,1)} %collective-permute-done.20.refs_1_), channel_id=1, source_target_pairs={{0,1},{1,0},{2,3},{3,2},{4,5},{5,4},{6,7},{7,6},{8,9},{9,8},{10,11... | collective-permute-start | bytes 2211848 | tf_op jit(solution)/shard_map/ppermute | solution.py:452
  80.1 15.0 %collective-permute-start.23 = (bf16[4,24,3840]{2,1,0:T(8,128)(2,1)}, bf16[4,24,3840]{2,1,0:T(8,128)(2,1)}, u32[]{:S(2)}, u32[]{:S(2)}) collective-permute-start(bf16[4,24,3840]{2,1,0:T(8,128)(2,1)} %collective-permute-done.20.refs_1_), channel_id=1, source_target_pairs={{0,4},{1,3},{2,6},{3,1},{4,0},{5,7},{6,2},{7,5},{8,12},{9,11},{10,... | collective-permute-start | bytes 2211848 | tf_op jit(solution)/shard_map/ppermute | solution.py:464
  80.6 14.5 %collective-permute-start.22 = (bf16[4,24,2176]{2,1,0:T(8,128)(2,1)}, bf16[4,24,2176]{2,1,0:T(8,128)(2,1)}, u32[]{:S(2)}, u32[]{:S(2)}) collective-permute-start(bf16[4,24,2176]{2,1,0:T(8,128)(2,1)} %collective-permute-done.15.refs_1_), channel_id=1, source_target_pairs={{0,8},{8,16},{16,24},{24,0},{1,9},{9,17},{17,25},{25,1},{2,10},{10... | collective-permute-start | bytes 1253384 | tf_op jit(solution)/shard_map/ppermute | solution.py:448
  95.3 16.4 %collective-permute-start.29 = (bf16[4,24,3072]{2,1,0:T(8,128)(2,1)}, bf16[4,24,3072]{2,1,0:T(8,128)(2,1)}, u32[]{:S(2)}, u32[]{:S(2)}) collective-permute-start(bf16[4,24,3072]{2,1,0:T(8,128)(2,1)} %shard_map.295.refs_0_), channel_id=1, source_target_pairs={{0,4},{1,3},{2,6},{3,1},{4,0},{5,7},{6,2},{7,5},{8,12},{9,11},{10,... | collective-permute-start | bytes 1769480 | tf_op jit(solution)/shard_map/ppermute | solution.py:464
  96.1 15.7 %collective-permute-start.28 = (bf16[4,24,3072]{2,1,0:T(8,128)(2,1)}, bf16[4,24,3072]{2,1,0:T(8,128)(2,1)}, u32[]{:S(2)}, u32[]{:S(2)}) collective-permute-start(bf16[4,24,3072]{2,1,0:T(8,128)(2,1)} %shard_map.295.refs_0_), channel_id=1, source_target_pairs={{0,2},{1,5},{2,0},{3,7},{4,6},{5,1},{6,4},{7,3},{8,10},{9,13},{10,... | collective-permute-start | bytes 1769480 | tf_op jit(solution)/shard_map/ppermute | solution.py:460
  205.3 18.0 %collective-permute-start.59 = (bf16[4,4,24,3072]{3,2,1,0:T(8,128)(2,1)}, bf16[4,4,24,3072]{3,2,1,0:T(8,128)(2,1)}, u32[]{:S(2)}, u32[]{:S(2)}) collective-permute-start(bf16[4,4,24,3072]{3,2,1,0:T(8,128)(2,1)} %bitcast.72), channel_id=1, source_target_pairs={{0,1},{1,0},{2,3},{3,2},{4,5},{5,4},{6,7},{7,6},{8,9},{9,8},{10,11... | collective-permute-start | bytes 7077896 | tf_op jit(solution)/shard_map/ppermute | solution.py:452
  208.0 18.1 %collective-permute-start.58 = (bf16[2,4,96,768]{3,2,1,0:T(8,128)(2,1)}, bf16[2,4,96,768]{3,2,1,0:T(8,128)(2,1)}, u32[]{:S(2)}, u32[]{:S(2)}) collective-permute-start(bf16[2,4,96,768]{3,2,1,0:T(8,128)(2,1)} %shard_map.312), channel_id=1, source_target_pairs={{0,2},{1,5},{2,0},{3,7},{4,6},{5,1},{6,4},{7,3},{8,10},{9,13},{10,... | collective-permute-start | bytes 3538952 | tf_op jit(solution)/shard_map/ppermute | solution.py:460
  210.4 15.7 %collective-permute-start.61 = (bf16[4,48,768]{2,1,0:T(8,128)(2,1)}, bf16[4,48,768]{2,1,0:T(8,128)(2,1)}, u32[]{:S(2)}, u32[]{:S(2)}) collective-permute-start(bf16[4,48,768]{2,1,0:T(8,128)(2,1)} %shard_map.314.refs_0_), channel_id=1, source_target_pairs={{0,24},{8,0},{16,8},{24,16},{1,25},{9,1},{17,9},{25,17},{2,26},{10... | collective-permute-start | bytes 884744 | tf_op jit(solution)/shard_map/ppermute | solution.py:448
  212.2 13.9 %collective-permute-start.60 = (bf16[4,48,768]{2,1,0:T(8,128)(2,1)}, bf16[4,48,768]{2,1,0:T(8,128)(2,1)}, u32[]{:S(2)}, u32[]{:S(2)}) collective-permute-start(bf16[4,48,768]{2,1,0:T(8,128)(2,1)} %shard_map.314.refs_0_), channel_id=1, source_target_pairs={{0,8},{8,16},{16,24},{24,0},{1,9},{9,17},{17,25},{25,1},{2,10},{10... | collective-permute-start | bytes 884744 | tf_op jit(solution)/shard_map/ppermute | solution.py:448
  226.1 17.1 %collective-permute-start.62 = (bf16[2,4,24,3072]{3,2,1,0:T(8,128)(2,1)}, bf16[2,4,24,3072]{3,2,1,0:T(8,128)(2,1)}, u32[]{:S(2)}, u32[]{:S(2)}) collective-permute-start(bf16[2,4,24,3072]{3,2,1,0:T(8,128)(2,1)} %shard_map.313), channel_id=1, source_target_pairs={{0,2},{1,5},{2,0},{3,7},{4,6},{5,1},{6,4},{7,3},{8,10},{9,13},{10,... | collective-permute-start | bytes 3538952 | tf_op jit(solution)/shard_map/ppermute | solution.py:460
  227.4 15.8 %collective-permute-start.63 = (bf16[4,48,768]{2,1,0:T(8,128)(2,1)}, bf16[4,48,768]{2,1,0:T(8,128)(2,1)}, u32[]{:S(2)}, u32[]{:S(2)}) collective-permute-start(bf16[4,48,768]{2,1,0:T(8,128)(2,1)} %shard_map.314.refs_0_), channel_id=1, source_target_pairs={{0,16},{8,24},{16,0},{24,8},{1,17},{9,25},{17,1},{25,9},{2,18},{10... | collective-permute-start | bytes 884744 | tf_op jit(solution)/shard_map/ppermute | solution.py:448
  259.7 17.0 %collective-permute-start.67 = (bf16[2,4,24,3200]{3,2,1,0:T(8,128)(2,1)}, bf16[2,4,24,3200]{3,2,1,0:T(8,128)(2,1)}, u32[]{:S(2)}, u32[]{:S(2)}) collective-permute-start(bf16[2,4,24,3200]{3,2,1,0:T(8,128)(2,1)} %shard_map.318), channel_id=1, source_target_pairs={{0,2},{1,5},{2,0},{3,7},{4,6},{5,1},{6,4},{7,3},{8,10},{9,13},{10,... | collective-permute-start | bytes 3686408 | tf_op jit(solution)/shard_map/ppermute | solution.py:460
  260.5 14.8 %collective-permute-start.68 = (bf16[4,4,48,768]{3,2,1,0:T(8,128)(2,1)}, bf16[4,4,48,768]{3,2,1,0:T(8,128)(2,1)}, u32[]{:S(2)}, u32[]{:S(2)}) collective-permute-start(bf16[4,4,48,768]{3,2,1,0:T(8,128)(2,1)} %shard_map.319.mine_ref), channel_id=1, source_target_pairs={{0,1},{1,0},{2,3},{3,2},{4,5},{5,4},{6,7},{7,6},{8,9},{9,8},{10,11... | collective-permute-start | bytes 3538952 | tf_op jit(solution)/shard_map/ppermute | solution.py:452
  280.2 15.7 %collective-permute-start.76 = (bf16[24,3072]{1,0:T(8,128)(2,1)}, bf16[24,3072]{1,0:T(8,128)(2,1)}, u32[]{:S(2)}, u32[]{:S(2)}) collective-permute-start(bf16[24,3072]{1,0:T(8,128)(2,1)} %get-tuple-element.383), channel_id=1, source_target_pairs={{0,8},{8,16},{16,24},{24,0},{1,9},{9,17},{17,25},{25,1},{2,10},{10... | collective-permute-start | bytes 442376 | tf_op jit(solution)/shard_map/ppermute | solution.py:448
  282.4 14.7 %collective-permute-start.77 = (bf16[24,3072]{1,0:T(8,128)(2,1)}, bf16[24,3072]{1,0:T(8,128)(2,1)}, u32[]{:S(2)}, u32[]{:S(2)}) collective-permute-start(bf16[24,3072]{1,0:T(8,128)(2,1)} %get-tuple-element.384), channel_id=1, source_target_pairs={{0,16},{8,24},{16,0},{24,8},{1,17},{9,25},{17,1},{25,9},{2,18},{10... | collective-permute-start | bytes 442376 | tf_op jit(solution)/shard_map/ppermute | solution.py:448
  (62 other events, 390.6 us)

commit v8 on v7

--- a/solution.py
+++ b/solution.py
@@ -1438,9 +1438,7 @@
     cross_bias = rows_later.reshape(4, 4, 4, 2, 24)
     cross_bias = lax.dynamic_index_in_dim(cross_bias, chip, 2, keepdims=False)
     cross_bias = cross_bias.transpose(1, 2, 0, 3).reshape(1, D)
-    third_three, cross_column, cross_bias, *others = stage(
-        third_three, join_dp(cross_moved), cross_bias, *others
-    )
+    cross_column = join_dp(cross_moved)
 
     others.append(swap_core(third_three))
     down_weight = gather_down([column_three, first_three, second_three, third_three], others)

time: 311 us -> 308 us (level)
    ppermute x11, waiting for transfers between devices: 18.7 us -> 22 us  [swap_two(): lax.ppermute(array_in, 'seq', [(i, i ^ (4 if i % 2 == 0 else 2)) for i in...]
    unnamed x31 -> x25, local copies, waits for them, and re-layouts: 10.8 us -> 8.8 us
where the time goes in v8:
time: 308 us; the launch traced here: 306 us
  Pallas kernels  129 us (42%)
  waiting for transfers between devices  87.2 us (28%)
  starting transfers between devices  72.4 us (24%)
  local copies, waits for them, and re-layouts  12 us (4%)
  other arithmetic  3.85 us (1%)
    pallas_call x17, Pallas kernels, on_core(): pl.pallas_call(kernel, out_shape=out_shape, grid=grid, scratch_shapes=scr...  74.9 us
    ppermute x24, waiting for transfers between devices, swap_dp(): lax.ppermute(array_in, 'dp', [(i, (i + shift) % 4) for i in range(4)])  43.6 us
    pallas_call x11, Pallas kernels, copies(): pl.pallas_call(kernel, out_shape=[jax.ShapeDtypeStruct(shape, pieces[0].d...  31.1 us
    ppermute x24, starting transfers between devices, swap_dp(): lax.ppermute(array_in, 'dp', [(i, (i + shift) % 4) for i in range(4)])  29.6 us
    pallas_call x9, Pallas kernels, run(): pl.pallas_call(kernel, out_shape=out_shapes, in_specs=[far] * count, out_...  23.4 us
    ppermute x18, starting transfers between devices, swap_chip(): return lax.ppermute(array_in, 'seq', [(i, i ^ 2 * mask) for i in range(8)])  23.1 us
    ppermute x11, waiting for transfers between devices, swap_two(): lax.ppermute(array_in, 'seq', [(i, i ^ (4 if i % 2 == 0 else 2)) for i in...  22 us
    ppermute x18, waiting for transfers between devices, swap_chip(): return lax.ppermute(array_in, 'seq', [(i, i ^ 2 * mask) for i in range(8)])  17.1 us
  transfers between devices with their start and end apart: 79, of which 35 were waited for; matrix products, arithmetic and copies ran while one was open for 3% of the time, Pallas kernels for 36%

profile of v8, /device:TPU:0, one launch (start us, length us, event | category | flops | bytes accessed | tf_op | source)
XLA Modules:
  0.0 306.1 jit_solution(1139907890769660372)
XLA Ops:
  0.6 2.5 shard_map.289
  3.1 5.1 %collective-permute-start.5 = (bf16[24,3200]{1,0:T(8,128)(2,1)}, bf16[24,3200]{1,0:T(8,128)(2,1)}, u32[]{:S(2)}, u32[]{:S(2)}) collective-permute-start(bf16[24,3200]{1,0:T(8,128)(2,1)} %get-tuple-element.207.refs_0_), channel_id=1, source_target_pairs={{0,24},{8,0},{16,8},{24,16},{1,25},{9,1},{17,9},{25,17},{2,26},{10... | collective-permute-start | bytes 460808 | tf_op jit(solution)/shard_map/ppermute | solution.py:448
  13.8 2.4 collective-permute-start.8
  16.3 3.1 collective-permute-done.8.refs_3_
  33.2 11.7 %collective-permute-done.10.refs_2_ = bf16[24,3840]{1,0:T(8,128)(2,1)} collective-permute-done((bf16[24,3840]{1,0:T(8,128)(2,1)}, bf16[24,3840]{1,0:T(8,128)(2,1)}, u32[]{:S(2)}, u32[]{:S(2)}) %collective-permute-start.10) | collective-permute-done | bytes 184352 | tf_op jit(solution)/shard_map/ppermute | solution.py:448
  48.1 11.9 %collective-permute-done.15.refs_1_ = bf16[4,24,2176]{2,1,0:T(8,128)(2,1)} collective-permute-done((bf16[4,24,2176]{2,1,0:T(8,128)(2,1)}, bf16[4,24,2176]{2,1,0:T(8,128)(2,1)}, u32[]{:S(2)}, u32[]{:S(2)}) %collective-permute-start.15) | collective-permute-done | bytes 417824 | tf_op jit(solution)/shard_map/ppermute | solution.py:448
  64.1 4.3 %shard_map.293 = bf16[4,4,2,24,3200]{4,3,2,1,0:T(8,128)(2,1)} custom-call(bf16[4,24,3200]{2,1,0:T(8,128)(2,1)} %shard_map.290.refs_0_, bf16[4,24,3200]{2,1,0:T(8,128)(2,1)} %collective-permute-done.12.refs_1_, bf16[4,24,3200]{2,1,0:T(8,128)(2,1)} %collective-permute-done.13.refs_2_, bf16[4,24,3200]{2,1,0:T(8,128)(2,1)} %collective-permute-done.14.refs_3_, ...), custom_call_target="tpu_custom_call" | custom-call | tf_op jit(solution)/shard_map/pallas_call | solution.py:510
  68.5 7.7 %shard_map.294 = (bf16[256,2304]{1,0:T(8,128)(2,1)}, bf16[128,768]{1,0:T(8,128)(2,1)}, f32[12,128,128]{2,1,0:T(8,128)}, f32[128,768]{1,0:T(8,128)}, f32[2,768]{1,0:T(2,128)}) custom-call(bf16[256,768]{1,0:T(8,128)(2,1)} %bitcast.61, bf16[768,3200]{1,0:T(8,128)(2,1)} %bitcast.41, s32[2,128]{1,0:T(2,128)} %docs_ref.4, s32[1,2]{1,0:T(1,128)} %bitcast.39), custom_call_target="tpu_custom_call" | custom-call | tf_op jit(solution)/shard_map/pallas_call | solution.py:719
  76.2 3.3 %collective-permute-done.21.refs_2_ = bf16[4,24,3840]{2,1,0:T(8,128)(2,1)} collective-permute-done((bf16[4,24,3840]{2,1,0:T(8,128)(2,1)}, bf16[4,24,3840]{2,1,0:T(8,128)(2,1)}, u32[]{:S(2)}, u32[]{:S(2)}) %collective-permute-start.21) | collective-permute-done | bytes 737312 | tf_op jit(solution)/shard_map/ppermute | solution.py:464
  82.9 6.9 %shard_map.296 = (bf16[256,768]{1,0:T(8,128)(2,1)}, f32[12,128,128]{2,1,0:T(8,128)}, f32[256,768]{1,0:T(8,128)}, f32[256,1]{1,0:T(8,128)}, bf16[256,768]{1,0:T(8,128)(2,1)}) custom-call(bf16[256,768]{1,0:T(8,128)(2,1)} %bitcast.62, bf16[256,2304]{1,0:T(8,128)(2,1)} %get-tuple-element.240.mixed_ref, bf16[128,768]{1,0:T(8,128)(2,1)} %get-tuple-element.241.before_ref, ...), custom_call_target="tpu_custom_call" | custom-call | tf_op jit(solution)/shard_map/pallas_call | solution.py:719
  91.7 3.4 %collective-permute-done.22.refs_2_ = bf16[4,24,2176]{2,1,0:T(8,128)(2,1)} collective-permute-done((bf16[4,24,2176]{2,1,0:T(8,128)(2,1)}, bf16[4,24,2176]{2,1,0:T(8,128)(2,1)}, u32[]{:S(2)}, u32[]{:S(2)}) %collective-permute-start.22) | collective-permute-done | bytes 417824 | tf_op jit(solution)/shard_map/ppermute | solution.py:448
  97.8 5.4 %shard_map.297 = (bf16[4,4,2,24,3072]{4,3,2,1,0:T(8,128)(2,1)}, bf16[4,4,2,24,768]{4,3,2,1,0:T(8,128)(2,1)}) custom-call(bf16[4,24,3840]{2,1,0:T(8,128)(2,1)} %shard_map.292.refs_0_, bf16[4,24,3840]{2,1,0:T(8,128)(2,1)} %collective-permute-done.20.refs_1_, bf16[4,24,3840]{2,1,0:T(8,128)(2,1)} %collective-permute-done.21.refs_2_, ...), custom_call_target="tpu_custom_call" | custom-call | tf_op jit(solution)/shard_map/pallas_call | solution.py:510
  103.2 6.4 %shard_map.298 = (bf16[256,3072]{1,0:T(8,128)(2,1)}, bf16[256,3072]{1,0:T(8,128)(2,1)}) custom-call(bf16[256,768]{1,0:T(8,128)(2,1)} %get-tuple-element.246.low_ref, bf16[768,3072]{1,0:T(8,128)(2,1)} %bitcast.56, f32[1,3072]{1,0:T(1,128)} %reshape.119.bias_ref), custom_call_target="tpu_custom_call" | custom-call | tf_op jit(solution)/shard_map/pallas_call | solution.py:719
  112.6 9.3 %collective-permute-done.31.refs_3_ = bf16[4,24,3072]{2,1,0:T(8,128)(2,1)} collective-permute-done((bf16[4,24,3072]{2,1,0:T(8,128)(2,1)}, bf16[4,24,3072]{2,1,0:T(8,128)(2,1)}, u32[]{:S(2)}, u32[]{:S(2)}) %collective-permute-start.31) | collective-permute-done | bytes 589856 | tf_op jit(solution)/shard_map/ppermute | solution.py:464
  124.3 4.5 %shard_map.299 = bf16[4,4,2,4,24,768]{5,4,3,2,1,0:T(8,128)(2,1)} custom-call(bf16[4,24,3072]{2,1,0:T(8,128)(2,1)} %shard_map.295.refs_0_, bf16[4,24,3072]{2,1,0:T(8,128)(2,1)} %collective-permute-done.28.refs_1_, bf16[4,24,3072]{2,1,0:T(8,128)(2,1)} %collective-permute-done.29.refs_2_, bf16[4,24,3072]{2,1,0:T(8,128)(2,1)} %collective-permute-done.31.refs_3_, ...), custom_call_target="tpu_custom_call" | custom-call | tf_op jit(solution)/shard_map/pallas_call | solution.py:510
  129.4 5.3 %shard_map.301 = (f32[256,768]{1,0:T(8,128)}, f32[256,1]{1,0:T(8,128)}, f32[8,768]{1,0:T(8,128)}, f32[8,768]{1,0:T(8,128)}) custom-call(bf16[256,3072]{1,0:T(8,128)(2,1)} %get-tuple-element.257.active_ref, bf16[3072,768]{1,0:T(8,128)(2,1)} %bitcast.45, f32[256,768]{1,0:T(8,128)} %get-tuple-element.263.first_ref.n_ref, ...), custom_call_target="tpu_custom_call" | custom-call | tf_op jit(solution)/shard_map/pallas_call | solution.py:719
  134.9 3.3 %shard_map.302 = (bf16[4,4,2,24,768]{4,3,2,1,0:T(8,128)(2,1)}, bf16[4,4,2,24,640]{4,3,2,1,0:T(8,128)(2,1)}, bf16[4,2,4,24,768]{4,3,2,1,0:T(8,128)(2,1)}) custom-call(bf16[4,4,24,2176]{3,2,1,0:T(8,128)(2,1)} %shard_map.300.refs_0_, bf16[4,4,24,2176]{3,2,1,0:T(8,128)(2,1)} %collective-permute-done.36.refs_1_), custom_call_target="tpu_custom_call" | custom-call | tf_op jit(solution)/shard_map/pallas_call | solution.py:510
  185.5 8.3 %shard_map.309 = (bf16[256,768]{1,0:T(8,128)(2,1)}, f32[256,768]{1,0:T(8,128)}, bf16[16,96,768]{2,1,0:T(8,128)(2,1)}, bf16[16,96,768]{2,1,0:T(8,128)(2,1)}, bf16...) custom-call(bf16[256,768]{1,0:T(8,128)(2,1)} %bitcast.60, f32[8,768]{1,0:T(8,128)} %copy-done.7, ...), custom_call_target="tpu_custom_call" | custom-call | tf_op jit(solution)/shard_map/pallas_call | solution.py:719
  195.7 7.0 %shard_map.310 = (bf16[16,24,3072]{2,1,0:T(8,128)(2,1)}, bf16[16,24,3072]{2,1,0:T(8,128)(2,1)}, f32[256,768]{1,0:T(8,128)}) custom-call(bf16[256,768]{1,0:T(8,128)(2,1)} %get-tuple-element.246.low_ref, bf16[256,3072]{1,0:T(8,128)(2,1)} %get-tuple-element.310.hidden_ref, bf16[768,3072]{1,0:T(8,128)(2,1)} %bitcast.57, f32[256,768]{1,0:T(8,128)} %get-tuple-element.311.second_ref), custom_call_target="tpu_custom_call" | custom-call | tf_op jit(solution)/shard_map/pallas_call | solution.py:719
  202.8 2.7 shard_map.312
  209.7 10.7 %shard_map.311 = (bf16[768,768]{1,0:T(8,128)(2,1)}, f32[256,768]{1,0:T(8,128)}, f32[8,768]{1,0:T(8,128)}, bf16[256,2304]{1,0:T(8,128)(2,1)}) custom-call(f32[256,768]{1,0:T(8,128)} %get-tuple-element.315.first_ref, f32[256,768]{1,0:T(8,128)} %get-tuple-element.263.first_ref.n_ref, f32[256,1]{1,0:T(8,128)} %get-tuple-element.316.scale_ref, ...), custom_call_target="tpu_custom_call" | custom-call | tf_op jit(solution)/shard_map/pallas_call | solution.py:719
  220.5 2.7 shard_map.313
  228.6 8.0 %shard_map.315 = (f32[256,768]{1,0:T(8,128)}, bf16[16,24,3200]{2,1,0:T(8,128)(2,1)}, bf16[16,24,3200]{2,1,0:T(8,128)(2,1)}) custom-call(f32[256,768]{1,0:T(8,128)} %get-tuple-element.320.total_ref, bf16[256,2304]{1,0:T(8,128)(2,1)} %get-tuple-element.328.back_ref, bf16[256,768]{1,0:T(8,128)(2,1)} %bitcast.63, bf16[768,3200]{1,0:T(8,128)(2,1)} %bitcast.44, ...), custom_call_target="tpu_custom_call" | custom-call | tf_op jit(solution)/shard_map/pallas_call | solution.py:719
  236.6 4.0 %collective-permute-done.63.refs_2_ = bf16[4,48,768]{2,1,0:T(8,128)(2,1)} collective-permute-done((bf16[4,48,768]{2,1,0:T(8,128)(2,1)}, bf16[4,48,768]{2,1,0:T(8,128)(2,1)}, u32[]{:S(2)}, u32[]{:S(2)}) %collective-permute-start.63) | collective-permute-done | bytes 294944 | tf_op jit(solution)/shard_map/ppermute | solution.py:448
  247.2 3.6 %collective-permute-done.66.refs_3_ = bf16[4,96,768]{2,1,0:T(8,128)(2,1)} collective-permute-done((bf16[4,96,768]{2,1,0:T(8,128)(2,1)}, bf16[4,96,768]{2,1,0:T(8,128)(2,1)}, u32[]{:S(2)}, u32[]{:S(2)}) %collective-permute-start.66) | collective-permute-done | bytes 589856 | tf_op jit(solution)/shard_map/ppermute | solution.py:464
  250.8 2.7 shard_map.320
  253.5 2.7 shard_map.318
  262.2 2.7 shard_map.321
  266.7 5.9 %collective-permute-done.70 = bf16[96,768]{1,0:T(8,128)(2,1)} collective-permute-done((bf16[96,768]{1,0:T(8,128)(2,1)}, bf16[96,768]{1,0:T(8,128)(2,1)}, u32[]{:S(2)}, u32[]{:S(2)}) %collective-permute-start.70) | collective-permute-done | bytes 147488 | tf_op jit(solution)/shard_map/ppermute | solution.py:448
  284.1 3.0 collective-permute-done.72.refs_3_
  287.2 2.7 shard_map.323
  296.4 4.4 %shard_map.325 = (f32[24,2304]{1,0:T(8,128)}, f32[24,768]{1,0:T(8,128)}, f32[24,3072]{1,0:T(8,128)}, f32[96,768]{1,0:T(8,128)}, f32[8,24]{1,0:T(8,128)}, /*index=5*/f32[1,96]{1,0:T(1,128)}, f32[64,24]{1,0:T(8,128)}) custom-call(bf16[4,4,48,768]{3,2,1,0:T(8,128)(2,1)} %shard_map.319.mine_ref, bf16[4,4,48,768]{3,2,1,0:T(8,128)(2,1)} %collective-permute-done.68.other_ref, ...), custom_call_target="tpu_custom_call" | custom-call | tf_op jit(solution)/shard_map/pallas_call | solution.py:719
  (198 shorter events, 137.2 us)
Async XLA Ops:
  3.1 16.2 %collective-permute-start.5 = (bf16[24,3200]{1,0:T(8,128)(2,1)}, bf16[24,3200]{1,0:T(8,128)(2,1)}, u32[]{:S(2)}, u32[]{:S(2)}) collective-permute-start(bf16[24,3200]{1,0:T(8,128)(2,1)} %get-tuple-element.207.refs_0_), channel_id=1, source_target_pairs={{0,24},{8,0},{16,8},{24,16},{1,25},{9,1},{17,9},{25,17},{2,26},{10... | collective-permute-start | bytes 460808 | tf_op jit(solution)/shard_map/ppermute | solution.py:448
  23.4 21.5 %collective-permute-start.13 = (bf16[4,24,3200]{2,1,0:T(8,128)(2,1)}, bf16[4,24,3200]{2,1,0:T(8,128)(2,1)}, u32[]{:S(2)}, u32[]{:S(2)}) collective-permute-start(bf16[4,24,3200]{2,1,0:T(8,128)(2,1)} %shard_map.290.refs_0_), channel_id=1, source_target_pairs={{0,4},{1,3},{2,6},{3,1},{4,0},{5,7},{6,2},{7,5},{8,12},{9,11},{10,... | collective-permute-start | bytes 1843208 | tf_op jit(solution)/shard_map/ppermute | solution.py:464
  25.0 19.9 %collective-permute-start.12 = (bf16[4,24,3200]{2,1,0:T(8,128)(2,1)}, bf16[4,24,3200]{2,1,0:T(8,128)(2,1)}, u32[]{:S(2)}, u32[]{:S(2)}) collective-permute-start(bf16[4,24,3200]{2,1,0:T(8,128)(2,1)} %shard_map.290.refs_0_), channel_id=1, source_target_pairs={{0,2},{1,5},{2,0},{3,7},{4,6},{5,1},{6,4},{7,3},{8,10},{9,13},{10,... | collective-permute-start | bytes 1843208 | tf_op jit(solution)/shard_map/ppermute | solution.py:460
  27.8 17.1 %collective-permute-start.10 = (bf16[24,3840]{1,0:T(8,128)(2,1)}, bf16[24,3840]{1,0:T(8,128)(2,1)}, u32[]{:S(2)}, u32[]{:S(2)}) collective-permute-start(bf16[24,3840]{1,0:T(8,128)(2,1)} %get-tuple-element.222.refs_0_), channel_id=1, source_target_pairs={{0,16},{8,24},{16,0},{24,8},{1,17},{9,25},{17,1},{25,9},{2,18},{10... | collective-permute-start | bytes 552968 | tf_op jit(solution)/shard_map/ppermute | solution.py:448
  29.3 15.6 %collective-permute-start.9 = (bf16[24,3840]{1,0:T(8,128)(2,1)}, bf16[24,3840]{1,0:T(8,128)(2,1)}, u32[]{:S(2)}, u32[]{:S(2)}) collective-permute-start(bf16[24,3840]{1,0:T(8,128)(2,1)} %get-tuple-element.222.refs_0_), channel_id=1, source_target_pairs={{0,8},{8,16},{16,24},{24,0},{1,9},{9,17},{17,25},{25,1},{2,10},{10... | collective-permute-start | bytes 552968 | tf_op jit(solution)/shard_map/ppermute | solution.py:448
  44.9 15.0 %collective-permute-start.16 = (bf16[4,24,3200]{2,1,0:T(8,128)(2,1)}, bf16[4,24,3200]{2,1,0:T(8,128)(2,1)}, u32[]{:S(2)}, u32[]{:S(2)}) collective-permute-start(bf16[4,24,3200]{2,1,0:T(8,128)(2,1)} %shard_map.290.refs_0_), channel_id=1, source_target_pairs={{0,1},{1,0},{2,3},{3,2},{4,5},{5,4},{6,7},{7,6},{8,9},{9,8},{10,11... | collective-permute-start | bytes 1843208 | tf_op jit(solution)/shard_map/ppermute | solution.py:452
  45.0 14.9 %collective-permute-start.18 = (bf16[4,24,3200]{2,1,0:T(8,128)(2,1)}, bf16[4,24,3200]{2,1,0:T(8,128)(2,1)}, u32[]{:S(2)}, u32[]{:S(2)}) collective-permute-start(bf16[4,24,3200]{2,1,0:T(8,128)(2,1)} %collective-permute-done.13.refs_2_), channel_id=1, source_target_pairs={{0,1},{1,0},{2,3},{3,2},{4,5},{5,4},{6,7},{7,6},{8,9},{9,8},{10,11... | collective-permute-start | bytes 1843208 | tf_op jit(solution)/shard_map/ppermute | solution.py:452
  45.5 14.4 %collective-permute-start.17 = (bf16[4,24,3200]{2,1,0:T(8,128)(2,1)}, bf16[4,24,3200]{2,1,0:T(8,128)(2,1)}, u32[]{:S(2)}, u32[]{:S(2)}) collective-permute-start(bf16[4,24,3200]{2,1,0:T(8,128)(2,1)} %collective-permute-done.12.refs_1_), channel_id=1, source_target_pairs={{0,1},{1,0},{2,3},{3,2},{4,5},{5,4},{6,7},{7,6},{8,9},{9,8},{10,11... | collective-permute-start | bytes 1843208 | tf_op jit(solution)/shard_map/ppermute | solution.py:452
  45.6 14.4 %collective-permute-start.14 = (bf16[4,24,3200]{2,1,0:T(8,128)(2,1)}, bf16[4,24,3200]{2,1,0:T(8,128)(2,1)}, u32[]{:S(2)}, u32[]{:S(2)}) collective-permute-start(bf16[4,24,3200]{2,1,0:T(8,128)(2,1)} %collective-permute-done.12.refs_1_), channel_id=1, source_target_pairs={{0,4},{1,3},{2,6},{3,1},{4,0},{5,7},{6,2},{7,5},{8,12},{9,11},{10,... | collective-permute-start | bytes 1843208 | tf_op jit(solution)/shard_map/ppermute | solution.py:464
  46.1 13.8 %collective-permute-start.15 = (bf16[4,24,2176]{2,1,0:T(8,128)(2,1)}, bf16[4,24,2176]{2,1,0:T(8,128)(2,1)}, u32[]{:S(2)}, u32[]{:S(2)}) collective-permute-start(bf16[4,24,2176]{2,1,0:T(8,128)(2,1)} %shard_map.291.refs_0_), channel_id=1, source_target_pairs={{0,8},{8,16},{16,24},{24,0},{1,9},{9,17},{17,25},{25,1},{2,10},{10... | collective-permute-start | bytes 1253384 | tf_op jit(solution)/shard_map/ppermute | solution.py:448
  60.0 19.4 %collective-permute-start.21 = (bf16[4,24,3840]{2,1,0:T(8,128)(2,1)}, bf16[4,24,3840]{2,1,0:T(8,128)(2,1)}, u32[]{:S(2)}, u32[]{:S(2)}) collective-permute-start(bf16[4,24,3840]{2,1,0:T(8,128)(2,1)} %shard_map.292.refs_0_), channel_id=1, source_target_pairs={{0,4},{1,3},{2,6},{3,1},{4,0},{5,7},{6,2},{7,5},{8,12},{9,11},{10,... | collective-permute-start | bytes 2211848 | tf_op jit(solution)/shard_map/ppermute | solution.py:464
  60.6 18.8 %collective-permute-start.20 = (bf16[4,24,3840]{2,1,0:T(8,128)(2,1)}, bf16[4,24,3840]{2,1,0:T(8,128)(2,1)}, u32[]{:S(2)}, u32[]{:S(2)}) collective-permute-start(bf16[4,24,3840]{2,1,0:T(8,128)(2,1)} %shard_map.292.refs_0_), channel_id=1, source_target_pairs={{0,2},{1,5},{2,0},{3,7},{4,6},{5,1},{6,4},{7,3},{8,10},{9,13},{10,... | collective-permute-start | bytes 2211848 | tf_op jit(solution)/shard_map/ppermute | solution.py:460
  62.1 14.0 %collective-permute-start.2 = (bf16[24,3072]{1,0:T(8,128)(2,1)}, bf16[24,3072]{1,0:T(8,128)(2,1)}, u32[]{:S(2)}, u32[]{:S(2)}) collective-permute-start(bf16[24,3072]{1,0:T(8,128)(2,1)} %get-tuple-element.236.refs_0_), channel_id=1, source_target_pairs={{0,24},{8,0},{16,8},{24,16},{1,25},{9,1},{17,9},{25,17},{2,26},{10... | collective-permute-start | bytes 442376 | tf_op jit(solution)/shard_map/ppermute | solution.py:448
  62.1 14.0 %collective-permute-start.1 = (bf16[24,3072]{1,0:T(8,128)(2,1)}, bf16[24,3072]{1,0:T(8,128)(2,1)}, u32[]{:S(2)}, u32[]{:S(2)}) collective-permute-start(bf16[24,3072]{1,0:T(8,128)(2,1)} %get-tuple-element.236.refs_0_), channel_id=1, source_target_pairs={{0,16},{8,24},{16,0},{24,8},{1,17},{9,25},{17,1},{25,9},{2,18},{10... | collective-permute-start | bytes 442376 | tf_op jit(solution)/shard_map/ppermute | solution.py:448
  62.4 13.8 %collective-permute-start = (bf16[24,3072]{1,0:T(8,128)(2,1)}, bf16[24,3072]{1,0:T(8,128)(2,1)}, u32[]{:S(2)}, u32[]{:S(2)}) collective-permute-start(bf16[24,3072]{1,0:T(8,128)(2,1)} %get-tuple-element.236.refs_0_), channel_id=1, source_target_pairs={{0,8},{8,16},{16,24},{24,0},{1,9},{9,17},{17,25},{25,1},{2,10},{10... | collective-permute-start | bytes 442376 | tf_op jit(solution)/shard_map/ppermute | solution.py:448
  79.5 15.7 %collective-permute-start.24 = (bf16[4,24,3840]{2,1,0:T(8,128)(2,1)}, bf16[4,24,3840]{2,1,0:T(8,128)(2,1)}, u32[]{:S(2)}, u32[]{:S(2)}) collective-permute-start(bf16[4,24,3840]{2,1,0:T(8,128)(2,1)} %shard_map.292.refs_0_), channel_id=1, source_target_pairs={{0,1},{1,0},{2,3},{3,2},{4,5},{5,4},{6,7},{7,6},{8,9},{9,8},{10,11... | collective-permute-start | bytes 2211848 | tf_op jit(solution)/shard_map/ppermute | solution.py:452
  79.6 15.5 %collective-permute-start.26 = (bf16[4,24,3840]{2,1,0:T(8,128)(2,1)}, bf16[4,24,3840]{2,1,0:T(8,128)(2,1)}, u32[]{:S(2)}, u32[]{:S(2)}) collective-permute-start(bf16[4,24,3840]{2,1,0:T(8,128)(2,1)} %collective-permute-done.21.refs_2_), channel_id=1, source_target_pairs={{0,1},{1,0},{2,3},{3,2},{4,5},{5,4},{6,7},{7,6},{8,9},{9,8},{10,11... | collective-permute-start | bytes 2211848 | tf_op jit(solution)/shard_map/ppermute | solution.py:452
  80.0 15.2 %collective-permute-start.25 = (bf16[4,24,3840]{2,1,0:T(8,128)(2,1)}, bf16[4,24,3840]{2,1,0:T(8,128)(2,1)}, u32[]{:S(2)}, u32[]{:S(2)}) collective-permute-start(bf16[4,24,3840]{2,1,0:T(8,128)(2,1)} %collective-permute-done.20.refs_1_), channel_id=1, source_target_pairs={{0,1},{1,0},{2,3},{3,2},{4,5},{5,4},{6,7},{7,6},{8,9},{9,8},{10,11... | collective-permute-start | bytes 2211848 | tf_op jit(solution)/shard_map/ppermute | solution.py:452
  80.1 15.0 %collective-permute-start.23 = (bf16[4,24,3840]{2,1,0:T(8,128)(2,1)}, bf16[4,24,3840]{2,1,0:T(8,128)(2,1)}, u32[]{:S(2)}, u32[]{:S(2)}) collective-permute-start(bf16[4,24,3840]{2,1,0:T(8,128)(2,1)} %collective-permute-done.20.refs_1_), channel_id=1, source_target_pairs={{0,4},{1,3},{2,6},{3,1},{4,0},{5,7},{6,2},{7,5},{8,12},{9,11},{10,... | collective-permute-start | bytes 2211848 | tf_op jit(solution)/shard_map/ppermute | solution.py:464
  80.6 14.5 %collective-permute-start.22 = (bf16[4,24,2176]{2,1,0:T(8,128)(2,1)}, bf16[4,24,2176]{2,1,0:T(8,128)(2,1)}, u32[]{:S(2)}, u32[]{:S(2)}) collective-permute-start(bf16[4,24,2176]{2,1,0:T(8,128)(2,1)} %collective-permute-done.15.refs_1_), channel_id=1, source_target_pairs={{0,8},{8,16},{16,24},{24,0},{1,9},{9,17},{17,25},{25,1},{2,10},{10... | collective-permute-start | bytes 1253384 | tf_op jit(solution)/shard_map/ppermute | solution.py:448
  95.3 16.4 %collective-permute-start.29 = (bf16[4,24,3072]{2,1,0:T(8,128)(2,1)}, bf16[4,24,3072]{2,1,0:T(8,128)(2,1)}, u32[]{:S(2)}, u32[]{:S(2)}) collective-permute-start(bf16[4,24,3072]{2,1,0:T(8,128)(2,1)} %shard_map.295.refs_0_), channel_id=1, source_target_pairs={{0,4},{1,3},{2,6},{3,1},{4,0},{5,7},{6,2},{7,5},{8,12},{9,11},{10,... | collective-permute-start | bytes 1769480 | tf_op jit(solution)/shard_map/ppermute | solution.py:464
  96.1 15.7 %collective-permute-start.28 = (bf16[4,24,3072]{2,1,0:T(8,128)(2,1)}, bf16[4,24,3072]{2,1,0:T(8,128)(2,1)}, u32[]{:S(2)}, u32[]{:S(2)}) collective-permute-start(bf16[4,24,3072]{2,1,0:T(8,128)(2,1)} %shard_map.295.refs_0_), channel_id=1, source_target_pairs={{0,2},{1,5},{2,0},{3,7},{4,6},{5,1},{6,4},{7,3},{8,10},{9,13},{10,... | collective-permute-start | bytes 1769480 | tf_op jit(solution)/shard_map/ppermute | solution.py:460
  202.7 17.8 %collective-permute-start.59 = (bf16[4,4,24,3072]{3,2,1,0:T(8,128)(2,1)}, bf16[4,4,24,3072]{3,2,1,0:T(8,128)(2,1)}, u32[]{:S(2)}, u32[]{:S(2)}) collective-permute-start(bf16[4,4,24,3072]{3,2,1,0:T(8,128)(2,1)} %bitcast.72), channel_id=1, source_target_pairs={{0,1},{1,0},{2,3},{3,2},{4,5},{5,4},{6,7},{7,6},{8,9},{9,8},{10,11... | collective-permute-start | bytes 7077896 | tf_op jit(solution)/shard_map/ppermute | solution.py:452
  205.4 18.1 %collective-permute-start.58 = (bf16[2,4,96,768]{3,2,1,0:T(8,128)(2,1)}, bf16[2,4,96,768]{3,2,1,0:T(8,128)(2,1)}, u32[]{:S(2)}, u32[]{:S(2)}) collective-permute-start(bf16[2,4,96,768]{3,2,1,0:T(8,128)(2,1)} %shard_map.312), channel_id=1, source_target_pairs={{0,2},{1,5},{2,0},{3,7},{4,6},{5,1},{6,4},{7,3},{8,10},{9,13},{10,... | collective-permute-start | bytes 3538952 | tf_op jit(solution)/shard_map/ppermute | solution.py:460
  207.7 15.5 %collective-permute-start.61 = (bf16[4,48,768]{2,1,0:T(8,128)(2,1)}, bf16[4,48,768]{2,1,0:T(8,128)(2,1)}, u32[]{:S(2)}, u32[]{:S(2)}) collective-permute-start(bf16[4,48,768]{2,1,0:T(8,128)(2,1)} %shard_map.314.refs_0_), channel_id=1, source_target_pairs={{0,24},{8,0},{16,8},{24,16},{1,25},{9,1},{17,9},{25,17},{2,26},{10... | collective-permute-start | bytes 884744 | tf_op jit(solution)/shard_map/ppermute | solution.py:448
  209.6 13.9 %collective-permute-start.60 = (bf16[4,48,768]{2,1,0:T(8,128)(2,1)}, bf16[4,48,768]{2,1,0:T(8,128)(2,1)}, u32[]{:S(2)}, u32[]{:S(2)}) collective-permute-start(bf16[4,48,768]{2,1,0:T(8,128)(2,1)} %shard_map.314.refs_0_), channel_id=1, source_target_pairs={{0,8},{8,16},{16,24},{24,0},{1,9},{9,17},{17,25},{25,1},{2,10},{10... | collective-permute-start | bytes 884744 | tf_op jit(solution)/shard_map/ppermute | solution.py:448
  223.5 17.1 %collective-permute-start.62 = (bf16[2,4,24,3072]{3,2,1,0:T(8,128)(2,1)}, bf16[2,4,24,3072]{3,2,1,0:T(8,128)(2,1)}, u32[]{:S(2)}, u32[]{:S(2)}) collective-permute-start(bf16[2,4,24,3072]{3,2,1,0:T(8,128)(2,1)} %shard_map.313), channel_id=1, source_target_pairs={{0,2},{1,5},{2,0},{3,7},{4,6},{5,1},{6,4},{7,3},{8,10},{9,13},{10,... | collective-permute-start | bytes 3538952 | tf_op jit(solution)/shard_map/ppermute | solution.py:460
  224.8 15.8 %collective-permute-start.63 = (bf16[4,48,768]{2,1,0:T(8,128)(2,1)}, bf16[4,48,768]{2,1,0:T(8,128)(2,1)}, u32[]{:S(2)}, u32[]{:S(2)}) collective-permute-start(bf16[4,48,768]{2,1,0:T(8,128)(2,1)} %shard_map.314.refs_0_), channel_id=1, source_target_pairs={{0,16},{8,24},{16,0},{24,8},{1,17},{9,25},{17,1},{25,9},{2,18},{10... | collective-permute-start | bytes 884744 | tf_op jit(solution)/shard_map/ppermute | solution.py:448
  257.1 17.0 %collective-permute-start.67 = (bf16[2,4,24,3200]{3,2,1,0:T(8,128)(2,1)}, bf16[2,4,24,3200]{3,2,1,0:T(8,128)(2,1)}, u32[]{:S(2)}, u32[]{:S(2)}) collective-permute-start(bf16[2,4,24,3200]{3,2,1,0:T(8,128)(2,1)} %shard_map.318), channel_id=1, source_target_pairs={{0,2},{1,5},{2,0},{3,7},{4,6},{5,1},{6,4},{7,3},{8,10},{9,13},{10,... | collective-permute-start | bytes 3686408 | tf_op jit(solution)/shard_map/ppermute | solution.py:460
  257.8 14.8 %collective-permute-start.68 = (bf16[4,4,48,768]{3,2,1,0:T(8,128)(2,1)}, bf16[4,4,48,768]{3,2,1,0:T(8,128)(2,1)}, u32[]{:S(2)}, u32[]{:S(2)}) collective-permute-start(bf16[4,4,48,768]{3,2,1,0:T(8,128)(2,1)} %shard_map.319.mine_ref), channel_id=1, source_target_pairs={{0,1},{1,0},{2,3},{3,2},{4,5},{5,4},{6,7},{7,6},{8,9},{9,8},{10,11... | collective-permute-start | bytes 3538952 | tf_op jit(solution)/shard_map/ppermute | solution.py:452
  277.6 15.7 %collective-permute-start.76 = (bf16[24,3072]{1,0:T(8,128)(2,1)}, bf16[24,3072]{1,0:T(8,128)(2,1)}, u32[]{:S(2)}, u32[]{:S(2)}) collective-permute-start(bf16[24,3072]{1,0:T(8,128)(2,1)} %get-tuple-element.371), channel_id=1, source_target_pairs={{0,8},{8,16},{16,24},{24,0},{1,9},{9,17},{17,25},{25,1},{2,10},{10... | collective-permute-start | bytes 442376 | tf_op jit(solution)/shard_map/ppermute | solution.py:448
  279.8 14.7 %collective-permute-start.77 = (bf16[24,3072]{1,0:T(8,128)(2,1)}, bf16[24,3072]{1,0:T(8,128)(2,1)}, u32[]{:S(2)}, u32[]{:S(2)}) collective-permute-start(bf16[24,3072]{1,0:T(8,128)(2,1)} %get-tuple-element.372), channel_id=1, source_target_pairs={{0,16},{8,24},{16,0},{24,8},{1,17},{9,25},{17,1},{25,9},{2,18},{10... | collective-permute-start | bytes 442376 | tf_op jit(solution)/shard_map/ppermute | solution.py:448
  (59 other events, 405.5 us)
